TPU v7x, 256 devices: a whole 4x4x8 slice. The times are simulated.
256 devices in a mesh: user: 16 (over x, y), loader: 16 (over z, core).
Axes of the slice: x: 4, y: 4, z: 8, core: 2. Of those that a mesh axis runs over, the one named last changes fastest.
Arguments:
- history_items: bfloat16 [256, 128, 1024], P(('user', 'loader')), may hold values from -6 to 6
- history_events: int32 [256, 128], P(('user', 'loader')), may hold values from 0 to 63
- history_lengths: int32 [256], P(('user', 'loader')), may hold values from 1 to 128, 20480 in all
- action_table: float32 [64, 1024], replicated, may hold values from -6 to 6
- mix_weight: bfloat16 [1024, 4096], P('loader'), may hold values from -0.1875 to 0.1875
- out_weight: bfloat16 [1024, 1024], P('loader'), may hold values from -0.1875 to 0.1875
- query_weight: bfloat16 [1024, 1024], replicated, may hold values from -0.1875 to 0.1875
- score_weight: float32 [1024], replicated, may hold values from -0.375 to 0.375
- self_weight: float32 [1024], replicated, may hold values from -0.1875 to 0.1875
- candidates: bfloat16 [1024, 128, 1024], P(('user', 'loader')), may hold values from -24 to 24
- block_owner: int32 [1024, 1], P(('user', 'loader')), may hold values from 0 to 15; in each aligned block of 4 rows (0 to 3, 4 to 7, ...) at most 2 rows name the same one
- row_counts: int32 [1024], P(('user', 'loader')), may hold values from 64 to 128
- labels: float32 [1024, 128], P(('user', 'loader')), may hold values from 0 to 1
Outputs:
- scores: float32 [1024, 128], P(('user', 'loader'))
- row_grads: bfloat16 [1024, 128, 1024], P(('user', 'loader'))
- query_grad: float32 [1024, 1024], P('loader')
Inputs may be any that keep to these rules, and one draw needn't show every extreme that they name: `block_owner`: no index is named by more than 2 of one device's 4 blocks, and in some device one index is named by exactly 2.
All inputs are finite; a program needn't handle non-finite values. No bound on the sum of `history_lengths` on one device may be relied on, other than what follows from the above.
Results may differ from a plain program's by a relative error of at most 0.017.
Values may be sent and summed in bfloat16 or wider, within the bound.
No kernel may reach another device: no remote copies, remote signals or barrier semaphores. Data moves between devices by JAX's collectives and lax.ppermute only.
A program may use at most 128 MiB of HBM per device.

v0:
```python
import math

import jax
import jax.numpy as jnp
from jax import lax
from jax.sharding import PartitionSpec as P

HEADS = 8
HIST = 128


def encode_user(items, events, length, action_table, mix_full, out_full):
    hist_len, width = items.shape
    head_dim = width // HEADS
    onehot = (
        events[:, None] == jnp.arange(action_table.shape[0], dtype=jnp.int32)[None, :]
    ).astype(jnp.float32)
    base = items.astype(jnp.float32) + jnp.dot(
        onehot, action_table, precision=lax.Precision.HIGHEST
    )
    normed = (base * lax.rsqrt(jnp.mean(base * base, -1, keepdims=True) + 1e-06)).astype(
        jnp.bfloat16
    )
    projected = jax.nn.silu(jnp.dot(normed, mix_full, preferred_element_type=jnp.float32))
    gate = projected[:, :width]
    values = projected[:, width : 2 * width].astype(jnp.bfloat16).reshape(hist_len, HEADS, head_dim)
    queries = (
        projected[:, 2 * width : 3 * width].astype(jnp.bfloat16).reshape(hist_len, HEADS, head_dim)
    )
    keys = projected[:, 3 * width :].astype(jnp.bfloat16).reshape(hist_len, HEADS, head_dim)
    logits = jnp.einsum(
        "ihd,jhd->hij", queries, keys, preferred_element_type=jnp.float32
    ) / math.sqrt(head_dim)
    positions = jnp.arange(hist_len, dtype=jnp.int32)
    causal = positions[None, :] <= positions[:, None]
    weights = jnp.where(causal[None], jax.nn.silu(logits) / HIST, 0.0).astype(jnp.bfloat16)
    mixed = jnp.einsum("hij,jhd->ihd", weights, values, preferred_element_type=jnp.float32).reshape(
        hist_len, width
    )
    gated = (mixed * lax.rsqrt(jnp.mean(mixed * mixed, -1, keepdims=True) + 1e-06) * gate).astype(
        jnp.bfloat16
    )
    encoded = base + jnp.dot(gated, out_full, preferred_element_type=jnp.float32)
    active = positions < length
    return jnp.where(active[:, None], encoded, 0.0).astype(jnp.bfloat16)


def cross_attend(query_rows, keys, score_weight, lead):
    count, rows, width = query_rows.shape
    head_dim = width // HEADS
    hist_len = keys.shape[-2]
    query_heads = query_rows.reshape(count, rows, HEADS, head_dim)
    key_heads = keys.reshape(keys.shape[:-1] + (HEADS, head_dim))
    logits = jnp.einsum(
        "nrhd," + lead + "jhd->nhrj", query_heads, key_heads, preferred_element_type=jnp.float32
    ) / math.sqrt(head_dim)
    weights = (jax.nn.silu(logits) / hist_len).astype(jnp.bfloat16)
    attended = jnp.einsum(
        "nhrj," + lead + "jhd->nrhd", weights, key_heads, preferred_element_type=jnp.float32
    ).reshape(count, rows, width)
    partial_value = jnp.sum(attended * score_weight, -1).astype(jnp.bfloat16)
    along = jnp.sum(key_heads.astype(jnp.float32) * score_weight.reshape(HEADS, head_dim), -1)
    sigmoid_z = jax.nn.sigmoid(logits)
    silu_slope = sigmoid_z * (1.0 + logits * (1.0 - sigmoid_z))
    slope = (
        silu_slope * jnp.swapaxes(along, -1, -2)[..., None, :] / (hist_len * math.sqrt(head_dim))
    ).astype(jnp.bfloat16)
    direction = jnp.einsum(
        "nhrj," + lead + "jhd->nrhd", slope, key_heads, preferred_element_type=jnp.float32
    ).reshape(count, rows, width)
    return (partial_value, direction.astype(jnp.bfloat16))


def body(
    history_items,
    history_events,
    history_lengths,
    action_table,
    mix_weight,
    out_weight,
    query_weight,
    score_weight,
    self_weight,
    candidates,
    block_owner,
    row_counts,
    labels,
):
    mix_full, out_full = (
        lax.all_gather(mix_weight, "loader", axis=0, tiled=True),
        lax.all_gather(out_weight, "loader", axis=0, tiled=True),
    )
    encoded = encode_user(
        history_items[0], history_events[0], history_lengths[0], action_table, mix_full, out_full
    )
    nblocks, rows, width = candidates.shape
    queries_c = jnp.dot(
        candidates.reshape(-1, width), query_weight, preferred_element_type=jnp.float32
    )
    queries_c = queries_c.astype(jnp.bfloat16).reshape(nblocks, rows, width)
    owner = block_owner[:, 0]
    users = lax.axis_size("user")
    capacity = max(2, (2 * nblocks + users - 1) // users)
    order = jnp.arange(nblocks, dtype=jnp.int32)
    earlier = (owner[:, None] == owner[None, :]) & (order[None, :] < order[:, None])
    target = owner * capacity + jnp.sum(earlier.astype(jnp.int32), 1)
    dispatch = (target[None, :] == jnp.arange(users * capacity, dtype=jnp.int32)[:, None]).astype(
        jnp.bfloat16
    )
    outgoing = jnp.einsum("sb,brd->srd", dispatch, queries_c, preferred_element_type=jnp.float32)
    outgoing = outgoing.astype(jnp.bfloat16).reshape(users, capacity, rows, width)

    def attend_one(query_block):
        partial_value, direction = cross_attend(query_block[None], encoded, score_weight, "")
        return (partial_value[0], direction[0])

    arrived = lax.all_to_all(outgoing, "user", split_axis=0, concat_axis=0, tiled=True)
    sources = arrived.shape[0]
    slots = arrived.shape[1]
    partial_value, direction = lax.map(attend_one, arrived.reshape(sources * slots, rows, width))
    partial_value = partial_value.reshape(sources, slots, rows)
    direction = direction.reshape(sources, slots, rows, width)
    back_partial = lax.all_to_all(partial_value, "user", split_axis=0, concat_axis=0, tiled=True)
    back_direction = lax.all_to_all(direction, "user", split_axis=0, concat_axis=0, tiled=True)
    partial_blocks = jnp.einsum(
        "sb,sr->br",
        dispatch,
        back_partial.reshape(users * capacity, rows),
        preferred_element_type=jnp.float32,
    )
    direction_blocks = jnp.einsum(
        "sb,srd->brd",
        dispatch,
        back_direction.reshape(users * capacity, rows, width),
        preferred_element_type=jnp.float32,
    )
    direction_blocks = direction_blocks.astype(jnp.bfloat16)
    active = jnp.arange(rows, dtype=jnp.int32)[None, :] < row_counts[:, None]
    own_term = jnp.sum(candidates.astype(jnp.float32) * self_weight, -1)
    scores = jnp.where(active, partial_blocks + own_term, 0.0)
    error = jnp.where(active, jax.nn.sigmoid(scores) - labels, 0.0)
    query_slope = (error[..., None] * direction_blocks.astype(jnp.float32)).astype(jnp.bfloat16)
    flat_slope = query_slope.reshape(-1, width)
    back = jnp.einsum(
        "rk,dk->rd", flat_slope, query_weight, preferred_element_type=jnp.float32
    ).reshape(nblocks, rows, width)
    row_grads = (error[..., None] * self_weight + back).astype(jnp.bfloat16)
    weight_part = jnp.einsum(
        "rd,rk->dk", candidates.reshape(-1, width), flat_slope, preferred_element_type=jnp.float32
    )
    grad_share = lax.psum_scatter(
        weight_part.astype(jnp.bfloat16), "loader", scatter_dimension=0, tiled=True
    )
    query_grad = lax.psum(grad_share, "user").astype(jnp.float32)
    return (scores, row_grads, query_grad)


def solution(mesh):
    placed = (
        P(("user", "loader"), None, None),
        P(("user", "loader"), None),
        P(("user", "loader")),
        P(),
        P("loader", None),
        P("loader", None),
        P(),
        P(),
        P(),
        P(("user", "loader"), None, None),
        P(("user", "loader"), None),
        P(("user", "loader")),
        P(("user", "loader"), None),
    )
    return jax.shard_map(
        body,
        mesh=mesh,
        in_specs=placed,
        out_specs=(
            P(("user", "loader"), None),
            P(("user", "loader"), None, None),
            P("loader", None),
        ),
        check_vma=False,
    )
```

profile of v0, /device:TPU:2, one launch (start us, length us, event | category | flops | bytes accessed | tf_op | source)
XLA Modules:
  0.0 730.5 jit_solution(17824366087650619377)
XLA Ops:
  9.5 2.5 convolution_convert_fusion.2
  12.0 4.8 convolution_convert_fusion.1
  16.8 13.4 %reshape.164 = bf16[16,2,128,1024]{3,1,0,2:T(2,128)(2,1)} reshape(bf16[32,128,1024]{2,0,1:T(8,128)(2,1)} %convolution_convert_fusion.1) | data formatting | bytes 16777216 | tf_op jit(solution)/shard_map/reshape | solution.py:111
  30.2 8.0 %copy.114 = bf16[16,2,128,1024]{3,1,2,0:T(2,128)(2,1)} copy(bf16[16,2,128,1024]{3,1,0,2:T(2,128)(2,1)} %reshape.164) | data formatting | bytes 16777216 | tf_op jit(solution)/shard_map/reshape | solution.py:111
  38.2 7.6 %all-to-all-start = ((bf16[16,2,128,1024]{3,1,2,0:T(2,128)(2,1)}), bf16[16,2,128,1024]{3,1,2,0:T(2,128)(2,1)}, u32[]{:S(2)}, u32[]{:S(2)}) async-start(bf16[16,2,128,1024]{3,1,2,0:T(2,128)(2,1)} %copy.114), calls=%async_computation | async-start | bytes 16777216 | tf_op jit(solution)/shard_map/all_to_all | solution.py:117
  47.9 102.7 %all-to-all-done = bf16[16,2,128,1024]{3,1,2,0:T(2,128)(2,1)} async-done(((bf16[16,2,128,1024]{3,1,2,0:T(2,128)(2,1)}), bf16[16,2,128,1024]{3,1,2,0:T(2,128)(2,1)}, u32[]{:S(2)}, u32[]{:S(2)}) %all-to-all-start) | async-done | bytes 8388640 | tf_op jit(solution)/shard_map/all_to_all | solution.py:117
  150.6 21.2 %copy.133 = bf16[16,2,128,1024]{2,3,1,0:T(8,128)(2,1)} copy(bf16[16,2,128,1024]{3,1,2,0:T(2,128)(2,1)} %all-to-all-done) | data formatting | bytes 16777216 | tf_op jit(solution)/shard_map/reshape | solution.py:120
  171.7 6.1 fusion.54
  178.8 2.3 fusion.21
  181.1 1.2 copy.135
  182.4 2.3 fusion.17
  184.8 135.1 %while.12 = (s32[]{:T(128)}, bf16[32,128]{1,0:T(8,128)(2,1)}, bf16[32,128,1024]{1,2,0:T(8,128)(2,1)}, bf16[32,128,1024]{1,2,0:T(8,128)(2,1)}, bf16[128,1024]{0,1...) while((s32[]{:T(128)}, bf16[32,128]{1,0:T(8,128)(2,1)}, bf16[32,128,1024]{1,2,0:T(8,128)(2,1)}, ...), condition=%wide.region_6.7_spmd, body=%wide.region_3.6_spmd.sunk | while | flops 103676800 | bytes 4211561 | solution.py:120
  185.1 1.0 constant_dynamic-slice_fusion.2
  187.1 1.3 dynamic_update_slice.12
  191.3 1.3 dynamic_update_slice.12
  195.5 1.3 dynamic_update_slice.12
  197.7 1.0 constant_dynamic-slice_fusion.2
  199.7 1.3 dynamic_update_slice.12
  203.9 1.3 dynamic_update_slice.12
  206.1 1.0 constant_dynamic-slice_fusion.2
  208.2 1.3 dynamic_update_slice.12
  210.4 1.0 constant_dynamic-slice_fusion.2
  212.4 1.3 dynamic_update_slice.12
  214.6 1.0 constant_dynamic-slice_fusion.2
  216.6 1.3 dynamic_update_slice.12
  220.8 1.3 dynamic_update_slice.12
  223.0 1.0 constant_dynamic-slice_fusion.2
  225.0 1.3 dynamic_update_slice.12
  229.2 1.3 dynamic_update_slice.12
  233.4 1.3 dynamic_update_slice.12
  237.6 1.3 dynamic_update_slice.12
  241.8 1.3 dynamic_update_slice.12
  246.0 1.3 dynamic_update_slice.12
  250.2 1.3 dynamic_update_slice.12
  254.4 1.3 dynamic_update_slice.12
  258.7 1.3 dynamic_update_slice.12
  262.9 1.3 dynamic_update_slice.12
  267.1 1.3 dynamic_update_slice.12
  271.4 1.3 dynamic_update_slice.12
  275.6 1.3 dynamic_update_slice.12
  279.9 1.3 dynamic_update_slice.12
  284.1 1.3 dynamic_update_slice.12
  288.3 1.3 dynamic_update_slice.12
  292.6 1.3 dynamic_update_slice.12
  296.8 1.3 dynamic_update_slice.12
  301.0 1.3 dynamic_update_slice.12
  305.3 1.3 dynamic_update_slice.12
  309.5 1.3 dynamic_update_slice.12
  313.7 1.3 dynamic_update_slice.12
  317.9 1.3 dynamic_update_slice.12
  320.0 51.1 %all-to-all-start.1 = ((bf16[16,2,128]{2,1,0:T(2,128)(2,1)}), bf16[16,2,128]{2,1,0:T(2,128)(2,1)S(1)}, u32[]{:S(2)}, u32[]{:S(2)}) async-start(bf16[16,2,128]{2,1,0:T(2,128)(2,1)} %bitcast.30), calls=%async_computation.1 | async-start | bytes 16384 | tf_op jit(solution)/shard_map/all_to_all | solution.py:123
  371.1 21.2 %copy.125 = bf16[16,2,128,1024]{3,1,2,0:T(2,128)(2,1)} copy(bf16[16,2,128,1024]{2,3,1,0:T(8,128)(2,1)} %bitcast.143) | data formatting | bytes 16777216 | tf_op jit(solution)/shard_map/reshape | solution.py:122
  392.3 7.4 %all-to-all-start.2 = ((bf16[16,2,128,1024]{3,1,2,0:T(2,128)(2,1)}), bf16[16,2,128,1024]{3,1,2,0:T(2,128)(2,1)}, u32[]{:S(2)}, u32[]{:S(2)}) async-start(bf16[16,2,128,1024]{3,1,2,0:T(2,128)(2,1)} %copy.125), calls=%async_computation.2 | async-start | bytes 16777216 | tf_op jit(solution)/shard_map/all_to_all | solution.py:124
  401.0 105.0 %all-to-all-done.2 = bf16[16,2,128,1024]{3,1,2,0:T(2,128)(2,1)} async-done(((bf16[16,2,128,1024]{3,1,2,0:T(2,128)(2,1)}), bf16[16,2,128,1024]{3,1,2,0:T(2,128)(2,1)}, u32[]{:S(2)}, u32[]{:S(2)}) %all-to-all-start.2) | async-done | bytes 8388640 | tf_op jit(solution)/shard_map/all_to_all | solution.py:124
  506.0 8.1 %copy.126 = bf16[16,2,128,1024]{3,1,0,2:T(2,128)(2,1)} copy(bf16[16,2,128,1024]{3,1,2,0:T(2,128)(2,1)} %all-to-all-done.2) | data formatting | bytes 16777216 | tf_op jit(solution)/shard_map/all_to_all | solution.py:124
  514.1 13.1 %reshape.173 = bf16[32,128,1024]{2,0,1:T(8,128)(2,1)} reshape(bf16[16,2,128,1024]{3,1,0,2:T(2,128)(2,1)} %copy.126) | data formatting | bytes 16777216 | tf_op jit(solution)/shard_map/reshape | solution.py:134
  527.3 4.7 fusion.44
  532.0 2.9 fusion.13
  534.9 3.9 copy.138
  538.9 87.0 %reduce-scatter.4.cloned.1.call-done = bf16[64,1024]{1,0:T(8,128)(2,1)} async-done(((bf16[1024,1024]{1,0:T(8,128)(2,1)}), bf16[64,1024]{1,0:T(8,128)(2,1)}) %reduce-scatter.4.cloned.1.call-update) | async-done | bytes 131088
  625.9 1.7 copy.139
  627.7 2.4 add_convert_fusion
  630.1 92.1 %all-reduce.2.cloned.1.call-done = bf16[64,1024]{0,1:T(8,128)(2,1)} async-done(((bf16[64,1024]{0,1:T(8,128)(2,1)}), bf16[64,1024]{0,1:T(8,128)(2,1)}) %all-reduce.2.cloned.1.call-update) | async-done | bytes 131088 | tf_op jit(solution)/shard_map/psum | solution.py:154
  722.2 1.8 copy.129
  (231 shorter events, 93.9 us)
Async XLA Ops:
  7.2 2.3 copy-start
  7.2 164.5 %all-gather.3.cloned.1.call-start = ((), (), s32[]{:S(2)}) async-start(), calls=%async_computation.4 | async-start | bytes 8912896 | tf_op jit(solution)/shard_map/all_gather | solution.py:90
  38.2 9.1 %copy-start.3 = (f32[64,1024]{1,0:T(8,128)S(1)}, f32[64,1024]{1,0:T(8,128)}, u32[]{:S(2)}) copy-start(f32[64,1024]{1,0:T(8,128)} %param.18) | copy-start | bytes 786436
  38.2 9.1 %copy-start.4 = (bf16[1,128,1024]{2,1,0:T(8,128)(2,1)S(1)}, bf16[1,128,1024]{2,1,0:T(8,128)(2,1)}, u32[]{:S(2)}) copy-start(bf16[1,128,1024]{2,1,0:T(8,128)(2,1)} %param.15) | copy-start | bytes 786436
  38.2 9.1 %copy-start.7 = (s32[1,128]{1,0:T(1,128)S(1)}, s32[1,128]{1,0:T(1,128)}, u32[]{:S(2)}) copy-start(s32[1,128]{1,0:T(1,128)} %param.16) | copy-start | bytes 1540
  38.2 112.3 %all-to-all-start = ((bf16[16,2,128,1024]{3,1,2,0:T(2,128)(2,1)}), bf16[16,2,128,1024]{3,1,2,0:T(2,128)(2,1)}, u32[]{:S(2)}, u32[]{:S(2)}) async-start(bf16[16,2,128,1024]{3,1,2,0:T(2,128)(2,1)} %copy.114), calls=%async_computation | async-start | bytes 16777216 | tf_op jit(solution)/shard_map/all_to_all | solution.py:117
  45.9 136.5 %all-gather.5.cloned.1.call-start = ((), (), s32[]{:S(2)}) async-start(), calls=%async_computation.5 | async-start | bytes 2228224 | tf_op jit(solution)/shard_map/all_gather | solution.py:91
  182.4 2.5 copy-start.5
  320.0 72.3 %all-to-all-start.1 = ((bf16[16,2,128]{2,1,0:T(2,128)(2,1)}), bf16[16,2,128]{2,1,0:T(2,128)(2,1)S(1)}, u32[]{:S(2)}, u32[]{:S(2)}) async-start(bf16[16,2,128]{2,1,0:T(2,128)(2,1)} %bitcast.30), calls=%async_computation.1 | async-start | bytes 16384 | tf_op jit(solution)/shard_map/all_to_all | solution.py:123
  392.3 7.6 %copy-start.1 = (bf16[4,128,1024]{2,1,0:T(8,128)(2,1)S(1)}, bf16[4,128,1024]{2,1,0:T(8,128)(2,1)}, u32[]{:S(2)}) copy-start(bf16[4,128,1024]{2,1,0:T(8,128)(2,1)} %param.24) | copy-start | bytes 3145732
  392.3 7.6 %copy-start.6 = (f32[1024]{0:T(1024)S(1)}, f32[1024]{0:T(1024)}, u32[]{:S(2)}) copy-start(f32[1024]{0:T(1024)} %param.23) | copy-start | bytes 12292
  392.3 7.9 %copy-start.8 = (f32[4,128]{1,0:T(4,128)S(1)}, f32[4,128]{1,0:T(4,128)}, u32[]{:S(2)}) copy-start(f32[4,128]{1,0:T(4,128)} %param.27) | copy-start | bytes 6148
  392.3 7.9 %copy-start.9 = (s32[4]{0:T(128)S(1)}, s32[4]{0:T(128)}, u32[]{:S(2)}) copy-start(s32[4]{0:T(128)} %param.26) | copy-start | bytes 52
  392.3 113.7 %all-to-all-start.2 = ((bf16[16,2,128,1024]{3,1,2,0:T(2,128)(2,1)}), bf16[16,2,128,1024]{3,1,2,0:T(2,128)(2,1)}, u32[]{:S(2)}, u32[]{:S(2)}) async-start(bf16[16,2,128,1024]{3,1,2,0:T(2,128)(2,1)} %copy.125), calls=%async_computation.2 | async-start | bytes 16777216 | tf_op jit(solution)/shard_map/all_to_all | solution.py:124
  399.7 226.2 %reduce-scatter.4.cloned.1.call-start = ((), (), s32[]{:S(2)}) async-start(), calls=%async_computation.7 | async-start | bytes 2228224
  527.3 4.7 copy-start.2
  538.9 183.3 %all-reduce.2.cloned.1.call-start = ((), (), s32[]{:S(2)}) async-start(), calls=%async_computation.6 | async-start | bytes 524288 | tf_op jit(solution)/shard_map/psum | solution.py:154
Sparse Core Ops, SparseCore 0:
  9.8 58.8 all-gather.2
  70.6 38.2 all-gather.4
  539.0 86.8 reduce-scatter.3
  629.5 92.6 all-reduce.1
where the time goes:
time: 735 us; the launch traced here: 730 us
  waiting for transfers between devices  388 us (53%)
  local copies, waits for them, and re-layouts  190 us (26%)
  starting transfers between devices  66.4 us (9%)
  matrix products  62.1 us (8%)
  between operations  14.6 us (2%)
  other arithmetic  8.5 us (1%)
    all_to_all x1, waiting for transfers between devices, body(): lax.all_to_all(direction, 'user', split_axis=0, concat_axis=0, tiled=True)  105 us
    all_to_all x1, waiting for transfers between devices, body(): lax.all_to_all(outgoing, 'user', split_axis=0, concat_axis=0, tiled=True)  103 us
    psum x1, waiting for transfers between devices, body(): query_grad = lax.psum(grad_share, 'user').astype(jnp.float32)  92.1 us
    unnamed x5, waiting for transfers between devices  88.4 us
    dynamic_update_slice x64, local copies, waits for them, and re-layouts, body(): lax.map(attend_one, arrived.reshape(sources * slots, rows, width))  64.1 us
    all_to_all x1, starting transfers between devices, body(): lax.all_to_all(partial_value, 'user', split_axis=0, concat_axis=0, tiled=...  51.1 us
    dynamic_slice x32, local copies, waits for them, and re-layouts, body(): lax.map(attend_one, arrived.reshape(sources * slots, rows, width))  31.2 us
    reshape x2, local copies, waits for them, and re-layouts, body(): outgoing.astype(jnp.bfloat16).reshape(users, capacity, rows, width)  21.4 us
  transfers between devices with their start and end apart: 7, of which 4 were waited for; matrix products, arithmetic and copies ran while one was open for 12% of the time, Pallas kernels for 0%

commit v1 on v0

v1 whole, which is shorter than its diff:
```python
import functools
import math

import jax
import jax.numpy as jnp
from jax import lax
from jax.experimental import pallas as pl
from jax.experimental.pallas import tpu as pltpu
from jax.sharding import PartitionSpec as P

HEADS = 8
HIST = 128
LANES = 128
BF = jnp.bfloat16
F32 = jnp.float32
VMEM_BYTES = 56 * 1024 * 1024


def sigmoid(v):
    return 0.5 * jnp.tanh(0.5 * v) + 0.5


def dot(a, b):
    return jnp.dot(a, b, preferred_element_type=F32)


def dot_t(a, b):
    return lax.dot_general(a, b, (((1,), (1,)), ((), ())), preferred_element_type=F32)


def split3(v):
    high = v.astype(BF)
    rest = v - high.astype(F32)
    middle = rest.astype(BF)
    low = (rest - middle.astype(F32)).astype(BF)
    return high, middle, low


def prepare_kernel(owner, packed, table, base, normed, mask):
    width = base.shape[1]
    actions = table.shape[0]
    rows = packed[0]
    tail = rows[:, width:].astype(F32)
    lane = lax.broadcasted_iota(jnp.int32, (HIST, actions), 1).astype(F32)
    onehot = jnp.where(tail[:, :actions] == lane, 1.0, 0.0).astype(BF)
    value = rows[:, :width].astype(F32)
    high, middle, low = split3(table[...])
    value = value + ((dot(onehot, low) + dot(onehot, middle)) + dot(onehot, high))
    scale = lax.rsqrt(jnp.mean(value * value, -1, keepdims=True) + 1e-06)
    base[...] = value
    normed[...] = (value * scale).astype(BF)
    position = lax.broadcasted_iota(jnp.int32, (HIST, LANES), 0).astype(F32)
    mask[...] = jnp.where(position < tail[:, LANES - 1 :], 1.0, 0.0)


def prepare(owner, packed, table):
    nblocks = owner.shape[0]
    width = table.shape[1]
    total = nblocks * HIST
    return pl.pallas_call(
        prepare_kernel,
        grid_spec=pltpu.PrefetchScalarGridSpec(
            num_scalar_prefetch=1,
            grid=(nblocks,),
            in_specs=[
                pl.BlockSpec((1, HIST, packed.shape[2]), lambda b, o: (o[b], 0, 0)),
                pl.BlockSpec(table.shape, lambda b, o: (0, 0)),
            ],
            out_specs=[
                pl.BlockSpec((HIST, width), lambda b, o: (b, 0)),
                pl.BlockSpec((HIST, width), lambda b, o: (b, 0)),
                pl.BlockSpec((HIST, LANES), lambda b, o: (b, 0)),
            ],
        ),
        out_shape=[
            jax.ShapeDtypeStruct((total, width), F32),
            jax.ShapeDtypeStruct((total, width), BF),
            jax.ShapeDtypeStruct((total, LANES), F32),
        ],
        compiler_params=pltpu.CompilerParams(vmem_limit_bytes=VMEM_BYTES),
        name="prepare",
    )(owner, packed, table)


def encode_kernel(normed, base, mask, wg, wv, wq, wk, wo, encoded, gate_s, mixed_s, ssq_s, gated_s):
    head = pl.program_id(0)
    total, width = normed.shape
    weights = jnp.concatenate([wg[...], wv[...], wq[...], wk[...]], axis=1)
    projected = dot(normed[...], weights)
    projected = projected * sigmoid(projected)
    gate_s[head] = projected[:, :LANES]
    values = projected[:, LANES : 2 * LANES].astype(BF)
    queries = projected[:, 2 * LANES : 3 * LANES].astype(BF)
    keys = projected[:, 3 * LANES :].astype(BF)
    row = lax.broadcasted_iota(jnp.int32, (HIST, HIST), 0)
    column = lax.broadcasted_iota(jnp.int32, (HIST, HIST), 1)
    causal = column <= row

    @pl.when(head == 0)
    def _():
        ssq_s[...] = jnp.zeros_like(ssq_s)

    for u in range(total // HIST):
        part = slice(u * HIST, (u + 1) * HIST)
        logits = dot_t(queries[part], keys[part]) * (1.0 / math.sqrt(LANES))
        weight = jnp.where(causal, logits * sigmoid(logits) * (1.0 / HIST), 0.0).astype(BF)
        mixed = dot(weight, values[part])
        mixed_s[head, part] = mixed
        ssq_s[part] += mixed * mixed

    @pl.when(head == pl.num_programs(0) - 1)
    def _():
        scale = lax.rsqrt(jnp.sum(ssq_s[...], -1, keepdims=True) * (1.0 / width) + 1e-06)
        for h in range(HEADS):
            gated_s[:, h * LANES : (h + 1) * LANES] = (mixed_s[h] * scale * gate_s[h]).astype(BF)
        active = mask[:, :1] > 0.0
        step = 256
        for n in range(width // step):
            cols = slice(n * step, (n + 1) * step)
            value = base[:, cols] + dot(gated_s[...], wo[:, cols])
            encoded[:, cols] = jnp.where(active, value, 0.0).astype(BF)


def encode(normed, base, mask, weights):
    total, width = normed.shape
    whole = lambda h: (0, 0)
    column = lambda group: pl.BlockSpec((width, LANES), lambda h: (0, group * HEADS + h))
    return pl.pallas_call(
        encode_kernel,
        grid=(HEADS,),
        in_specs=[
            pl.BlockSpec((total, width), whole),
            pl.BlockSpec((total, width), whole),
            pl.BlockSpec((total, LANES), whole),
            column(0),
            column(1),
            column(2),
            column(3),
            pl.BlockSpec((width, width), lambda h: (0, 4)),
        ],
        out_specs=pl.BlockSpec((total, width), whole),
        out_shape=jax.ShapeDtypeStruct((total, width), BF),
        scratch_shapes=[
            pltpu.VMEM((HEADS, total, LANES), F32),
            pltpu.VMEM((HEADS, total, LANES), F32),
            pltpu.VMEM((total, LANES), F32),
            pltpu.VMEM((total, width), BF),
        ],
        compiler_params=pltpu.CompilerParams(vmem_limit_bytes=VMEM_BYTES),
        name="encode",
    )(normed, base, mask, weights, weights, weights, weights, weights)


def cross_kernel(
    counts,
    core,
    queries,
    encoded,
    score_weight,
    own,
    labels,
    cand_t,
    scores,
    error,
    slopes,
    mine,
    other,
    slope_s,
    dir_s,
):
    block = pl.program_id(0)
    width = queries.shape[1]
    lane = lax.broadcasted_iota(jnp.int32, (HEADS, width), 1) // LANES
    head_row = lax.broadcasted_iota(jnp.int32, (HEADS, width), 0)
    spread = jnp.where(lane == head_row, score_weight[...], 0.0)
    high, middle, low = split3(spread)
    keys = encoded[...]
    along = (dot_t(low, keys) + dot_t(middle, keys)) + dot_t(high, keys)
    along_scaled = along * (1.0 / (HIST * math.sqrt(LANES)))
    total = jnp.zeros((queries.shape[0], HIST), F32)
    for h in range(HEADS):
        cols = slice(h * LANES, (h + 1) * LANES)
        key_head = keys[:, cols]
        logits = dot_t(queries[:, cols], key_head) * (1.0 / math.sqrt(LANES))
        gate = sigmoid(logits)
        product = logits * gate
        weight = (product * (1.0 / HIST)).astype(BF).astype(F32)
        total = total + weight * along[h : h + 1]
        slope = (gate + product * (1.0 - gate)) * along_scaled[h : h + 1]
        dir_s[:, cols] = dot(slope.astype(BF), key_head).astype(BF)
    partial = jnp.sum(total, -1, keepdims=True).astype(BF).astype(F32)
    partial_row = jnp.broadcast_to(partial, (HIST, HIST)).T[:1]
    active = lax.broadcasted_iota(jnp.int32, (1, HIST), 1) < counts[block]
    score = jnp.where(active, partial_row + own[0], 0.0)
    err = jnp.where(active, sigmoid(score) - labels[0], 0.0)
    scores[0] = score
    error[0] = err
    err_rows = jnp.broadcast_to(err, (HIST, HIST)).T
    for h in range(HEADS):
        cols = slice(h * LANES, (h + 1) * LANES)
        slope = (err_rows * dir_s[:, cols].astype(F32)).astype(BF)
        slopes[:, cols] = slope
        slope_s[block, :, cols] = slope

    @pl.when(block == pl.num_programs(0) - 1)
    def _():
        step = 256
        pairs, piece = mine.shape[0], mine.shape[1]
        first = core[0] == 0
        for n in range(width // step):
            cols = slice(n * step, (n + 1) * step)
            right = slope_s[:, :, cols].reshape(-1, step)
            grad = dot(cand_t[...], right)
            for p in range(pairs):
                one = grad[2 * p * piece : (2 * p + 1) * piece]
                two = grad[(2 * p + 1) * piece : (2 * p + 2) * piece]
                mine[p, :, cols] = jnp.where(first, one, two)
                other[p, :, cols] = jnp.where(first, two, one).astype(BF)


def cross(counts, core, queries, encoded, score_weight, own, labels, cand_t, pairs):
    nblocks = counts.shape[0]
    total, width = queries.shape
    rows = total // nblocks
    piece = width // (2 * pairs)
    block_rows = pl.BlockSpec((rows, width), lambda b, n, c: (b, 0))
    row = pl.BlockSpec((1, 1, rows), lambda b, n, c: (b, 0, 0))
    whole3 = lambda b, n, c: (0, 0, 0)
    return pl.pallas_call(
        cross_kernel,
        grid_spec=pltpu.PrefetchScalarGridSpec(
            num_scalar_prefetch=2,
            grid=(nblocks,),
            in_specs=[
                block_rows,
                block_rows,
                pl.BlockSpec((1, width), lambda b, n, c: (0, 0)),
                row,
                row,
                pl.BlockSpec((width, total), lambda b, n, c: (0, 0)),
            ],
            out_specs=[
                row,
                row,
                block_rows,
                pl.BlockSpec((pairs, piece, width), whole3),
                pl.BlockSpec((pairs, piece, width), whole3),
            ],
            scratch_shapes=[
                pltpu.VMEM((nblocks, rows, width), BF),
                pltpu.VMEM((rows, width), BF),
            ],
        ),
        out_shape=[
            jax.ShapeDtypeStruct((nblocks, 1, rows), F32),
            jax.ShapeDtypeStruct((nblocks, 1, rows), F32),
            jax.ShapeDtypeStruct((total, width), BF),
            jax.ShapeDtypeStruct((pairs, piece, width), F32),
            jax.ShapeDtypeStruct((pairs, piece, width), BF),
        ],
        compiler_params=pltpu.CompilerParams(vmem_limit_bytes=VMEM_BYTES),
        name="cross",
    )(counts, core, queries, encoded, score_weight, own, labels, cand_t)


def fold_kernel(mine, arrived, out):
    pairs, piece, width = mine.shape
    tall, wide = out.shape[2], out.shape[3]
    down, right = piece // tall, width // wide
    for a in range(down):
        for b in range(right):
            rows, cols = slice(a * tall, (a + 1) * tall), slice(b * wide, (b + 1) * wide)
            value = mine[:, rows, cols] + arrived[:, rows, cols].astype(F32)
            out[a * right + b] = value.astype(BF)


def fold(mine, arrived, users):
    pairs, piece, width = mine.shape
    right = math.isqrt(users)
    down = users // right
    return pl.pallas_call(
        fold_kernel,
        out_shape=jax.ShapeDtypeStruct((users, pairs, piece // down, width // right), BF),
        compiler_params=pltpu.CompilerParams(vmem_limit_bytes=VMEM_BYTES),
        name="fold",
    )(mine, arrived)


def body(
    history_items,
    history_events,
    history_lengths,
    action_table,
    mix_weight,
    out_weight,
    query_weight,
    score_weight,
    self_weight,
    candidates,
    block_owner,
    row_counts,
    labels,
):
    users = lax.axis_size("user")
    loaders = lax.axis_size("loader")
    pairs = loaders // 2
    nblocks, rows, width = candidates.shape

    shard = jnp.concatenate([mix_weight, out_weight], axis=1)
    weights = lax.all_gather(shard, "loader", axis=0, tiled=True)
    actions = action_table.shape[0]
    packed = jnp.concatenate(
        [
            history_items[0],
            jnp.broadcast_to(history_events[0][:, None].astype(BF), (HIST, actions)),
            jnp.broadcast_to(history_lengths[0].astype(BF), (HIST, LANES - actions)),
        ],
        axis=1,
    )
    packed = lax.all_to_all(
        jnp.broadcast_to(packed[None], (users,) + packed.shape), "user", 0, 0, tiled=True
    )

    flat = candidates.reshape(-1, width)
    queries = jnp.dot(flat, query_weight, preferred_element_type=F32).astype(BF)
    cand_t = flat.T
    own = jnp.sum(candidates.astype(F32) * self_weight, -1)

    owner = block_owner[:, 0]
    base, normed, mask = prepare(owner, packed, action_table)
    encoded = encode(normed, base, mask, weights)
    core = lax.rem(lax.axis_index("loader"), 2)[None].astype(jnp.int32)
    scores, error, slopes, mine, other = cross(
        row_counts,
        core,
        queries,
        encoded,
        score_weight[None],
        own[:, None],
        labels[:, None],
        cand_t,
        pairs,
    )

    arrived = lax.ppermute(other, "loader", [(i, i ^ 1) for i in range(loaders)])
    pieces = lax.all_to_all(fold(mine, arrived, users), "user", 0, 0, tiled=True)
    pieces = jnp.sum(pieces.astype(F32), 0).astype(BF)
    groups = [[c + 2 * i for i in range(pairs)] for c in range(2)]
    pieces = lax.all_to_all(pieces, "loader", 0, 0, axis_index_groups=groups, tiled=True)
    piece = jnp.sum(pieces.astype(F32), 0).astype(BF)
    pieces = lax.all_to_all(
        jnp.broadcast_to(piece[None], (users,) + piece.shape), "user", 0, 0, tiled=True
    )
    right = math.isqrt(users)
    tall, wide = piece.shape
    query_grad = pieces.reshape(users // right, right, tall, wide).transpose(0, 2, 1, 3)
    query_grad = query_grad.reshape(users // right * tall, right * wide).astype(F32)

    back = lax.dot_general(slopes, query_weight, (((1,), (1,)), ((), ())), preferred_element_type=F32)
    row_grads = (error.reshape(-1)[:, None] * self_weight + back).astype(BF)
    return (scores[:, 0], row_grads.reshape(nblocks, rows, width), query_grad)


def solution(mesh):
    placed = (
        P(("user", "loader"), None, None),
        P(("user", "loader"), None),
        P(("user", "loader")),
        P(),
        P("loader", None),
        P("loader", None),
        P(),
        P(),
        P(),
        P(("user", "loader"), None, None),
        P(("user", "loader"), None),
        P(("user", "loader")),
        P(("user", "loader"), None),
    )
    return jax.shard_map(
        body,
        mesh=mesh,
        in_specs=placed,
        out_specs=(
            P(("user", "loader"), None),
            P(("user", "loader"), None, None),
            P("loader", None),
        ),
        check_vma=False,
    )
```

time: 735 us -> 200 us (0.27)
  waiting for transfers between devices: 388 us -> 62.1 us
  local copies, waits for them, and re-layouts: 190 us -> 6.84 us
  matrix products: 62.1 us -> 5.73 us
  blocking collectives: 0 us -> 54 us
  starting transfers between devices: 66.4 us -> 13.5 us
  Pallas kernels: 0 us -> 39.1 us
    all_to_all x3 -> x2, waiting for transfers between devices: 208 us -> 59.2 us  [the longest x1 56.3 us: body(): lax.all_to_all(jnp.broadcast_to(packed[None], (users,) + packed.shape), '...]
    psum x1 -> x0, waiting for transfers between devices: 92.1 us -> none  [body(): query_grad = lax.psum(grad_share, 'user').astype(jnp.float32)]
    unnamed x5 -> x1, waiting for transfers between devices: 88.4 us -> 0.02 us
    reshape x7 -> x1, local copies, waits for them, and re-layouts: 78.3 us -> 1.31 us  [body(): flat = candidates.reshape(-1, width)]
    dynamic_update_slice x64 -> x0, local copies, waits for them, and re-layouts: 64.1 us -> none  [body(): lax.map(attend_one, arrived.reshape(sources * slots, rows, width))]
    dot_general x106 -> x2, matrix products: 62.1 us -> 5.73 us  [the longest x1 3.48 us: body(): lax.dot_general(slopes, query_weight, (((1,), (1,)), ((), ())), preferred...]
    all_to_all x0 -> x2, blocking collectives: none -> 54 us  [the longest x1 37.4 us: body(): lax.all_to_all(fold(mine, arrived, users), 'user', 0, 0, tiled=True)]
    all_to_all x3 -> x2, starting transfers between devices: 66.1 us -> 13.4 us  [the longest x1 7.61 us: body(): lax.all_to_all(jnp.broadcast_to(packed[None], (users,) + packed.shape), '...]
  transfers between devices with their start and end apart: 7 -> 4, of which waited for: 4 -> 3; matrix products, arithmetic and copies ran while one was open for 12% -> 6% of each run, Pallas kernels for 0% -> 3%
where the time goes in v1:
time: 200 us
  waiting for transfers between devices  62.1 us (31%)
  blocking collectives  54 us (27%)
  Pallas kernels  39.1 us (20%)
  between operations  14.8 us (7%)
  starting transfers between devices  13.5 us (7%)
  local copies, waits for them, and re-layouts  6.84 us (3%)
  matrix products  5.73 us (3%)
  other arithmetic  3.86 us (2%)
    all_to_all x1, waiting for transfers between devices, body(): lax.all_to_all(jnp.broadcast_to(packed[None], (users,) + packed.shape), '...  56.3 us
    all_to_all x1, blocking collectives, body(): lax.all_to_all(fold(mine, arrived, users), 'user', 0, 0, tiled=True)  37.4 us
    pallas_call x1, Pallas kernels, encode(): pl.pallas_call(encode_kernel, grid=(HEADS,), in_specs=[pl.BlockSpec((tota...  17.3 us
    all_to_all x1, blocking collectives, body(): lax.all_to_all(pieces, 'loader', 0, 0, axis_index_groups=groups, tiled=True)  16.6 us
    pallas_call x1, Pallas kernels, cross(): pl.pallas_call(cross_kernel, grid_spec=pltpu.PrefetchScalarGridSpec(num_s...  13.5 us
    all_to_all x1, starting transfers between devices, body(): lax.all_to_all(jnp.broadcast_to(packed[None], (users,) + packed.shape), '...  7.61 us
    all_to_all x1, starting transfers between devices, body(): lax.all_to_all(jnp.broadcast_to(piece[None], (users,) + piece.shape), 'us...  5.74 us
    pallas_call x1, Pallas kernels, prepare(): pl.pallas_call(prepare_kernel, grid_spec=pltpu.PrefetchScalarGridSpec(num...  5.24 us
  transfers between devices with their start and end apart: 4, of which 3 were waited for; matrix products, arithmetic and copies ran while one was open for 6% of the time, Pallas kernels for 3%

profile of v1, /device:TPU:2, one launch (start us, length us, event | category | flops | bytes accessed | tf_op | source)
XLA Modules:
  0.0 199.9 jit_solution(3706169627128966762)
XLA Ops:
  7.2 0.0 copy-start
  7.2 0.0 copy-start.3
  7.2 0.0 all-gather.2.cloned.1.call-start
  7.2 2.2 %pad_maximum_fusion = bf16[64,5120]{1,0:T(8,128)(2,1)} fusion(bf16[64,1024]{1,0:T(8,128)(2,1)} %param.18, bf16[64,4096]{1,0:T(8,128)(2,1)} %param.17), kind=kLoop, calls=%fused_computation.3 | loop fusion | flops 1310720 | bytes 1310720 | tf_op jit(solution)/shard_map/concatenate | solution.py:309
  9.4 0.0 all-gather.2.cloned.1.call-update
  10.1 0.7 convert_bitcast_fusion.1
  10.7 0.1 broadcast_in_dim.17
  10.8 0.0 copy-done.3
  10.8 0.1 concatenate.6
  10.9 2.7 %broadcast_in_dim.37 = bf16[16,128,1152]{2,1,0:T(8,128)(2,1)} broadcast(bf16[128,1152]{1,0:T(8,128)(2,1)S(1)} %concatenate.6), dimensions={1,2} | broadcast | bytes 5013504 | tf_op jit(solution)/shard_map/broadcast_in_dim | solution.py:321
  13.7 0.0 copy-start.1
  13.7 7.6 %all-to-all-start = ((bf16[16,128,1152]{2,1,0:T(8,128)(2,1)}), bf16[16,128,1152]{2,1,0:T(8,128)(2,1)}, u32[]{:S(2)}, u32[]{:S(2)}) async-start(bf16[16,128,1152]{2,1,0:T(8,128)(2,1)} %broadcast_in_dim.37), calls=%async_computation | async-start | bytes 9437184 | tf_op jit(solution)/shard_map/all_to_all | solution.py:320
  21.3 0.0 copy-start.4
  21.3 0.0 copy-done.1
  21.3 1.3 copy.22
  22.6 0.0 copy-done.4
  22.6 0.9 multiply_reduce_fusion
  23.5 0.0 copy-done
  23.5 2.2 %convolution_convert_fusion.queries = bf16[512,1024]{1,0:T(8,128)(2,1)} fusion(bf16[512,1024]{1,0:T(8,128)(2,1)S(1)} %bitcast.26, bf16[1024,1024]{1,0:T(8,128)(2,1)S(1)} %copy-done), kind=kOutput, calls=%fused_computation.2 | convolution fusion | flops 1074266112 | bytes 4194304 | tf_op jit(solution)/shard_map/dot_general | solution.py:325
  25.8 56.3 %all-to-all-done.packed = bf16[16,128,1152]{2,1,0:T(8,128)(2,1)} async-done(((bf16[16,128,1152]{2,1,0:T(8,128)(2,1)}), bf16[16,128,1152]{2,1,0:T(8,128)(2,1)}, u32[]{:S(2)}, u32[]{:S(2)}) %all-to-all-start) | async-done | bytes 4718624 | tf_op jit(solution)/shard_map/all_to_all | solution.py:320
  82.1 5.2 %prepare.1 = (f32[512,1024]{1,0:T(8,128)}, bf16[512,1024]{1,0:T(8,128)(2,1)}, f32[512,128]{1,0:T(8,128)}) custom-call(s32[4]{0:T(128)} %bitcast.35, bf16[16,128,1152]{2,1,0:T(8,128)(2,1)} %all-to-all-done.packed, f32[64,1024]{1,0:T(8,128)} %table.1), custom_call_target="tpu_custom_call" | custom-call | tf_op jit(solution)/shard_map/prepare/pallas_call | solution.py:60
  87.3 0.0 all-gather.2.cloned.1.call-done.wg.wv.wq.wk.wo
  87.3 17.3 %encode.1.encoded = bf16[512,1024]{1,0:T(8,128)(2,1)} custom-call(bf16[512,1024]{1,0:T(8,128)(2,1)} %get-tuple-element.11.normed, f32[512,1024]{1,0:T(8,128)} %get-tuple-element.12.base, f32[512,128]{1,0:T(8,128)} %get-tuple-element.13.mask, bf16[1024,5120]{1,0:T(8,128)(2,1)} %all-gather.2.cloned.1.call-done.wg.wv.wq.wk.wo, ...), custom_call_target="tpu_custom_call" | custom-call | tf_op jit(solution)/shard_map/encode/pallas_call | solution.py:128
  104.6 13.5 %cross.1 = (f32[4,1,128]{2,1,0:T(1,128)}, f32[4,1,128]{2,1,0:T(1,128)}, bf16[512,1024]{1,0:T(8,128)(2,1)}, f32[8,64,1024]{2,1,0:T(8,128)}, bf16[8,64,1024]{2,1,0:T(8,128)(2,1)}) custom-call(s32[4]{0:T(128)} %counts.1, s32[1]{0:T(128)} %bitcast.core, bf16[512,1024]{1,0:T(8,128)(2,1)} %convolution_convert_fusion.queries, bf16[512,1024]{1,0:T(8,128)(2,1)} %encode.1.encoded, ...), custom_call_target="tpu_custom_call" | custom-call | tf_op jit(solution)/shard_map/cross/pallas_call | solution.py:229
  118.1 0.1 collective-permute-start
  118.2 2.9 %collective-permute-done.arrived = bf16[8,64,1024]{2,1,0:T(8,128)(2,1)S(1)} collective-permute-done((bf16[8,64,1024]{2,1,0:T(8,128)(2,1)}, bf16[8,64,1024]{2,1,0:T(8,128)(2,1)S(1)}, u32[]{:S(2)}, u32[]{:S(2)}) %collective-permute-start) | collective-permute-done | bytes 1048608 | tf_op jit(solution)/shard_map/ppermute | solution.py:345
  121.1 0.0 copy-start.2
  121.1 1.0 copy-done.2
  122.1 3.0 %fold.1 = bf16[16,8,16,256]{3,2,1,0:T(8,128)(2,1)} custom-call(f32[8,64,1024]{2,1,0:T(8,128)} %get-tuple-element.17.mine, bf16[8,64,1024]{2,1,0:T(8,128)(2,1)} %copy-done.2), custom_call_target="tpu_custom_call" | custom-call | tf_op jit(solution)/shard_map/fold/pallas_call | solution.py:281
  125.1 0.0 copy-start.5
  125.1 37.4 %all_to_all.20 = bf16[16,8,16,256]{3,2,1,0:T(8,128)(2,1)S(1)} all-to-all(bf16[16,8,16,256]{3,2,1,0:T(8,128)(2,1)} %fold.1), channel_id=1, replica_groups=mesh['user'=16,'loader'=16] {'user'}, dimensions={0} | all-to-all | bytes 2097152 | tf_op jit(solution)/shard_map/all_to_all | solution.py:346
  162.5 0.1 reduce_sum.34
  162.6 16.6 %all_to_all.21 = bf16[8,16,256]{2,1,0:T(8,128)(2,1)S(1)} all-to-all(bf16[8,16,256]{2,1,0:T(8,128)(2,1)S(1)} %reduce_sum.34), channel_id=1, replica_groups={{0,2,4,6,8,10,12,14},{1,3,5,7,9,11,13,15},{16,18,20,22,24,26,28,30},{17..., dimensions={0} | all-to-all | bytes 131072 | tf_op jit(solution)/shard_map/all_to_all | solution.py:349
  179.2 0.7 broadcast_in_dim.41
  179.9 5.7 %all-to-all-start.3 = ((bf16[16,16,256]{2,1,0:T(8,128)(2,1)}), bf16[16,16,256]{2,1,0:T(8,128)(2,1)S(1)}, u32[]{:S(2)}, u32[]{:S(2)}) async-start(bf16[16,16,256]{2,1,0:T(8,128)(2,1)} %broadcast_in_dim.41), calls=%async_computation.3 | async-start | bytes 262144 | tf_op jit(solution)/shard_map/all_to_all | solution.py:351
  185.6 0.0 copy-done.5
  185.7 3.5 %add_convert_fusion = bf16[512,1024]{1,0:T(8,128)(2,1)} fusion(bf16[512,1024]{1,0:T(8,128)(2,1)} %get-tuple-element.16, bf16[1024,1024]{1,0:T(8,128)(2,1)S(1)} %copy-done, f32[1024]{0:T(1024)S(1)} %copy-done.4, f32[512]{0:T(512)S(1)} %bitcast.37), kind=kOutput, calls=%fused_computation | convolution fusion | flops 1075314688 | bytes 4200448 | tf_op jit(solution)/shard_map/dot_general | solution.py:359
  189.1 2.9 %all-to-all-done.3 = bf16[16,16,256]{2,1,0:T(8,128)(2,1)S(1)} async-done(((bf16[16,16,256]{2,1,0:T(8,128)(2,1)}), bf16[16,16,256]{2,1,0:T(8,128)(2,1)S(1)}, u32[]{:S(2)}, u32[]{:S(2)}) %all-to-all-start.3) | async-done | bytes 131104 | tf_op jit(solution)/shard_map/all_to_all | solution.py:351
  192.1 0.2 copy.21
  192.3 0.8 copy.23
  (3 shorter events, 0.0 us)
Async XLA Ops:
  7.2 16.3 %copy-start = (bf16[1024,1024]{1,0:T(8,128)(2,1)S(1)}, bf16[1024,1024]{1,0:T(8,128)(2,1)}, u32[]{:S(2)}) copy-start(bf16[1024,1024]{1,0:T(8,128)(2,1)} %param.19) | copy-start | bytes 6291460
  7.2 3.7 %copy-start.3 = (bf16[1,128,1024]{2,1,0:T(8,128)(2,1)S(1)}, bf16[1,128,1024]{2,1,0:T(8,128)(2,1)}, u32[]{:S(2)}) copy-start(bf16[1,128,1024]{2,1,0:T(8,128)(2,1)} %param.13) | copy-start | bytes 786436
  7.2 80.1 %all-gather.2.cloned.1.call-start = ((), (), s32[]{:S(2)}) async-start(), calls=%async_computation.4 | async-start | bytes 11141120 | tf_op jit(solution)/shard_map/all_gather | solution.py:310
  13.7 7.6 %copy-start.1 = (bf16[4,128,1024]{2,1,0:T(8,128)(2,1)S(1)}, bf16[4,128,1024]{2,1,0:T(8,128)(2,1)}, u32[]{:S(2)}) copy-start(bf16[4,128,1024]{2,1,0:T(8,128)(2,1)} %param.22) | copy-start | bytes 3145732
  13.7 68.4 %all-to-all-start = ((bf16[16,128,1152]{2,1,0:T(8,128)(2,1)}), bf16[16,128,1152]{2,1,0:T(8,128)(2,1)}, u32[]{:S(2)}, u32[]{:S(2)}) async-start(bf16[16,128,1152]{2,1,0:T(8,128)(2,1)} %broadcast_in_dim.37), calls=%async_computation | async-start | bytes 9437184 | tf_op jit(solution)/shard_map/all_to_all | solution.py:320
  21.3 1.3 copy-start.4
  118.1 3.0 %collective-permute-start = (bf16[8,64,1024]{2,1,0:T(8,128)(2,1)}, bf16[8,64,1024]{2,1,0:T(8,128)(2,1)S(1)}, u32[]{:S(2)}, u32[]{:S(2)}) collective-permute-start(bf16[8,64,1024]{2,1,0:T(8,128)(2,1)} %get-tuple-element.18), channel_id=1, source_target_pairs={{0,1},{1,0},{2,3},{3,2},{4,5},{5,4},{6,7},{7,6},{8,9},{9,8},{10,11... | collective-permute-start | bytes 3145736 | tf_op jit(solution)/shard_map/ppermute | solution.py:345
  121.1 1.0 copy-start.2
  125.1 60.6 %copy-start.5 = (f32[4,1,128]{2,1,0:T(1,128)S(1)}, f32[4,1,128]{2,1,0:T(1,128)}, u32[]{:S(2)}) copy-start(f32[4,1,128]{2,1,0:T(1,128)} %get-tuple-element.15) | copy-start | bytes 6148
  179.9 12.2 %all-to-all-start.3 = ((bf16[16,16,256]{2,1,0:T(8,128)(2,1)}), bf16[16,16,256]{2,1,0:T(8,128)(2,1)S(1)}, u32[]{:S(2)}, u32[]{:S(2)}) async-start(bf16[16,16,256]{2,1,0:T(8,128)(2,1)} %broadcast_in_dim.41), calls=%async_computation.3 | async-start | bytes 262144 | tf_op jit(solution)/shard_map/all_to_all | solution.py:351
Sparse Core Ops, SparseCore 0:
  9.9 68.7 all-gather.1

commit v2 on v1

--- a/solution.py
+++ b/solution.py
@@ -36,10 +36,10 @@
     return high, middle, low
 
 
-def prepare_kernel(owner, packed, table, base, normed, mask):
+def prepare_kernel(place_a, place_b, half_a, half_b, table, base, normed, mask):
     width = base.shape[1]
     actions = table.shape[0]
-    rows = packed[0]
+    rows = jnp.concatenate([half_a[0], half_b[0]], axis=0)
     tail = rows[:, width:].astype(F32)
     lane = lax.broadcasted_iota(jnp.int32, (HIST, actions), 1).astype(F32)
     onehot = jnp.where(tail[:, :actions] == lane, 1.0, 0.0).astype(BF)
@@ -53,23 +53,24 @@
     mask[...] = jnp.where(position < tail[:, LANES - 1 :], 1.0, 0.0)
 
 
-def prepare(owner, packed, table):
-    nblocks = owner.shape[0]
+def prepare(place_a, place_b, half_a, half_b, table):
+    nblocks = place_a.shape[0]
     width = table.shape[1]
     total = nblocks * HIST
     return pl.pallas_call(
         prepare_kernel,
         grid_spec=pltpu.PrefetchScalarGridSpec(
-            num_scalar_prefetch=1,
+            num_scalar_prefetch=2,
             grid=(nblocks,),
             in_specs=[
-                pl.BlockSpec((1, HIST, packed.shape[2]), lambda b, o: (o[b], 0, 0)),
-                pl.BlockSpec(table.shape, lambda b, o: (0, 0)),
+                pl.BlockSpec((1,) + half_a.shape[1:], lambda b, p, q: (p[b], 0, 0)),
+                pl.BlockSpec((1,) + half_b.shape[1:], lambda b, p, q: (q[b], 0, 0)),
+                pl.BlockSpec(table.shape, lambda b, p, q: (0, 0)),
             ],
             out_specs=[
-                pl.BlockSpec((HIST, width), lambda b, o: (b, 0)),
-                pl.BlockSpec((HIST, width), lambda b, o: (b, 0)),
-                pl.BlockSpec((HIST, LANES), lambda b, o: (b, 0)),
+                pl.BlockSpec((HIST, width), lambda b, p, q: (b, 0)),
+                pl.BlockSpec((HIST, width), lambda b, p, q: (b, 0)),
+                pl.BlockSpec((HIST, LANES), lambda b, p, q: (b, 0)),
             ],
         ),
         out_shape=[
@@ -79,7 +80,7 @@
         ],
         compiler_params=pltpu.CompilerParams(vmem_limit_bytes=VMEM_BYTES),
         name="prepare",
-    )(owner, packed, table)
+    )(place_a, place_b, half_a, half_b, table)
 
 
 def encode_kernel(normed, base, mask, wg, wv, wq, wk, wo, encoded, gate_s, mixed_s, ssq_s, gated_s):
@@ -286,6 +287,24 @@
     )(mine, arrived)
 
 
+def shift(array, side, dx, dy):
+    moves = []
+    for x in range(side):
+        for y in range(side):
+            moves.append(((x + dx) % side * side + (y + dy) % side, x * side + y))
+    return lax.ppermute(array, "user", moves)
+
+
+def ring(array, side, along_x):
+    move = lambda a, d: shift(a, side, d if along_x else 0, 0 if along_x else d)
+    half = array.shape[1] // 2
+    after = move(array, 1)
+    before = move(array, -1)
+    first = move(after[:, :half], 1)
+    second = move(before[:, half:], -1)
+    return jnp.stack([array, after, jnp.concatenate([first, second], axis=1), before])
+
+
 def body(
     history_items,
     history_events,
@@ -317,9 +336,12 @@
         ],
         axis=1,
     )
-    packed = lax.all_to_all(
-        jnp.broadcast_to(packed[None], (users,) + packed.shape), "user", 0, 0, tiled=True
-    )
+    side = math.isqrt(users)
+    half = HIST // 2
+    half_a = ring(packed[None, :half], side, True).reshape(side, half, -1)
+    half_b = ring(packed[None, half:], side, False).reshape(side, half, -1)
+    half_a = ring(half_a, side, False).reshape(users, half, -1)
+    half_b = ring(half_b, side, True).reshape(users, half, -1)
 
     flat = candidates.reshape(-1, width)
     queries = jnp.dot(flat, query_weight, preferred_element_type=F32).astype(BF)
@@ -327,7 +349,12 @@
     own = jnp.sum(candidates.astype(F32) * self_weight, -1)
 
     owner = block_owner[:, 0]
-    base, normed, mask = prepare(owner, packed, action_table)
+    here = lax.axis_index("user").astype(jnp.int32)
+    far_x = lax.rem(owner // side - here // side + side, side)
+    far_y = lax.rem(lax.rem(owner, side) - lax.rem(here, side) + side, side)
+    base, normed, mask = prepare(
+        far_y * side + far_x, far_x * side + far_y, half_a, half_b, action_table
+    )
     encoded = encode(normed, base, mask, weights)
     core = lax.rem(lax.axis_index("loader"), 2)[None].astype(jnp.int32)
     scores, error, slopes, mine, other = cross(

time: 200 us -> 173 us (0.86)
  waiting for transfers between devices: 62.1 us -> 27 us
  blocking collectives: 54 us -> 35.1 us
  starting transfers between devices: 13.5 us -> 25.4 us
  other arithmetic: 3.86 us -> 13.6 us
  local copies, waits for them, and re-layouts: 6.84 us -> 11.3 us
    all_to_all x1 -> x0, waiting for transfers between devices: 56.3 us -> none  [body(): lax.all_to_all(jnp.broadcast_to(packed[None], (users,) + packed.shape), '...]
    ppermute x0 -> x16, starting transfers between devices: none -> 19.3 us  [shift(): return lax.ppermute(array, 'user', moves)]
    all_to_all x1, blocking collectives: 37.4 us -> 22.7 us  [body(): lax.all_to_all(fold(mine, arrived, users), 'user', 0, 0, tiled=True)]
    ppermute x0 -> x16, waiting for transfers between devices: none -> 11.9 us  [shift(): return lax.ppermute(array, 'user', moves)]
    all_gather x1, waiting for transfers between devices: 0.01 us -> 9.59 us  [body(): weights = lax.all_gather(shard, 'loader', axis=0, tiled=True)]
    another operation x0 -> x8, other arithmetic: none -> 8.69 us  [ring(): jnp.stack([array, after, jnp.concatenate([first, second], axis=1), before])]
    all_to_all x1 -> x0, starting transfers between devices: 7.61 us -> none  [body(): lax.all_to_all(jnp.broadcast_to(packed[None], (users,) + packed.shape), '...]
    all_to_all x1, blocking collectives: 16.6 us -> 12.4 us  [body(): lax.all_to_all(pieces, 'loader', 0, 0, axis_index_groups=groups, tiled=True)]
  transfers between devices with their start and end apart: 4 -> 19, of which waited for: 3 -> 8; matrix products, arithmetic and copies ran while one was open for 6% -> 13% of each run, Pallas kernels for 3% -> 3%
where the time goes in v2:
time: 173 us; the launch traced here: 172 us
  Pallas kernels  39.2 us (23%)
  blocking collectives  35.1 us (20%)
  waiting for transfers between devices  27 us (16%)
  starting transfers between devices  25.4 us (15%)
  between operations  14.9 us (9%)
  other arithmetic  13.6 us (8%)
  local copies, waits for them, and re-layouts  11.3 us (7%)
  matrix products  5.73 us (3%)
    all_to_all x1, blocking collectives, body(): lax.all_to_all(fold(mine, arrived, users), 'user', 0, 0, tiled=True)  22.7 us
    ppermute x16, starting transfers between devices, shift(): return lax.ppermute(array, 'user', moves)  19.3 us
    pallas_call x1, Pallas kernels, encode(): pl.pallas_call(encode_kernel, grid=(HEADS,), in_specs=[pl.BlockSpec((tota...  17.3 us
    pallas_call x1, Pallas kernels, cross(): pl.pallas_call(cross_kernel, grid_spec=pltpu.PrefetchScalarGridSpec(num_s...  13.5 us
    all_to_all x1, blocking collectives, body(): lax.all_to_all(pieces, 'loader', 0, 0, axis_index_groups=groups, tiled=True)  12.4 us
    ppermute x16, waiting for transfers between devices, shift(): return lax.ppermute(array, 'user', moves)  11.9 us
    all_gather x1, waiting for transfers between devices, body(): weights = lax.all_gather(shard, 'loader', axis=0, tiled=True)  9.59 us
    another operation x8, other arithmetic, ring(): jnp.stack([array, after, jnp.concatenate([first, second], axis=1), before])  8.69 us
  transfers between devices with their start and end apart: 19, of which 8 were waited for; matrix products, arithmetic and copies ran while one was open for 13% of the time, Pallas kernels for 3%

profile of v2, /device:TPU:2, one launch (start us, length us, event | category | flops | bytes accessed | tf_op | source)
XLA Modules:
  0.0 172.3 jit_solution(11282656835707866214)
XLA Ops:
  7.2 0.0 all-gather.2.cloned.1.call-start
  7.2 2.1 %pad_maximum_fusion.2 = bf16[64,5120]{1,0:T(8,128)(2,1)} fusion(bf16[64,1024]{1,0:T(8,128)(2,1)} %param.18, bf16[64,4096]{1,0:T(8,128)(2,1)} %param.17), kind=kLoop, calls=%fused_computation.5 | loop fusion | flops 1310720 | bytes 1310720 | tf_op jit(solution)/shard_map/concatenate | solution.py:328
  9.4 0.0 all-gather.2.cloned.1.call-update
  10.1 0.7 convert_bitcast_fusion.1
  10.7 0.1 broadcast_in_dim.35
  10.8 0.1 concatenate.18
  11.0 1.7 collective-permute-start.10
  12.6 1.7 collective-permute-start.8
  14.3 2.3 %collective-permute-start = (bf16[1,64,1152]{2,1,0:T(8,128)(2,1)S(1)}, bf16[1,64,1152]{2,1,0:T(8,128)(2,1)S(1)}, u32[]{:S(2)}, u32[]{:S(2)}) collective-permute-start(bf16[1,64,1152]{2,1,0:T(8,128)(2,1)S(1)} %get-tuple-element.27), channel_id=1, source_target_pairs={{64,0},{80,16},{96,32},{112,48},{128,64},{144,80},{160,96},{176,11... | collective-permute-start | bytes 442376 | tf_op jit(solution)/shard_map/ppermute | solution.py:295
  16.6 1.4 collective-permute-done.10
  17.9 0.4 collective-permute-start.11
  18.3 3.0 %collective-permute-start.9 = (bf16[1,32,1152]{2,1,0:T(8,128)(2,1)S(1)}, bf16[1,32,1152]{2,1,0:T(8,128)(2,1)S(1)}, u32[]{:S(2)}, u32[]{:S(2)}) collective-permute-start(bf16[1,32,1152]{2,1,0:T(8,128)(2,1)S(1)} %slice.46), channel_id=1, source_target_pairs={{16,0},{32,16},{48,32},{0,48},{80,64},{96,80},{112,96},{64,112},{1... | collective-permute-start | bytes 221192 | tf_op jit(solution)/shard_map/ppermute | solution.py:295
  21.4 0.5 multiply_add_fusion
  21.9 1.8 %collective-permute-start.1 = (bf16[1,32,1152]{2,1,0:T(8,128)(2,1)S(1)}, bf16[1,32,1152]{2,1,0:T(8,128)(2,1)S(1)}, u32[]{:S(2)}, u32[]{:S(2)}) collective-permute-start(bf16[1,32,1152]{2,1,0:T(8,128)(2,1)S(1)} %slice.41), channel_id=1, source_target_pairs={{64,0},{80,16},{96,32},{112,48},{128,64},{144,80},{160,96},{176,11... | collective-permute-start | bytes 221192 | tf_op jit(solution)/shard_map/ppermute | solution.py:295
  23.8 0.7 copy-done.15
  24.5 0.4 collective-permute-start.3
  24.8 2.0 %fusion.1 = (bf16[1,4,64,1152]{3,2,1,0:T(8,128)(2,1)}, bf16[4,64,1152]{2,1,0:T(8,128)(2,1)S(1)}) fusion(bf16[1,1,64,1152]{3,2,1,0:T(8,128)(2,1)} %bitcast.90, bf16[1,1,64,1152]{3,2,1,0:T(8,128)(2,1)S(1)} %maximum_bitcast_fusion.3, bf16[1,1,64,1152]{3,2,1,0:T(8,128)(2,1)} %bitcast.91, bf16[1,1,64,1152]{3,2,1,0:T(8,128)(2,1)S(1)} %get-tuple-element.26), kind=kLoop, calls=%fused_computation.18 | loop fusion | flops 884736 | bytes 1769472 | tf_op jit(solution)/shard_map/stack;reshape | solution.py:305
  26.8 1.7 collective-permute-start.12
  28.5 0.3 collective-permute-start.14
  28.8 0.1 collective-permute-done.3
  28.9 0.9 fusion.3
  29.9 2.0 %collective-permute-start.4 = (bf16[4,64,1152]{2,1,0:T(8,128)(2,1)S(1)}, bf16[4,64,1152]{2,1,0:T(8,128)(2,1)S(1)}, u32[]{:S(2)}, u32[]{:S(2)}) collective-permute-start(bf16[4,64,1152]{2,1,0:T(8,128)(2,1)S(1)} %get-tuple-element.25), channel_id=1, source_target_pairs={{16,0},{32,16},{48,32},{0,48},{80,64},{96,80},{112,96},{64,112},{1... | collective-permute-start | bytes 1769480 | tf_op jit(solution)/shard_map/ppermute | solution.py:295
  31.9 0.0 collective-permute-start.6
  31.9 2.2 %convolution_convert_fusion.queries = bf16[512,1024]{1,0:T(8,128)(2,1)} fusion(bf16[512,1024]{1,0:T(8,128)(2,1)S(1)} %bitcast.79, bf16[1024,1024]{1,0:T(8,128)(2,1)S(1)} %copy-done), kind=kOutput, calls=%fused_computation.4 | convolution fusion | flops 1074266112 | bytes 4194304 | tf_op jit(solution)/shard_map/dot_general | solution.py:347
  34.1 6.0 %collective-permute-done.12 = bf16[4,64,1152]{2,1,0:T(8,128)(2,1)S(1)} collective-permute-done((bf16[4,64,1152]{2,1,0:T(8,128)(2,1)S(1)}, bf16[4,64,1152]{2,1,0:T(8,128)(2,1)S(1)}, u32[]{:S(2)}, u32[]{:S(2)}) %collective-permute-start.12) | collective-permute-done | bytes 589856 | tf_op jit(solution)/shard_map/ppermute | solution.py:295
  40.2 0.8 copy-done.4
  41.0 0.8 slice.48
  41.8 1.8 %collective-permute-start.13 = (bf16[4,32,1152]{2,1,0:T(8,128)(2,1)}, bf16[4,32,1152]{2,1,0:T(8,128)(2,1)}, u32[]{:S(2)}, u32[]{:S(2)}) collective-permute-start(bf16[4,32,1152]{2,1,0:T(8,128)(2,1)} %slice.48), channel_id=1, source_target_pairs={{64,0},{80,16},{96,32},{112,48},{128,64},{144,80},{160,96},{176,11... | collective-permute-start | bytes 884744 | tf_op jit(solution)/shard_map/ppermute | solution.py:295
  43.5 0.8 copy-done.6
  44.4 0.7 slice.49
  45.1 0.3 collective-permute-start.15
  45.4 0.5 multiply_add_fusion.1.place_a
  45.9 0.8 copy-done.8
  46.7 0.7 slice.43
  47.4 1.5 collective-permute-start.5
  48.9 0.8 copy-done.10
  49.8 0.7 slice.44
  50.5 0.5 collective-permute-start.7
  51.0 0.9 multiply_reduce_fusion
  51.9 1.3 copy.22
  53.2 0.6 collective-permute-done.15
  53.8 1.1 maximum_bitcast_fusion.1
  54.9 3.8 %collective-permute-done.7 = bf16[4,32,1152]{2,1,0:T(8,128)(2,1)} collective-permute-done((bf16[4,32,1152]{2,1,0:T(8,128)(2,1)}, bf16[4,32,1152]{2,1,0:T(8,128)(2,1)}, u32[]{:S(2)}, u32[]{:S(2)}) %collective-permute-start.7) | collective-permute-done | bytes 294944 | tf_op jit(solution)/shard_map/ppermute | solution.py:295
  58.8 1.1 maximum_bitcast_fusion
  59.9 1.9 %pad_maximum_fusion.1 = bf16[4,4,64,1152]{3,2,1,0:T(8,128)(2,1)} fusion(bf16[1,4,64,1152]{3,2,1,0:T(8,128)(2,1)S(1)} %bitcast.83, bf16[1,4,64,1152]{3,2,1,0:T(8,128)(2,1)S(1)} %maximum_bitcast_fusion.1, bf16[1,4,64,1152]{3,2,1,0:T(8,128)(2,1)S(1)} %bitcast.82, bf16[1,4,64,1152]{3,2,1,0:T(8,128)(2,1)S(1)} %copy-done.2), kind=kLoop, calls=%fused_computation.1 | loop fusion | flops 3538944 | bytes 4718592 | tf_op jit(solution)/shard_map/stack | solution.py:305
  61.8 0.1 copy-done.11
  61.9 1.7 %pad_maximum_fusion = bf16[4,4,64,1152]{3,2,1,0:T(8,128)(2,1)} fusion(bf16[1,4,64,1152]{3,2,1,0:T(8,128)(2,1)S(1)} %bitcast.85, bf16[1,4,64,1152]{3,2,1,0:T(8,128)(2,1)S(1)} %maximum_bitcast_fusion, bf16[1,4,64,1152]{3,2,1,0:T(8,128)(2,1)S(1)} %bitcast.84, bf16[1,4,64,1152]{3,2,1,0:T(8,128)(2,1)S(1)} %copy-done.3), kind=kLoop, calls=%fused_computation | loop fusion | flops 3538944 | bytes 4718592 | tf_op jit(solution)/shard_map/stack | solution.py:305
  63.6 5.4 %prepare.1 = (f32[512,1024]{1,0:T(8,128)}, bf16[512,1024]{1,0:T(8,128)(2,1)}, f32[512,128]{1,0:T(8,128)}) custom-call(s32[4]{0:T(128)} %multiply_add_fusion.1.place_a, s32[4]{0:T(128)} %get-tuple-element.19.place_b, bf16[16,64,1152]{2,1,0:T(8,128)(2,1)} %bitcast.78, bf16[16,64,1152]{2,1,0:T(8,128)(2,1)} %bitcast.77, f32[64,1024]{1,0:T(8,128)} %table.1), custom_call_target="tpu_custom_call" | custom-call | tf_op jit(solution)/shard_map/prepare/pallas_call | solution.py:60
  69.0 9.6 %all-gather.2.cloned.1.call-done.wg.wv.wq.wk.wo = bf16[1024,5120]{1,0:T(8,128)(2,1)} async-done(((bf16[64,5120]{1,0:T(8,128)(2,1)}), bf16[1024,5120]{1,0:T(8,128)(2,1)}) %all-gather.2.cloned.1.call-update) | async-done | bytes 10485776 | tf_op jit(solution)/shard_map/all_gather | solution.py:329
  78.6 17.3 %encode.1.encoded = bf16[512,1024]{1,0:T(8,128)(2,1)} custom-call(bf16[512,1024]{1,0:T(8,128)(2,1)} %get-tuple-element.11.normed, f32[512,1024]{1,0:T(8,128)} %get-tuple-element.12.base, f32[512,128]{1,0:T(8,128)} %get-tuple-element.13.mask, bf16[1024,5120]{1,0:T(8,128)(2,1)} %all-gather.2.cloned.1.call-done.wg.wv.wq.wk.wo, ...), custom_call_target="tpu_custom_call" | custom-call | tf_op jit(solution)/shard_map/encode/pallas_call | solution.py:129
  95.9 13.5 %cross.1 = (f32[4,1,128]{2,1,0:T(1,128)}, f32[4,1,128]{2,1,0:T(1,128)}, bf16[512,1024]{1,0:T(8,128)(2,1)}, f32[8,64,1024]{2,1,0:T(8,128)}, bf16[8,64,1024]{2,1,0:T(8,128)(2,1)}) custom-call(s32[4]{0:T(128)} %counts.1, s32[1]{0:T(128)} %bitcast.core, bf16[512,1024]{1,0:T(8,128)(2,1)} %convolution_convert_fusion.queries, bf16[512,1024]{1,0:T(8,128)(2,1)} %encode.1.encoded, ...), custom_call_target="tpu_custom_call" | custom-call | tf_op jit(solution)/shard_map/cross/pallas_call | solution.py:230
  109.4 0.3 collective-permute-start.16
  109.8 2.6 %collective-permute-done.16.arrived = bf16[8,64,1024]{2,1,0:T(8,128)(2,1)S(1)} collective-permute-done((bf16[8,64,1024]{2,1,0:T(8,128)(2,1)}, bf16[8,64,1024]{2,1,0:T(8,128)(2,1)S(1)}, u32[]{:S(2)}, u32[]{:S(2)}) %collective-permute-start.16) | collective-permute-done | bytes 1048608 | tf_op jit(solution)/shard_map/ppermute | solution.py:372
  112.4 1.0 copy-done.12
  113.3 3.0 %fold.1 = bf16[16,8,16,256]{3,2,1,0:T(8,128)(2,1)} custom-call(f32[8,64,1024]{2,1,0:T(8,128)} %get-tuple-element.17.mine, bf16[8,64,1024]{2,1,0:T(8,128)(2,1)} %copy-done.12), custom_call_target="tpu_custom_call" | custom-call | tf_op jit(solution)/shard_map/fold/pallas_call | solution.py:282
  116.4 22.7 %all_to_all.15 = bf16[16,8,16,256]{3,2,1,0:T(8,128)(2,1)S(1)} all-to-all(bf16[16,8,16,256]{3,2,1,0:T(8,128)(2,1)} %fold.1), channel_id=1, replica_groups=mesh['user'=16,'loader'=16] {'user'}, dimensions={0} | all-to-all | bytes 2097152 | tf_op jit(solution)/shard_map/all_to_all | solution.py:373
  139.0 0.1 reduce_sum.34
  139.2 12.4 %all_to_all.16 = bf16[8,16,256]{2,1,0:T(8,128)(2,1)S(1)} all-to-all(bf16[8,16,256]{2,1,0:T(8,128)(2,1)S(1)} %reduce_sum.34), channel_id=1, replica_groups={{0,2,4,6,8,10,12,14},{1,3,5,7,9,11,13,15},{16,18,20,22,24,26,28,30},{17..., dimensions={0} | all-to-all | bytes 131072 | tf_op jit(solution)/shard_map/all_to_all | solution.py:376
  151.7 0.7 broadcast_in_dim.42
  152.3 5.7 %all-to-all-start.2 = ((bf16[16,16,256]{2,1,0:T(8,128)(2,1)}), bf16[16,16,256]{2,1,0:T(8,128)(2,1)S(1)}, u32[]{:S(2)}, u32[]{:S(2)}) async-start(bf16[16,16,256]{2,1,0:T(8,128)(2,1)} %broadcast_in_dim.42), calls=%async_computation.2 | async-start | bytes 262144 | tf_op jit(solution)/shard_map/all_to_all | solution.py:378
  158.0 3.5 %add_convert_fusion = bf16[512,1024]{1,0:T(8,128)(2,1)} fusion(bf16[512,1024]{1,0:T(8,128)(2,1)} %get-tuple-element.16, bf16[1024,1024]{1,0:T(8,128)(2,1)S(1)} %copy-done, f32[1024]{0:T(1024)S(1)} %copy-done.20, f32[512]{0:T(512)S(1)} %bitcast.98), kind=kOutput, calls=%fused_computation.2 | convolution fusion | flops 1075314688 | bytes 4200448 | tf_op jit(solution)/shard_map/dot_general | solution.py:386
  161.5 2.9 %all-to-all-done.2 = bf16[16,16,256]{2,1,0:T(8,128)(2,1)S(1)} async-done(((bf16[16,16,256]{2,1,0:T(8,128)(2,1)}), bf16[16,16,256]{2,1,0:T(8,128)(2,1)S(1)}, u32[]{:S(2)}, u32[]{:S(2)}) %all-to-all-start.2) | async-done | bytes 131104 | tf_op jit(solution)/shard_map/all_to_all | solution.py:378
  164.5 0.2 copy.21
  164.7 0.8 copy.23
  (61 shorter events, 0.3 us)
Async XLA Ops:
  7.2 24.7 %copy-start = (bf16[1024,1024]{1,0:T(8,128)(2,1)S(1)}, bf16[1024,1024]{1,0:T(8,128)(2,1)}, u32[]{:S(2)}) copy-start(bf16[1024,1024]{1,0:T(8,128)(2,1)} %param.19) | copy-start | bytes 6291460
  7.2 3.6 %copy-start.19 = (bf16[1,128,1024]{2,1,0:T(8,128)(2,1)S(1)}, bf16[1,128,1024]{2,1,0:T(8,128)(2,1)}, u32[]{:S(2)}) copy-start(bf16[1,128,1024]{2,1,0:T(8,128)(2,1)} %param.13) | copy-start | bytes 786436
  7.2 14.2 %copy-start.21 = (s32[4,1]{0,1:T(1,128)S(1)}, s32[4,1]{0,1:T(1,128)}, u32[]{:S(2)}) copy-start(s32[4,1]{0,1:T(1,128)} %param.23) | copy-start | bytes 52
  7.2 71.4 %all-gather.2.cloned.1.call-start = ((), (), s32[]{:S(2)}) async-start(), calls=%async_computation.3 | async-start | bytes 11141120 | tf_op jit(solution)/shard_map/all_gather | solution.py:329
  11.0 6.9 %collective-permute-start.10 = (bf16[1,64,1152]{2,1,0:T(8,128)(2,1)S(1)}, bf16[1,64,1152]{2,1,0:T(8,128)(2,1)S(1)}, u32[]{:S(2)}, u32[]{:S(2)}) collective-permute-start(bf16[1,64,1152]{2,1,0:T(8,128)(2,1)S(1)} %get-tuple-element.28), channel_id=1, source_target_pairs={{48,0},{0,16},{16,32},{32,48},{112,64},{64,80},{80,96},{96,112},{1... | collective-permute-start | bytes 442376 | tf_op jit(solution)/shard_map/ppermute | solution.py:295
  12.6 5.7 %collective-permute-start.8 = (bf16[1,64,1152]{2,1,0:T(8,128)(2,1)S(1)}, bf16[1,64,1152]{2,1,0:T(8,128)(2,1)S(1)}, u32[]{:S(2)}, u32[]{:S(2)}) collective-permute-start(bf16[1,64,1152]{2,1,0:T(8,128)(2,1)S(1)} %get-tuple-element.28), channel_id=1, source_target_pairs={{16,0},{32,16},{48,32},{0,48},{80,64},{96,80},{112,96},{64,112},{1... | collective-permute-start | bytes 442376 | tf_op jit(solution)/shard_map/ppermute | solution.py:295
  14.3 7.6 %collective-permute-start = (bf16[1,64,1152]{2,1,0:T(8,128)(2,1)S(1)}, bf16[1,64,1152]{2,1,0:T(8,128)(2,1)S(1)}, u32[]{:S(2)}, u32[]{:S(2)}) collective-permute-start(bf16[1,64,1152]{2,1,0:T(8,128)(2,1)S(1)} %get-tuple-element.27), channel_id=1, source_target_pairs={{64,0},{80,16},{96,32},{112,48},{128,64},{144,80},{160,96},{176,11... | collective-permute-start | bytes 442376 | tf_op jit(solution)/shard_map/ppermute | solution.py:295
  16.6 7.2 %collective-permute-start.2 = (bf16[1,64,1152]{2,1,0:T(8,128)(2,1)S(1)}, bf16[1,64,1152]{2,1,0:T(8,128)(2,1)S(1)}, u32[]{:S(2)}, u32[]{:S(2)}) collective-permute-start(bf16[1,64,1152]{2,1,0:T(8,128)(2,1)S(1)} %get-tuple-element.27), channel_id=1, source_target_pairs={{192,0},{208,16},{224,32},{240,48},{0,64},{16,80},{32,96},{48,112}... | collective-permute-start | bytes 442376 | tf_op jit(solution)/shard_map/ppermute | solution.py:295
  17.9 5.8 %copy-start.17 = (bf16[1,64,1152]{2,1,0:T(8,128)(2,1)}, bf16[1,64,1152]{2,1,0:T(8,128)(2,1)S(1)}, u32[]{:S(2)}) copy-start(bf16[1,64,1152]{2,1,0:T(8,128)(2,1)S(1)} %collective-permute-done.10) | copy-start | bytes 442372
  17.9 6.9 %collective-permute-start.11 = (bf16[1,32,1152]{2,1,0:T(8,128)(2,1)S(1)}, bf16[1,32,1152]{2,1,0:T(8,128)(2,1)S(1)}, u32[]{:S(2)}, u32[]{:S(2)}) collective-permute-start(bf16[1,32,1152]{2,1,0:T(8,128)(2,1)S(1)} %slice.47), channel_id=1, source_target_pairs={{48,0},{0,16},{16,32},{32,48},{112,64},{64,80},{80,96},{96,112},{1... | collective-permute-start | bytes 221192 | tf_op jit(solution)/shard_map/ppermute | solution.py:295
  18.3 5.4 %copy-start.18 = (bf16[1,64,1152]{2,1,0:T(8,128)(2,1)}, bf16[1,64,1152]{2,1,0:T(8,128)(2,1)S(1)}, u32[]{:S(2)}) copy-start(bf16[1,64,1152]{2,1,0:T(8,128)(2,1)S(1)} %collective-permute-done.8) | copy-start | bytes 442372
  18.3 6.5 %collective-permute-start.9 = (bf16[1,32,1152]{2,1,0:T(8,128)(2,1)S(1)}, bf16[1,32,1152]{2,1,0:T(8,128)(2,1)S(1)}, u32[]{:S(2)}, u32[]{:S(2)}) collective-permute-start(bf16[1,32,1152]{2,1,0:T(8,128)(2,1)S(1)} %slice.46), channel_id=1, source_target_pairs={{16,0},{32,16},{48,32},{0,48},{80,64},{96,80},{112,96},{64,112},{1... | collective-permute-start | bytes 221192 | tf_op jit(solution)/shard_map/ppermute | solution.py:295
  21.9 1.9 %copy-start.13 = (bf16[1,64,1152]{2,1,0:T(8,128)(2,1)}, bf16[1,64,1152]{2,1,0:T(8,128)(2,1)S(1)}, u32[]{:S(2)}) copy-start(bf16[1,64,1152]{2,1,0:T(8,128)(2,1)S(1)} %collective-permute-done) | copy-start | bytes 442372
  21.9 6.9 %collective-permute-start.1 = (bf16[1,32,1152]{2,1,0:T(8,128)(2,1)S(1)}, bf16[1,32,1152]{2,1,0:T(8,128)(2,1)S(1)}, u32[]{:S(2)}, u32[]{:S(2)}) collective-permute-start(bf16[1,32,1152]{2,1,0:T(8,128)(2,1)S(1)} %slice.41), channel_id=1, source_target_pairs={{64,0},{80,16},{96,32},{112,48},{128,64},{144,80},{160,96},{176,11... | collective-permute-start | bytes 221192 | tf_op jit(solution)/shard_map/ppermute | solution.py:295
  23.8 0.7 copy-start.15
  24.4 4.5 %copy-start.14 = (bf16[1,64,1152]{2,1,0:T(8,128)(2,1)S(1)}, bf16[1,64,1152]{2,1,0:T(8,128)(2,1)}, u32[]{:S(2)}) copy-start(bf16[1,64,1152]{2,1,0:T(8,128)(2,1)} %copy-done.13) | copy-start | bytes 442372
  24.4 4.5 %copy-start.16 = (bf16[1,64,1152]{2,1,0:T(8,128)(2,1)S(1)}, bf16[1,64,1152]{2,1,0:T(8,128)(2,1)}, u32[]{:S(2)}) copy-start(bf16[1,64,1152]{2,1,0:T(8,128)(2,1)} %copy-done.15) | copy-start | bytes 442372
  24.4 7.4 %copy-start.1 = (bf16[4,128,1024]{2,1,0:T(8,128)(2,1)S(1)}, bf16[4,128,1024]{2,1,0:T(8,128)(2,1)}, u32[]{:S(2)}) copy-start(bf16[4,128,1024]{2,1,0:T(8,128)(2,1)} %param.22) | copy-start | bytes 3145732
  24.5 4.4 %collective-permute-start.3 = (bf16[1,32,1152]{2,1,0:T(8,128)(2,1)S(1)}, bf16[1,32,1152]{2,1,0:T(8,128)(2,1)S(1)}, u32[]{:S(2)}, u32[]{:S(2)}) collective-permute-start(bf16[1,32,1152]{2,1,0:T(8,128)(2,1)S(1)} %slice.42), channel_id=1, source_target_pairs={{192,0},{208,16},{224,32},{240,48},{0,64},{16,80},{32,96},{48,112}... | collective-permute-start | bytes 221192 | tf_op jit(solution)/shard_map/ppermute | solution.py:295
  26.8 13.4 %collective-permute-start.12 = (bf16[4,64,1152]{2,1,0:T(8,128)(2,1)S(1)}, bf16[4,64,1152]{2,1,0:T(8,128)(2,1)S(1)}, u32[]{:S(2)}, u32[]{:S(2)}) collective-permute-start(bf16[4,64,1152]{2,1,0:T(8,128)(2,1)S(1)} %get-tuple-element.23), channel_id=1, source_target_pairs={{64,0},{80,16},{96,32},{112,48},{128,64},{144,80},{160,96},{176,11... | collective-permute-start | bytes 1769480 | tf_op jit(solution)/shard_map/ppermute | solution.py:295
  28.5 15.0 %collective-permute-start.14 = (bf16[4,64,1152]{2,1,0:T(8,128)(2,1)S(1)}, bf16[4,64,1152]{2,1,0:T(8,128)(2,1)S(1)}, u32[]{:S(2)}, u32[]{:S(2)}) collective-permute-start(bf16[4,64,1152]{2,1,0:T(8,128)(2,1)S(1)} %get-tuple-element.23), channel_id=1, source_target_pairs={{192,0},{208,16},{224,32},{240,48},{0,64},{16,80},{32,96},{48,112}... | collective-permute-start | bytes 1769480 | tf_op jit(solution)/shard_map/ppermute | solution.py:295
  29.9 16.0 %collective-permute-start.4 = (bf16[4,64,1152]{2,1,0:T(8,128)(2,1)S(1)}, bf16[4,64,1152]{2,1,0:T(8,128)(2,1)S(1)}, u32[]{:S(2)}, u32[]{:S(2)}) collective-permute-start(bf16[4,64,1152]{2,1,0:T(8,128)(2,1)S(1)} %get-tuple-element.25), channel_id=1, source_target_pairs={{16,0},{32,16},{48,32},{0,48},{80,64},{96,80},{112,96},{64,112},{1... | collective-permute-start | bytes 1769480 | tf_op jit(solution)/shard_map/ppermute | solution.py:295
  31.9 17.1 %collective-permute-start.6 = (bf16[4,64,1152]{2,1,0:T(8,128)(2,1)S(1)}, bf16[4,64,1152]{2,1,0:T(8,128)(2,1)S(1)}, u32[]{:S(2)}, u32[]{:S(2)}) collective-permute-start(bf16[4,64,1152]{2,1,0:T(8,128)(2,1)S(1)} %get-tuple-element.25), channel_id=1, source_target_pairs={{48,0},{0,16},{16,32},{32,48},{112,64},{64,80},{80,96},{96,112},{1... | collective-permute-start | bytes 1769480 | tf_op jit(solution)/shard_map/ppermute | solution.py:295
  34.1 16.9 %copy-start.20 = (f32[1024]{0:T(1024)S(1)}, f32[1024]{0:T(1024)}, u32[]{:S(2)}) copy-start(f32[1024]{0:T(1024)} %param.21) | copy-start | bytes 12292
  40.2 0.8 copy-start.4
  41.8 11.5 %collective-permute-start.13 = (bf16[4,32,1152]{2,1,0:T(8,128)(2,1)}, bf16[4,32,1152]{2,1,0:T(8,128)(2,1)}, u32[]{:S(2)}, u32[]{:S(2)}) collective-permute-start(bf16[4,32,1152]{2,1,0:T(8,128)(2,1)} %slice.48), channel_id=1, source_target_pairs={{64,0},{80,16},{96,32},{112,48},{128,64},{144,80},{160,96},{176,11... | collective-permute-start | bytes 884744 | tf_op jit(solution)/shard_map/ppermute | solution.py:295
  43.5 0.8 copy-start.6
  45.1 8.7 %collective-permute-start.15 = (bf16[4,32,1152]{2,1,0:T(8,128)(2,1)}, bf16[4,32,1152]{2,1,0:T(8,128)(2,1)}, u32[]{:S(2)}, u32[]{:S(2)}) collective-permute-start(bf16[4,32,1152]{2,1,0:T(8,128)(2,1)} %slice.49), channel_id=1, source_target_pairs={{192,0},{208,16},{224,32},{240,48},{0,64},{16,80},{32,96},{48,112}... | collective-permute-start | bytes 884744 | tf_op jit(solution)/shard_map/ppermute | solution.py:295
  45.9 0.8 copy-start.8
  47.4 7.5 %collective-permute-start.5 = (bf16[4,32,1152]{2,1,0:T(8,128)(2,1)}, bf16[4,32,1152]{2,1,0:T(8,128)(2,1)}, u32[]{:S(2)}, u32[]{:S(2)}) collective-permute-start(bf16[4,32,1152]{2,1,0:T(8,128)(2,1)} %slice.43), channel_id=1, source_target_pairs={{16,0},{32,16},{48,32},{0,48},{80,64},{96,80},{112,96},{64,112},{1... | collective-permute-start | bytes 884744 | tf_op jit(solution)/shard_map/ppermute | solution.py:295
  48.9 0.8 copy-start.10
  50.5 8.2 %collective-permute-start.7 = (bf16[4,32,1152]{2,1,0:T(8,128)(2,1)}, bf16[4,32,1152]{2,1,0:T(8,128)(2,1)}, u32[]{:S(2)}, u32[]{:S(2)}) collective-permute-start(bf16[4,32,1152]{2,1,0:T(8,128)(2,1)} %slice.44), channel_id=1, source_target_pairs={{48,0},{0,16},{16,32},{32,48},{112,64},{64,80},{80,96},{96,112},{1... | collective-permute-start | bytes 884744 | tf_op jit(solution)/shard_map/ppermute | solution.py:295
  53.2 6.6 %copy-start.2 = (bf16[1,4,64,1152]{3,2,1,0:T(8,128)(2,1)S(1)}, bf16[1,4,64,1152]{3,2,1,0:T(8,128)(2,1)}, u32[]{:S(2)}) copy-start(bf16[1,4,64,1152]{3,2,1,0:T(8,128)(2,1)} %get-tuple-element.22) | copy-start | bytes 1769476
  53.2 6.7 %copy-start.5 = (bf16[4,64,1152]{2,1,0:T(8,128)(2,1)S(1)}, bf16[4,64,1152]{2,1,0:T(8,128)(2,1)}, u32[]{:S(2)}) copy-start(bf16[4,64,1152]{2,1,0:T(8,128)(2,1)} %copy-done.4) | copy-start | bytes 1769476
  53.2 6.7 %copy-start.7 = (bf16[4,64,1152]{2,1,0:T(8,128)(2,1)S(1)}, bf16[4,64,1152]{2,1,0:T(8,128)(2,1)}, u32[]{:S(2)}) copy-start(bf16[4,64,1152]{2,1,0:T(8,128)(2,1)} %copy-done.6) | copy-start | bytes 1769476
  59.9 1.9 %copy-start.3 = (bf16[1,4,64,1152]{3,2,1,0:T(8,128)(2,1)S(1)}, bf16[1,4,64,1152]{3,2,1,0:T(8,128)(2,1)}, u32[]{:S(2)}) copy-start(bf16[1,4,64,1152]{3,2,1,0:T(8,128)(2,1)} %get-tuple-element.24) | copy-start | bytes 1769476
  59.9 1.9 %copy-start.9 = (bf16[4,64,1152]{2,1,0:T(8,128)(2,1)S(1)}, bf16[4,64,1152]{2,1,0:T(8,128)(2,1)}, u32[]{:S(2)}) copy-start(bf16[4,64,1152]{2,1,0:T(8,128)(2,1)} %copy-done.8) | copy-start | bytes 1769476
  59.9 2.0 %copy-start.11 = (bf16[4,64,1152]{2,1,0:T(8,128)(2,1)S(1)}, bf16[4,64,1152]{2,1,0:T(8,128)(2,1)}, u32[]{:S(2)}) copy-start(bf16[4,64,1152]{2,1,0:T(8,128)(2,1)} %copy-done.10) | copy-start | bytes 1769476
  109.4 3.0 %collective-permute-start.16 = (bf16[8,64,1024]{2,1,0:T(8,128)(2,1)}, bf16[8,64,1024]{2,1,0:T(8,128)(2,1)S(1)}, u32[]{:S(2)}, u32[]{:S(2)}) collective-permute-start(bf16[8,64,1024]{2,1,0:T(8,128)(2,1)} %get-tuple-element.18), channel_id=1, source_target_pairs={{0,1},{1,0},{2,3},{3,2},{4,5},{5,4},{6,7},{7,6},{8,9},{9,8},{10,11... | collective-permute-start | bytes 3145736 | tf_op jit(solution)/shard_map/ppermute | solution.py:372
  112.4 1.0 copy-start.12
  116.4 41.7 %copy-start.22 = (f32[4,1,128]{2,1,0:T(1,128)S(1)}, f32[4,1,128]{2,1,0:T(1,128)}, u32[]{:S(2)}) copy-start(f32[4,1,128]{2,1,0:T(1,128)} %get-tuple-element.15) | copy-start | bytes 6148
  152.3 12.1 %all-to-all-start.2 = ((bf16[16,16,256]{2,1,0:T(8,128)(2,1)}), bf16[16,16,256]{2,1,0:T(8,128)(2,1)S(1)}, u32[]{:S(2)}, u32[]{:S(2)}) async-start(bf16[16,16,256]{2,1,0:T(8,128)(2,1)} %broadcast_in_dim.42), calls=%async_computation.2 | async-start | bytes 262144 | tf_op jit(solution)/shard_map/all_to_all | solution.py:378
Sparse Core Ops, SparseCore 0:
  9.9 68.7 all-gather.1

commit v3 on v2

v3 whole, which is shorter than its diff:
```python
import functools
import math

import jax
import jax.numpy as jnp
from jax import lax
from jax.experimental import pallas as pl
from jax.experimental.pallas import tpu as pltpu
from jax.sharding import PartitionSpec as P

HEADS = 8
HIST = 128
LANES = 128
BF = jnp.bfloat16
F32 = jnp.float32
VMEM_BYTES = 56 * 1024 * 1024


def sigmoid(v):
    return 0.5 * jnp.tanh(0.5 * v) + 0.5


def dot(a, b):
    return jnp.dot(a, b, preferred_element_type=F32)


def dot_t(a, b):
    return lax.dot_general(a, b, (((1,), (1,)), ((), ())), preferred_element_type=F32)


def split3(v):
    high = v.astype(BF)
    rest = v - high.astype(F32)
    middle = rest.astype(BF)
    low = (rest - middle.astype(F32)).astype(BF)
    return high, middle, low


def prepare_kernel(nblocks, place_a, place_b, *refs):
    count = (len(refs) - 6) // 2
    halves = ((place_a, refs[:count]), (place_b, refs[count : 2 * count]))
    table, base, normed, mask, rows_s, sems = refs[2 * count :]
    block = pl.program_id(0)
    width = base.shape[1]
    actions = table.shape[0]
    half = HIST // 2

    def fetch(which, b, source):
        return pltpu.make_async_copy(
            source, rows_s.at[b, pl.ds(which * half, half)], sems.at[which, b]
        )

    @pl.when(block == 0)
    def _():
        for b in range(nblocks):
            for which, (place, arrays) in enumerate(halves):
                for k, array in enumerate(arrays):

                    @pl.when(place[b] // 2 == k)
                    def _():
                        fetch(which, b, array.at[lax.rem(place[b], 2)]).start()

    for which, (place, arrays) in enumerate(halves):
        fetch(which, block, arrays[0].at[0]).wait()
    rows = rows_s[block]
    tail = rows[:, width:].astype(F32)
    lane = lax.broadcasted_iota(jnp.int32, (HIST, actions), 1).astype(F32)
    onehot = jnp.where(tail[:, :actions] == lane, 1.0, 0.0).astype(BF)
    value = rows[:, :width].astype(F32)
    high, middle, low = split3(table[...])
    value = value + ((dot(onehot, low) + dot(onehot, middle)) + dot(onehot, high))
    scale = lax.rsqrt(jnp.mean(value * value, -1, keepdims=True) + 1e-06)
    base[...] = value
    normed[...] = (value * scale).astype(BF)
    position = lax.broadcasted_iota(jnp.int32, (HIST, LANES), 0).astype(F32)
    mask[...] = jnp.where(position < tail[:, LANES - 1 :], 1.0, 0.0)


def prepare(place_a, place_b, halves_a, halves_b, table):
    nblocks = place_a.shape[0]
    width = table.shape[1]
    total = nblocks * HIST
    arrays = list(halves_a) + list(halves_b)
    return pl.pallas_call(
        functools.partial(prepare_kernel, nblocks),
        grid_spec=pltpu.PrefetchScalarGridSpec(
            num_scalar_prefetch=2,
            grid=(nblocks,),
            in_specs=[pl.BlockSpec(memory_space=pl.ANY)] * len(arrays)
            + [pl.BlockSpec(table.shape, lambda b, p, q: (0, 0))],
            out_specs=[
                pl.BlockSpec((HIST, width), lambda b, p, q: (b, 0)),
                pl.BlockSpec((HIST, width), lambda b, p, q: (b, 0)),
                pl.BlockSpec((HIST, LANES), lambda b, p, q: (b, 0)),
            ],
            scratch_shapes=[
                pltpu.VMEM((nblocks, HIST, arrays[0].shape[-1]), BF),
                pltpu.SemaphoreType.DMA((2, nblocks)),
            ],
        ),
        out_shape=[
            jax.ShapeDtypeStruct((total, width), F32),
            jax.ShapeDtypeStruct((total, width), BF),
            jax.ShapeDtypeStruct((total, LANES), F32),
        ],
        compiler_params=pltpu.CompilerParams(vmem_limit_bytes=VMEM_BYTES),
        name="prepare",
    )(place_a, place_b, *arrays, table)


def encode_kernel(
    place,
    normed,
    wg,
    wv,
    wq,
    wk,
    mask,
    base,
    out_own,
    out_other,
    encoded,
    gate_s,
    mixed_s,
    even_s,
    odd_s,
    gated_s,
    base_s,
    wo_s,
    sems,
):
    step = pl.program_id(0)
    last = pl.num_programs(0) - 1
    total, width = normed.shape
    base_copy = pltpu.make_async_copy(base, base_s, sems.at[0])
    pairs, piece = out_own.shape[0], out_own.shape[1]
    wo_copies = []
    for d in range(pairs):
        first = 2 * lax.rem(place[0] + d, pairs)
        for k, (source, core) in enumerate(((out_own, place[1]), (out_other, 1 - place[1]))):
            start = pl.multiple_of((first + core) * piece, piece)
            wo_copies.append(
                pltpu.make_async_copy(
                    source.at[d], wo_s.at[pl.ds(start, piece)], sems.at[1 + 2 * d + k]
                )
            )
    row = lax.broadcasted_iota(jnp.int32, (HIST, HIST), 0)
    column = lax.broadcasted_iota(jnp.int32, (HIST, HIST), 1)
    causal = column <= row

    def project(which, head, store):
        cols = slice(which * LANES, (which + 1) * LANES)
        columns = jnp.concatenate([wg[:, cols], wv[:, cols], wq[:, cols], wk[:, cols]], axis=1)
        projected = dot(normed[...], columns)
        projected = projected * sigmoid(projected)
        gate_s[head] = projected[:, :LANES]
        store[...] = projected[:, LANES:].astype(BF)

    def attend(head, store):
        for u in range(total // HIST):
            part = slice(u * HIST, (u + 1) * HIST)
            queries = store[part, LANES : 2 * LANES]
            keys = store[part, 2 * LANES :]
            logits = dot_t(queries, keys) * (1.0 / math.sqrt(LANES))
            weight = jnp.where(causal, logits * sigmoid(logits) * (1.0 / HIST), 0.0).astype(BF)
            mixed_s[head, part] = dot(weight, store[part, :LANES])

    @pl.when(step == 0)
    def _():
        base_copy.start()
        for copy in wo_copies:
            copy.start()
        project(0, 0, even_s)
        attend(0, even_s)
        project(1, 1, odd_s)

    @pl.when(step > 0)
    def _():
        attend(2 * step - 1, odd_s)
        project(0, 2 * step, even_s)
        attend(2 * step, even_s)
        project(1, 2 * step + 1, odd_s)

    @pl.when(step == last)
    def _():
        attend(HEADS - 1, odd_s)
        square = mixed_s[0] * mixed_s[0]
        for h in range(1, HEADS):
            square = square + mixed_s[h] * mixed_s[h]
        scale = lax.rsqrt(jnp.sum(square, -1, keepdims=True) * (1.0 / width) + 1e-06)
        for h in range(HEADS):
            gated_s[:, h * LANES : (h + 1) * LANES] = (mixed_s[h] * scale * gate_s[h]).astype(BF)
        active = mask[:, :1] > 0.0
        base_copy.wait()
        for copy in wo_copies:
            copy.wait()
        size = 256
        for n in range(width // size):
            cols = slice(n * size, (n + 1) * size)
            value = base_s[:, cols] + dot(gated_s[...], wo_s[:, cols])
            encoded[:, cols] = jnp.where(active, value, 0.0).astype(BF)


def encode(place, normed, base, mask, weights, out_own, out_other):
    total, width = normed.shape
    pairs = out_own.shape[0]
    whole = lambda h, p: (0, 0)
    column = lambda group: pl.BlockSpec(
        (width, 2 * LANES), lambda h, p: (0, group * HEADS // 2 + h)
    )
    anywhere = pl.BlockSpec(memory_space=pl.ANY)
    return pl.pallas_call(
        encode_kernel,
        grid_spec=pltpu.PrefetchScalarGridSpec(
            num_scalar_prefetch=1,
            grid=(HEADS // 2,),
            in_specs=[
                pl.BlockSpec((total, width), whole),
                column(0),
                column(1),
                column(2),
                column(3),
                pl.BlockSpec((total, LANES), whole),
                anywhere,
                anywhere,
                anywhere,
            ],
            out_specs=pl.BlockSpec((total, width), whole),
            scratch_shapes=[
                pltpu.VMEM((HEADS, total, LANES), F32),
                pltpu.VMEM((HEADS, total, LANES), F32),
                pltpu.VMEM((total, 3 * LANES), BF),
                pltpu.VMEM((total, 3 * LANES), BF),
                pltpu.VMEM((total, width), BF),
                pltpu.VMEM((total, width), F32),
                pltpu.VMEM((width, width), BF),
                pltpu.SemaphoreType.DMA((1 + 2 * pairs,)),
            ],
        ),
        out_shape=jax.ShapeDtypeStruct((total, width), BF),
        compiler_params=pltpu.CompilerParams(vmem_limit_bytes=VMEM_BYTES),
        name="encode",
    )(place, normed, weights, weights, weights, weights, mask, base, out_own, out_other)


GROUP = 2


def cross_kernel(
    counts,
    core,
    queries,
    encoded,
    score_weight,
    own,
    labels,
    cand_t,
    scores,
    error,
    slopes,
    mine,
    other,
    slope_s,
    dir_s,
):
    step = pl.program_id(0)
    width = queries.shape[1]
    lane = lax.broadcasted_iota(jnp.int32, (HEADS, width), 1) // LANES
    head_row = lax.broadcasted_iota(jnp.int32, (HEADS, width), 0)
    spread = jnp.where(lane == head_row, score_weight[...], 0.0)
    high, middle, low = split3(spread)
    parts = [slice(g * HIST, (g + 1) * HIST) for g in range(GROUP)]
    along, along_scaled, totals = [], [], []
    for part in parts:
        keys = encoded[part]
        value = (dot_t(low, keys) + dot_t(middle, keys)) + dot_t(high, keys)
        along.append(value)
        along_scaled.append(value * (1.0 / (HIST * math.sqrt(LANES))))
        totals.append(jnp.zeros((HIST, HIST), F32))
    for h in range(HEADS):
        cols = slice(h * LANES, (h + 1) * LANES)
        for g, part in enumerate(parts):
            key_head = encoded[part, cols]
            logits = dot_t(queries[part, cols], key_head) * (1.0 / math.sqrt(LANES))
            gate = sigmoid(logits)
            product = logits * gate
            weight = (product * (1.0 / HIST)).astype(BF).astype(F32)
            totals[g] = totals[g] + weight * along[g][h : h + 1]
            slope = (gate + product * (1.0 - gate)) * along_scaled[g][h : h + 1]
            dir_s[part, cols] = dot(slope.astype(BF), key_head).astype(BF)
    for g, part in enumerate(parts):
        partial = jnp.sum(totals[g], -1, keepdims=True).astype(BF).astype(F32)
        partial_row = jnp.broadcast_to(partial, (HIST, HIST)).T[:1]
        active = lax.broadcasted_iota(jnp.int32, (1, HIST), 1) < counts[step * GROUP + g]
        score = jnp.where(active, partial_row + own[g], 0.0)
        err = jnp.where(active, sigmoid(score) - labels[g], 0.0)
        scores[g] = score
        error[g] = err
        err_rows = jnp.broadcast_to(err, (HIST, HIST)).T
        for h in range(HEADS):
            cols = slice(h * LANES, (h + 1) * LANES)
            slope = (err_rows * dir_s[part, cols].astype(F32)).astype(BF)
            slopes[part, cols] = slope
            slope_s[step, part, cols] = slope

    @pl.when(step == pl.num_programs(0) - 1)
    def _():
        _, pairs, tall, wide = mine.shape
        right = width // wide
        down = mine.shape[0] // right
        piece = tall * down
        first = core[0] == 0
        for n in range(right):
            cols = slice(n * wide, (n + 1) * wide)
            grad = dot(cand_t[...], slope_s[:, :, cols].reshape(-1, wide))
            for p in range(pairs):
                one = grad[2 * p * piece : (2 * p + 1) * piece]
                two = grad[(2 * p + 1) * piece : (2 * p + 2) * piece]
                kept = jnp.where(first, one, two).astype(BF)
                sent = jnp.where(first, two, one).astype(BF)
                for a in range(down):
                    rows = slice(a * tall, (a + 1) * tall)
                    mine[a * right + n, p] = kept[rows]
                    other[a * right + n, p] = sent[rows]


def cross(counts, core, queries, encoded, score_weight, own, labels, cand_t, pairs, users):
    nblocks = counts.shape[0]
    total, width = queries.shape
    rows = total // nblocks
    side = math.isqrt(users)
    shape = (users, pairs, width // (2 * pairs * side), width // side)
    block_rows = pl.BlockSpec((GROUP * rows, width), lambda b, n, c: (b, 0))
    row = pl.BlockSpec((GROUP, 1, rows), lambda b, n, c: (b, 0, 0))
    whole4 = lambda b, n, c: (0, 0, 0, 0)
    return pl.pallas_call(
        cross_kernel,
        grid_spec=pltpu.PrefetchScalarGridSpec(
            num_scalar_prefetch=2,
            grid=(nblocks // GROUP,),
            in_specs=[
                block_rows,
                block_rows,
                pl.BlockSpec((1, width), lambda b, n, c: (0, 0)),
                row,
                row,
                pl.BlockSpec((width, total), lambda b, n, c: (0, 0)),
            ],
            out_specs=[
                row,
                row,
                block_rows,
                pl.BlockSpec(shape, whole4),
                pl.BlockSpec(shape, whole4),
            ],
            scratch_shapes=[
                pltpu.VMEM((nblocks // GROUP, GROUP * rows, width), BF),
                pltpu.VMEM((GROUP * rows, width), BF),
            ],
        ),
        out_shape=[
            jax.ShapeDtypeStruct((nblocks, 1, rows), F32),
            jax.ShapeDtypeStruct((nblocks, 1, rows), F32),
            jax.ShapeDtypeStruct((total, width), BF),
            jax.ShapeDtypeStruct(shape, BF),
            jax.ShapeDtypeStruct(shape, BF),
        ],
        compiler_params=pltpu.CompilerParams(vmem_limit_bytes=VMEM_BYTES),
        name="cross",
    )(counts, core, queries, encoded, score_weight, own, labels, cand_t)


def shift(array, side, dx, dy):
    moves = []
    for x in range(side):
        for y in range(side):
            moves.append(((x + dx) % side * side + (y + dy) % side, x * side + y))
    return lax.ppermute(array, "user", moves)


def spread(piece, side, x_first):
    first = lambda a, d: shift(a, side, d, 0) if x_first else shift(a, side, 0, d)
    second = lambda a, d: shift(a, side, 0, d) if x_first else shift(a, side, d, 0)
    low = jnp.stack([piece, first(piece, 1)])
    high = jnp.stack([first(piece, 2), first(piece, -1)])
    low_after, high_before = second(low, 1), second(high, -1)
    high_after, low_before = second(high, 1), second(low, -1)
    low_two, high_two = second(low_after, 1), second(high_before, -1)
    return (low, high, low_after, high_after, low_two, high_two, low_before, high_before)


def around(array, loaders):
    move = lambda a, d: lax.ppermute(
        a, "loader", [((i + 2 * d) % loaders, i) for i in range(loaders)]
    )
    pairs = loaders // 2
    after, before = [array], [array]
    for d in range(pairs // 2):
        after.append(move(after[-1], 1))
        if d < pairs // 2 - 1:
            before.append(move(before[-1], -1))
    own = jnp.stack(after + before[:0:-1])
    return own, lax.ppermute(own, "loader", [(i, i ^ 1) for i in range(loaders)])


def body(
    history_items,
    history_events,
    history_lengths,
    action_table,
    mix_weight,
    out_weight,
    query_weight,
    score_weight,
    self_weight,
    candidates,
    block_owner,
    row_counts,
    labels,
):
    users = lax.axis_size("user")
    loaders = lax.axis_size("loader")
    pairs = loaders // 2
    nblocks, rows, width = candidates.shape

    weights = lax.all_gather(mix_weight, "loader", axis=0, tiled=True)
    out_own, out_other = around(out_weight, loaders)
    actions = action_table.shape[0]
    packed = jnp.concatenate(
        [
            history_items[0],
            jnp.broadcast_to(history_events[0][:, None].astype(BF), (HIST, actions)),
            jnp.broadcast_to(history_lengths[0].astype(BF), (HIST, LANES - actions)),
        ],
        axis=1,
    )
    side = math.isqrt(users)
    half = HIST // 2
    halves_a = spread(packed[:half], side, True)
    halves_b = spread(packed[half:], side, False)

    flat = candidates.reshape(-1, width)
    queries = jnp.dot(flat, query_weight, preferred_element_type=F32).astype(BF)
    cand_t = flat.T
    own = jnp.sum(candidates.astype(F32) * self_weight, -1)

    owner = block_owner[:, 0]
    here = lax.axis_index("user").astype(jnp.int32)
    far_x = lax.rem(owner // side - here // side + side, side)
    far_y = lax.rem(lax.rem(owner, side) - lax.rem(here, side) + side, side)
    base, normed, mask = prepare(
        far_y * side + far_x, far_x * side + far_y, halves_a, halves_b, action_table
    )
    loader = lax.axis_index("loader").astype(jnp.int32)
    core = lax.rem(loader, 2)[None]
    place = jnp.stack([loader // 2, lax.rem(loader, 2)])
    encoded = encode(place, normed, base, mask, weights, out_own, out_other)
    scores, error, slopes, mine, other = cross(
        row_counts,
        core,
        queries,
        encoded,
        score_weight[None],
        own[:, None],
        labels[:, None],
        cand_t,
        pairs,
        users,
    )

    arrived = lax.ppermute(other, "loader", [(i, i ^ 1) for i in range(loaders)])
    pieces = (mine.astype(F32) + arrived.astype(F32)).astype(BF)
    pieces = lax.all_to_all(pieces, "user", 0, 0, tiled=True)
    pieces = jnp.sum(pieces.astype(F32), 0).astype(BF)
    groups = [[c + 2 * i for i in range(pairs)] for c in range(2)]
    pieces = lax.all_to_all(pieces, "loader", 0, 0, axis_index_groups=groups, tiled=True)
    piece = jnp.sum(pieces.astype(F32), 0).astype(BF)
    pieces = lax.all_to_all(
        jnp.broadcast_to(piece[None], (users,) + piece.shape), "user", 0, 0, tiled=True
    )
    right = math.isqrt(users)
    tall, wide = piece.shape
    query_grad = pieces.reshape(users // right, right, tall, wide).transpose(0, 2, 1, 3)
    query_grad = query_grad.reshape(users // right * tall, right * wide).astype(F32)

    back = lax.dot_general(slopes, query_weight, (((1,), (1,)), ((), ())), preferred_element_type=F32)
    row_grads = (error.reshape(-1)[:, None] * self_weight + back).astype(BF)
    return (scores[:, 0], row_grads.reshape(nblocks, rows, width), query_grad)


def solution(mesh):
    placed = (
        P(("user", "loader"), None, None),
        P(("user", "loader"), None),
        P(("user", "loader")),
        P(),
        P("loader", None),
        P("loader", None),
        P(),
        P(),
        P(),
        P(("user", "loader"), None, None),
        P(("user", "loader"), None),
        P(("user", "loader")),
        P(("user", "loader"), None),
    )
    return jax.shard_map(
        body,
        mesh=mesh,
        in_specs=placed,
        out_specs=(
            P(("user", "loader"), None),
            P(("user", "loader"), None, None),
            P("loader", None),
        ),
        check_vma=False,
    )
```

time: 173 us -> 199 us (1.15)
  starting transfers between devices: 25.4 us -> 47.7 us
  waiting for transfers between devices: 27 us -> 46.3 us
  other arithmetic: 13.6 us -> 6.59 us
  Pallas kernels: 39.2 us -> 34 us
  blocking collectives: 35.1 us -> 32.6 us
    ppermute x0 -> x8, waiting for transfers between devices: none -> 31.3 us  [the longest x7 31.3 us: around(): lax.ppermute(a, 'loader', [((i + 2 * d) % loaders, i) for i in range(load...]
    ppermute x0 -> x8, starting transfers between devices: none -> 14.6 us  [the longest x7 14.6 us: around(): lax.ppermute(a, 'loader', [((i + 2 * d) % loaders, i) for i in range(load...]
    all_gather x1, waiting for transfers between devices: 9.59 us -> 0.02 us  [body(): weights = lax.all_gather(mix_weight, 'loader', axis=0, tiled=True)]
    ppermute x16 -> x18, starting transfers between devices: 19.3 us -> 27.2 us  [shift(): return lax.ppermute(array, 'user', moves)]
    another operation x8 -> x5, other arithmetic: 8.69 us -> 2.19 us  [the longest x2 1.49 us: spread(): low = jnp.stack([piece, first(piece, 1)])]
    pallas_call x3 -> x2, Pallas kernels: 25.7 us -> 21.7 us  [the longest x1 15.9 us: encode(): pl.pallas_call(encode_kernel, grid_spec=pltpu.PrefetchScalarGridSpec(num_...]
    ppermute x16 -> x18, waiting for transfers between devices: 11.9 us -> 8.45 us  [shift(): return lax.ppermute(array, 'user', moves)]
    slice x8 -> x0, local copies, waits for them, and re-layouts: 3.01 us -> none  [the longest x4 1.53 us: ring(): first = move(after[:, :half], 1)]
  transfers between devices with their start and end apart: 19 -> 29, of which waited for: 8 -> 14; matrix products, arithmetic and copies ran while one was open for 13% -> 9% of each run, Pallas kernels for 3% -> 3%
where the time goes in v3:
time: 199 us
  starting transfers between devices  47.7 us (24%)
  waiting for transfers between devices  46.3 us (23%)
  Pallas kernels  34 us (17%)
  blocking collectives  32.6 us (16%)
  between operations  15.1 us (8%)
  local copies, waits for them, and re-layouts  10.9 us (5%)
  other arithmetic  6.59 us (3%)
  matrix products  5.72 us (3%)
    ppermute x7, waiting for transfers between devices, around(): lax.ppermute(a, 'loader', [((i + 2 * d) % loaders, i) for i in range(load...  31.3 us
    ppermute x18, starting transfers between devices, shift(): return lax.ppermute(array, 'user', moves)  27.2 us
    all_to_all x1, blocking collectives, body(): pieces = lax.all_to_all(pieces, 'user', 0, 0, tiled=True)  21.1 us
    pallas_call x1, Pallas kernels, encode(): pl.pallas_call(encode_kernel, grid_spec=pltpu.PrefetchScalarGridSpec(num_...  15.9 us
    ppermute x7, starting transfers between devices, around(): lax.ppermute(a, 'loader', [((i + 2 * d) % loaders, i) for i in range(load...  14.6 us
    pallas_call x1, Pallas kernels, cross(): pl.pallas_call(cross_kernel, grid_spec=pltpu.PrefetchScalarGridSpec(num_s...  12.3 us
    all_to_all x1, blocking collectives, body(): lax.all_to_all(pieces, 'loader', 0, 0, axis_index_groups=groups, tiled=True)  11.5 us
    ppermute x18, waiting for transfers between devices, shift(): return lax.ppermute(array, 'user', moves)  8.45 us
  transfers between devices with their start and end apart: 29, of which 14 were waited for; matrix products, arithmetic and copies ran while one was open for 9% of the time, Pallas kernels for 3%

profile of v3, /device:TPU:2, one launch (start us, length us, event | category | flops | bytes accessed | tf_op | source)
XLA Modules:
  0.0 198.8 jit_solution(6536990643041678391)
XLA Ops:
  7.2 0.7 all-gather.2.cloned.1.call-update
  8.8 0.7 convert_bitcast_fusion.1
  9.5 1.1 concatenate.3
  10.6 3.3 %collective-permute-start.10 = (bf16[64,1152]{1,0:T(8,128)(2,1)S(1)}, bf16[64,1152]{1,0:T(8,128)(2,1)S(1)}, u32[]{:S(2)}, u32[]{:S(2)}) collective-permute-start(bf16[64,1152]{1,0:T(8,128)(2,1)S(1)} %get-tuple-element.24), channel_id=1, source_target_pairs={{32,0},{48,16},{0,32},{16,48},{96,64},{112,80},{64,96},{80,112},{1... | collective-permute-start | bytes 442376 | tf_op jit(solution)/shard_map/ppermute | solution.py:378
  13.9 0.7 collective-permute-start.11
  14.6 1.5 collective-permute-start.2
  16.1 1.1 collective-permute-start.1
  17.2 5.9 %collective-permute-start.18 = (bf16[64,1024]{1,0:T(8,128)(2,1)}, bf16[64,1024]{1,0:T(8,128)(2,1)S(1)}, u32[]{:S(2)}, u32[]{:S(2)}) collective-permute-start(bf16[64,1024]{1,0:T(8,128)(2,1)} %param.18), channel_id=1, source_target_pairs={{2,0},{3,1},{4,2},{5,3},{6,4},{7,5},{8,6},{9,7},{10,8},{11,9},{12,... | collective-permute-start | bytes 393224 | tf_op jit(solution)/shard_map/ppermute | solution.py:393
  23.1 2.2 %convolution_convert_fusion.queries = bf16[512,1024]{1,0:T(8,128)(2,1)} fusion(bf16[512,1024]{1,0:T(8,128)(2,1)S(1)} %bitcast.70, bf16[1024,1024]{1,0:T(8,128)(2,1)S(1)} %copy-done), kind=kOutput, calls=%fused_computation.3 | convolution fusion | flops 1074266112 | bytes 4194304 | tf_op jit(solution)/shard_map/dot_general | solution.py:443
  25.3 0.7 bitcast_dynamic-update-slice_fusion.7
  26.0 2.5 %collective-permute-done.18 = bf16[64,1024]{1,0:T(8,128)(2,1)S(1)} collective-permute-done((bf16[64,1024]{1,0:T(8,128)(2,1)}, bf16[64,1024]{1,0:T(8,128)(2,1)S(1)}, u32[]{:S(2)}, u32[]{:S(2)}) %collective-permute-start.18) | collective-permute-done | bytes 131104 | tf_op jit(solution)/shard_map/ppermute | solution.py:393
  28.5 2.5 %collective-permute-start.9 = (bf16[64,1152]{1,0:T(8,128)(2,1)S(1)}, bf16[64,1152]{1,0:T(8,128)(2,1)S(1)}, u32[]{:S(2)}, u32[]{:S(2)}) collective-permute-start(bf16[64,1152]{1,0:T(8,128)(2,1)S(1)} %get-tuple-element.24), channel_id=1, source_target_pairs={{16,0},{32,16},{48,32},{0,48},{80,64},{96,80},{112,96},{64,112},{1... | collective-permute-start | bytes 442376 | tf_op jit(solution)/shard_map/ppermute | solution.py:378
  31.0 0.7 bitcast_dynamic-update-slice_fusion.6
  31.7 2.7 %collective-permute-start = (bf16[64,1152]{1,0:T(8,128)(2,1)S(1)}, bf16[64,1152]{1,0:T(8,128)(2,1)S(1)}, u32[]{:S(2)}, u32[]{:S(2)}) collective-permute-start(bf16[64,1152]{1,0:T(8,128)(2,1)S(1)} %get-tuple-element.25), channel_id=1, source_target_pairs={{64,0},{80,16},{96,32},{112,48},{128,64},{144,80},{160,96},{176,11... | collective-permute-start | bytes 442376 | tf_op jit(solution)/shard_map/ppermute | solution.py:378
  34.4 9.3 %collective-permute-done.22 = bf16[64,1024]{1,0:T(8,128)(2,1)S(1)} collective-permute-done((bf16[64,1024]{1,0:T(8,128)(2,1)S(1)}, bf16[64,1024]{1,0:T(8,128)(2,1)S(1)}, u32[]{:S(2)}, u32[]{:S(2)}) %collective-permute-start.22) | collective-permute-done | bytes 131104 | tf_op jit(solution)/shard_map/ppermute | solution.py:393
  43.8 2.4 %collective-permute-start.19 = (bf16[64,1024]{1,0:T(8,128)(2,1)S(1)}, bf16[64,1024]{1,0:T(8,128)(2,1)S(1)}, u32[]{:S(2)}, u32[]{:S(2)}) collective-permute-start(bf16[64,1024]{1,0:T(8,128)(2,1)S(1)} %collective-permute-done.18), channel_id=1, source_target_pairs={{2,0},{3,1},{4,2},{5,3},{6,4},{7,5},{8,6},{9,7},{10,8},{11,9},{12,... | collective-permute-start | bytes 393224 | tf_op jit(solution)/shard_map/ppermute | solution.py:393
  46.4 5.9 %collective-permute-done.19 = bf16[64,1024]{1,0:T(8,128)(2,1)S(1)} collective-permute-done((bf16[64,1024]{1,0:T(8,128)(2,1)S(1)}, bf16[64,1024]{1,0:T(8,128)(2,1)S(1)}, u32[]{:S(2)}, u32[]{:S(2)}) %collective-permute-start.19) | collective-permute-done | bytes 131104 | tf_op jit(solution)/shard_map/ppermute | solution.py:393
  52.3 2.8 %collective-permute-start.20 = (bf16[64,1024]{1,0:T(8,128)(2,1)S(1)}, bf16[64,1024]{1,0:T(8,128)(2,1)S(1)}, u32[]{:S(2)}, u32[]{:S(2)}) collective-permute-start(bf16[64,1024]{1,0:T(8,128)(2,1)S(1)} %collective-permute-done.19), channel_id=1, source_target_pairs={{2,0},{3,1},{4,2},{5,3},{6,4},{7,5},{8,6},{9,7},{10,8},{11,9},{12,... | collective-permute-start | bytes 393224 | tf_op jit(solution)/shard_map/ppermute | solution.py:393
  55.1 0.7 bitcast_dynamic-update-slice_fusion.5
  55.7 5.3 %collective-permute-done.20 = bf16[64,1024]{1,0:T(8,128)(2,1)S(1)} collective-permute-done((bf16[64,1024]{1,0:T(8,128)(2,1)S(1)}, bf16[64,1024]{1,0:T(8,128)(2,1)S(1)}, u32[]{:S(2)}, u32[]{:S(2)}) %collective-permute-start.20) | collective-permute-done | bytes 131104 | tf_op jit(solution)/shard_map/ppermute | solution.py:393
  61.0 3.5 %collective-permute-start.21 = (bf16[64,1024]{1,0:T(8,128)(2,1)S(1)}, bf16[64,1024]{1,0:T(8,128)(2,1)S(1)}, u32[]{:S(2)}, u32[]{:S(2)}) collective-permute-start(bf16[64,1024]{1,0:T(8,128)(2,1)S(1)} %collective-permute-done.20), channel_id=1, source_target_pairs={{2,0},{3,1},{4,2},{5,3},{6,4},{7,5},{8,6},{9,7},{10,8},{11,9},{12,... | collective-permute-start | bytes 393224 | tf_op jit(solution)/shard_map/ppermute | solution.py:393
  64.6 0.7 bitcast_dynamic-update-slice_fusion.4
  65.2 2.3 %collective-permute-start.13 = (bf16[2,64,1152]{2,1,0:T(8,128)(2,1)S(1)}, bf16[2,64,1152]{2,1,0:T(8,128)(2,1)S(1)}, u32[]{:S(2)}, u32[]{:S(2)}) collective-permute-start(bf16[2,64,1152]{2,1,0:T(8,128)(2,1)S(1)} %pad_maximum_fusion.3.refs_9_), channel_id=1, source_target_pairs={{64,0},{80,16},{96,32},{112,48},{128,64},{144,80},{160,96},{176,11... | collective-permute-start | bytes 884744 | tf_op jit(solution)/shard_map/ppermute | solution.py:378
  67.5 2.3 %collective-permute-done.21 = bf16[64,1024]{1,0:T(8,128)(2,1)S(1)} collective-permute-done((bf16[64,1024]{1,0:T(8,128)(2,1)S(1)}, bf16[64,1024]{1,0:T(8,128)(2,1)S(1)}, u32[]{:S(2)}, u32[]{:S(2)}) %collective-permute-start.21) | collective-permute-done | bytes 131104 | tf_op jit(solution)/shard_map/ppermute | solution.py:393
  69.8 0.7 bitcast_dynamic-update-slice_fusion.3
  70.5 6.0 %collective-permute-done.24 = bf16[64,1024]{1,0:T(8,128)(2,1)S(1)} collective-permute-done((bf16[64,1024]{1,0:T(8,128)(2,1)S(1)}, bf16[64,1024]{1,0:T(8,128)(2,1)S(1)}, u32[]{:S(2)}, u32[]{:S(2)}) %collective-permute-start.24) | collective-permute-done | bytes 131104 | tf_op jit(solution)/shard_map/ppermute | solution.py:393
  76.5 0.5 collective-permute-start.6
  76.9 0.7 bitcast_dynamic-update-slice_fusion.2
  77.6 0.7 bitcast_dynamic-update-slice_fusion.1
  78.3 0.7 bitcast_dynamic-update-slice_fusion.out_own
  78.9 2.8 %collective-permute-start.4 = (bf16[2,64,1152]{2,1,0:T(8,128)(2,1)S(1)}, bf16[2,64,1152]{2,1,0:T(8,128)(2,1)S(1)}, u32[]{:S(2)}, u32[]{:S(2)}) collective-permute-start(bf16[2,64,1152]{2,1,0:T(8,128)(2,1)S(1)} %pad_maximum_fusion.1.refs_1_), channel_id=1, source_target_pairs={{16,0},{32,16},{48,32},{0,48},{80,64},{96,80},{112,96},{64,112},{1... | collective-permute-start | bytes 884744 | tf_op jit(solution)/shard_map/ppermute | solution.py:378
  81.7 0.8 pad_maximum_fusion.2.refs_8_
  82.4 0.7 pad_maximum_fusion.refs_0_
  83.2 2.3 %collective-permute-start.12 = (bf16[2,64,1152]{2,1,0:T(8,128)(2,1)}, bf16[2,64,1152]{2,1,0:T(8,128)(2,1)}, u32[]{:S(2)}, u32[]{:S(2)}) collective-permute-start(bf16[2,64,1152]{2,1,0:T(8,128)(2,1)} %pad_maximum_fusion.2.refs_8_), channel_id=1, source_target_pairs={{64,0},{80,16},{96,32},{112,48},{128,64},{144,80},{160,96},{176,11... | collective-permute-start | bytes 884744 | tf_op jit(solution)/shard_map/ppermute | solution.py:378
  85.6 0.9 collective-permute-start.3
  86.5 0.7 copy-done.8
  87.2 1.2 collective-permute-start.8
  88.5 0.9 multiply_reduce_fusion
  89.3 1.3 copy.22
  90.6 0.6 multiply_add_fusion
  91.2 1.7 collective-permute-done.12.refs_10_
  92.9 1.2 collective-permute-start.16
  94.1 0.9 collective-permute-done.3.refs_2_
  95.1 1.7 collective-permute-start.14
  96.8 0.9 collective-permute-done.8.refs_6_
  97.7 2.3 %collective-permute-start.5 = (bf16[2,64,1152]{2,1,0:T(8,128)(2,1)}, bf16[2,64,1152]{2,1,0:T(8,128)(2,1)S(1)}, u32[]{:S(2)}, u32[]{:S(2)}) collective-permute-start(bf16[2,64,1152]{2,1,0:T(8,128)(2,1)} %collective-permute-done.3.refs_2_), channel_id=1, source_target_pairs={{16,0},{32,16},{48,32},{0,48},{80,64},{96,80},{112,96},{64,112},{1... | collective-permute-start | bytes 884744 | tf_op jit(solution)/shard_map/ppermute | solution.py:378
  100.0 0.6 pad_add_fusion.place
  100.7 0.5 multiply_add_fusion.1.place_a
  101.2 0.9 collective-permute-done.16.refs_13_
  102.1 2.6 %collective-permute-done.7.refs_5_ = bf16[2,64,1152]{2,1,0:T(8,128)(2,1)S(1)} collective-permute-done((bf16[2,64,1152]{2,1,0:T(8,128)(2,1)}, bf16[2,64,1152]{2,1,0:T(8,128)(2,1)S(1)}, u32[]{:S(2)}, u32[]{:S(2)}) %collective-permute-start.7) | collective-permute-done | bytes 294944 | tf_op jit(solution)/shard_map/ppermute | solution.py:378
  104.7 1.3 collective-permute-done.5.refs_4_
  106.1 0.7 copy-done.12
  106.8 5.8 %prepare.1 = (f32[512,1024]{1,0:T(8,128)}, bf16[512,1024]{1,0:T(8,128)(2,1)}, f32[512,128]{1,0:T(8,128)}) custom-call(s32[4]{0:T(128)} %multiply_add_fusion.1.place_a, s32[4]{0:T(128)} %get-tuple-element.19.place_b, bf16[2,64,1152]{2,1,0:T(8,128)(2,1)} %pad_maximum_fusion.refs_0_, bf16[2,64,1152]{2,1,0:T(8,128)(2,1)} %copy-done.3, ...), custom_call_target="tpu_custom_call" | custom-call | tf_op jit(solution)/shard_map/prepare/pallas_call | solution.py:84
  112.6 15.9 %encode.1.encoded = bf16[512,1024]{1,0:T(8,128)(2,1)} custom-call(s32[2]{0:T(128)} %pad_add_fusion.place, bf16[512,1024]{1,0:T(8,128)(2,1)} %get-tuple-element.11.normed, bf16[1024,4096]{1,0:T(8,128)(2,1)} %all-gather.2.cloned.1.call-done.wg.wv.wq.wk, bf16[1024,4096]{1,0:T(8,128)(2,1)} %all-gather.2.cloned.1.call-done.wg.wv.wq.wk, ...), custom_call_target="tpu_custom_call" | custom-call | tf_op jit(solution)/shard_map/encode/pallas_call | solution.py:212
  128.5 12.3 %cross.1 = (f32[4,1,128]{2,1,0:T(1,128)}, f32[4,1,128]{2,1,0:T(1,128)}, bf16[512,1024]{1,0:T(8,128)(2,1)}, bf16[16,8,16,256]{3,2,1,0:T(8,128)(2,1)}, bf16[16,8,16,256]{3,2,1,0:T(8,128)(2,1)}) custom-call(s32[4]{0:T(128)} %counts.1, s32[1]{0:T(128)} %bitcast.core, bf16[512,1024]{1,0:T(8,128)(2,1)} %convolution_convert_fusion.queries, ...), custom_call_target="tpu_custom_call" | custom-call | tf_op jit(solution)/shard_map/cross/pallas_call | solution.py:336
  141.0 2.9 %collective-permute-done.26 = bf16[16,8,16,256]{3,2,1,0:T(8,128)(2,1)S(1)} collective-permute-done((bf16[16,8,16,256]{3,2,1,0:T(8,128)(2,1)}, bf16[16,8,16,256]{3,2,1,0:T(8,128)(2,1)S(1)}, u32[]{:S(2)}, u32[]{:S(2)}) %collective-permute-start.26) | collective-permute-done | bytes 1048608 | tf_op jit(solution)/shard_map/ppermute | solution.py:471
  143.8 1.6 add_convert_fusion
  145.4 21.1 %all_to_all.15 = bf16[16,8,16,256]{3,2,1,0:T(8,128)(2,1)S(1)} all-to-all(bf16[16,8,16,256]{3,2,1,0:T(8,128)(2,1)S(1)} %add_convert_fusion), channel_id=1, replica_groups=mesh['user'=16,'loader'=16] {'user'}, dimensions={0} | all-to-all | bytes 2097152 | tf_op jit(solution)/shard_map/all_to_all | solution.py:473
  166.7 11.5 %all_to_all.16 = bf16[8,16,256]{2,1,0:T(8,128)(2,1)S(1)} all-to-all(bf16[8,16,256]{2,1,0:T(8,128)(2,1)S(1)} %reduce_sum.34), channel_id=1, replica_groups={{0,2,4,6,8,10,12,14},{1,3,5,7,9,11,13,15},{16,18,20,22,24,26,28,30},{17..., dimensions={0} | all-to-all | bytes 131072 | tf_op jit(solution)/shard_map/all_to_all | solution.py:476
  178.2 0.7 broadcast_in_dim.34
  178.8 5.7 %all-to-all-start.2 = ((bf16[16,16,256]{2,1,0:T(8,128)(2,1)}), bf16[16,16,256]{2,1,0:T(8,128)(2,1)S(1)}, u32[]{:S(2)}, u32[]{:S(2)}) async-start(bf16[16,16,256]{2,1,0:T(8,128)(2,1)} %broadcast_in_dim.34), calls=%async_computation.2 | async-start | bytes 262144 | tf_op jit(solution)/shard_map/all_to_all | solution.py:478
  184.6 3.5 %add_convert_fusion.1 = bf16[512,1024]{1,0:T(8,128)(2,1)} fusion(bf16[512,1024]{1,0:T(8,128)(2,1)} %get-tuple-element.16, bf16[1024,1024]{1,0:T(8,128)(2,1)S(1)} %copy-done, f32[1024]{0:T(1024)S(1)} %copy-done.14, f32[512]{0:T(512)S(1)} %bitcast.87), kind=kOutput, calls=%fused_computation.1 | convolution fusion | flops 1075314688 | bytes 4200448 | tf_op jit(solution)/shard_map/dot_general | solution.py:486
  188.1 2.9 %all-to-all-done.2 = bf16[16,16,256]{2,1,0:T(8,128)(2,1)S(1)} async-done(((bf16[16,16,256]{2,1,0:T(8,128)(2,1)}), bf16[16,16,256]{2,1,0:T(8,128)(2,1)S(1)}, u32[]{:S(2)}, u32[]{:S(2)}) %all-to-all-start.2) | async-done | bytes 131104 | tf_op jit(solution)/shard_map/all_to_all | solution.py:478
  191.2 0.8 copy.23
  (65 shorter events, 1.0 us)
Async XLA Ops:
  7.2 15.9 %copy-start = (bf16[1024,1024]{1,0:T(8,128)(2,1)S(1)}, bf16[1024,1024]{1,0:T(8,128)(2,1)}, u32[]{:S(2)}) copy-start(bf16[1024,1024]{1,0:T(8,128)(2,1)} %param.19) | copy-start | bytes 6291460
  7.2 15.9 %copy-start.1 = (bf16[4,128,1024]{2,1,0:T(8,128)(2,1)S(1)}, bf16[4,128,1024]{2,1,0:T(8,128)(2,1)}, u32[]{:S(2)}) copy-start(bf16[4,128,1024]{2,1,0:T(8,128)(2,1)} %param.22) | copy-start | bytes 3145732
  7.2 105.4 %all-gather.2.cloned.1.call-start = ((), (), s32[]{:S(2)}) async-start(), calls=%async_computation.3 | async-start | bytes 8912896 | tf_op jit(solution)/shard_map/all_gather | solution.py:426
  10.6 21.0 %collective-permute-start.10 = (bf16[64,1152]{1,0:T(8,128)(2,1)S(1)}, bf16[64,1152]{1,0:T(8,128)(2,1)S(1)}, u32[]{:S(2)}, u32[]{:S(2)}) collective-permute-start(bf16[64,1152]{1,0:T(8,128)(2,1)S(1)} %get-tuple-element.24), channel_id=1, source_target_pairs={{32,0},{48,16},{0,32},{16,48},{96,64},{112,80},{64,96},{80,112},{1... | collective-permute-start | bytes 442376 | tf_op jit(solution)/shard_map/ppermute | solution.py:378
  13.9 20.4 %collective-permute-start.11 = (bf16[64,1152]{1,0:T(8,128)(2,1)S(1)}, bf16[64,1152]{1,0:T(8,128)(2,1)S(1)}, u32[]{:S(2)}, u32[]{:S(2)}) collective-permute-start(bf16[64,1152]{1,0:T(8,128)(2,1)S(1)} %get-tuple-element.24), channel_id=1, source_target_pairs={{48,0},{0,16},{16,32},{32,48},{112,64},{64,80},{80,96},{96,112},{1... | collective-permute-start | bytes 442376 | tf_op jit(solution)/shard_map/ppermute | solution.py:378
  14.6 31.6 %collective-permute-start.2 = (bf16[64,1152]{1,0:T(8,128)(2,1)S(1)}, bf16[64,1152]{1,0:T(8,128)(2,1)S(1)}, u32[]{:S(2)}, u32[]{:S(2)}) collective-permute-start(bf16[64,1152]{1,0:T(8,128)(2,1)S(1)} %get-tuple-element.25), channel_id=1, source_target_pairs={{192,0},{208,16},{224,32},{240,48},{0,64},{16,80},{32,96},{48,112}... | collective-permute-start | bytes 442376 | tf_op jit(solution)/shard_map/ppermute | solution.py:378
  16.1 30.1 %collective-permute-start.1 = (bf16[64,1152]{1,0:T(8,128)(2,1)S(1)}, bf16[64,1152]{1,0:T(8,128)(2,1)S(1)}, u32[]{:S(2)}, u32[]{:S(2)}) collective-permute-start(bf16[64,1152]{1,0:T(8,128)(2,1)S(1)} %get-tuple-element.25), channel_id=1, source_target_pairs={{128,0},{144,16},{160,32},{176,48},{192,64},{208,80},{224,96},{240... | collective-permute-start | bytes 442376 | tf_op jit(solution)/shard_map/ppermute | solution.py:378
  17.2 11.3 %collective-permute-start.18 = (bf16[64,1024]{1,0:T(8,128)(2,1)}, bf16[64,1024]{1,0:T(8,128)(2,1)S(1)}, u32[]{:S(2)}, u32[]{:S(2)}) collective-permute-start(bf16[64,1024]{1,0:T(8,128)(2,1)} %param.18), channel_id=1, source_target_pairs={{2,0},{3,1},{4,2},{5,3},{6,4},{7,5},{8,6},{9,7},{10,8},{11,9},{12,... | collective-permute-start | bytes 393224 | tf_op jit(solution)/shard_map/ppermute | solution.py:393
  23.1 2.2 %copy-start.13 = (bf16[64,1024]{1,0:T(8,128)(2,1)S(1)}, bf16[64,1024]{1,0:T(8,128)(2,1)}, u32[]{:S(2)}) copy-start(bf16[64,1024]{1,0:T(8,128)(2,1)} %param.18) | copy-start | bytes 393220
  26.0 62.5 %copy-start.14 = (f32[1024]{0:T(1024)S(1)}, f32[1024]{0:T(1024)}, u32[]{:S(2)}) copy-start(f32[1024]{0:T(1024)} %param.21) | copy-start | bytes 12292
  28.5 50.4 %collective-permute-start.9 = (bf16[64,1152]{1,0:T(8,128)(2,1)S(1)}, bf16[64,1152]{1,0:T(8,128)(2,1)S(1)}, u32[]{:S(2)}, u32[]{:S(2)}) collective-permute-start(bf16[64,1152]{1,0:T(8,128)(2,1)S(1)} %get-tuple-element.24), channel_id=1, source_target_pairs={{16,0},{32,16},{48,32},{0,48},{80,64},{96,80},{112,96},{64,112},{1... | collective-permute-start | bytes 442376 | tf_op jit(solution)/shard_map/ppermute | solution.py:378
  31.7 50.0 %collective-permute-start = (bf16[64,1152]{1,0:T(8,128)(2,1)S(1)}, bf16[64,1152]{1,0:T(8,128)(2,1)S(1)}, u32[]{:S(2)}, u32[]{:S(2)}) collective-permute-start(bf16[64,1152]{1,0:T(8,128)(2,1)S(1)} %get-tuple-element.25), channel_id=1, source_target_pairs={{64,0},{80,16},{96,32},{112,48},{128,64},{144,80},{160,96},{176,11... | collective-permute-start | bytes 442376 | tf_op jit(solution)/shard_map/ppermute | solution.py:378
  34.4 9.4 %collective-permute-start.22 = (bf16[64,1024]{1,0:T(8,128)(2,1)S(1)}, bf16[64,1024]{1,0:T(8,128)(2,1)S(1)}, u32[]{:S(2)}, u32[]{:S(2)}) collective-permute-start(bf16[64,1024]{1,0:T(8,128)(2,1)S(1)} %copy-done.13), channel_id=1, source_target_pairs={{14,0},{15,1},{0,2},{1,3},{2,4},{3,5},{4,6},{5,7},{6,8},{7,9},{8,1... | collective-permute-start | bytes 393224 | tf_op jit(solution)/shard_map/ppermute | solution.py:393
  34.4 54.9 %copy-start.2 = (bf16[2,64,1152]{2,1,0:T(8,128)(2,1)}, bf16[2,64,1152]{2,1,0:T(8,128)(2,1)S(1)}, u32[]{:S(2)}) copy-start(bf16[2,64,1152]{2,1,0:T(8,128)(2,1)S(1)} %pad_maximum_fusion.3.refs_9_) | copy-start | bytes 884740
  43.8 8.5 %collective-permute-start.19 = (bf16[64,1024]{1,0:T(8,128)(2,1)S(1)}, bf16[64,1024]{1,0:T(8,128)(2,1)S(1)}, u32[]{:S(2)}, u32[]{:S(2)}) collective-permute-start(bf16[64,1024]{1,0:T(8,128)(2,1)S(1)} %collective-permute-done.18), channel_id=1, source_target_pairs={{2,0},{3,1},{4,2},{5,3},{6,4},{7,5},{8,6},{9,7},{10,8},{11,9},{12,... | collective-permute-start | bytes 393224 | tf_op jit(solution)/shard_map/ppermute | solution.py:393
  46.2 19.0 %collective-permute-start.23 = (bf16[64,1024]{1,0:T(8,128)(2,1)S(1)}, bf16[64,1024]{1,0:T(8,128)(2,1)S(1)}, u32[]{:S(2)}, u32[]{:S(2)}) collective-permute-start(bf16[64,1024]{1,0:T(8,128)(2,1)S(1)} %collective-permute-done.22), channel_id=1, source_target_pairs={{14,0},{15,1},{0,2},{1,3},{2,4},{3,5},{4,6},{5,7},{6,8},{7,9},{8,1... | collective-permute-start | bytes 393224 | tf_op jit(solution)/shard_map/ppermute | solution.py:393
  46.2 37.0 %collective-permute-start.15 = (bf16[2,64,1152]{2,1,0:T(8,128)(2,1)S(1)}, bf16[2,64,1152]{2,1,0:T(8,128)(2,1)S(1)}, u32[]{:S(2)}, u32[]{:S(2)}) collective-permute-start(bf16[2,64,1152]{2,1,0:T(8,128)(2,1)S(1)} %pad_maximum_fusion.3.refs_9_), channel_id=1, source_target_pairs={{192,0},{208,16},{224,32},{240,48},{0,64},{16,80},{32,96},{48,112}... | collective-permute-start | bytes 884744 | tf_op jit(solution)/shard_map/ppermute | solution.py:378
  46.3 39.3 %copy-start.3 = (bf16[2,64,1152]{2,1,0:T(8,128)(2,1)}, bf16[2,64,1152]{2,1,0:T(8,128)(2,1)S(1)}, u32[]{:S(2)}) copy-start(bf16[2,64,1152]{2,1,0:T(8,128)(2,1)S(1)} %pad_maximum_fusion.1.refs_1_) | copy-start | bytes 884740
  52.3 8.8 %collective-permute-start.20 = (bf16[64,1024]{1,0:T(8,128)(2,1)S(1)}, bf16[64,1024]{1,0:T(8,128)(2,1)S(1)}, u32[]{:S(2)}, u32[]{:S(2)}) collective-permute-start(bf16[64,1024]{1,0:T(8,128)(2,1)S(1)} %collective-permute-done.19), channel_id=1, source_target_pairs={{2,0},{3,1},{4,2},{5,3},{6,4},{7,5},{8,6},{9,7},{10,8},{11,9},{12,... | collective-permute-start | bytes 393224 | tf_op jit(solution)/shard_map/ppermute | solution.py:393
  61.0 8.8 %collective-permute-start.21 = (bf16[64,1024]{1,0:T(8,128)(2,1)S(1)}, bf16[64,1024]{1,0:T(8,128)(2,1)S(1)}, u32[]{:S(2)}, u32[]{:S(2)}) collective-permute-start(bf16[64,1024]{1,0:T(8,128)(2,1)S(1)} %collective-permute-done.20), channel_id=1, source_target_pairs={{2,0},{3,1},{4,2},{5,3},{6,4},{7,5},{8,6},{9,7},{10,8},{11,9},{12,... | collective-permute-start | bytes 393224 | tf_op jit(solution)/shard_map/ppermute | solution.py:393
  65.2 20.4 %collective-permute-start.13 = (bf16[2,64,1152]{2,1,0:T(8,128)(2,1)S(1)}, bf16[2,64,1152]{2,1,0:T(8,128)(2,1)S(1)}, u32[]{:S(2)}, u32[]{:S(2)}) collective-permute-start(bf16[2,64,1152]{2,1,0:T(8,128)(2,1)S(1)} %pad_maximum_fusion.3.refs_9_), channel_id=1, source_target_pairs={{64,0},{80,16},{96,32},{112,48},{128,64},{144,80},{160,96},{176,11... | collective-permute-start | bytes 884744 | tf_op jit(solution)/shard_map/ppermute | solution.py:378
  69.8 6.6 %collective-permute-start.24 = (bf16[64,1024]{1,0:T(8,128)(2,1)S(1)}, bf16[64,1024]{1,0:T(8,128)(2,1)S(1)}, u32[]{:S(2)}, u32[]{:S(2)}) collective-permute-start(bf16[64,1024]{1,0:T(8,128)(2,1)S(1)} %collective-permute-done.23), channel_id=1, source_target_pairs={{14,0},{15,1},{0,2},{1,3},{2,4},{3,5},{4,6},{5,7},{6,8},{7,9},{8,1... | collective-permute-start | bytes 393224 | tf_op jit(solution)/shard_map/ppermute | solution.py:393
  76.5 9.0 %collective-permute-start.6 = (bf16[2,64,1152]{2,1,0:T(8,128)(2,1)S(1)}, bf16[2,64,1152]{2,1,0:T(8,128)(2,1)S(1)}, u32[]{:S(2)}, u32[]{:S(2)}) collective-permute-start(bf16[2,64,1152]{2,1,0:T(8,128)(2,1)S(1)} %pad_maximum_fusion.1.refs_1_), channel_id=1, source_target_pairs={{48,0},{0,16},{16,32},{32,48},{112,64},{64,80},{80,96},{96,112},{1... | collective-permute-start | bytes 884744 | tf_op jit(solution)/shard_map/ppermute | solution.py:378
  78.9 7.5 %collective-permute-start.4 = (bf16[2,64,1152]{2,1,0:T(8,128)(2,1)S(1)}, bf16[2,64,1152]{2,1,0:T(8,128)(2,1)S(1)}, u32[]{:S(2)}, u32[]{:S(2)}) collective-permute-start(bf16[2,64,1152]{2,1,0:T(8,128)(2,1)S(1)} %pad_maximum_fusion.1.refs_1_), channel_id=1, source_target_pairs={{16,0},{32,16},{48,32},{0,48},{80,64},{96,80},{112,96},{64,112},{1... | collective-permute-start | bytes 884744 | tf_op jit(solution)/shard_map/ppermute | solution.py:378
  81.7 30.9 %collective-permute-start.25 = (bf16[8,64,1024]{2,1,0:T(8,128)(2,1)}, bf16[8,64,1024]{2,1,0:T(8,128)(2,1)}, u32[]{:S(2)}, u32[]{:S(2)}) collective-permute-start(bf16[8,64,1024]{2,1,0:T(8,128)(2,1)} %bitcast_dynamic-update-slice_fusion.out_own), channel_id=1, source_target_pairs={{0,1},{1,0},{2,3},{3,2},{4,5},{5,4},{6,7},{7,6},{8,9},{9,8},{10,11... | collective-permute-start | bytes 3145736 | tf_op jit(solution)/shard_map/ppermute | solution.py:403
  81.7 9.0 %copy-start.15 = (s32[4,1]{0,1:T(1,128)S(1)}, s32[4,1]{0,1:T(1,128)}, u32[]{:S(2)}) copy-start(s32[4,1]{0,1:T(1,128)} %param.23) | copy-start | bytes 52
  83.2 3.3 %copy-start.4 = (bf16[2,64,1152]{2,1,0:T(8,128)(2,1)}, bf16[2,64,1152]{2,1,0:T(8,128)(2,1)S(1)}, u32[]{:S(2)}) copy-start(bf16[2,64,1152]{2,1,0:T(8,128)(2,1)S(1)} %collective-permute-done.15.refs_15_) | copy-start | bytes 884740
  83.2 9.7 %collective-permute-start.12 = (bf16[2,64,1152]{2,1,0:T(8,128)(2,1)}, bf16[2,64,1152]{2,1,0:T(8,128)(2,1)}, u32[]{:S(2)}, u32[]{:S(2)}) collective-permute-start(bf16[2,64,1152]{2,1,0:T(8,128)(2,1)} %pad_maximum_fusion.2.refs_8_), channel_id=1, source_target_pairs={{64,0},{80,16},{96,32},{112,48},{128,64},{144,80},{160,96},{176,11... | collective-permute-start | bytes 884744 | tf_op jit(solution)/shard_map/ppermute | solution.py:378
  85.5 1.0 copy-start.7
  85.5 9.6 %collective-permute-start.17 = (bf16[2,64,1152]{2,1,0:T(8,128)(2,1)}, bf16[2,64,1152]{2,1,0:T(8,128)(2,1)}, u32[]{:S(2)}, u32[]{:S(2)}) collective-permute-start(bf16[2,64,1152]{2,1,0:T(8,128)(2,1)} %pad_maximum_fusion.2.refs_8_), channel_id=1, source_target_pairs={{192,0},{208,16},{224,32},{240,48},{0,64},{16,80},{32,96},{48,112}... | collective-permute-start | bytes 884744 | tf_op jit(solution)/shard_map/ppermute | solution.py:378
  85.6 0.9 copy-start.6
  85.6 9.5 %collective-permute-start.3 = (bf16[2,64,1152]{2,1,0:T(8,128)(2,1)}, bf16[2,64,1152]{2,1,0:T(8,128)(2,1)}, u32[]{:S(2)}, u32[]{:S(2)}) collective-permute-start(bf16[2,64,1152]{2,1,0:T(8,128)(2,1)} %pad_maximum_fusion.refs_0_), channel_id=1, source_target_pairs={{16,0},{32,16},{48,32},{0,48},{80,64},{96,80},{112,96},{64,112},{1... | collective-permute-start | bytes 884744 | tf_op jit(solution)/shard_map/ppermute | solution.py:378
  86.5 0.7 copy-start.8
  87.2 10.5 %collective-permute-start.8 = (bf16[2,64,1152]{2,1,0:T(8,128)(2,1)}, bf16[2,64,1152]{2,1,0:T(8,128)(2,1)}, u32[]{:S(2)}, u32[]{:S(2)}) collective-permute-start(bf16[2,64,1152]{2,1,0:T(8,128)(2,1)} %pad_maximum_fusion.refs_0_), channel_id=1, source_target_pairs={{48,0},{0,16},{16,32},{32,48},{112,64},{64,80},{80,96},{96,112},{1... | collective-permute-start | bytes 884744 | tf_op jit(solution)/shard_map/ppermute | solution.py:378
  89.3 3.6 %copy-start.5 = (bf16[2,64,1152]{2,1,0:T(8,128)(2,1)S(1)}, bf16[2,64,1152]{2,1,0:T(8,128)(2,1)}, u32[]{:S(2)}) copy-start(bf16[2,64,1152]{2,1,0:T(8,128)(2,1)} %copy-done.4) | copy-start | bytes 884740
  92.9 9.2 %collective-permute-start.16 = (bf16[2,64,1152]{2,1,0:T(8,128)(2,1)S(1)}, bf16[2,64,1152]{2,1,0:T(8,128)(2,1)S(1)}, u32[]{:S(2)}, u32[]{:S(2)}) collective-permute-start(bf16[2,64,1152]{2,1,0:T(8,128)(2,1)S(1)} %copy-done.5), channel_id=1, source_target_pairs={{192,0},{208,16},{224,32},{240,48},{0,64},{16,80},{32,96},{48,112}... | collective-permute-start | bytes 884744 | tf_op jit(solution)/shard_map/ppermute | solution.py:378
  95.1 9.7 %collective-permute-start.7 = (bf16[2,64,1152]{2,1,0:T(8,128)(2,1)}, bf16[2,64,1152]{2,1,0:T(8,128)(2,1)S(1)}, u32[]{:S(2)}, u32[]{:S(2)}) collective-permute-start(bf16[2,64,1152]{2,1,0:T(8,128)(2,1)} %copy-done.7), channel_id=1, source_target_pairs={{48,0},{0,16},{16,32},{32,48},{112,64},{64,80},{80,96},{96,112},{1... | collective-permute-start | bytes 884744 | tf_op jit(solution)/shard_map/ppermute | solution.py:378
  95.1 9.7 %collective-permute-start.14 = (bf16[2,64,1152]{2,1,0:T(8,128)(2,1)}, bf16[2,64,1152]{2,1,0:T(8,128)(2,1)S(1)}, u32[]{:S(2)}, u32[]{:S(2)}) collective-permute-start(bf16[2,64,1152]{2,1,0:T(8,128)(2,1)} %collective-permute-done.12.refs_10_), channel_id=1, source_target_pairs={{64,0},{80,16},{96,32},{112,48},{128,64},{144,80},{160,96},{176,11... | collective-permute-start | bytes 884744 | tf_op jit(solution)/shard_map/ppermute | solution.py:378
  97.7 8.3 %collective-permute-start.5 = (bf16[2,64,1152]{2,1,0:T(8,128)(2,1)}, bf16[2,64,1152]{2,1,0:T(8,128)(2,1)S(1)}, u32[]{:S(2)}, u32[]{:S(2)}) collective-permute-start(bf16[2,64,1152]{2,1,0:T(8,128)(2,1)} %collective-permute-done.3.refs_2_), channel_id=1, source_target_pairs={{16,0},{32,16},{48,32},{0,48},{80,64},{96,80},{112,96},{64,112},{1... | collective-permute-start | bytes 884744 | tf_op jit(solution)/shard_map/ppermute | solution.py:378
  102.1 3.9 %copy-start.9 = (bf16[2,64,1152]{2,1,0:T(8,128)(2,1)}, bf16[2,64,1152]{2,1,0:T(8,128)(2,1)S(1)}, u32[]{:S(2)}) copy-start(bf16[2,64,1152]{2,1,0:T(8,128)(2,1)S(1)} %collective-permute-done.16.refs_13_) | copy-start | bytes 884740
  104.7 1.3 copy-start.10
  104.7 1.3 copy-start.11
  106.1 0.7 copy-start.12
  140.9 3.0 %collective-permute-start.26 = (bf16[16,8,16,256]{3,2,1,0:T(8,128)(2,1)}, bf16[16,8,16,256]{3,2,1,0:T(8,128)(2,1)S(1)}, u32[]{:S(2)}, u32[]{:S(2)}) collective-permute-start(bf16[16,8,16,256]{3,2,1,0:T(8,128)(2,1)} %get-tuple-element.18), channel_id=1, source_target_pairs={{0,1},{1,0},{2,3},{3,2},{4,5},{5,4},{6,7},{7,6},{8,9},{9,8},{10,11... | collective-permute-start | bytes 3145736 | tf_op jit(solution)/shard_map/ppermute | solution.py:471
  145.4 39.2 %copy-start.16 = (f32[4,1,128]{2,1,0:T(1,128)S(1)}, f32[4,1,128]{2,1,0:T(1,128)}, u32[]{:S(2)}) copy-start(f32[4,1,128]{2,1,0:T(1,128)} %get-tuple-element.15) | copy-start | bytes 6148
  178.8 12.2 %all-to-all-start.2 = ((bf16[16,16,256]{2,1,0:T(8,128)(2,1)}), bf16[16,16,256]{2,1,0:T(8,128)(2,1)S(1)}, u32[]{:S(2)}, u32[]{:S(2)}) async-start(bf16[16,16,256]{2,1,0:T(8,128)(2,1)} %broadcast_in_dim.34), calls=%async_computation.2 | async-start | bytes 262144 | tf_op jit(solution)/shard_map/all_to_all | solution.py:478
Sparse Core Ops, SparseCore 0:
  9.9 65.9 all-gather.1

commit v4 on v3

v4 whole, which is shorter than its diff:
```python
import functools
import math

import jax
import jax.numpy as jnp
from jax import lax
from jax.experimental import pallas as pl
from jax.experimental.pallas import tpu as pltpu
from jax.sharding import PartitionSpec as P

HEADS = 8
HIST = 128
LANES = 128
BF = jnp.bfloat16
F32 = jnp.float32
VMEM_BYTES = 56 * 1024 * 1024


def sigmoid(v):
    return 0.5 * jnp.tanh(0.5 * v) + 0.5


def dot(a, b):
    return jnp.dot(a, b, preferred_element_type=F32)


def dot_t(a, b):
    return lax.dot_general(a, b, (((1,), (1,)), ((), ())), preferred_element_type=F32)


def split3(v):
    high = v.astype(BF)
    rest = v - high.astype(F32)
    middle = rest.astype(BF)
    low = (rest - middle.astype(F32)).astype(BF)
    return high, middle, low


def prepare_kernel(nblocks, place_a, place_b, *refs):
    count = (len(refs) - 6) // 2
    halves = ((place_a, refs[:count]), (place_b, refs[count : 2 * count]))
    table, base, normed, mask, rows_s, sems = refs[2 * count :]
    block = pl.program_id(0)
    width = base.shape[1]
    actions = table.shape[0]
    half = HIST // 2

    def fetch(which, b, source):
        return pltpu.make_async_copy(
            source, rows_s.at[b, pl.ds(which * half, half)], sems.at[which, b]
        )

    @pl.when(block == 0)
    def _():
        for b in range(nblocks):
            for which, (place, arrays) in enumerate(halves):
                for k, array in enumerate(arrays):

                    @pl.when(place[b] // 2 == k)
                    def _():
                        fetch(which, b, array.at[lax.rem(place[b], 2)]).start()

    for which, (place, arrays) in enumerate(halves):
        fetch(which, block, arrays[0].at[0]).wait()
    rows = rows_s[block]
    tail = rows[:, width:].astype(F32)
    lane = lax.broadcasted_iota(jnp.int32, (HIST, actions), 1).astype(F32)
    onehot = jnp.where(tail[:, :actions] == lane, 1.0, 0.0).astype(BF)
    value = rows[:, :width].astype(F32)
    high, middle, low = split3(table[...])
    value = value + ((dot(onehot, low) + dot(onehot, middle)) + dot(onehot, high))
    scale = lax.rsqrt(jnp.mean(value * value, -1, keepdims=True) + 1e-06)
    base[...] = value
    normed[...] = (value * scale).astype(BF)
    position = lax.broadcasted_iota(jnp.int32, (HIST, LANES), 0).astype(F32)
    mask[...] = jnp.where(position < tail[:, LANES - 1 :], 1.0, 0.0)


def prepare(place_a, place_b, halves_a, halves_b, table):
    nblocks = place_a.shape[0]
    width = table.shape[1]
    total = nblocks * HIST
    arrays = list(halves_a) + list(halves_b)
    return pl.pallas_call(
        functools.partial(prepare_kernel, nblocks),
        grid_spec=pltpu.PrefetchScalarGridSpec(
            num_scalar_prefetch=2,
            grid=(nblocks,),
            in_specs=[pl.BlockSpec(memory_space=pl.ANY)] * len(arrays)
            + [pl.BlockSpec(table.shape, lambda b, p, q: (0, 0))],
            out_specs=[
                pl.BlockSpec((HIST, width), lambda b, p, q: (b, 0)),
                pl.BlockSpec((HIST, width), lambda b, p, q: (b, 0)),
                pl.BlockSpec((HIST, LANES), lambda b, p, q: (b, 0)),
            ],
            scratch_shapes=[
                pltpu.VMEM((nblocks, HIST, arrays[0].shape[-1]), BF),
                pltpu.SemaphoreType.DMA((2, nblocks)),
            ],
        ),
        out_shape=[
            jax.ShapeDtypeStruct((total, width), F32),
            jax.ShapeDtypeStruct((total, width), BF),
            jax.ShapeDtypeStruct((total, LANES), F32),
        ],
        compiler_params=pltpu.CompilerParams(vmem_limit_bytes=VMEM_BYTES),
        name="prepare",
    )(place_a, place_b, *arrays, table)


ENCODE_STEPS = HEADS // 2
GROUP = 2


def attention_kernel(
    counts,
    core,
    normed,
    base,
    weights,
    queries,
    cand_t,
    mask,
    score_weight,
    own,
    labels,
    scores,
    error,
    slopes,
    mine,
    other,
    normed_s,
    base_s,
    mix_s,
    out_s,
    queries_s,
    cand_s,
    gate_s,
    mixed_s,
    qkv_s,
    gated_s,
    encoded_s,
    logit_s,
    weight_s,
    slope_s,
    sems,
    mix_sems,
):
    step = pl.program_id(0)
    total, width = normed_s.shape
    pair = 2 * LANES

    def mix_copy(i, group):
        start = pl.multiple_of(group * width + i * pair, pair)
        return pltpu.make_async_copy(
            weights.at[:, pl.ds(start, pair)], mix_s.at[i, group], mix_sems.at[i, group]
        )

    normed_copy = pltpu.make_async_copy(normed, normed_s, sems.at[0])
    base_copy = pltpu.make_async_copy(base, base_s, sems.at[1])
    out_copy = pltpu.make_async_copy(weights.at[:, pl.ds(4 * width, width)], out_s, sems.at[2])
    query_copy = pltpu.make_async_copy(queries, queries_s, sems.at[3])
    cand_copy = pltpu.make_async_copy(cand_t, cand_s, sems.at[4])

    @pl.when(step == 0)
    def _():
        normed_copy.start()
        for i in range(ENCODE_STEPS):
            for group in range(4):
                mix_copy(i, group).start()
        for copy in (base_copy, out_copy, query_copy, cand_copy):
            copy.start()
        normed_copy.wait()

    @pl.when(step < ENCODE_STEPS)
    def _():
        for group in range(4):
            mix_copy(step, group).wait()
        users = total // HIST
        for k in range(2):
            cols = slice(k * LANES, (k + 1) * LANES)
            columns = jnp.concatenate([mix_s[step, g, :, cols] for g in range(4)], axis=1)
            projected = dot(normed_s[...], columns)
            projected = projected * sigmoid(projected)
            gate_s[2 * step + k] = projected[:, :LANES]
            qkv_s[k] = projected[:, LANES:].astype(BF)
        units = [(k, slice(u * HIST, (u + 1) * HIST)) for k in range(2) for u in range(users)]
        for n, (k, part) in enumerate(units):
            logit_s[n] = dot_t(qkv_s[k, part, LANES : 2 * LANES], qkv_s[k, part, 2 * LANES :])
        row = lax.broadcasted_iota(jnp.int32, (HIST, HIST), 0)
        column = lax.broadcasted_iota(jnp.int32, (HIST, HIST), 1)
        causal = column <= row
        for n in range(len(units)):
            logits = logit_s[n] * (1.0 / math.sqrt(LANES))
            weight = jnp.where(causal, logits * sigmoid(logits) * (1.0 / HIST), 0.0)
            weight_s[n] = weight.astype(BF)
        for n, (k, part) in enumerate(units):
            mixed_s[2 * step + k, part] = dot(weight_s[n], qkv_s[k, part, :LANES])

    @pl.when(step == ENCODE_STEPS - 1)
    def _():
        square = mixed_s[0] * mixed_s[0]
        for h in range(1, HEADS):
            square = square + mixed_s[h] * mixed_s[h]
        scale = lax.rsqrt(jnp.sum(square, -1, keepdims=True) * (1.0 / width) + 1e-06)
        for h in range(HEADS):
            gated_s[:, h * LANES : (h + 1) * LANES] = (mixed_s[h] * scale * gate_s[h]).astype(BF)
        active = mask[:, :1] > 0.0
        base_copy.wait()
        out_copy.wait()
        for n in range(width // pair):
            cols = slice(n * pair, (n + 1) * pair)
            value = base_s[:, cols] + dot(gated_s[...], out_s[:, cols])
            value = jnp.where(active, value, 0.0).astype(BF)
            encoded_s[:, :, cols] = value.reshape(total // (GROUP * HIST), GROUP * HIST, pair)
        query_copy.wait()
        cand_copy.wait()

    @pl.when(step >= ENCODE_STEPS)
    def _():
        now = step - ENCODE_STEPS
        lane = lax.broadcasted_iota(jnp.int32, (HEADS, width), 1) // LANES
        head_row = lax.broadcasted_iota(jnp.int32, (HEADS, width), 0)
        spread_weight = jnp.where(lane == head_row, score_weight[...], 0.0)
        high, middle, low = split3(spread_weight)
        parts = [slice(g * HIST, (g + 1) * HIST) for g in range(GROUP)]
        units = [(h, g) for g in range(GROUP) for h in range(HEADS)]
        heads = [slice(h * LANES, (h + 1) * LANES) for h in range(HEADS)]
        for n, (h, g) in enumerate(units):
            logit_s[n] = dot_t(
                queries_s[now, parts[g], heads[h]], encoded_s[now, parts[g], heads[h]]
            )
        along = []
        for part in parts:
            keys = encoded_s[now, part]
            along.append((dot_t(low, keys) + dot_t(middle, keys)) + dot_t(high, keys))
        totals = [jnp.zeros((HIST, HIST), F32) for _ in range(GROUP)]
        for n, (h, g) in enumerate(units):
            row = along[g][h : h + 1]
            logits = logit_s[n] * (1.0 / math.sqrt(LANES))
            gate = sigmoid(logits)
            product = logits * gate
            weight = (product * (1.0 / HIST)).astype(BF).astype(F32)
            totals[g] = totals[g] + weight * row
            slope = gate + product * (1.0 - gate)
            weight_s[n] = (slope * (row * (1.0 / (HIST * math.sqrt(LANES))))).astype(BF)
        for n, (h, g) in enumerate(units):
            logit_s[n] = dot(weight_s[n], encoded_s[now, parts[g], heads[h]])
        for g, part in enumerate(parts):
            partial = jnp.sum(totals[g], -1, keepdims=True).astype(BF).astype(F32)
            partial_row = jnp.broadcast_to(partial, (HIST, HIST)).T[:1]
            active = lax.broadcasted_iota(jnp.int32, (1, HIST), 1) < counts[now * GROUP + g]
            score = jnp.where(active, partial_row + own[g], 0.0)
            err = jnp.where(active, sigmoid(score) - labels[g], 0.0)
            scores[g] = score
            error[g] = err
            err_rows = jnp.broadcast_to(err, (HIST, HIST)).T
            for h in range(HEADS):
                direction = logit_s[g * HEADS + h].astype(BF).astype(F32)
                slope = (err_rows * direction).astype(BF)
                slopes[part, heads[h]] = slope
                slope_s[now, part, heads[h]] = slope

    @pl.when(step == pl.num_programs(0) - 1)
    def _():
        _, pairs, tall, wide = mine.shape
        right = width // wide
        down = mine.shape[0] // right
        piece = tall * down
        first = core[0] == 0
        for n in range(right):
            cols = slice(n * wide, (n + 1) * wide)
            grad = dot(cand_s[...], slope_s[:, :, cols].reshape(-1, wide))
            for p in range(pairs):
                one = grad[2 * p * piece : (2 * p + 1) * piece]
                two = grad[(2 * p + 1) * piece : (2 * p + 2) * piece]
                kept = jnp.where(first, one, two).astype(BF)
                sent = jnp.where(first, two, one).astype(BF)
                for a in range(down):
                    rows = slice(a * tall, (a + 1) * tall)
                    mine[a * right + n, p] = kept[rows]
                    other[a * right + n, p] = sent[rows]


def attention(
    counts,
    core,
    normed,
    base,
    mask,
    weights,
    queries,
    cand_t,
    score_weight,
    own,
    labels,
    pairs,
    users,
):
    nblocks = counts.shape[0]
    total, width = queries.shape
    rows = total // nblocks
    groups = nblocks // GROUP
    side = math.isqrt(users)
    shape = (users, pairs, width // (2 * pairs * side), width // side)
    current = lambda i: jnp.maximum(i - ENCODE_STEPS, 0)
    row = pl.BlockSpec((GROUP, 1, rows), lambda i, n, c: (current(i), 0, 0))
    whole = lambda i, n, c: (0, 0)
    whole4 = lambda i, n, c: (0, 0, 0, 0)
    anywhere = pl.BlockSpec(memory_space=pl.ANY)
    return pl.pallas_call(
        attention_kernel,
        grid_spec=pltpu.PrefetchScalarGridSpec(
            num_scalar_prefetch=2,
            grid=(ENCODE_STEPS + groups,),
            in_specs=[anywhere] * 5
            + [
                pl.BlockSpec((total, LANES), whole),
                pl.BlockSpec((1, width), whole),
                row,
                row,
            ],
            out_specs=[
                row,
                row,
                pl.BlockSpec((GROUP * rows, width), lambda i, n, c: (current(i), 0)),
                pl.BlockSpec(shape, whole4),
                pl.BlockSpec(shape, whole4),
            ],
            scratch_shapes=[
                pltpu.VMEM((total, width), BF),
                pltpu.VMEM((total, width), F32),
                pltpu.VMEM((ENCODE_STEPS, 4, width, 2 * LANES), BF),
                pltpu.VMEM((width, width), BF),
                pltpu.VMEM((groups, GROUP * rows, width), BF),
                pltpu.VMEM((width, total), BF),
                pltpu.VMEM((HEADS, total, LANES), F32),
                pltpu.VMEM((HEADS, total, LANES), F32),
                pltpu.VMEM((2, total, 3 * LANES), BF),
                pltpu.VMEM((total, width), BF),
                pltpu.VMEM((groups, GROUP * rows, width), BF),
                pltpu.VMEM((GROUP * HEADS, HIST, HIST), F32),
                pltpu.VMEM((GROUP * HEADS, HIST, HIST), BF),
                pltpu.VMEM((groups, GROUP * rows, width), BF),
                pltpu.SemaphoreType.DMA((5,)),
                pltpu.SemaphoreType.DMA((ENCODE_STEPS, 4)),
            ],
        ),
        out_shape=[
            jax.ShapeDtypeStruct((nblocks, 1, rows), F32),
            jax.ShapeDtypeStruct((nblocks, 1, rows), F32),
            jax.ShapeDtypeStruct((total, width), BF),
            jax.ShapeDtypeStruct(shape, BF),
            jax.ShapeDtypeStruct(shape, BF),
        ],
        compiler_params=pltpu.CompilerParams(vmem_limit_bytes=VMEM_BYTES),
        name="attention",
    )(
        counts,
        core,
        normed,
        base,
        weights,
        queries.reshape(groups, GROUP * rows, width),
        cand_t,
        mask,
        score_weight,
        own,
        labels,
    )


def shift(array, side, dx, dy):
    moves = []
    for x in range(side):
        for y in range(side):
            moves.append(((x + dx) % side * side + (y + dy) % side, x * side + y))
    return lax.ppermute(array, "user", moves)


def spread(piece, side, x_first):
    first = lambda a, d: shift(a, side, d, 0) if x_first else shift(a, side, 0, d)
    second = lambda a, d: shift(a, side, 0, d) if x_first else shift(a, side, d, 0)
    low = jnp.stack([piece, first(piece, 1)])
    high = jnp.stack([first(piece, 2), first(piece, -1)])
    low_after, high_before = second(low, 1), second(high, -1)
    high_after, low_before = second(high, 1), second(low, -1)
    low_two, high_two = second(low_after, 1), second(high_before, -1)
    return (low, high, low_after, high_after, low_two, high_two, low_before, high_before)


def join_kernel(left, right, out, sems):
    wide = left.shape[1]
    first = pltpu.make_async_copy(left, out.at[:, pl.ds(0, wide)], sems.at[0])
    second = pltpu.make_async_copy(right, out.at[:, pl.ds(wide, right.shape[1])], sems.at[1])
    first.start()
    second.start()
    first.wait()
    second.wait()


def join(left, right):
    anywhere = pl.BlockSpec(memory_space=pl.ANY)
    return pl.pallas_call(
        join_kernel,
        in_specs=[anywhere, anywhere],
        out_specs=anywhere,
        out_shape=jax.ShapeDtypeStruct((left.shape[0], left.shape[1] + right.shape[1]), left.dtype),
        scratch_shapes=[pltpu.SemaphoreType.DMA((2,))],
        name="join",
    )(left, right)


def assemble_kernel(pieces, out):
    count, tall, wide = pieces.shape
    right = out.shape[1] // wide
    for k in range(count):
        a, b = k // right, k % right
        rows, cols = slice(a * tall, (a + 1) * tall), slice(b * wide, (b + 1) * wide)
        out[rows, cols] = pieces[k].astype(F32)


def assemble(pieces, right):
    count, tall, wide = pieces.shape
    return pl.pallas_call(
        assemble_kernel,
        out_shape=jax.ShapeDtypeStruct((count // right * tall, right * wide), F32),
        name="assemble",
    )(pieces)


def body(
    history_items,
    history_events,
    history_lengths,
    action_table,
    mix_weight,
    out_weight,
    query_weight,
    score_weight,
    self_weight,
    candidates,
    block_owner,
    row_counts,
    labels,
):
    users = lax.axis_size("user")
    loaders = lax.axis_size("loader")
    pairs = loaders // 2
    nblocks, rows, width = candidates.shape

    weights = lax.all_gather(join(mix_weight, out_weight), "loader", axis=0, tiled=True)
    actions = action_table.shape[0]
    packed = jnp.concatenate(
        [
            history_items[0],
            jnp.broadcast_to(history_events[0][:, None].astype(BF), (HIST, actions)),
            jnp.broadcast_to(history_lengths[0].astype(BF), (HIST, LANES - actions)),
        ],
        axis=1,
    )
    side = math.isqrt(users)
    half = HIST // 2
    halves_a = spread(packed[:half], side, True)
    halves_b = spread(packed[half:], side, False)

    flat = candidates.reshape(-1, width)
    queries = jnp.dot(flat, query_weight, preferred_element_type=F32).astype(BF)
    cand_t = flat.T
    own = jnp.sum(candidates.astype(F32) * self_weight, -1)

    owner = block_owner[:, 0]
    here = lax.axis_index("user").astype(jnp.int32)
    far_x = lax.rem(owner // side - here // side + side, side)
    far_y = lax.rem(lax.rem(owner, side) - lax.rem(here, side) + side, side)
    base, normed, mask = prepare(
        far_y * side + far_x, far_x * side + far_y, halves_a, halves_b, action_table
    )
    core = lax.rem(lax.axis_index("loader").astype(jnp.int32), 2)[None]
    scores, error, slopes, mine, other = attention(
        row_counts,
        core,
        normed,
        base,
        mask,
        weights,
        queries,
        cand_t,
        score_weight[None],
        own[:, None],
        labels[:, None],
        pairs,
        users,
    )

    arrived = lax.ppermute(other, "loader", [(i, i ^ 1) for i in range(loaders)])
    pieces = (mine.astype(F32) + arrived.astype(F32)).astype(BF)
    pieces = lax.all_to_all(pieces, "user", 0, 0, tiled=True)
    pieces = jnp.sum(pieces.astype(F32), 0).astype(BF)
    groups = [[c + 2 * i for i in range(pairs)] for c in range(2)]
    pieces = lax.all_to_all(pieces, "loader", 0, 0, axis_index_groups=groups, tiled=True)
    piece = jnp.sum(pieces.astype(F32), 0).astype(BF)
    pieces = lax.all_to_all(
        jnp.broadcast_to(piece[None], (users,) + piece.shape), "user", 0, 0, tiled=True
    )
    query_grad = assemble(pieces, side)

    back = lax.dot_general(slopes, query_weight, (((1,), (1,)), ((), ())), preferred_element_type=F32)
    row_grads = (error.reshape(-1)[:, None] * self_weight + back).astype(BF)
    return (scores[:, 0], row_grads.reshape(nblocks, rows, width), query_grad)


def solution(mesh):
    placed = (
        P(("user", "loader"), None, None),
        P(("user", "loader"), None),
        P(("user", "loader")),
        P(),
        P("loader", None),
        P("loader", None),
        P(),
        P(),
        P(),
        P(("user", "loader"), None, None),
        P(("user", "loader"), None),
        P(("user", "loader")),
        P(("user", "loader"), None),
    )
    return jax.shard_map(
        body,
        mesh=mesh,
        in_specs=placed,
        out_specs=(
            P(("user", "loader"), None),
            P(("user", "loader"), None, None),
            P("loader", None),
        ),
        check_vma=False,
    )
```

time: 199 us -> 179 us (0.90)
  waiting for transfers between devices: 46.3 us -> 30.2 us
  starting transfers between devices: 47.7 us -> 33.2 us
  Pallas kernels: 34 us -> 48.3 us
  local copies, waits for them, and re-layouts: 10.9 us -> 4.66 us
  blocking collectives: 32.6 us -> 34.8 us
    ppermute x8 -> x0, waiting for transfers between devices: 31.3 us -> none  [the longest x7 31.3 us: around(): lax.ppermute(a, 'loader', [((i + 2 * d) % loaders, i) for i in range(load...]
    all_gather x1, waiting for transfers between devices: 0.02 us -> 16.3 us  [body(): lax.all_gather(join(mix_weight, out_weight), 'loader', axis=0, tiled=True)]
    ppermute x8 -> x0, starting transfers between devices: 14.6 us -> none  [the longest x7 14.6 us: around(): lax.ppermute(a, 'loader', [((i + 2 * d) % loaders, i) for i in range(load...]
    pallas_call x2 -> x3, Pallas kernels: 28.2 us -> 42.4 us  [the longest x1 21 us: join(): pl.pallas_call(join_kernel, in_specs=[anywhere, anywhere], out_specs=anyw...]
    unnamed x42 -> x18, local copies, waits for them, and re-layouts: 6.87 us -> 1.47 us
  transfers between devices with their start and end apart: 29 -> 21, of which waited for: 14 -> 8; matrix products, arithmetic and copies ran while one was open for 9% -> 7% of each run, Pallas kernels for 3% -> 3%
where the time goes in v4:
time: 179 us; the launch traced here: 178 us
  Pallas kernels  48.3 us (27%)
  blocking collectives  34.8 us (19%)
  starting transfers between devices  33.2 us (19%)
  waiting for transfers between devices  30.2 us (17%)
  between operations  14.9 us (8%)
  other arithmetic  6.48 us (4%)
  matrix products  5.76 us (3%)
  local copies, waits for them, and re-layouts  4.66 us (3%)
    ppermute x18, starting transfers between devices, shift(): return lax.ppermute(array, 'user', moves)  27.1 us
    all_to_all x1, blocking collectives, body(): pieces = lax.all_to_all(pieces, 'user', 0, 0, tiled=True)  22.3 us
    pallas_call x1, Pallas kernels, join(): pl.pallas_call(join_kernel, in_specs=[anywhere, anywhere], out_specs=anyw...  21 us
    pallas_call x1, Pallas kernels, attention(): pl.pallas_call(attention_kernel, grid_spec=pltpu.PrefetchScalarGridSpec(n...  19.9 us
    all_gather x1, waiting for transfers between devices, body(): lax.all_gather(join(mix_weight, out_weight), 'loader', axis=0, tiled=True)  16.3 us
    all_to_all x1, blocking collectives, body(): lax.all_to_all(pieces, 'loader', 0, 0, axis_index_groups=groups, tiled=True)  12.4 us
    ppermute x18, waiting for transfers between devices, shift(): return lax.ppermute(array, 'user', moves)  8.38 us
    pallas_call x1, Pallas kernels, prepare(): pl.pallas_call(functools.partial(prepare_kernel, nblocks), grid_spec=pltp...  5.83 us
  transfers between devices with their start and end apart: 21, of which 8 were waited for; matrix products, arithmetic and copies ran while one was open for 7% of the time, Pallas kernels for 3%

profile of v4, /device:TPU:2, one launch (start us, length us, event | category | flops | bytes accessed | tf_op | source)
XLA Modules:
  0.0 178.3 jit_solution(184178290416691543)
XLA Ops:
  7.2 0.0 copy-start
  7.2 0.0 all-gather.2.cloned.1.call-start
  7.2 21.0 %join.1 = bf16[64,5120]{1,0:T(8,128)(2,1)} custom-call(bf16[64,4096]{1,0:T(8,128)(2,1)} %left.1, bf16[64,1024]{1,0:T(8,128)(2,1)} %right.1), custom_call_target="tpu_custom_call" | custom-call | tf_op jit(solution)/shard_map/join/pallas_call | solution.py:404
  28.2 0.0 all-gather.2.cloned.1.call-update
  28.2 0.0 copy-start.1
  29.0 0.7 convert_bitcast_fusion
  29.6 0.1 broadcast_in_dim.29
  29.7 1.1 concatenate.3
  30.9 2.2 %collective-permute-start.1 = (bf16[64,1152]{1,0:T(8,128)(2,1)S(1)}, bf16[64,1152]{1,0:T(8,128)(2,1)S(1)}, u32[]{:S(2)}, u32[]{:S(2)}) collective-permute-start(bf16[64,1152]{1,0:T(8,128)(2,1)S(1)} %get-tuple-element.25), channel_id=1, source_target_pairs={{128,0},{144,16},{160,32},{176,48},{192,64},{208,80},{224,96},{240... | collective-permute-start | bytes 442376 | tf_op jit(solution)/shard_map/ppermute | solution.py:378
  33.1 1.6 collective-permute-start.2
  34.7 1.6 collective-permute-start.10
  36.3 1.1 collective-permute-start.9
  37.3 1.0 collective-permute-start.11
  38.3 0.0 collective-permute-done.1
  38.3 2.2 %collective-permute-start = (bf16[64,1152]{1,0:T(8,128)(2,1)S(1)}, bf16[64,1152]{1,0:T(8,128)(2,1)S(1)}, u32[]{:S(2)}, u32[]{:S(2)}) collective-permute-start(bf16[64,1152]{1,0:T(8,128)(2,1)S(1)} %get-tuple-element.25), channel_id=1, source_target_pairs={{64,0},{80,16},{96,32},{112,48},{128,64},{144,80},{160,96},{176,11... | collective-permute-start | bytes 442376 | tf_op jit(solution)/shard_map/ppermute | solution.py:378
  40.5 0.8 collective-permute-done.2
  41.3 1.7 collective-permute-start.6
  43.0 0.8 collective-permute-done
  43.8 3.0 %collective-permute-start.4 = (bf16[2,64,1152]{2,1,0:T(8,128)(2,1)S(1)}, bf16[2,64,1152]{2,1,0:T(8,128)(2,1)S(1)}, u32[]{:S(2)}, u32[]{:S(2)}) collective-permute-start(bf16[2,64,1152]{2,1,0:T(8,128)(2,1)S(1)} %pad_maximum_fusion.1.refs_1_), channel_id=1, source_target_pairs={{16,0},{32,16},{48,32},{0,48},{80,64},{96,80},{112,96},{64,112},{1... | collective-permute-start | bytes 884744 | tf_op jit(solution)/shard_map/ppermute | solution.py:378
  46.8 0.7 pad_maximum_fusion.refs_0_
  47.6 0.0 collective-permute-done.10
  47.6 0.0 collective-permute-start.8
  47.6 0.0 collective-permute-done.11
  47.6 3.2 %collective-permute-start.3 = (bf16[2,64,1152]{2,1,0:T(8,128)(2,1)}, bf16[2,64,1152]{2,1,0:T(8,128)(2,1)}, u32[]{:S(2)}, u32[]{:S(2)}) collective-permute-start(bf16[2,64,1152]{2,1,0:T(8,128)(2,1)} %pad_maximum_fusion.refs_0_), channel_id=1, source_target_pairs={{16,0},{32,16},{48,32},{0,48},{80,64},{96,80},{112,96},{64,112},{1... | collective-permute-start | bytes 884744 | tf_op jit(solution)/shard_map/ppermute | solution.py:378
  50.8 0.7 pad_maximum_fusion.3.refs_9_
  51.5 0.0 collective-permute-done.9
  51.5 2.0 %collective-permute-start.15 = (bf16[2,64,1152]{2,1,0:T(8,128)(2,1)}, bf16[2,64,1152]{2,1,0:T(8,128)(2,1)}, u32[]{:S(2)}, u32[]{:S(2)}) collective-permute-start(bf16[2,64,1152]{2,1,0:T(8,128)(2,1)} %pad_maximum_fusion.3.refs_9_), channel_id=1, source_target_pairs={{192,0},{208,16},{224,32},{240,48},{0,64},{16,80},{32,96},{48,112}... | collective-permute-start | bytes 884744 | tf_op jit(solution)/shard_map/ppermute | solution.py:378
  53.6 0.7 pad_maximum_fusion.2.refs_8_
  54.3 0.0 collective-permute-done.6.refs_7_
  54.3 0.0 collective-permute-start.13
  54.3 0.0 collective-permute-done.4.refs_3_
  54.3 0.8 copy-done.5
  55.1 2.7 %collective-permute-start.12 = (bf16[2,64,1152]{2,1,0:T(8,128)(2,1)}, bf16[2,64,1152]{2,1,0:T(8,128)(2,1)}, u32[]{:S(2)}, u32[]{:S(2)}) collective-permute-start(bf16[2,64,1152]{2,1,0:T(8,128)(2,1)} %pad_maximum_fusion.2.refs_8_), channel_id=1, source_target_pairs={{64,0},{80,16},{96,32},{112,48},{128,64},{144,80},{160,96},{176,11... | collective-permute-start | bytes 884744 | tf_op jit(solution)/shard_map/ppermute | solution.py:378
  57.8 2.3 %convolution_convert_fusion = bf16[512,1024]{1,0:T(8,128)(2,1)} fusion(bf16[512,1024]{1,0:T(8,128)(2,1)S(1)} %bitcast.48, bf16[1024,1024]{1,0:T(8,128)(2,1)S(1)} %copy-done), kind=kOutput, calls=%fused_computation.3 | convolution fusion | flops 1074266112 | bytes 4194304 | tf_op jit(solution)/shard_map/dot_general | solution.py:468
  60.1 0.5 multiply_add_fusion
  60.6 0.0 collective-permute-done.8.refs_6_
  60.6 0.0 collective-permute-start.17
  60.6 0.0 collective-permute-done.3.refs_2_
  60.6 0.4 collective-permute-start.7
  61.0 3.1 %collective-permute-start.5 = (bf16[2,64,1152]{2,1,0:T(8,128)(2,1)}, bf16[2,64,1152]{2,1,0:T(8,128)(2,1)}, u32[]{:S(2)}, u32[]{:S(2)}) collective-permute-start(bf16[2,64,1152]{2,1,0:T(8,128)(2,1)} %collective-permute-done.3.refs_2_), channel_id=1, source_target_pairs={{16,0},{32,16},{48,32},{0,48},{80,64},{96,80},{112,96},{64,112},{1... | collective-permute-start | bytes 884744 | tf_op jit(solution)/shard_map/ppermute | solution.py:378
  64.1 1.4 collective-permute-start.16
  65.5 2.4 %collective-permute-done.12.refs_10_ = bf16[2,64,1152]{2,1,0:T(8,128)(2,1)} collective-permute-done((bf16[2,64,1152]{2,1,0:T(8,128)(2,1)}, bf16[2,64,1152]{2,1,0:T(8,128)(2,1)}, u32[]{:S(2)}, u32[]{:S(2)}) %collective-permute-start.12) | collective-permute-done | bytes 294944 | tf_op jit(solution)/shard_map/ppermute | solution.py:378
  67.9 0.0 collective-permute-start.14
  67.9 0.9 multiply_reduce_fusion
  68.8 1.3 copy.18
  70.1 0.5 multiply_add_fusion.1.place_a
  70.7 0.0 collective-permute-done.17.refs_14_
  70.7 1.7 collective-permute-done.16.refs_13_
  72.3 2.6 %collective-permute-done.14.refs_12_ = bf16[2,64,1152]{2,1,0:T(8,128)(2,1)} collective-permute-done((bf16[2,64,1152]{2,1,0:T(8,128)(2,1)}, bf16[2,64,1152]{2,1,0:T(8,128)(2,1)}, u32[]{:S(2)}, u32[]{:S(2)}) %collective-permute-start.14) | collective-permute-done | bytes 294944 | tf_op jit(solution)/shard_map/ppermute | solution.py:378
  75.0 5.8 %prepare.1 = (f32[512,1024]{1,0:T(8,128)}, bf16[512,1024]{1,0:T(8,128)(2,1)}, f32[512,128]{1,0:T(8,128)}) custom-call(s32[4]{0:T(128)} %multiply_add_fusion.1.place_a, s32[4]{0:T(128)} %get-tuple-element.19.place_b, bf16[2,64,1152]{2,1,0:T(8,128)(2,1)} %pad_maximum_fusion.refs_0_, bf16[2,64,1152]{2,1,0:T(8,128)(2,1)} %copy-done.2, ...), custom_call_target="tpu_custom_call" | custom-call | tf_op jit(solution)/shard_map/prepare/pallas_call | solution.py:84
  80.8 16.3 %all-gather.2.cloned.1.call-done.weights = bf16[1024,5120]{1,0:T(8,128)(2,1)} async-done(((bf16[64,5120]{1,0:T(8,128)(2,1)}), bf16[1024,5120]{1,0:T(8,128)(2,1)}) %all-gather.2.cloned.1.call-update) | async-done | bytes 10485776 | tf_op jit(solution)/shard_map/all_gather | solution.py:452
  97.1 19.9 %attention.1 = (f32[4,1,128]{2,1,0:T(1,128)}, f32[4,1,128]{2,1,0:T(1,128)}, bf16[512,1024]{1,0:T(8,128)(2,1)}, bf16[16,8,16,256]{3,2,1,0:T(8,128)(2,1)}, bf16[16,8,16,256]{3,2,1,0:T(8,128)(2,1)}) custom-call(s32[4]{0:T(128)} %counts.1, s32[1]{0:T(128)} %bitcast.core, bf16[512,1024]{1,0:T(8,128)(2,1)} %get-tuple-element.11.normed, ...), custom_call_target="tpu_custom_call" | custom-call | tf_op jit(solution)/shard_map/attention/pallas_call | solution.py:311
  117.0 0.3 collective-permute-start.18
  117.3 2.6 %collective-permute-done.18 = bf16[16,8,16,256]{3,2,1,0:T(8,128)(2,1)S(1)} collective-permute-done((bf16[16,8,16,256]{3,2,1,0:T(8,128)(2,1)}, bf16[16,8,16,256]{3,2,1,0:T(8,128)(2,1)S(1)}, u32[]{:S(2)}, u32[]{:S(2)}) %collective-permute-start.18) | collective-permute-done | bytes 1048608 | tf_op jit(solution)/shard_map/ppermute | solution.py:496
  119.9 1.5 add_convert_fusion
  121.4 22.3 %all_to_all.15 = bf16[16,8,16,256]{3,2,1,0:T(8,128)(2,1)S(1)} all-to-all(bf16[16,8,16,256]{3,2,1,0:T(8,128)(2,1)S(1)} %add_convert_fusion), channel_id=1, replica_groups=mesh['user'=16,'loader'=16] {'user'}, dimensions={0} | all-to-all | bytes 2097152 | tf_op jit(solution)/shard_map/all_to_all | solution.py:498
  143.8 0.1 reduce_sum.34
  143.9 12.4 %all_to_all.16 = bf16[8,16,256]{2,1,0:T(8,128)(2,1)S(1)} all-to-all(bf16[8,16,256]{2,1,0:T(8,128)(2,1)S(1)} %reduce_sum.34), channel_id=1, replica_groups={{0,2,4,6,8,10,12,14},{1,3,5,7,9,11,13,15},{16,18,20,22,24,26,28,30},{17..., dimensions={0} | all-to-all | bytes 131072 | tf_op jit(solution)/shard_map/all_to_all | solution.py:501
  156.4 0.7 broadcast_in_dim.34
  157.0 5.7 %all-to-all-start.2 = ((bf16[16,16,256]{2,1,0:T(8,128)(2,1)}), bf16[16,16,256]{2,1,0:T(8,128)(2,1)S(1)}, u32[]{:S(2)}, u32[]{:S(2)}) async-start(bf16[16,16,256]{2,1,0:T(8,128)(2,1)} %broadcast_in_dim.34), calls=%async_computation.2 | async-start | bytes 262144 | tf_op jit(solution)/shard_map/all_to_all | solution.py:503
  162.8 3.5 %add_convert_fusion.1 = bf16[512,1024]{1,0:T(8,128)(2,1)} fusion(bf16[512,1024]{1,0:T(8,128)(2,1)} %get-tuple-element.16, bf16[1024,1024]{1,0:T(8,128)(2,1)S(1)} %copy-done, f32[1024]{0:T(1024)S(1)} %copy-done.6, f32[512]{0:T(512)S(1)} %bitcast.62), kind=kOutput, calls=%fused_computation.1 | convolution fusion | flops 1075314688 | bytes 4200448 | tf_op jit(solution)/shard_map/dot_general | solution.py:508
  166.3 2.9 %all-to-all-done.2.pieces = bf16[16,16,256]{2,1,0:T(8,128)(2,1)S(1)} async-done(((bf16[16,16,256]{2,1,0:T(8,128)(2,1)}), bf16[16,16,256]{2,1,0:T(8,128)(2,1)S(1)}, u32[]{:S(2)}, u32[]{:S(2)}) %all-to-all-start.2) | async-done | bytes 131104 | tf_op jit(solution)/shard_map/all_to_all | solution.py:503
  169.2 0.7 copy-done.3
  169.8 1.6 assemble.1
  (22 shorter events, 0.1 us)
Async XLA Ops:
  7.2 50.6 %copy-start = (bf16[1024,1024]{1,0:T(8,128)(2,1)S(1)}, bf16[1024,1024]{1,0:T(8,128)(2,1)}, u32[]{:S(2)}) copy-start(bf16[1024,1024]{1,0:T(8,128)(2,1)} %param.19) | copy-start | bytes 6291460
  7.2 89.9 %all-gather.2.cloned.1.call-start = ((), (), s32[]{:S(2)}) async-start(), calls=%async_computation.3 | async-start | bytes 11141120 | tf_op jit(solution)/shard_map/all_gather | solution.py:452
  28.2 29.6 %copy-start.1 = (bf16[4,128,1024]{2,1,0:T(8,128)(2,1)S(1)}, bf16[4,128,1024]{2,1,0:T(8,128)(2,1)}, u32[]{:S(2)}) copy-start(bf16[4,128,1024]{2,1,0:T(8,128)(2,1)} %param.22) | copy-start | bytes 3145732
  30.9 7.4 %collective-permute-start.1 = (bf16[64,1152]{1,0:T(8,128)(2,1)S(1)}, bf16[64,1152]{1,0:T(8,128)(2,1)S(1)}, u32[]{:S(2)}, u32[]{:S(2)}) collective-permute-start(bf16[64,1152]{1,0:T(8,128)(2,1)S(1)} %get-tuple-element.25), channel_id=1, source_target_pairs={{128,0},{144,16},{160,32},{176,48},{192,64},{208,80},{224,96},{240... | collective-permute-start | bytes 442376 | tf_op jit(solution)/shard_map/ppermute | solution.py:378
  33.1 8.2 %collective-permute-start.2 = (bf16[64,1152]{1,0:T(8,128)(2,1)S(1)}, bf16[64,1152]{1,0:T(8,128)(2,1)S(1)}, u32[]{:S(2)}, u32[]{:S(2)}) collective-permute-start(bf16[64,1152]{1,0:T(8,128)(2,1)S(1)} %get-tuple-element.25), channel_id=1, source_target_pairs={{192,0},{208,16},{224,32},{240,48},{0,64},{16,80},{32,96},{48,112}... | collective-permute-start | bytes 442376 | tf_op jit(solution)/shard_map/ppermute | solution.py:378
  34.7 12.9 %collective-permute-start.10 = (bf16[64,1152]{1,0:T(8,128)(2,1)S(1)}, bf16[64,1152]{1,0:T(8,128)(2,1)S(1)}, u32[]{:S(2)}, u32[]{:S(2)}) collective-permute-start(bf16[64,1152]{1,0:T(8,128)(2,1)S(1)} %get-tuple-element.24), channel_id=1, source_target_pairs={{32,0},{48,16},{0,32},{16,48},{96,64},{112,80},{64,96},{80,112},{1... | collective-permute-start | bytes 442376 | tf_op jit(solution)/shard_map/ppermute | solution.py:378
  36.3 15.3 %collective-permute-start.9 = (bf16[64,1152]{1,0:T(8,128)(2,1)S(1)}, bf16[64,1152]{1,0:T(8,128)(2,1)S(1)}, u32[]{:S(2)}, u32[]{:S(2)}) collective-permute-start(bf16[64,1152]{1,0:T(8,128)(2,1)S(1)} %get-tuple-element.24), channel_id=1, source_target_pairs={{16,0},{32,16},{48,32},{0,48},{80,64},{96,80},{112,96},{64,112},{1... | collective-permute-start | bytes 442376 | tf_op jit(solution)/shard_map/ppermute | solution.py:378
  37.3 10.2 %collective-permute-start.11 = (bf16[64,1152]{1,0:T(8,128)(2,1)S(1)}, bf16[64,1152]{1,0:T(8,128)(2,1)S(1)}, u32[]{:S(2)}, u32[]{:S(2)}) collective-permute-start(bf16[64,1152]{1,0:T(8,128)(2,1)S(1)} %get-tuple-element.24), channel_id=1, source_target_pairs={{48,0},{0,16},{16,32},{32,48},{112,64},{64,80},{80,96},{96,112},{1... | collective-permute-start | bytes 442376 | tf_op jit(solution)/shard_map/ppermute | solution.py:378
  38.3 5.5 %collective-permute-start = (bf16[64,1152]{1,0:T(8,128)(2,1)S(1)}, bf16[64,1152]{1,0:T(8,128)(2,1)S(1)}, u32[]{:S(2)}, u32[]{:S(2)}) collective-permute-start(bf16[64,1152]{1,0:T(8,128)(2,1)S(1)} %get-tuple-element.25), channel_id=1, source_target_pairs={{64,0},{80,16},{96,32},{112,48},{128,64},{144,80},{160,96},{176,11... | collective-permute-start | bytes 442376 | tf_op jit(solution)/shard_map/ppermute | solution.py:378
  41.3 18.8 %copy-start.2 = (bf16[2,64,1152]{2,1,0:T(8,128)(2,1)}, bf16[2,64,1152]{2,1,0:T(8,128)(2,1)S(1)}, u32[]{:S(2)}) copy-start(bf16[2,64,1152]{2,1,0:T(8,128)(2,1)S(1)} %pad_maximum_fusion.1.refs_1_) | copy-start | bytes 884740
  41.3 13.0 %collective-permute-start.6 = (bf16[2,64,1152]{2,1,0:T(8,128)(2,1)S(1)}, bf16[2,64,1152]{2,1,0:T(8,128)(2,1)S(1)}, u32[]{:S(2)}, u32[]{:S(2)}) collective-permute-start(bf16[2,64,1152]{2,1,0:T(8,128)(2,1)S(1)} %pad_maximum_fusion.1.refs_1_), channel_id=1, source_target_pairs={{48,0},{0,16},{16,32},{32,48},{112,64},{64,80},{80,96},{96,112},{1... | collective-permute-start | bytes 884744 | tf_op jit(solution)/shard_map/ppermute | solution.py:378
  43.8 10.5 %collective-permute-start.4 = (bf16[2,64,1152]{2,1,0:T(8,128)(2,1)S(1)}, bf16[2,64,1152]{2,1,0:T(8,128)(2,1)S(1)}, u32[]{:S(2)}, u32[]{:S(2)}) collective-permute-start(bf16[2,64,1152]{2,1,0:T(8,128)(2,1)S(1)} %pad_maximum_fusion.1.refs_1_), channel_id=1, source_target_pairs={{16,0},{32,16},{48,32},{0,48},{80,64},{96,80},{112,96},{64,112},{1... | collective-permute-start | bytes 884744 | tf_op jit(solution)/shard_map/ppermute | solution.py:378
  47.6 13.1 %collective-permute-start.8 = (bf16[2,64,1152]{2,1,0:T(8,128)(2,1)}, bf16[2,64,1152]{2,1,0:T(8,128)(2,1)}, u32[]{:S(2)}, u32[]{:S(2)}) collective-permute-start(bf16[2,64,1152]{2,1,0:T(8,128)(2,1)} %pad_maximum_fusion.refs_0_), channel_id=1, source_target_pairs={{48,0},{0,16},{16,32},{32,48},{112,64},{64,80},{80,96},{96,112},{1... | collective-permute-start | bytes 884744 | tf_op jit(solution)/shard_map/ppermute | solution.py:378
  47.6 13.1 %collective-permute-start.3 = (bf16[2,64,1152]{2,1,0:T(8,128)(2,1)}, bf16[2,64,1152]{2,1,0:T(8,128)(2,1)}, u32[]{:S(2)}, u32[]{:S(2)}) collective-permute-start(bf16[2,64,1152]{2,1,0:T(8,128)(2,1)} %pad_maximum_fusion.refs_0_), channel_id=1, source_target_pairs={{16,0},{32,16},{48,32},{0,48},{80,64},{96,80},{112,96},{64,112},{1... | collective-permute-start | bytes 884744 | tf_op jit(solution)/shard_map/ppermute | solution.py:378
  51.5 9.5 %collective-permute-start.15 = (bf16[2,64,1152]{2,1,0:T(8,128)(2,1)}, bf16[2,64,1152]{2,1,0:T(8,128)(2,1)}, u32[]{:S(2)}, u32[]{:S(2)}) collective-permute-start(bf16[2,64,1152]{2,1,0:T(8,128)(2,1)} %pad_maximum_fusion.3.refs_9_), channel_id=1, source_target_pairs={{192,0},{208,16},{224,32},{240,48},{0,64},{16,80},{32,96},{48,112}... | collective-permute-start | bytes 884744 | tf_op jit(solution)/shard_map/ppermute | solution.py:378
  54.3 20.7 %copy-start.4 = (bf16[2,64,1152]{2,1,0:T(8,128)(2,1)}, bf16[2,64,1152]{2,1,0:T(8,128)(2,1)S(1)}, u32[]{:S(2)}) copy-start(bf16[2,64,1152]{2,1,0:T(8,128)(2,1)S(1)} %collective-permute-done.6.refs_7_) | copy-start | bytes 884740
  54.3 9.8 %collective-permute-start.13 = (bf16[2,64,1152]{2,1,0:T(8,128)(2,1)}, bf16[2,64,1152]{2,1,0:T(8,128)(2,1)}, u32[]{:S(2)}, u32[]{:S(2)}) collective-permute-start(bf16[2,64,1152]{2,1,0:T(8,128)(2,1)} %pad_maximum_fusion.3.refs_9_), channel_id=1, source_target_pairs={{64,0},{80,16},{96,32},{112,48},{128,64},{144,80},{160,96},{176,11... | collective-permute-start | bytes 884744 | tf_op jit(solution)/shard_map/ppermute | solution.py:378
  54.3 0.8 copy-start.5
  55.1 12.8 %collective-permute-start.12 = (bf16[2,64,1152]{2,1,0:T(8,128)(2,1)}, bf16[2,64,1152]{2,1,0:T(8,128)(2,1)}, u32[]{:S(2)}, u32[]{:S(2)}) collective-permute-start(bf16[2,64,1152]{2,1,0:T(8,128)(2,1)} %pad_maximum_fusion.2.refs_8_), channel_id=1, source_target_pairs={{64,0},{80,16},{96,32},{112,48},{128,64},{144,80},{160,96},{176,11... | collective-permute-start | bytes 884744 | tf_op jit(solution)/shard_map/ppermute | solution.py:378
  57.8 2.3 %copy-start.7 = (s32[4,1]{0,1:T(1,128)S(1)}, s32[4,1]{0,1:T(1,128)}, u32[]{:S(2)}) copy-start(s32[4,1]{0,1:T(1,128)} %param.23) | copy-start | bytes 52
  57.8 10.1 %copy-start.6 = (f32[1024]{0:T(1024)S(1)}, f32[1024]{0:T(1024)}, u32[]{:S(2)}) copy-start(f32[1024]{0:T(1024)} %param.21) | copy-start | bytes 12292
  60.6 10.1 %collective-permute-start.17 = (bf16[2,64,1152]{2,1,0:T(8,128)(2,1)}, bf16[2,64,1152]{2,1,0:T(8,128)(2,1)}, u32[]{:S(2)}, u32[]{:S(2)}) collective-permute-start(bf16[2,64,1152]{2,1,0:T(8,128)(2,1)} %pad_maximum_fusion.2.refs_8_), channel_id=1, source_target_pairs={{192,0},{208,16},{224,32},{240,48},{0,64},{16,80},{32,96},{48,112}... | collective-permute-start | bytes 884744 | tf_op jit(solution)/shard_map/ppermute | solution.py:378
  60.6 10.0 %collective-permute-start.7 = (bf16[2,64,1152]{2,1,0:T(8,128)(2,1)S(1)}, bf16[2,64,1152]{2,1,0:T(8,128)(2,1)}, u32[]{:S(2)}, u32[]{:S(2)}) collective-permute-start(bf16[2,64,1152]{2,1,0:T(8,128)(2,1)S(1)} %collective-permute-done.6.refs_7_), channel_id=1, source_target_pairs={{48,0},{0,16},{16,32},{32,48},{112,64},{64,80},{80,96},{96,112},{1... | collective-permute-start | bytes 884744 | tf_op jit(solution)/shard_map/ppermute | solution.py:378
  61.0 9.6 %collective-permute-start.5 = (bf16[2,64,1152]{2,1,0:T(8,128)(2,1)}, bf16[2,64,1152]{2,1,0:T(8,128)(2,1)}, u32[]{:S(2)}, u32[]{:S(2)}) collective-permute-start(bf16[2,64,1152]{2,1,0:T(8,128)(2,1)} %collective-permute-done.3.refs_2_), channel_id=1, source_target_pairs={{16,0},{32,16},{48,32},{0,48},{80,64},{96,80},{112,96},{64,112},{1... | collective-permute-start | bytes 884744 | tf_op jit(solution)/shard_map/ppermute | solution.py:378
  64.1 8.2 %collective-permute-start.16 = (bf16[2,64,1152]{2,1,0:T(8,128)(2,1)}, bf16[2,64,1152]{2,1,0:T(8,128)(2,1)}, u32[]{:S(2)}, u32[]{:S(2)}) collective-permute-start(bf16[2,64,1152]{2,1,0:T(8,128)(2,1)} %collective-permute-done.15.refs_15_), channel_id=1, source_target_pairs={{192,0},{208,16},{224,32},{240,48},{0,64},{16,80},{32,96},{48,112}... | collective-permute-start | bytes 884744 | tf_op jit(solution)/shard_map/ppermute | solution.py:378
  67.9 7.0 %collective-permute-start.14 = (bf16[2,64,1152]{2,1,0:T(8,128)(2,1)}, bf16[2,64,1152]{2,1,0:T(8,128)(2,1)}, u32[]{:S(2)}, u32[]{:S(2)}) collective-permute-start(bf16[2,64,1152]{2,1,0:T(8,128)(2,1)} %collective-permute-done.12.refs_10_), channel_id=1, source_target_pairs={{64,0},{80,16},{96,32},{112,48},{128,64},{144,80},{160,96},{176,11... | collective-permute-start | bytes 884744 | tf_op jit(solution)/shard_map/ppermute | solution.py:378
  117.0 3.0 %collective-permute-start.18 = (bf16[16,8,16,256]{3,2,1,0:T(8,128)(2,1)}, bf16[16,8,16,256]{3,2,1,0:T(8,128)(2,1)S(1)}, u32[]{:S(2)}, u32[]{:S(2)}) collective-permute-start(bf16[16,8,16,256]{3,2,1,0:T(8,128)(2,1)} %get-tuple-element.18), channel_id=1, source_target_pairs={{0,1},{1,0},{2,3},{3,2},{4,5},{5,4},{6,7},{7,6},{8,9},{9,8},{10,11... | collective-permute-start | bytes 3145736 | tf_op jit(solution)/shard_map/ppermute | solution.py:496
  121.4 41.3 %copy-start.8 = (f32[4,1,128]{2,1,0:T(1,128)S(1)}, f32[4,1,128]{2,1,0:T(1,128)}, u32[]{:S(2)}) copy-start(f32[4,1,128]{2,1,0:T(1,128)} %get-tuple-element.15) | copy-start | bytes 6148
  157.0 12.1 %all-to-all-start.2 = ((bf16[16,16,256]{2,1,0:T(8,128)(2,1)}), bf16[16,16,256]{2,1,0:T(8,128)(2,1)S(1)}, u32[]{:S(2)}, u32[]{:S(2)}) async-start(bf16[16,16,256]{2,1,0:T(8,128)(2,1)} %broadcast_in_dim.34), calls=%async_computation.2 | async-start | bytes 262144 | tf_op jit(solution)/shard_map/all_to_all | solution.py:503
  169.2 0.7 copy-start.3
Sparse Core Ops, SparseCore 0:
  28.4 68.7 all-gather.1

commit v5 on v4

--- a/solution.py
+++ b/solution.py
@@ -143,8 +143,11 @@
     logit_s,
     weight_s,
     slope_s,
+    mine_s,
+    other_s,
     sems,
     mix_sems,
+    grad_sems,
 ):
     step = pl.program_id(0)
     total, width = normed_s.shape
@@ -165,17 +168,33 @@
     @pl.when(step == 0)
     def _():
         normed_copy.start()
-        for i in range(ENCODE_STEPS):
-            for group in range(4):
-                mix_copy(i, group).start()
-        for copy in (base_copy, out_copy, query_copy, cand_copy):
-            copy.start()
+        for group in range(4):
+            mix_copy(0, group).start()
         normed_copy.wait()
 
     @pl.when(step < ENCODE_STEPS)
     def _():
         for group in range(4):
             mix_copy(step, group).wait()
+
+        @pl.when(step + 1 < ENCODE_STEPS)
+        def _():
+            for group in range(4):
+                mix_copy(step + 1, group).start()
+
+        @pl.when(step == 1)
+        def _():
+            base_copy.start()
+
+        @pl.when(step == 2)
+        def _():
+            out_copy.start()
+
+        @pl.when(step == 3)
+        def _():
+            query_copy.start()
+            cand_copy.start()
+
         users = total // HIST
         for k in range(2):
             cols = slice(k * LANES, (k + 1) * LANES)
@@ -267,19 +286,26 @@
         right = width // wide
         down = mine.shape[0] // right
         piece = tall * down
-        first = core[0] == 0
+        copies = []
         for n in range(right):
             cols = slice(n * wide, (n + 1) * wide)
-            grad = dot(cand_s[...], slope_s[:, :, cols].reshape(-1, wide))
-            for p in range(pairs):
-                one = grad[2 * p * piece : (2 * p + 1) * piece]
-                two = grad[(2 * p + 1) * piece : (2 * p + 2) * piece]
-                kept = jnp.where(first, one, two).astype(BF)
-                sent = jnp.where(first, two, one).astype(BF)
-                for a in range(down):
-                    rows = slice(a * tall, (a + 1) * tall)
-                    mine[a * right + n, p] = kept[rows]
-                    other[a * right + n, p] = sent[rows]
+            slope = slope_s[:, :, cols].reshape(-1, wide)
+            for which, store in ((core[0], mine_s), (1 - core[0], other_s)):
+                rows = cand_s[:, which].reshape(pairs * piece, -1)
+                grad = dot(rows, slope).astype(BF)
+                for p in range(pairs):
+                    for a in range(down):
+                        start = p * piece + a * tall
+                        store[n * down + a, p] = grad[start : start + tall]
+            chunk = pl.ds(n * down, down)
+            for k, (source, target) in enumerate(((mine_s, mine), (other_s, other))):
+                copy = pltpu.make_async_copy(
+                    source.at[chunk], target.at[chunk], grad_sems.at[k, n]
+                )
+                copy.start()
+                copies.append(copy)
+        for copy in copies:
+            copy.wait()
 
 
 def attention(
@@ -306,7 +332,6 @@
     current = lambda i: jnp.maximum(i - ENCODE_STEPS, 0)
     row = pl.BlockSpec((GROUP, 1, rows), lambda i, n, c: (current(i), 0, 0))
     whole = lambda i, n, c: (0, 0)
-    whole4 = lambda i, n, c: (0, 0, 0, 0)
     anywhere = pl.BlockSpec(memory_space=pl.ANY)
     return pl.pallas_call(
         attention_kernel,
@@ -324,8 +349,8 @@
                 row,
                 row,
                 pl.BlockSpec((GROUP * rows, width), lambda i, n, c: (current(i), 0)),
-                pl.BlockSpec(shape, whole4),
-                pl.BlockSpec(shape, whole4),
+                anywhere,
+                anywhere,
             ],
             scratch_shapes=[
                 pltpu.VMEM((total, width), BF),
@@ -333,7 +358,7 @@
                 pltpu.VMEM((ENCODE_STEPS, 4, width, 2 * LANES), BF),
                 pltpu.VMEM((width, width), BF),
                 pltpu.VMEM((groups, GROUP * rows, width), BF),
-                pltpu.VMEM((width, total), BF),
+                pltpu.VMEM((pairs, 2, width // (2 * pairs), total), BF),
                 pltpu.VMEM((HEADS, total, LANES), F32),
                 pltpu.VMEM((HEADS, total, LANES), F32),
                 pltpu.VMEM((2, total, 3 * LANES), BF),
@@ -342,8 +367,11 @@
                 pltpu.VMEM((GROUP * HEADS, HIST, HIST), F32),
                 pltpu.VMEM((GROUP * HEADS, HIST, HIST), BF),
                 pltpu.VMEM((groups, GROUP * rows, width), BF),
+                pltpu.VMEM(shape, BF),
+                pltpu.VMEM(shape, BF),
                 pltpu.SemaphoreType.DMA((5,)),
                 pltpu.SemaphoreType.DMA((ENCODE_STEPS, 4)),
+                pltpu.SemaphoreType.DMA((2, side)),
             ],
         ),
         out_shape=[
@@ -362,7 +390,7 @@
         base,
         weights,
         queries.reshape(groups, GROUP * rows, width),
-        cand_t,
+        cand_t.reshape(pairs, 2, width // (2 * pairs), total),
         mask,
         score_weight,
         own,
@@ -389,33 +417,25 @@
     return (low, high, low_after, high_after, low_two, high_two, low_before, high_before)
 
 
-def join_kernel(left, right, out, sems):
+def join_kernel(left, right, out):
     wide = left.shape[1]
-    first = pltpu.make_async_copy(left, out.at[:, pl.ds(0, wide)], sems.at[0])
-    second = pltpu.make_async_copy(right, out.at[:, pl.ds(wide, right.shape[1])], sems.at[1])
-    first.start()
-    second.start()
-    first.wait()
-    second.wait()
+    out[:, :wide] = left[...]
+    out[:, wide:] = right[...]
 
 
 def join(left, right):
-    anywhere = pl.BlockSpec(memory_space=pl.ANY)
     return pl.pallas_call(
         join_kernel,
-        in_specs=[anywhere, anywhere],
-        out_specs=anywhere,
         out_shape=jax.ShapeDtypeStruct((left.shape[0], left.shape[1] + right.shape[1]), left.dtype),
-        scratch_shapes=[pltpu.SemaphoreType.DMA((2,))],
         name="join",
     )(left, right)
 
 
 def assemble_kernel(pieces, out):
     count, tall, wide = pieces.shape
-    right = out.shape[1] // wide
+    down = out.shape[0] // tall
     for k in range(count):
-        a, b = k // right, k % right
+        a, b = k % down, k // down
         rows, cols = slice(a * tall, (a + 1) * tall), slice(b * wide, (b + 1) * wide)
         out[rows, cols] = pieces[k].astype(F32)
 
@@ -494,6 +514,9 @@
     )
 
     arrived = lax.ppermute(other, "loader", [(i, i ^ 1) for i in range(loaders)])
+    back = lax.dot_general(slopes, query_weight, (((1,), (1,)), ((), ())), preferred_element_type=F32)
+    row_grads = (error.reshape(-1)[:, None] * self_weight + back).astype(BF)
+    mine, row_grads = lax.optimization_barrier((mine, row_grads))
     pieces = (mine.astype(F32) + arrived.astype(F32)).astype(BF)
     pieces = lax.all_to_all(pieces, "user", 0, 0, tiled=True)
     pieces = jnp.sum(pieces.astype(F32), 0).astype(BF)
@@ -505,8 +528,6 @@
     )
     query_grad = assemble(pieces, side)
 
-    back = lax.dot_general(slopes, query_weight, (((1,), (1,)), ((), ())), preferred_element_type=F32)
-    row_grads = (error.reshape(-1)[:, None] * self_weight + back).astype(BF)
     return (scores[:, 0], row_grads.reshape(nblocks, rows, width), query_grad)
 
 

time: 179 us -> 157 us (0.88)
  Pallas kernels: 48.3 us -> 28.2 us
  blocking collectives: 34.8 us -> 46.8 us
  starting transfers between devices: 33.2 us -> 27.5 us
  waiting for transfers between devices: 30.2 us -> 25.1 us
    pallas_call x1, Pallas kernels: 21 us -> 2.1 us  [join(): pl.pallas_call(join_kernel, out_shape=jax.ShapeDtypeStruct((left.shape[0]...]
    all_to_all x0 -> x1, blocking collectives: none -> 12 us  [body(): lax.all_to_all(jnp.broadcast_to(piece[None], (users,) + piece.shape), 'us...]
    all_to_all x1 -> x0, starting transfers between devices: 5.72 us -> none  [body(): lax.all_to_all(jnp.broadcast_to(piece[None], (users,) + piece.shape), 'us...]
    all_to_all x1 -> x0, waiting for transfers between devices: 2.93 us -> none  [body(): lax.all_to_all(jnp.broadcast_to(piece[None], (users,) + piece.shape), 'us...]
    ppermute x1, waiting for transfers between devices: 2.62 us -> 0.01 us  [body(): lax.ppermute(other, 'loader', [(i, i ^ 1) for i in range(loaders)])]
  transfers between devices with their start and end apart: 21 -> 20, of which waited for: 8 -> 6; matrix products, arithmetic and copies ran while one was open for 7% -> 8% of each run, Pallas kernels for 3% -> 4%
where the time goes in v5:
time: 157 us
  blocking collectives  46.8 us (30%)
  Pallas kernels  28.2 us (18%)
  starting transfers between devices  27.5 us (18%)
  waiting for transfers between devices  25.1 us (16%)
  between operations  14.9 us (9%)
  matrix products  5.87 us (4%)
  other arithmetic  5.4 us (3%)
  local copies, waits for them, and re-layouts  3.32 us (2%)
    ppermute x18, starting transfers between devices, shift(): return lax.ppermute(array, 'user', moves)  27.1 us
    all_to_all x1, blocking collectives, body(): pieces = lax.all_to_all(pieces, 'user', 0, 0, tiled=True)  22.3 us
    pallas_call x1, Pallas kernels, attention(): pl.pallas_call(attention_kernel, grid_spec=pltpu.PrefetchScalarGridSpec(n...  18.7 us
    all_gather x1, waiting for transfers between devices, body(): lax.all_gather(join(mix_weight, out_weight), 'loader', axis=0, tiled=True)  16.7 us
    all_to_all x1, blocking collectives, body(): lax.all_to_all(pieces, 'loader', 0, 0, axis_index_groups=groups, tiled=True)  12.4 us
    all_to_all x1, blocking collectives, body(): lax.all_to_all(jnp.broadcast_to(piece[None], (users,) + piece.shape), 'us...  12 us
    ppermute x18, waiting for transfers between devices, shift(): return lax.ppermute(array, 'user', moves)  8.36 us
    pallas_call x1, Pallas kernels, prepare(): pl.pallas_call(functools.partial(prepare_kernel, nblocks), grid_spec=pltp...  5.79 us
  transfers between devices with their start and end apart: 20, of which 6 were waited for; matrix products, arithmetic and copies ran while one was open for 8% of the time, Pallas kernels for 4%

profile of v5, /device:TPU:2, one launch (start us, length us, event | category | flops | bytes accessed | tf_op | source)
XLA Modules:
  0.0 157.0 jit_solution(14797719812617923003)
XLA Ops:
  7.2 0.0 copy-start
  7.2 0.0 all-gather.2.cloned.1.call-start
  7.2 2.1 %join.1 = bf16[64,5120]{1,0:T(8,128)(2,1)} custom-call(bf16[64,4096]{1,0:T(8,128)(2,1)} %left.1, bf16[64,1024]{1,0:T(8,128)(2,1)} %right.1), custom_call_target="tpu_custom_call" | custom-call | tf_op jit(solution)/shard_map/join/pallas_call | solution.py:427
  9.3 0.0 all-gather.2.cloned.1.call-update
  9.4 0.0 copy-start.1
  10.1 0.7 convert_bitcast_fusion
  10.8 0.1 broadcast_in_dim.29
  10.9 1.1 concatenate.3
  12.0 2.2 %collective-permute-start.1 = (bf16[64,1152]{1,0:T(8,128)(2,1)S(1)}, bf16[64,1152]{1,0:T(8,128)(2,1)S(1)}, u32[]{:S(2)}, u32[]{:S(2)}) collective-permute-start(bf16[64,1152]{1,0:T(8,128)(2,1)S(1)} %get-tuple-element.29), channel_id=1, source_target_pairs={{128,0},{144,16},{160,32},{176,48},{192,64},{208,80},{224,96},{240... | collective-permute-start | bytes 442376 | tf_op jit(solution)/shard_map/ppermute | solution.py:406
  14.2 1.6 %collective-permute-start.2 = (bf16[64,1152]{1,0:T(8,128)(2,1)S(1)}, bf16[64,1152]{1,0:T(8,128)(2,1)S(1)}, u32[]{:S(2)}, u32[]{:S(2)}) collective-permute-start(bf16[64,1152]{1,0:T(8,128)(2,1)S(1)} %get-tuple-element.29), channel_id=1, source_target_pairs={{192,0},{208,16},{224,32},{240,48},{0,64},{16,80},{32,96},{48,112}... | collective-permute-start | bytes 442376 | tf_op jit(solution)/shard_map/ppermute | solution.py:406
  15.8 1.6 %collective-permute-start.10 = (bf16[64,1152]{1,0:T(8,128)(2,1)S(1)}, bf16[64,1152]{1,0:T(8,128)(2,1)S(1)}, u32[]{:S(2)}, u32[]{:S(2)}) collective-permute-start(bf16[64,1152]{1,0:T(8,128)(2,1)S(1)} %get-tuple-element.28), channel_id=1, source_target_pairs={{32,0},{48,16},{0,32},{16,48},{96,64},{112,80},{64,96},{80,112},{1... | collective-permute-start | bytes 442376 | tf_op jit(solution)/shard_map/ppermute | solution.py:406
  17.4 1.1 collective-permute-start.9
  18.4 1.0 collective-permute-start.11
  19.4 0.0 collective-permute-done.1
  19.4 2.2 %collective-permute-start = (bf16[64,1152]{1,0:T(8,128)(2,1)S(1)}, bf16[64,1152]{1,0:T(8,128)(2,1)S(1)}, u32[]{:S(2)}, u32[]{:S(2)}) collective-permute-start(bf16[64,1152]{1,0:T(8,128)(2,1)S(1)} %get-tuple-element.29), channel_id=1, source_target_pairs={{64,0},{80,16},{96,32},{112,48},{128,64},{144,80},{160,96},{176,11... | collective-permute-start | bytes 442376 | tf_op jit(solution)/shard_map/ppermute | solution.py:406
  21.6 0.8 collective-permute-done.2
  22.4 1.7 %collective-permute-start.6 = (bf16[2,64,1152]{2,1,0:T(8,128)(2,1)S(1)}, bf16[2,64,1152]{2,1,0:T(8,128)(2,1)S(1)}, u32[]{:S(2)}, u32[]{:S(2)}) collective-permute-start(bf16[2,64,1152]{2,1,0:T(8,128)(2,1)S(1)} %pad_maximum_fusion.1.refs_1_), channel_id=1, source_target_pairs={{48,0},{0,16},{16,32},{32,48},{112,64},{64,80},{80,96},{96,112},{1... | collective-permute-start | bytes 884744 | tf_op jit(solution)/shard_map/ppermute | solution.py:406
  24.1 0.8 collective-permute-done
  24.9 3.0 %collective-permute-start.4 = (bf16[2,64,1152]{2,1,0:T(8,128)(2,1)S(1)}, bf16[2,64,1152]{2,1,0:T(8,128)(2,1)S(1)}, u32[]{:S(2)}, u32[]{:S(2)}) collective-permute-start(bf16[2,64,1152]{2,1,0:T(8,128)(2,1)S(1)} %pad_maximum_fusion.1.refs_1_), channel_id=1, source_target_pairs={{16,0},{32,16},{48,32},{0,48},{80,64},{96,80},{112,96},{64,112},{1... | collective-permute-start | bytes 884744 | tf_op jit(solution)/shard_map/ppermute | solution.py:406
  27.9 0.7 pad_maximum_fusion.refs_0_
  28.7 0.0 collective-permute-done.10
  28.7 0.0 collective-permute-start.8
  28.7 0.0 collective-permute-done.11
  28.7 3.2 %collective-permute-start.3 = (bf16[2,64,1152]{2,1,0:T(8,128)(2,1)}, bf16[2,64,1152]{2,1,0:T(8,128)(2,1)}, u32[]{:S(2)}, u32[]{:S(2)}) collective-permute-start(bf16[2,64,1152]{2,1,0:T(8,128)(2,1)} %pad_maximum_fusion.refs_0_), channel_id=1, source_target_pairs={{16,0},{32,16},{48,32},{0,48},{80,64},{96,80},{112,96},{64,112},{1... | collective-permute-start | bytes 884744 | tf_op jit(solution)/shard_map/ppermute | solution.py:406
  31.9 0.8 pad_maximum_fusion.3.refs_9_
  32.7 0.0 collective-permute-done.9
  32.7 2.0 %collective-permute-start.15 = (bf16[2,64,1152]{2,1,0:T(8,128)(2,1)}, bf16[2,64,1152]{2,1,0:T(8,128)(2,1)}, u32[]{:S(2)}, u32[]{:S(2)}) collective-permute-start(bf16[2,64,1152]{2,1,0:T(8,128)(2,1)} %pad_maximum_fusion.3.refs_9_), channel_id=1, source_target_pairs={{192,0},{208,16},{224,32},{240,48},{0,64},{16,80},{32,96},{48,112}... | collective-permute-start | bytes 884744 | tf_op jit(solution)/shard_map/ppermute | solution.py:406
  34.7 0.8 pad_maximum_fusion.2.refs_8_
  35.5 0.0 collective-permute-done.6.refs_7_
  35.5 0.0 collective-permute-start.13
  35.5 0.0 collective-permute-done.4.refs_3_
  35.5 0.8 copy-done.5
  36.3 2.7 %collective-permute-start.12 = (bf16[2,64,1152]{2,1,0:T(8,128)(2,1)}, bf16[2,64,1152]{2,1,0:T(8,128)(2,1)}, u32[]{:S(2)}, u32[]{:S(2)}) collective-permute-start(bf16[2,64,1152]{2,1,0:T(8,128)(2,1)} %pad_maximum_fusion.2.refs_8_), channel_id=1, source_target_pairs={{64,0},{80,16},{96,32},{112,48},{128,64},{144,80},{160,96},{176,11... | collective-permute-start | bytes 884744 | tf_op jit(solution)/shard_map/ppermute | solution.py:406
  39.0 2.3 %convolution_convert_fusion = bf16[512,1024]{1,0:T(8,128)(2,1)} fusion(bf16[512,1024]{1,0:T(8,128)(2,1)S(1)} %bitcast.50, bf16[1024,1024]{1,0:T(8,128)(2,1)S(1)} %copy-done), kind=kOutput, calls=%fused_computation.3 | convolution fusion | flops 1074266112 | bytes 4194304 | tf_op jit(solution)/shard_map/dot_general | solution.py:488
  41.3 0.5 multiply_add_fusion
  41.8 0.0 collective-permute-done.8.refs_6_
  41.8 0.0 collective-permute-start.17
  41.8 0.0 collective-permute-done.3.refs_2_
  41.8 0.4 collective-permute-start.7
  42.2 0.0 collective-permute-done.15.refs_15_
  42.2 3.1 %collective-permute-start.5 = (bf16[2,64,1152]{2,1,0:T(8,128)(2,1)}, bf16[2,64,1152]{2,1,0:T(8,128)(2,1)}, u32[]{:S(2)}, u32[]{:S(2)}) collective-permute-start(bf16[2,64,1152]{2,1,0:T(8,128)(2,1)} %collective-permute-done.3.refs_2_), channel_id=1, source_target_pairs={{16,0},{32,16},{48,32},{0,48},{80,64},{96,80},{112,96},{64,112},{1... | collective-permute-start | bytes 884744 | tf_op jit(solution)/shard_map/ppermute | solution.py:406
  45.3 0.0 collective-permute-done.13.refs_11_
  45.3 1.3 collective-permute-start.16
  46.6 2.5 %collective-permute-done.12.refs_10_ = bf16[2,64,1152]{2,1,0:T(8,128)(2,1)} collective-permute-done((bf16[2,64,1152]{2,1,0:T(8,128)(2,1)}, bf16[2,64,1152]{2,1,0:T(8,128)(2,1)}, u32[]{:S(2)}, u32[]{:S(2)}) %collective-permute-start.12) | collective-permute-done | bytes 294944 | tf_op jit(solution)/shard_map/ppermute | solution.py:406
  49.1 0.8 multiply_reduce_fusion
  49.9 1.3 copy.17
  51.3 0.6 multiply_add_fusion.1.place_a
  51.9 0.0 collective-permute-done.17.refs_14_
  51.9 0.0 collective-permute-done.7.refs_5_
  51.9 0.0 collective-permute-done.5.refs_4_
  51.9 1.7 %collective-permute-done.16.refs_13_ = bf16[2,64,1152]{2,1,0:T(8,128)(2,1)} collective-permute-done((bf16[2,64,1152]{2,1,0:T(8,128)(2,1)}, bf16[2,64,1152]{2,1,0:T(8,128)(2,1)}, u32[]{:S(2)}, u32[]{:S(2)}) %collective-permute-start.16) | collective-permute-done | bytes 294944 | tf_op jit(solution)/shard_map/ppermute | solution.py:406
  53.5 2.6 %collective-permute-done.14.refs_12_ = bf16[2,64,1152]{2,1,0:T(8,128)(2,1)} collective-permute-done((bf16[2,64,1152]{2,1,0:T(8,128)(2,1)}, bf16[2,64,1152]{2,1,0:T(8,128)(2,1)}, u32[]{:S(2)}, u32[]{:S(2)}) %collective-permute-start.14) | collective-permute-done | bytes 294944 | tf_op jit(solution)/shard_map/ppermute | solution.py:406
  56.1 5.8 %prepare.1 = (f32[512,1024]{1,0:T(8,128)}, bf16[512,1024]{1,0:T(8,128)(2,1)}, f32[512,128]{1,0:T(8,128)}) custom-call(s32[4]{0:T(128)} %multiply_add_fusion.1.place_a, s32[4]{0:T(128)} %get-tuple-element.23.place_b, bf16[2,64,1152]{2,1,0:T(8,128)(2,1)} %pad_maximum_fusion.refs_0_, bf16[2,64,1152]{2,1,0:T(8,128)(2,1)} %copy-done.2, ...), custom_call_target="tpu_custom_call" | custom-call | tf_op jit(solution)/shard_map/prepare/pallas_call | solution.py:84
  61.9 16.7 %all-gather.2.cloned.1.call-done.weights = bf16[1024,5120]{1,0:T(8,128)(2,1)} async-done(((bf16[64,5120]{1,0:T(8,128)(2,1)}), bf16[1024,5120]{1,0:T(8,128)(2,1)}) %all-gather.2.cloned.1.call-update) | async-done | bytes 10485776 | tf_op jit(solution)/shard_map/all_gather | solution.py:472
  78.6 18.7 %attention.1 = (f32[4,1,128]{2,1,0:T(1,128)}, f32[4,1,128]{2,1,0:T(1,128)}, bf16[512,1024]{1,0:T(8,128)(2,1)}, bf16[16,8,16,256]{3,2,1,0:T(8,128)(2,1)}, bf16[16,8,16,256]{3,2,1,0:T(8,128)(2,1)}) custom-call(s32[4]{0:T(128)} %counts.1, s32[1]{0:T(128)} %bitcast.core, bf16[512,1024]{1,0:T(8,128)(2,1)} %get-tuple-element.13.normed, ...), custom_call_target="tpu_custom_call" | custom-call | tf_op jit(solution)/shard_map/attention/pallas_call | solution.py:336
  97.3 0.3 collective-permute-start.18
  97.6 3.6 %add_convert_fusion.1 = bf16[512,1024]{1,0:T(8,128)(2,1)} fusion(bf16[512,1024]{1,0:T(8,128)(2,1)} %get-tuple-element.19, bf16[1024,1024]{1,0:T(8,128)(2,1)S(1)} %copy-done, f32[1024]{0:T(1024)S(1)} %copy-done.6, f32[512]{0:T(512)} %bitcast.64), kind=kOutput, calls=%fused_computation.1 | convolution fusion | flops 1075314688 | bytes 4200448 | tf_op jit(solution)/shard_map/dot_general | solution.py:517
  101.2 0.0 collective-permute-done.18
  101.2 0.3 add_convert_fusion
  101.5 22.3 %all_to_all.15 = bf16[16,8,16,256]{3,2,1,0:T(8,128)(2,1)S(1)} all-to-all(bf16[16,8,16,256]{3,2,1,0:T(8,128)(2,1)S(1)} %add_convert_fusion), channel_id=1, replica_groups=mesh['user'=16,'loader'=16] {'user'}, dimensions={0} | all-to-all | bytes 2097152 | tf_op jit(solution)/shard_map/all_to_all | solution.py:521
  123.9 0.1 reduce_sum.34
  124.0 12.4 %all_to_all.16 = bf16[8,16,256]{2,1,0:T(8,128)(2,1)S(1)} all-to-all(bf16[8,16,256]{2,1,0:T(8,128)(2,1)S(1)} %reduce_sum.34), channel_id=1, replica_groups={{0,2,4,6,8,10,12,14},{1,3,5,7,9,11,13,15},{16,18,20,22,24,26,28,30},{17..., dimensions={0} | all-to-all | bytes 131072 | tf_op jit(solution)/shard_map/all_to_all | solution.py:524
  136.5 12.0 %all_to_all.17.pieces = bf16[16,16,256]{2,1,0:T(8,128)(2,1)} all-to-all(bf16[16,16,256]{2,1,0:T(8,128)(2,1)S(1)} %broadcast_in_dim.34), channel_id=1, replica_groups=mesh['user'=16,'loader'=16] {'user'}, dimensions={0} | all-to-all | bytes 262144 | tf_op jit(solution)/shard_map/all_to_all | solution.py:526
  148.5 1.6 %assemble.1 = f32[64,1024]{1,0:T(8,128)} custom-call(bf16[16,16,256]{2,1,0:T(8,128)(2,1)} %all_to_all.17.pieces), custom_call_target="tpu_custom_call" | custom-call | tf_op jit(solution)/shard_map/assemble/pallas_call | solution.py:445
  (19 shorter events, 0.1 us)
Async XLA Ops:
  7.2 31.8 %copy-start = (bf16[1024,1024]{1,0:T(8,128)(2,1)S(1)}, bf16[1024,1024]{1,0:T(8,128)(2,1)}, u32[]{:S(2)}) copy-start(bf16[1024,1024]{1,0:T(8,128)(2,1)} %param.19) | copy-start | bytes 6291460
  7.2 71.4 %all-gather.2.cloned.1.call-start = ((), (), s32[]{:S(2)}) async-start(), calls=%async_computation.3 | async-start | bytes 11141120 | tf_op jit(solution)/shard_map/all_gather | solution.py:472
  9.4 29.6 %copy-start.1 = (bf16[4,128,1024]{2,1,0:T(8,128)(2,1)S(1)}, bf16[4,128,1024]{2,1,0:T(8,128)(2,1)}, u32[]{:S(2)}) copy-start(bf16[4,128,1024]{2,1,0:T(8,128)(2,1)} %param.22) | copy-start | bytes 3145732
  12.0 7.4 %collective-permute-start.1 = (bf16[64,1152]{1,0:T(8,128)(2,1)S(1)}, bf16[64,1152]{1,0:T(8,128)(2,1)S(1)}, u32[]{:S(2)}, u32[]{:S(2)}) collective-permute-start(bf16[64,1152]{1,0:T(8,128)(2,1)S(1)} %get-tuple-element.29), channel_id=1, source_target_pairs={{128,0},{144,16},{160,32},{176,48},{192,64},{208,80},{224,96},{240... | collective-permute-start | bytes 442376 | tf_op jit(solution)/shard_map/ppermute | solution.py:406
  14.2 8.2 %collective-permute-start.2 = (bf16[64,1152]{1,0:T(8,128)(2,1)S(1)}, bf16[64,1152]{1,0:T(8,128)(2,1)S(1)}, u32[]{:S(2)}, u32[]{:S(2)}) collective-permute-start(bf16[64,1152]{1,0:T(8,128)(2,1)S(1)} %get-tuple-element.29), channel_id=1, source_target_pairs={{192,0},{208,16},{224,32},{240,48},{0,64},{16,80},{32,96},{48,112}... | collective-permute-start | bytes 442376 | tf_op jit(solution)/shard_map/ppermute | solution.py:406
  15.8 12.9 %collective-permute-start.10 = (bf16[64,1152]{1,0:T(8,128)(2,1)S(1)}, bf16[64,1152]{1,0:T(8,128)(2,1)S(1)}, u32[]{:S(2)}, u32[]{:S(2)}) collective-permute-start(bf16[64,1152]{1,0:T(8,128)(2,1)S(1)} %get-tuple-element.28), channel_id=1, source_target_pairs={{32,0},{48,16},{0,32},{16,48},{96,64},{112,80},{64,96},{80,112},{1... | collective-permute-start | bytes 442376 | tf_op jit(solution)/shard_map/ppermute | solution.py:406
  17.4 15.3 %collective-permute-start.9 = (bf16[64,1152]{1,0:T(8,128)(2,1)S(1)}, bf16[64,1152]{1,0:T(8,128)(2,1)S(1)}, u32[]{:S(2)}, u32[]{:S(2)}) collective-permute-start(bf16[64,1152]{1,0:T(8,128)(2,1)S(1)} %get-tuple-element.28), channel_id=1, source_target_pairs={{16,0},{32,16},{48,32},{0,48},{80,64},{96,80},{112,96},{64,112},{1... | collective-permute-start | bytes 442376 | tf_op jit(solution)/shard_map/ppermute | solution.py:406
  18.4 10.2 %collective-permute-start.11 = (bf16[64,1152]{1,0:T(8,128)(2,1)S(1)}, bf16[64,1152]{1,0:T(8,128)(2,1)S(1)}, u32[]{:S(2)}, u32[]{:S(2)}) collective-permute-start(bf16[64,1152]{1,0:T(8,128)(2,1)S(1)} %get-tuple-element.28), channel_id=1, source_target_pairs={{48,0},{0,16},{16,32},{32,48},{112,64},{64,80},{80,96},{96,112},{1... | collective-permute-start | bytes 442376 | tf_op jit(solution)/shard_map/ppermute | solution.py:406
  19.4 5.5 %collective-permute-start = (bf16[64,1152]{1,0:T(8,128)(2,1)S(1)}, bf16[64,1152]{1,0:T(8,128)(2,1)S(1)}, u32[]{:S(2)}, u32[]{:S(2)}) collective-permute-start(bf16[64,1152]{1,0:T(8,128)(2,1)S(1)} %get-tuple-element.29), channel_id=1, source_target_pairs={{64,0},{80,16},{96,32},{112,48},{128,64},{144,80},{160,96},{176,11... | collective-permute-start | bytes 442376 | tf_op jit(solution)/shard_map/ppermute | solution.py:406
  22.4 18.8 %copy-start.2 = (bf16[2,64,1152]{2,1,0:T(8,128)(2,1)}, bf16[2,64,1152]{2,1,0:T(8,128)(2,1)S(1)}, u32[]{:S(2)}) copy-start(bf16[2,64,1152]{2,1,0:T(8,128)(2,1)S(1)} %pad_maximum_fusion.1.refs_1_) | copy-start | bytes 884740
  22.4 13.0 %collective-permute-start.6 = (bf16[2,64,1152]{2,1,0:T(8,128)(2,1)S(1)}, bf16[2,64,1152]{2,1,0:T(8,128)(2,1)S(1)}, u32[]{:S(2)}, u32[]{:S(2)}) collective-permute-start(bf16[2,64,1152]{2,1,0:T(8,128)(2,1)S(1)} %pad_maximum_fusion.1.refs_1_), channel_id=1, source_target_pairs={{48,0},{0,16},{16,32},{32,48},{112,64},{64,80},{80,96},{96,112},{1... | collective-permute-start | bytes 884744 | tf_op jit(solution)/shard_map/ppermute | solution.py:406
  24.9 10.6 %collective-permute-start.4 = (bf16[2,64,1152]{2,1,0:T(8,128)(2,1)S(1)}, bf16[2,64,1152]{2,1,0:T(8,128)(2,1)S(1)}, u32[]{:S(2)}, u32[]{:S(2)}) collective-permute-start(bf16[2,64,1152]{2,1,0:T(8,128)(2,1)S(1)} %pad_maximum_fusion.1.refs_1_), channel_id=1, source_target_pairs={{16,0},{32,16},{48,32},{0,48},{80,64},{96,80},{112,96},{64,112},{1... | collective-permute-start | bytes 884744 | tf_op jit(solution)/shard_map/ppermute | solution.py:406
  28.7 13.1 %collective-permute-start.8 = (bf16[2,64,1152]{2,1,0:T(8,128)(2,1)}, bf16[2,64,1152]{2,1,0:T(8,128)(2,1)}, u32[]{:S(2)}, u32[]{:S(2)}) collective-permute-start(bf16[2,64,1152]{2,1,0:T(8,128)(2,1)} %pad_maximum_fusion.refs_0_), channel_id=1, source_target_pairs={{48,0},{0,16},{16,32},{32,48},{112,64},{64,80},{80,96},{96,112},{1... | collective-permute-start | bytes 884744 | tf_op jit(solution)/shard_map/ppermute | solution.py:406
  28.7 13.1 %collective-permute-start.3 = (bf16[2,64,1152]{2,1,0:T(8,128)(2,1)}, bf16[2,64,1152]{2,1,0:T(8,128)(2,1)}, u32[]{:S(2)}, u32[]{:S(2)}) collective-permute-start(bf16[2,64,1152]{2,1,0:T(8,128)(2,1)} %pad_maximum_fusion.refs_0_), channel_id=1, source_target_pairs={{16,0},{32,16},{48,32},{0,48},{80,64},{96,80},{112,96},{64,112},{1... | collective-permute-start | bytes 884744 | tf_op jit(solution)/shard_map/ppermute | solution.py:406
  32.7 9.5 %collective-permute-start.15 = (bf16[2,64,1152]{2,1,0:T(8,128)(2,1)}, bf16[2,64,1152]{2,1,0:T(8,128)(2,1)}, u32[]{:S(2)}, u32[]{:S(2)}) collective-permute-start(bf16[2,64,1152]{2,1,0:T(8,128)(2,1)} %pad_maximum_fusion.3.refs_9_), channel_id=1, source_target_pairs={{192,0},{208,16},{224,32},{240,48},{0,64},{16,80},{32,96},{48,112}... | collective-permute-start | bytes 884744 | tf_op jit(solution)/shard_map/ppermute | solution.py:406
  35.5 20.7 %copy-start.4 = (bf16[2,64,1152]{2,1,0:T(8,128)(2,1)}, bf16[2,64,1152]{2,1,0:T(8,128)(2,1)S(1)}, u32[]{:S(2)}) copy-start(bf16[2,64,1152]{2,1,0:T(8,128)(2,1)S(1)} %collective-permute-done.6.refs_7_) | copy-start | bytes 884740
  35.5 9.8 %collective-permute-start.13 = (bf16[2,64,1152]{2,1,0:T(8,128)(2,1)}, bf16[2,64,1152]{2,1,0:T(8,128)(2,1)}, u32[]{:S(2)}, u32[]{:S(2)}) collective-permute-start(bf16[2,64,1152]{2,1,0:T(8,128)(2,1)} %pad_maximum_fusion.3.refs_9_), channel_id=1, source_target_pairs={{64,0},{80,16},{96,32},{112,48},{128,64},{144,80},{160,96},{176,11... | collective-permute-start | bytes 884744 | tf_op jit(solution)/shard_map/ppermute | solution.py:406
  35.5 0.8 copy-start.5
  36.3 12.8 %collective-permute-start.12 = (bf16[2,64,1152]{2,1,0:T(8,128)(2,1)}, bf16[2,64,1152]{2,1,0:T(8,128)(2,1)}, u32[]{:S(2)}, u32[]{:S(2)}) collective-permute-start(bf16[2,64,1152]{2,1,0:T(8,128)(2,1)} %pad_maximum_fusion.2.refs_8_), channel_id=1, source_target_pairs={{64,0},{80,16},{96,32},{112,48},{128,64},{144,80},{160,96},{176,11... | collective-permute-start | bytes 884744 | tf_op jit(solution)/shard_map/ppermute | solution.py:406
  39.0 2.3 %copy-start.7 = (s32[4,1]{0,1:T(1,128)S(1)}, s32[4,1]{0,1:T(1,128)}, u32[]{:S(2)}) copy-start(s32[4,1]{0,1:T(1,128)} %param.23) | copy-start | bytes 52
  39.0 10.1 %copy-start.6 = (f32[1024]{0:T(1024)S(1)}, f32[1024]{0:T(1024)}, u32[]{:S(2)}) copy-start(f32[1024]{0:T(1024)} %param.21) | copy-start | bytes 12292
  41.8 10.1 %collective-permute-start.17 = (bf16[2,64,1152]{2,1,0:T(8,128)(2,1)}, bf16[2,64,1152]{2,1,0:T(8,128)(2,1)}, u32[]{:S(2)}, u32[]{:S(2)}) collective-permute-start(bf16[2,64,1152]{2,1,0:T(8,128)(2,1)} %pad_maximum_fusion.2.refs_8_), channel_id=1, source_target_pairs={{192,0},{208,16},{224,32},{240,48},{0,64},{16,80},{32,96},{48,112}... | collective-permute-start | bytes 884744 | tf_op jit(solution)/shard_map/ppermute | solution.py:406
  41.8 10.0 %collective-permute-start.7 = (bf16[2,64,1152]{2,1,0:T(8,128)(2,1)S(1)}, bf16[2,64,1152]{2,1,0:T(8,128)(2,1)}, u32[]{:S(2)}, u32[]{:S(2)}) collective-permute-start(bf16[2,64,1152]{2,1,0:T(8,128)(2,1)S(1)} %collective-permute-done.6.refs_7_), channel_id=1, source_target_pairs={{48,0},{0,16},{16,32},{32,48},{112,64},{64,80},{80,96},{96,112},{1... | collective-permute-start | bytes 884744 | tf_op jit(solution)/shard_map/ppermute | solution.py:406
  42.2 9.7 %collective-permute-start.5 = (bf16[2,64,1152]{2,1,0:T(8,128)(2,1)}, bf16[2,64,1152]{2,1,0:T(8,128)(2,1)}, u32[]{:S(2)}, u32[]{:S(2)}) collective-permute-start(bf16[2,64,1152]{2,1,0:T(8,128)(2,1)} %collective-permute-done.3.refs_2_), channel_id=1, source_target_pairs={{16,0},{32,16},{48,32},{0,48},{80,64},{96,80},{112,96},{64,112},{1... | collective-permute-start | bytes 884744 | tf_op jit(solution)/shard_map/ppermute | solution.py:406
  45.3 8.2 %collective-permute-start.16 = (bf16[2,64,1152]{2,1,0:T(8,128)(2,1)}, bf16[2,64,1152]{2,1,0:T(8,128)(2,1)}, u32[]{:S(2)}, u32[]{:S(2)}) collective-permute-start(bf16[2,64,1152]{2,1,0:T(8,128)(2,1)} %collective-permute-done.15.refs_15_), channel_id=1, source_target_pairs={{192,0},{208,16},{224,32},{240,48},{0,64},{16,80},{32,96},{48,112}... | collective-permute-start | bytes 884744 | tf_op jit(solution)/shard_map/ppermute | solution.py:406
  49.1 7.0 %collective-permute-start.14 = (bf16[2,64,1152]{2,1,0:T(8,128)(2,1)}, bf16[2,64,1152]{2,1,0:T(8,128)(2,1)}, u32[]{:S(2)}, u32[]{:S(2)}) collective-permute-start(bf16[2,64,1152]{2,1,0:T(8,128)(2,1)} %collective-permute-done.12.refs_10_), channel_id=1, source_target_pairs={{64,0},{80,16},{96,32},{112,48},{128,64},{144,80},{160,96},{176,11... | collective-permute-start | bytes 884744 | tf_op jit(solution)/shard_map/ppermute | solution.py:406
  97.3 3.9 %collective-permute-start.18 = (bf16[16,8,16,256]{3,2,1,0:T(8,128)(2,1)}, bf16[16,8,16,256]{3,2,1,0:T(8,128)(2,1)S(1)}, u32[]{:S(2)}, u32[]{:S(2)}) collective-permute-start(bf16[16,8,16,256]{3,2,1,0:T(8,128)(2,1)} %get-tuple-element.22), channel_id=1, source_target_pairs={{0,1},{1,0},{2,3},{3,2},{4,5},{5,4},{6,7},{7,6},{8,9},{9,8},{10,11... | collective-permute-start | bytes 3145736 | tf_op jit(solution)/shard_map/ppermute | solution.py:516
  97.6 3.6 %copy-start.3 = (bf16[16,8,16,256]{3,2,1,0:T(8,128)(2,1)S(1)}, bf16[16,8,16,256]{3,2,1,0:T(8,128)(2,1)}, u32[]{:S(2)}) copy-start(bf16[16,8,16,256]{3,2,1,0:T(8,128)(2,1)} %get-tuple-element.21) | copy-start | bytes 3145732
Sparse Core Ops, SparseCore 0:
  9.8 68.7 all-gather.1

commit v6 on v5

--- a/solution.py
+++ b/solution.py
@@ -113,11 +113,22 @@
 
 
 def attention_kernel(
+    pairs,
+    counts,
+    core,
+    *refs,
+):
+    shards = refs[:pairs], refs[pairs : 2 * pairs]
+    attention_steps(pairs, shards, counts, core, *refs[2 * pairs :])
+
+
+def attention_steps(
+    pairs,
+    shards,
     counts,
     core,
     normed,
     base,
-    weights,
     queries,
     cand_t,
     mask,
@@ -147,40 +158,60 @@
     other_s,
     sems,
     mix_sems,
+    out_sems,
     grad_sems,
 ):
     step = pl.program_id(0)
     total, width = normed_s.shape
     pair = 2 * LANES
 
-    def mix_copy(i, group):
-        start = pl.multiple_of(group * width + i * pair, pair)
-        return pltpu.make_async_copy(
-            weights.at[:, pl.ds(start, pair)], mix_s.at[i, group], mix_sems.at[i, group]
-        )
+    piece = shards[0][0].shape[1]
+
+    def starts():
+        for k in range(2):
+            for d in range(pairs):
+                which = jnp.where(k == 0, core[0], 1 - core[0])
+                start = (2 * lax.rem(core[1] + d, pairs) + which) * piece
+                yield 2 * d + k, shards[k][d], pl.multiple_of(start, piece)
+
+    def mix_copies(i):
+        cols = pl.ds(pl.multiple_of(i * pair, pair), pair)
+        return [
+            pltpu.make_async_copy(
+                shard.at[pl.ds(0, 4), :, cols],
+                mix_s.at[i, :, pl.ds(start, piece)],
+                mix_sems.at[i, n],
+            )
+            for n, shard, start in starts()
+        ]
+
+    def out_copies():
+        return [
+            pltpu.make_async_copy(shard.at[4], out_s.at[pl.ds(start, piece)], out_sems.at[n])
+            for n, shard, start in starts()
+        ]
 
     normed_copy = pltpu.make_async_copy(normed, normed_s, sems.at[0])
     base_copy = pltpu.make_async_copy(base, base_s, sems.at[1])
-    out_copy = pltpu.make_async_copy(weights.at[:, pl.ds(4 * width, width)], out_s, sems.at[2])
     query_copy = pltpu.make_async_copy(queries, queries_s, sems.at[3])
     cand_copy = pltpu.make_async_copy(cand_t, cand_s, sems.at[4])
 
     @pl.when(step == 0)
     def _():
         normed_copy.start()
-        for group in range(4):
-            mix_copy(0, group).start()
+        for copy in mix_copies(0):
+            copy.start()
         normed_copy.wait()
 
     @pl.when(step < ENCODE_STEPS)
     def _():
-        for group in range(4):
-            mix_copy(step, group).wait()
+        for copy in mix_copies(step):
+            copy.wait()
 
         @pl.when(step + 1 < ENCODE_STEPS)
         def _():
-            for group in range(4):
-                mix_copy(step + 1, group).start()
+            for copy in mix_copies(step + 1):
+                copy.start()
 
         @pl.when(step == 1)
         def _():
@@ -188,7 +219,8 @@
 
         @pl.when(step == 2)
         def _():
-            out_copy.start()
+            for copy in out_copies():
+                copy.start()
 
         @pl.when(step == 3)
         def _():
@@ -226,7 +258,8 @@
             gated_s[:, h * LANES : (h + 1) * LANES] = (mixed_s[h] * scale * gate_s[h]).astype(BF)
         active = mask[:, :1] > 0.0
         base_copy.wait()
-        out_copy.wait()
+        for copy in out_copies():
+            copy.wait()
         for n in range(width // pair):
             cols = slice(n * pair, (n + 1) * pair)
             value = base_s[:, cols] + dot(gated_s[...], out_s[:, cols])
@@ -285,17 +318,17 @@
         _, pairs, tall, wide = mine.shape
         right = width // wide
         down = mine.shape[0] // right
-        piece = tall * down
+        tall_piece = tall * down
         copies = []
         for n in range(right):
             cols = slice(n * wide, (n + 1) * wide)
             slope = slope_s[:, :, cols].reshape(-1, wide)
             for which, store in ((core[0], mine_s), (1 - core[0], other_s)):
-                rows = cand_s[:, which].reshape(pairs * piece, -1)
+                rows = cand_s[:, which].reshape(pairs * tall_piece, -1)
                 grad = dot(rows, slope).astype(BF)
                 for p in range(pairs):
                     for a in range(down):
-                        start = p * piece + a * tall
+                        start = p * tall_piece + a * tall
                         store[n * down + a, p] = grad[start : start + tall]
             chunk = pl.ds(n * down, down)
             for k, (source, target) in enumerate(((mine_s, mine), (other_s, other))):
@@ -314,7 +347,8 @@
     normed,
     base,
     mask,
-    weights,
+    shards,
+    other_shards,
     queries,
     cand_t,
     score_weight,
@@ -334,11 +368,11 @@
     whole = lambda i, n, c: (0, 0)
     anywhere = pl.BlockSpec(memory_space=pl.ANY)
     return pl.pallas_call(
-        attention_kernel,
+        functools.partial(attention_kernel, pairs),
         grid_spec=pltpu.PrefetchScalarGridSpec(
             num_scalar_prefetch=2,
             grid=(ENCODE_STEPS + groups,),
-            in_specs=[anywhere] * 5
+            in_specs=[anywhere] * (2 * pairs + 4)
             + [
                 pl.BlockSpec((total, LANES), whole),
                 pl.BlockSpec((1, width), whole),
@@ -370,7 +404,8 @@
                 pltpu.VMEM(shape, BF),
                 pltpu.VMEM(shape, BF),
                 pltpu.SemaphoreType.DMA((5,)),
-                pltpu.SemaphoreType.DMA((ENCODE_STEPS, 4)),
+                pltpu.SemaphoreType.DMA((ENCODE_STEPS, 2 * pairs)),
+                pltpu.SemaphoreType.DMA((2 * pairs,)),
                 pltpu.SemaphoreType.DMA((2, side)),
             ],
         ),
@@ -386,9 +421,10 @@
     )(
         counts,
         core,
+        *shards,
+        *other_shards,
         normed,
         base,
-        weights,
         queries.reshape(groups, GROUP * rows, width),
         cand_t.reshape(pairs, 2, width // (2 * pairs), total),
         mask,
@@ -406,27 +442,64 @@
     return lax.ppermute(array, "user", moves)
 
 
-def spread(piece, side, x_first):
-    first = lambda a, d: shift(a, side, d, 0) if x_first else shift(a, side, 0, d)
-    second = lambda a, d: shift(a, side, 0, d) if x_first else shift(a, side, d, 0)
-    low = jnp.stack([piece, first(piece, 1)])
-    high = jnp.stack([first(piece, 2), first(piece, -1)])
-    low_after, high_before = second(low, 1), second(high, -1)
-    high_after, low_before = second(high, 1), second(low, -1)
-    low_two, high_two = second(low_after, 1), second(high_before, -1)
-    return (low, high, low_after, high_after, low_two, high_two, low_before, high_before)
+def travel(piece, shard, side, loaders):
+    along_x = lambda a, d: shift(a, side, d, 0)
+    along_y = lambda a, d: shift(a, side, 0, d)
+    along_z = lambda a, d: lax.ppermute(
+        a, "loader", [((i + 2 * d) % loaders, i) for i in range(loaders)]
+    )
+    swap = lambda a: lax.ppermute(a, "loader", [(i, i ^ 1) for i in range(loaders)])
+    half = piece.shape[0] // 2
+    halves = ((piece[:half], along_x, along_y), (piece[half:], along_y, along_x))
+    pairs = loaders // 2
+
+    after, before = [shard], [shard]
+    after.append(along_z(shard, 1))
+    before.append(along_z(shard, -1))
+    near = [[first(p, d) for d in (1, 2, -1)] for p, first, _ in halves]
+    others = [swap(shard)]
+    after, before, near, others = lax.optimization_barrier((after, before, near, others))
+
+    after.append(along_z(after[1], 1))
+    before.append(along_z(before[1], -1))
+    results = []
+    for (p, _, second), (one, two, three) in zip(halves, near):
+        low, high = jnp.stack([p, one]), jnp.stack([two, three])
+        results.append([low, high, second(low, 1), second(high, 1), second(low, -1), second(high, -1)])
+    after, before, results = lax.optimization_barrier((after, before, results))
+
+    after.append(along_z(after[2], 1))
+    before.append(along_z(before[2], -1))
+    spreads = []
+    for (p, _, second), (low, high, low1, high1, low3, high3) in zip(halves, results):
+        spreads.append((low, high, low1, high1, second(low1, 1), second(high3, -1), low3, high3))
+    others_after = [swap(a) for a in after[1:3]]
+    others_before = [swap(a) for a in before[1:3]]
+    after, before, spreads, others_after, others_before = lax.optimization_barrier(
+        (after, before, spreads, others_after, others_before)
+    )
+    cut = (shard.shape[0] + 1) // 2
+    middle = jnp.concatenate([along_z(after[3][:cut], 1), along_z(before[3][cut:], -1)])
+    others_after.append(swap(after[3]))
+    others_before.append(swap(before[3]))
+    own = after + [middle] + before[:0:-1]
+    others = others + others_after + [swap(middle)] + others_before[::-1]
+    assert len(own) == pairs and len(others) == pairs
+    return spreads[0], spreads[1], own, others
 
 
 def join_kernel(left, right, out):
-    wide = left.shape[1]
-    out[:, :wide] = left[...]
-    out[:, wide:] = right[...]
+    wide = right.shape[1]
+    for g in range(out.shape[0] - 1):
+        out[g] = left[:, g * wide : (g + 1) * wide]
+    out[out.shape[0] - 1] = right[...]
 
 
 def join(left, right):
+    groups = left.shape[1] // right.shape[1] + 1
     return pl.pallas_call(
         join_kernel,
-        out_shape=jax.ShapeDtypeStruct((left.shape[0], left.shape[1] + right.shape[1]), left.dtype),
+        out_shape=jax.ShapeDtypeStruct((groups,) + right.shape, left.dtype),
         name="join",
     )(left, right)
 
@@ -469,7 +542,6 @@
     pairs = loaders // 2
     nblocks, rows, width = candidates.shape
 
-    weights = lax.all_gather(join(mix_weight, out_weight), "loader", axis=0, tiled=True)
     actions = action_table.shape[0]
     packed = jnp.concatenate(
         [
@@ -481,8 +553,9 @@
     )
     side = math.isqrt(users)
     half = HIST // 2
-    halves_a = spread(packed[:half], side, True)
-    halves_b = spread(packed[half:], side, False)
+    halves_a, halves_b, shards, other_shards = travel(
+        packed, join(mix_weight, out_weight), side, loaders
+    )
 
     flat = candidates.reshape(-1, width)
     queries = jnp.dot(flat, query_weight, preferred_element_type=F32).astype(BF)
@@ -496,14 +569,16 @@
     base, normed, mask = prepare(
         far_y * side + far_x, far_x * side + far_y, halves_a, halves_b, action_table
     )
-    core = lax.rem(lax.axis_index("loader").astype(jnp.int32), 2)[None]
+    loader = lax.axis_index("loader").astype(jnp.int32)
+    place = jnp.stack([lax.rem(loader, 2), loader // 2])
     scores, error, slopes, mine, other = attention(
         row_counts,
-        core,
+        place,
         normed,
         base,
         mask,
-        weights,
+        shards,
+        other_shards,
         queries,
         cand_t,
         score_weight[None],
@@ -514,9 +589,6 @@
     )
 
     arrived = lax.ppermute(other, "loader", [(i, i ^ 1) for i in range(loaders)])
-    back = lax.dot_general(slopes, query_weight, (((1,), (1,)), ((), ())), preferred_element_type=F32)
-    row_grads = (error.reshape(-1)[:, None] * self_weight + back).astype(BF)
-    mine, row_grads = lax.optimization_barrier((mine, row_grads))
     pieces = (mine.astype(F32) + arrived.astype(F32)).astype(BF)
     pieces = lax.all_to_all(pieces, "user", 0, 0, tiled=True)
     pieces = jnp.sum(pieces.astype(F32), 0).astype(BF)
@@ -528,6 +600,8 @@
     )
     query_grad = assemble(pieces, side)
 
+    back = lax.dot_general(slopes, query_weight, (((1,), (1,)), ((), ())), preferred_element_type=F32)
+    row_grads = (error.reshape(-1)[:, None] * self_weight + back).astype(BF)
     return (scores[:, 0], row_grads.reshape(nblocks, rows, width), query_grad)
 
 

time: 157 us -> 191 us (1.22)
  waiting for transfers between devices: 25.1 us -> 56 us
  starting transfers between devices: 27.5 us -> 50.8 us
  between operations: 14.9 us -> 1.69 us
  blocking collectives: 46.8 us -> 34.4 us
  local copies, waits for them, and re-layouts: 3.32 us -> 7.28 us
    ppermute x18, waiting for transfers between devices: 8.36 us -> 36 us  [shift(): return lax.ppermute(array, 'user', moves)]
    all_gather x1 -> x0, waiting for transfers between devices: 16.7 us -> none  [body(): lax.all_gather(join(mix_weight, out_weight), 'loader', axis=0, tiled=True)]
    ppermute x0 -> x16, starting transfers between devices: none -> 16 us  [the longest x8 14.5 us: travel(): lax.ppermute(a, 'loader', [((i + 2 * d) % loaders, i) for i in range(load...]
    ppermute x0 -> x16, waiting for transfers between devices: none -> 14.6 us  [the longest x8 14.6 us: travel(): lax.ppermute(a, 'loader', [((i + 2 * d) % loaders, i) for i in range(load...]
    all_to_all x1 -> x0, blocking collectives: 12 us -> none  [body(): lax.all_to_all(jnp.broadcast_to(piece[None], (users,) + piece.shape), 'us...]
    all_to_all x0 -> x1, starting transfers between devices: none -> 5.69 us  [body(): lax.all_to_all(jnp.broadcast_to(piece[None], (users,) + piece.shape), 'us...]
    all_to_all x0 -> x1, waiting for transfers between devices: none -> 2.93 us  [body(): lax.all_to_all(jnp.broadcast_to(piece[None], (users,) + piece.shape), 'us...]
    ppermute x1, waiting for transfers between devices: 0.01 us -> 2.5 us  [body(): lax.ppermute(other, 'loader', [(i, i ^ 1) for i in range(loaders)])]
  transfers between devices with their start and end apart: 20 -> 36, of which waited for: 6 -> 18; matrix products, arithmetic and copies ran while one was open for 8% -> 7% of each run, Pallas kernels for 4% -> 3%
where the time goes in v6:
time: 191 us; the launch traced here: 190 us
  waiting for transfers between devices  56 us (29%)
  starting transfers between devices  50.8 us (27%)
  blocking collectives  34.4 us (18%)
  Pallas kernels  29.3 us (15%)
  local copies, waits for them, and re-layouts  7.28 us (4%)
  matrix products  5.71 us (3%)
  other arithmetic  4.98 us (3%)
    ppermute x18, waiting for transfers between devices, shift(): return lax.ppermute(array, 'user', moves)  36 us
    ppermute x18, starting transfers between devices, shift(): return lax.ppermute(array, 'user', moves)  28.6 us
    all_to_all x1, blocking collectives, body(): pieces = lax.all_to_all(pieces, 'user', 0, 0, tiled=True)  23.5 us
    pallas_call x1, Pallas kernels, attention(): pl.pallas_call(functools.partial(attention_kernel, pairs), grid_spec=pltp...  19.8 us
    ppermute x8, waiting for transfers between devices, travel(): lax.ppermute(a, 'loader', [((i + 2 * d) % loaders, i) for i in range(load...  14.6 us
    ppermute x8, starting transfers between devices, travel(): lax.ppermute(a, 'loader', [((i + 2 * d) % loaders, i) for i in range(load...  14.5 us
    all_to_all x1, blocking collectives, body(): lax.all_to_all(pieces, 'loader', 0, 0, axis_index_groups=groups, tiled=True)  10.9 us
    pallas_call x1, Pallas kernels, prepare(): pl.pallas_call(functools.partial(prepare_kernel, nblocks), grid_spec=pltp...  5.78 us
  transfers between devices with their start and end apart: 36, of which 18 were waited for; matrix products, arithmetic and copies ran while one was open for 7% of the time, Pallas kernels for 3%

profile of v6, /device:TPU:2, one launch (start us, length us, event | category | flops | bytes accessed | tf_op | source)
XLA Modules:
  0.0 190.2 jit_solution(1277072933461021509)
XLA Ops:
  0.6 2.2 %join.1.refs_0_ = bf16[5,64,1024]{2,1,0:T(8,128)(2,1)} custom-call(bf16[64,4096]{1,0:T(8,128)(2,1)} %left.1, bf16[64,1024]{1,0:T(8,128)(2,1)} %right.1), custom_call_target="tpu_custom_call" | custom-call | tf_op jit(solution)/shard_map/join/pallas_call | solution.py:500
  2.8 5.9 %collective-permute-start = (bf16[5,64,1024]{2,1,0:T(8,128)(2,1)}, bf16[5,64,1024]{2,1,0:T(8,128)(2,1)}, u32[]{:S(2)}, u32[]{:S(2)}) collective-permute-start(bf16[5,64,1024]{2,1,0:T(8,128)(2,1)} %join.1.refs_0_), channel_id=1, source_target_pairs={{2,0},{3,1},{4,2},{5,3},{6,4},{7,5},{8,6},{9,7},{10,8},{11,9},{12,... | collective-permute-start | bytes 1966088 | tf_op jit(solution)/shard_map/ppermute | solution.py:448
  9.3 0.7 convert_bitcast_fusion
  10.1 1.1 concatenate.6
  11.2 0.6 collective-permute-start.2
  11.8 2.4 %collective-permute-start.3 = (bf16[64,1152]{1,0:T(8,128)(2,1)S(1)}, bf16[64,1152]{1,0:T(8,128)(2,1)S(1)}, u32[]{:S(2)}, u32[]{:S(2)}) collective-permute-start(bf16[64,1152]{1,0:T(8,128)(2,1)S(1)} %get-tuple-element.133), channel_id=1, source_target_pairs={{128,0},{144,16},{160,32},{176,48},{192,64},{208,80},{224,96},{240... | collective-permute-start | bytes 442376 | tf_op jit(solution)/shard_map/ppermute | solution.py:442
  14.2 3.3 %collective-permute-done.2 = bf16[64,1152]{1,0:T(8,128)(2,1)S(1)} collective-permute-done((bf16[64,1152]{1,0:T(8,128)(2,1)S(1)}, bf16[64,1152]{1,0:T(8,128)(2,1)S(1)}, u32[]{:S(2)}, u32[]{:S(2)}) %collective-permute-start.2) | collective-permute-done | bytes 147488 | tf_op jit(solution)/shard_map/ppermute | solution.py:442
  17.5 1.9 collective-permute-start.4
  19.4 2.2 %collective-permute-done.3 = bf16[64,1152]{1,0:T(8,128)(2,1)S(1)} collective-permute-done((bf16[64,1152]{1,0:T(8,128)(2,1)S(1)}, bf16[64,1152]{1,0:T(8,128)(2,1)S(1)}, u32[]{:S(2)}, u32[]{:S(2)}) %collective-permute-start.3) | collective-permute-done | bytes 147488 | tf_op jit(solution)/shard_map/ppermute | solution.py:442
  21.6 3.0 %collective-permute-start.5 = (bf16[64,1152]{1,0:T(8,128)(2,1)S(1)}, bf16[64,1152]{1,0:T(8,128)(2,1)S(1)}, u32[]{:S(2)}, u32[]{:S(2)}) collective-permute-start(bf16[64,1152]{1,0:T(8,128)(2,1)S(1)} %get-tuple-element.132), channel_id=1, source_target_pairs={{16,0},{32,16},{48,32},{0,48},{80,64},{96,80},{112,96},{64,112},{1... | collective-permute-start | bytes 442376 | tf_op jit(solution)/shard_map/ppermute | solution.py:442
  24.6 0.5 collective-permute-done.4
  25.1 3.2 %collective-permute-start.6 = (bf16[64,1152]{1,0:T(8,128)(2,1)S(1)}, bf16[64,1152]{1,0:T(8,128)(2,1)S(1)}, u32[]{:S(2)}, u32[]{:S(2)}) collective-permute-start(bf16[64,1152]{1,0:T(8,128)(2,1)S(1)} %get-tuple-element.132), channel_id=1, source_target_pairs={{32,0},{48,16},{0,32},{16,48},{96,64},{112,80},{64,96},{80,112},{1... | collective-permute-start | bytes 442376 | tf_op jit(solution)/shard_map/ppermute | solution.py:442
  28.3 0.7 collective-permute-start.7
  29.0 3.2 %collective-permute-done.6 = bf16[64,1152]{1,0:T(8,128)(2,1)S(1)} collective-permute-done((bf16[64,1152]{1,0:T(8,128)(2,1)S(1)}, bf16[64,1152]{1,0:T(8,128)(2,1)S(1)}, u32[]{:S(2)}, u32[]{:S(2)}) %collective-permute-start.6) | collective-permute-done | bytes 147488 | tf_op jit(solution)/shard_map/ppermute | solution.py:442
  32.2 3.9 %collective-permute-done.7 = bf16[64,1152]{1,0:T(8,128)(2,1)S(1)} collective-permute-done((bf16[64,1152]{1,0:T(8,128)(2,1)S(1)}, bf16[64,1152]{1,0:T(8,128)(2,1)S(1)}, u32[]{:S(2)}, u32[]{:S(2)}) %collective-permute-start.7) | collective-permute-done | bytes 147488 | tf_op jit(solution)/shard_map/ppermute | solution.py:442
  36.2 3.2 %collective-permute-start.16 = (bf16[2,64,1152]{2,1,0:T(8,128)(2,1)S(1)}, bf16[2,64,1152]{2,1,0:T(8,128)(2,1)S(1)}, u32[]{:S(2)}, u32[]{:S(2)}) collective-permute-start(bf16[2,64,1152]{2,1,0:T(8,128)(2,1)S(1)} %pad_maximum_fusion.3.refs_9_), channel_id=1, source_target_pairs={{64,0},{80,16},{96,32},{112,48},{128,64},{144,80},{160,96},{176,11... | collective-permute-start | bytes 884744 | tf_op jit(solution)/shard_map/ppermute | solution.py:442
  39.4 1.8 collective-permute-start.12
  41.2 3.2 %collective-permute-start.9 = (bf16[5,64,1024]{2,1,0:T(8,128)(2,1)}, bf16[5,64,1024]{2,1,0:T(8,128)(2,1)}, u32[]{:S(2)}, u32[]{:S(2)}) collective-permute-start(bf16[5,64,1024]{2,1,0:T(8,128)(2,1)} %collective-permute-done.refs_1_), channel_id=1, source_target_pairs={{2,0},{3,1},{4,2},{5,3},{6,4},{7,5},{8,6},{9,7},{10,8},{11,9},{12,... | collective-permute-start | bytes 1966088 | tf_op jit(solution)/shard_map/ppermute | solution.py:448
  44.5 0.3 collective-permute-done.16.refs_11_
  44.8 0.3 collective-permute-start.14
  45.1 1.9 collective-permute-done.18.refs_15_
  47.0 1.1 collective-permute-start.11
  48.2 1.2 collective-permute-start.13
  49.4 6.6 %collective-permute-done.14.refs_7_ = bf16[2,64,1152]{2,1,0:T(8,128)(2,1)S(1)} collective-permute-done((bf16[2,64,1152]{2,1,0:T(8,128)(2,1)S(1)}, bf16[2,64,1152]{2,1,0:T(8,128)(2,1)S(1)}, u32[]{:S(2)}, u32[]{:S(2)}) %collective-permute-start.14) | collective-permute-done | bytes 294944 | tf_op jit(solution)/shard_map/ppermute | solution.py:442
  56.0 2.5 %collective-permute-start.15 = (bf16[2,64,1152]{2,1,0:T(8,128)(2,1)S(1)}, bf16[2,64,1152]{2,1,0:T(8,128)(2,1)S(1)}, u32[]{:S(2)}, u32[]{:S(2)}) collective-permute-start(bf16[2,64,1152]{2,1,0:T(8,128)(2,1)S(1)} %pad_maximum_fusion.2.refs_8_), channel_id=1, source_target_pairs={{64,0},{80,16},{96,32},{112,48},{128,64},{144,80},{160,96},{176,11... | collective-permute-start | bytes 884744 | tf_op jit(solution)/shard_map/ppermute | solution.py:442
  58.5 0.9 collective-permute-done.13.refs_6_
  59.4 3.3 %collective-permute-done.15.refs_10_ = bf16[2,64,1152]{2,1,0:T(8,128)(2,1)S(1)} collective-permute-done((bf16[2,64,1152]{2,1,0:T(8,128)(2,1)S(1)}, bf16[2,64,1152]{2,1,0:T(8,128)(2,1)S(1)}, u32[]{:S(2)}, u32[]{:S(2)}) %collective-permute-start.15) | collective-permute-done | bytes 294944 | tf_op jit(solution)/shard_map/ppermute | solution.py:442
  62.7 3.2 %collective-permute-done.17.refs_14_ = bf16[2,64,1152]{2,1,0:T(8,128)(2,1)S(1)} collective-permute-done((bf16[2,64,1152]{2,1,0:T(8,128)(2,1)S(1)}, bf16[2,64,1152]{2,1,0:T(8,128)(2,1)S(1)}, u32[]{:S(2)}, u32[]{:S(2)}) %collective-permute-start.17) | collective-permute-done | bytes 294944 | tf_op jit(solution)/shard_map/ppermute | solution.py:442
  65.9 3.3 %collective-permute-start.19 = (bf16[5,64,1024]{2,1,0:T(8,128)(2,1)}, bf16[5,64,1024]{2,1,0:T(8,128)(2,1)}, u32[]{:S(2)}, u32[]{:S(2)}) collective-permute-start(bf16[5,64,1024]{2,1,0:T(8,128)(2,1)} %collective-permute-done.9.refs_2_), channel_id=1, source_target_pairs={{2,0},{3,1},{4,2},{5,3},{6,4},{7,5},{8,6},{9,7},{10,8},{11,9},{12,... | collective-permute-start | bytes 1966088 | tf_op jit(solution)/shard_map/ppermute | solution.py:448
  69.2 2.0 %collective-permute-start.22 = (bf16[2,64,1152]{2,1,0:T(8,128)(2,1)S(1)}, bf16[2,64,1152]{2,1,0:T(8,128)(2,1)S(1)}, u32[]{:S(2)}, u32[]{:S(2)}) collective-permute-start(bf16[2,64,1152]{2,1,0:T(8,128)(2,1)S(1)} %collective-permute-done.14.refs_7_), channel_id=1, source_target_pairs={{48,0},{0,16},{16,32},{32,48},{112,64},{64,80},{80,96},{96,112},{1... | collective-permute-start | bytes 884744 | tf_op jit(solution)/shard_map/ppermute | solution.py:442
  71.2 4.7 %collective-permute-start.23 = (bf16[2,64,1152]{2,1,0:T(8,128)(2,1)S(1)}, bf16[2,64,1152]{2,1,0:T(8,128)(2,1)S(1)}, u32[]{:S(2)}, u32[]{:S(2)}) collective-permute-start(bf16[2,64,1152]{2,1,0:T(8,128)(2,1)S(1)} %collective-permute-done.15.refs_10_), channel_id=1, source_target_pairs={{64,0},{80,16},{96,32},{112,48},{128,64},{144,80},{160,96},{176,11... | collective-permute-start | bytes 884744 | tf_op jit(solution)/shard_map/ppermute | solution.py:442
  76.0 1.1 collective-permute-done.22.refs_5_
  77.1 3.0 %collective-permute-done.23.refs_12_ = bf16[2,64,1152]{2,1,0:T(8,128)(2,1)S(1)} collective-permute-done((bf16[2,64,1152]{2,1,0:T(8,128)(2,1)S(1)}, bf16[2,64,1152]{2,1,0:T(8,128)(2,1)S(1)}, u32[]{:S(2)}, u32[]{:S(2)}) %collective-permute-start.23) | collective-permute-done | bytes 294944 | tf_op jit(solution)/shard_map/ppermute | solution.py:442
  80.2 2.5 %collective-permute-done.24.refs_13_ = bf16[2,64,1152]{2,1,0:T(8,128)(2,1)S(1)} collective-permute-done((bf16[2,64,1152]{2,1,0:T(8,128)(2,1)S(1)}, bf16[2,64,1152]{2,1,0:T(8,128)(2,1)S(1)}, u32[]{:S(2)}, u32[]{:S(2)}) %collective-permute-start.24) | collective-permute-done | bytes 294944 | tf_op jit(solution)/shard_map/ppermute | solution.py:442
  82.7 0.6 collective-permute-start.28
  83.4 1.3 copy.17
  84.7 10.0 %collective-permute-done.20.refs_5_ = bf16[5,64,1024]{2,1,0:T(8,128)(2,1)} collective-permute-done((bf16[5,64,1024]{2,1,0:T(8,128)(2,1)}, bf16[5,64,1024]{2,1,0:T(8,128)(2,1)}, u32[]{:S(2)}, u32[]{:S(2)}) %collective-permute-start.20) | collective-permute-done | bytes 655392 | tf_op jit(solution)/shard_map/ppermute | solution.py:448
  94.7 1.0 slice.14
  95.9 0.5 multiply_add_fusion
  96.4 1.0 slice.15
  97.3 2.1 %collective-permute-start.30 = (bf16[2,64,1024]{2,1,0:T(8,128)(2,1)S(1)}, bf16[2,64,1024]{2,1,0:T(8,128)(2,1)S(1)}, u32[]{:S(2)}, u32[]{:S(2)}) collective-permute-start(bf16[2,64,1024]{2,1,0:T(8,128)(2,1)S(1)} %slice.15), channel_id=1, source_target_pairs={{14,0},{15,1},{0,2},{1,3},{2,4},{3,5},{4,6},{5,7},{6,8},{7,9},{8,1... | collective-permute-start | bytes 786440 | tf_op jit(solution)/shard_map/ppermute | solution.py:448
  99.4 0.9 multiply_reduce_fusion
  100.3 0.5 collective-permute-start.33
  100.8 4.6 %collective-permute-done.29 = bf16[3,64,1024]{2,1,0:T(8,128)(2,1)S(1)} collective-permute-done((bf16[3,64,1024]{2,1,0:T(8,128)(2,1)S(1)}, bf16[3,64,1024]{2,1,0:T(8,128)(2,1)S(1)}, u32[]{:S(2)}, u32[]{:S(2)}) %collective-permute-start.29) | collective-permute-done | bytes 393248 | tf_op jit(solution)/shard_map/ppermute | solution.py:448
  105.4 0.3 collective-permute-start.32
  105.8 0.7 pad_add_fusion.core
  106.4 0.5 multiply_add_fusion.1.place_a
  106.9 2.2 %convolution_convert_fusion = bf16[512,1024]{1,0:T(8,128)(2,1)} fusion(bf16[512,1024]{1,0:T(8,128)(2,1)S(1)} %bitcast.52, bf16[1024,1024]{1,0:T(8,128)(2,1)S(1)} %copy-done), kind=kOutput, calls=%fused_computation.3 | convolution fusion | flops 1074266112 | bytes 4194304 | tf_op jit(solution)/shard_map/dot_general | solution.py:561
  109.2 5.8 %prepare.1 = (f32[512,1024]{1,0:T(8,128)}, bf16[512,1024]{1,0:T(8,128)(2,1)}, f32[512,128]{1,0:T(8,128)}) custom-call(s32[4]{0:T(128)} %multiply_add_fusion.1.place_a, s32[4]{0:T(128)} %get-tuple-element.127.place_b, bf16[2,64,1152]{2,1,0:T(8,128)(2,1)} %copy-done.5, bf16[2,64,1152]{2,1,0:T(8,128)(2,1)} %copy-done.4, bf16[2,64,1152]{2,1,0:T(8,128)(2,1)} %copy-done.15, ...), custom_call_target="tpu_custom_call" | custom-call | tf_op jit(solution)/shard_map/prepare/pallas_call | solution.py:84
  115.0 0.8 copy-done.7
  115.8 0.2 copy-done.8
  116.1 0.2 copy-done.9
  116.2 19.8 %attention.1 = (f32[4,1,128]{2,1,0:T(1,128)}, f32[4,1,128]{2,1,0:T(1,128)}, bf16[512,1024]{1,0:T(8,128)(2,1)}, bf16[16,8,16,256]{3,2,1,0:T(8,128)(2,1)}, bf16[16,8,16,256]{3,2,1,0:T(8,128)(2,1)}) custom-call(s32[4]{0:T(128)} %counts.1, s32[2]{0:T(128)} %pad_add_fusion.core, bf16[5,64,1024]{2,1,0:T(8,128)(2,1)} %join.1.refs_0_, ...), custom_call_target="tpu_custom_call" | custom-call | tf_op jit(solution)/shard_map/attention/pallas_call | solution.py:370
  136.0 0.6 collective-permute-start.34
  136.6 2.5 %collective-permute-done.34 = bf16[16,8,16,256]{3,2,1,0:T(8,128)(2,1)S(1)} collective-permute-done((bf16[16,8,16,256]{3,2,1,0:T(8,128)(2,1)}, bf16[16,8,16,256]{3,2,1,0:T(8,128)(2,1)S(1)}, u32[]{:S(2)}, u32[]{:S(2)}) %collective-permute-start.34) | collective-permute-done | bytes 1048608 | tf_op jit(solution)/shard_map/ppermute | solution.py:591
  139.1 1.5 add_convert_fusion
  140.6 23.5 %all_to_all.15 = bf16[16,8,16,256]{3,2,1,0:T(8,128)(2,1)S(1)} all-to-all(bf16[16,8,16,256]{3,2,1,0:T(8,128)(2,1)S(1)} %add_convert_fusion), channel_id=1, replica_groups=mesh['user'=16,'loader'=16] {'user'}, dimensions={0} | all-to-all | bytes 2097152 | tf_op jit(solution)/shard_map/all_to_all | solution.py:593
  164.2 10.9 %all_to_all.16 = bf16[8,16,256]{2,1,0:T(8,128)(2,1)S(1)} all-to-all(bf16[8,16,256]{2,1,0:T(8,128)(2,1)S(1)} %reduce_sum.34), channel_id=1, replica_groups={{0,2,4,6,8,10,12,14},{1,3,5,7,9,11,13,15},{16,18,20,22,24,26,28,30},{17..., dimensions={0} | all-to-all | bytes 131072 | tf_op jit(solution)/shard_map/all_to_all | solution.py:596
  175.2 0.7 broadcast_in_dim.30
  175.8 5.7 %all-to-all-start.2 = ((bf16[16,16,256]{2,1,0:T(8,128)(2,1)}), bf16[16,16,256]{2,1,0:T(8,128)(2,1)S(1)}, u32[]{:S(2)}, u32[]{:S(2)}) async-start(bf16[16,16,256]{2,1,0:T(8,128)(2,1)} %broadcast_in_dim.30), calls=%async_computation.2 | async-start | bytes 262144 | tf_op jit(solution)/shard_map/all_to_all | solution.py:598
  181.5 3.5 %add_convert_fusion.1 = bf16[512,1024]{1,0:T(8,128)(2,1)} fusion(f32[1024]{0:T(1024)S(1)} %copy-done.23, f32[512]{0:T(512)S(1)} %bitcast.65, bf16[512,1024]{1,0:T(8,128)(2,1)} %get-tuple-element.124, bf16[1024,1024]{1,0:T(8,128)(2,1)S(1)} %copy-done), kind=kOutput, calls=%fused_computation.1 | convolution fusion | flops 1075314688 | bytes 4200448 | tf_op jit(solution)/shard_map/dot_general | solution.py:603
  185.0 2.9 %all-to-all-done.2.pieces = bf16[16,16,256]{2,1,0:T(8,128)(2,1)S(1)} async-done(((bf16[16,16,256]{2,1,0:T(8,128)(2,1)}), bf16[16,16,256]{2,1,0:T(8,128)(2,1)S(1)}, u32[]{:S(2)}, u32[]{:S(2)}) %all-to-all-start.2) | async-done | bytes 131104 | tf_op jit(solution)/shard_map/all_to_all | solution.py:598
  188.0 0.7 copy-done.10
  188.6 1.6 assemble.1
  (90 shorter events, 0.9 us)
Async XLA Ops:
  0.6 106.3 %copy-start = (bf16[1024,1024]{1,0:T(8,128)(2,1)S(1)}, bf16[1024,1024]{1,0:T(8,128)(2,1)}, u32[]{:S(2)}) copy-start(bf16[1024,1024]{1,0:T(8,128)(2,1)} %param.19) | copy-start | bytes 6291460
  2.8 80.6 %copy-start.1 = (bf16[4,128,1024]{2,1,0:T(8,128)(2,1)S(1)}, bf16[4,128,1024]{2,1,0:T(8,128)(2,1)}, u32[]{:S(2)}) copy-start(bf16[4,128,1024]{2,1,0:T(8,128)(2,1)} %param.22) | copy-start | bytes 3145732
  2.8 33.3 %collective-permute-start = (bf16[5,64,1024]{2,1,0:T(8,128)(2,1)}, bf16[5,64,1024]{2,1,0:T(8,128)(2,1)}, u32[]{:S(2)}, u32[]{:S(2)}) collective-permute-start(bf16[5,64,1024]{2,1,0:T(8,128)(2,1)} %join.1.refs_0_), channel_id=1, source_target_pairs={{2,0},{3,1},{4,2},{5,3},{6,4},{7,5},{8,6},{9,7},{10,8},{11,9},{12,... | collective-permute-start | bytes 1966088 | tf_op jit(solution)/shard_map/ppermute | solution.py:448
  8.7 27.5 %collective-permute-start.1 = (bf16[5,64,1024]{2,1,0:T(8,128)(2,1)}, bf16[5,64,1024]{2,1,0:T(8,128)(2,1)}, u32[]{:S(2)}, u32[]{:S(2)}) collective-permute-start(bf16[5,64,1024]{2,1,0:T(8,128)(2,1)} %join.1.refs_0_), channel_id=1, source_target_pairs={{14,0},{15,1},{0,2},{1,3},{2,4},{3,5},{4,6},{5,7},{6,8},{7,9},{8,1... | collective-permute-start | bytes 1966088 | tf_op jit(solution)/shard_map/ppermute | solution.py:448
  8.7 27.5 %collective-permute-start.8 = (bf16[5,64,1024]{2,1,0:T(8,128)(2,1)}, bf16[5,64,1024]{2,1,0:T(8,128)(2,1)}, u32[]{:S(2)}, u32[]{:S(2)}) collective-permute-start(bf16[5,64,1024]{2,1,0:T(8,128)(2,1)} %join.1.refs_0_), channel_id=1, source_target_pairs={{0,1},{1,0},{2,3},{3,2},{4,5},{5,4},{6,7},{7,6},{8,9},{9,8},{10,11... | collective-permute-start | bytes 1966088 | tf_op jit(solution)/shard_map/ppermute | solution.py:451
  11.2 6.3 %collective-permute-start.2 = (bf16[64,1152]{1,0:T(8,128)(2,1)S(1)}, bf16[64,1152]{1,0:T(8,128)(2,1)S(1)}, u32[]{:S(2)}, u32[]{:S(2)}) collective-permute-start(bf16[64,1152]{1,0:T(8,128)(2,1)S(1)} %get-tuple-element.133), channel_id=1, source_target_pairs={{64,0},{80,16},{96,32},{112,48},{128,64},{144,80},{160,96},{176,11... | collective-permute-start | bytes 442376 | tf_op jit(solution)/shard_map/ppermute | solution.py:442
  11.8 9.8 %collective-permute-start.3 = (bf16[64,1152]{1,0:T(8,128)(2,1)S(1)}, bf16[64,1152]{1,0:T(8,128)(2,1)S(1)}, u32[]{:S(2)}, u32[]{:S(2)}) collective-permute-start(bf16[64,1152]{1,0:T(8,128)(2,1)S(1)} %get-tuple-element.133), channel_id=1, source_target_pairs={{128,0},{144,16},{160,32},{176,48},{192,64},{208,80},{224,96},{240... | collective-permute-start | bytes 442376 | tf_op jit(solution)/shard_map/ppermute | solution.py:442
  17.5 7.6 %collective-permute-start.4 = (bf16[64,1152]{1,0:T(8,128)(2,1)S(1)}, bf16[64,1152]{1,0:T(8,128)(2,1)S(1)}, u32[]{:S(2)}, u32[]{:S(2)}) collective-permute-start(bf16[64,1152]{1,0:T(8,128)(2,1)S(1)} %get-tuple-element.133), channel_id=1, source_target_pairs={{192,0},{208,16},{224,32},{240,48},{0,64},{16,80},{32,96},{48,112}... | collective-permute-start | bytes 442376 | tf_op jit(solution)/shard_map/ppermute | solution.py:442
  21.6 6.7 %collective-permute-start.5 = (bf16[64,1152]{1,0:T(8,128)(2,1)S(1)}, bf16[64,1152]{1,0:T(8,128)(2,1)S(1)}, u32[]{:S(2)}, u32[]{:S(2)}) collective-permute-start(bf16[64,1152]{1,0:T(8,128)(2,1)S(1)} %get-tuple-element.132), channel_id=1, source_target_pairs={{16,0},{32,16},{48,32},{0,48},{80,64},{96,80},{112,96},{64,112},{1... | collective-permute-start | bytes 442376 | tf_op jit(solution)/shard_map/ppermute | solution.py:442
  25.1 7.1 %collective-permute-start.6 = (bf16[64,1152]{1,0:T(8,128)(2,1)S(1)}, bf16[64,1152]{1,0:T(8,128)(2,1)S(1)}, u32[]{:S(2)}, u32[]{:S(2)}) collective-permute-start(bf16[64,1152]{1,0:T(8,128)(2,1)S(1)} %get-tuple-element.132), channel_id=1, source_target_pairs={{32,0},{48,16},{0,32},{16,48},{96,64},{112,80},{64,96},{80,112},{1... | collective-permute-start | bytes 442376 | tf_op jit(solution)/shard_map/ppermute | solution.py:442
  28.3 7.8 %collective-permute-start.7 = (bf16[64,1152]{1,0:T(8,128)(2,1)S(1)}, bf16[64,1152]{1,0:T(8,128)(2,1)S(1)}, u32[]{:S(2)}, u32[]{:S(2)}) collective-permute-start(bf16[64,1152]{1,0:T(8,128)(2,1)S(1)} %get-tuple-element.132), channel_id=1, source_target_pairs={{48,0},{0,16},{16,32},{32,48},{112,64},{64,80},{80,96},{96,112},{1... | collective-permute-start | bytes 442376 | tf_op jit(solution)/shard_map/ppermute | solution.py:442
  36.2 59.6 %copy-start.3 = (bf16[2,64,1152]{2,1,0:T(8,128)(2,1)}, bf16[2,64,1152]{2,1,0:T(8,128)(2,1)S(1)}, u32[]{:S(2)}) copy-start(bf16[2,64,1152]{2,1,0:T(8,128)(2,1)S(1)} %pad_maximum_fusion.3.refs_9_) | copy-start | bytes 884740
  36.2 8.6 %collective-permute-start.16 = (bf16[2,64,1152]{2,1,0:T(8,128)(2,1)S(1)}, bf16[2,64,1152]{2,1,0:T(8,128)(2,1)S(1)}, u32[]{:S(2)}, u32[]{:S(2)}) collective-permute-start(bf16[2,64,1152]{2,1,0:T(8,128)(2,1)S(1)} %pad_maximum_fusion.3.refs_9_), channel_id=1, source_target_pairs={{64,0},{80,16},{96,32},{112,48},{128,64},{144,80},{160,96},{176,11... | collective-permute-start | bytes 884744 | tf_op jit(solution)/shard_map/ppermute | solution.py:442
  39.3 7.7 %collective-permute-start.18 = (bf16[2,64,1152]{2,1,0:T(8,128)(2,1)S(1)}, bf16[2,64,1152]{2,1,0:T(8,128)(2,1)S(1)}, u32[]{:S(2)}, u32[]{:S(2)}) collective-permute-start(bf16[2,64,1152]{2,1,0:T(8,128)(2,1)S(1)} %pad_maximum_fusion.3.refs_9_), channel_id=1, source_target_pairs={{192,0},{208,16},{224,32},{240,48},{0,64},{16,80},{32,96},{48,112}... | collective-permute-start | bytes 884744 | tf_op jit(solution)/shard_map/ppermute | solution.py:442
  39.4 7.7 %copy-start.4 = (bf16[2,64,1152]{2,1,0:T(8,128)(2,1)}, bf16[2,64,1152]{2,1,0:T(8,128)(2,1)S(1)}, u32[]{:S(2)}) copy-start(bf16[2,64,1152]{2,1,0:T(8,128)(2,1)S(1)} %pad_maximum_fusion.1.refs_1_) | copy-start | bytes 884740
  39.4 56.5 %copy-start.24 = (s32[4,1]{0,1:T(1,128)S(1)}, s32[4,1]{0,1:T(1,128)}, u32[]{:S(2)}) copy-start(s32[4,1]{0,1:T(1,128)} %param.23) | copy-start | bytes 52
  39.4 8.8 %collective-permute-start.12 = (bf16[2,64,1152]{2,1,0:T(8,128)(2,1)S(1)}, bf16[2,64,1152]{2,1,0:T(8,128)(2,1)S(1)}, u32[]{:S(2)}, u32[]{:S(2)}) collective-permute-start(bf16[2,64,1152]{2,1,0:T(8,128)(2,1)S(1)} %pad_maximum_fusion.1.refs_1_), channel_id=1, source_target_pairs={{16,0},{32,16},{48,32},{0,48},{80,64},{96,80},{112,96},{64,112},{1... | collective-permute-start | bytes 884744 | tf_op jit(solution)/shard_map/ppermute | solution.py:442
  41.2 24.7 %collective-permute-start.10 = (bf16[5,64,1024]{2,1,0:T(8,128)(2,1)}, bf16[5,64,1024]{2,1,0:T(8,128)(2,1)}, u32[]{:S(2)}, u32[]{:S(2)}) collective-permute-start(bf16[5,64,1024]{2,1,0:T(8,128)(2,1)} %collective-permute-done.1.refs_7_), channel_id=1, source_target_pairs={{14,0},{15,1},{0,2},{1,3},{2,4},{3,5},{4,6},{5,7},{6,8},{7,9},{8,1... | collective-permute-start | bytes 1966088 | tf_op jit(solution)/shard_map/ppermute | solution.py:448
  41.2 24.7 %collective-permute-start.9 = (bf16[5,64,1024]{2,1,0:T(8,128)(2,1)}, bf16[5,64,1024]{2,1,0:T(8,128)(2,1)}, u32[]{:S(2)}, u32[]{:S(2)}) collective-permute-start(bf16[5,64,1024]{2,1,0:T(8,128)(2,1)} %collective-permute-done.refs_1_), channel_id=1, source_target_pairs={{2,0},{3,1},{4,2},{5,3},{6,4},{7,5},{8,6},{9,7},{10,8},{11,9},{12,... | collective-permute-start | bytes 1966088 | tf_op jit(solution)/shard_map/ppermute | solution.py:448
  44.5 11.5 %copy-start.5 = (bf16[2,64,1152]{2,1,0:T(8,128)(2,1)}, bf16[2,64,1152]{2,1,0:T(8,128)(2,1)S(1)}, u32[]{:S(2)}) copy-start(bf16[2,64,1152]{2,1,0:T(8,128)(2,1)S(1)} %pad_maximum_fusion.refs_0_) | copy-start | bytes 884740
  44.5 54.9 %copy-start.23 = (f32[1024]{0:T(1024)S(1)}, f32[1024]{0:T(1024)}, u32[]{:S(2)}) copy-start(f32[1024]{0:T(1024)} %param.21) | copy-start | bytes 12292
  44.8 21.1 %copy-start.11 = (bf16[2,64,1152]{2,1,0:T(8,128)(2,1)}, bf16[2,64,1152]{2,1,0:T(8,128)(2,1)S(1)}, u32[]{:S(2)}) copy-start(bf16[2,64,1152]{2,1,0:T(8,128)(2,1)S(1)} %collective-permute-done.16.refs_11_) | copy-start | bytes 884740
  44.8 11.2 %collective-permute-start.14 = (bf16[2,64,1152]{2,1,0:T(8,128)(2,1)S(1)}, bf16[2,64,1152]{2,1,0:T(8,128)(2,1)S(1)}, u32[]{:S(2)}, u32[]{:S(2)}) collective-permute-start(bf16[2,64,1152]{2,1,0:T(8,128)(2,1)S(1)} %pad_maximum_fusion.1.refs_1_), channel_id=1, source_target_pairs={{48,0},{0,16},{16,32},{32,48},{112,64},{64,80},{80,96},{96,112},{1... | collective-permute-start | bytes 884744 | tf_op jit(solution)/shard_map/ppermute | solution.py:442
  47.0 28.9 %copy-start.12 = (bf16[2,64,1152]{2,1,0:T(8,128)(2,1)}, bf16[2,64,1152]{2,1,0:T(8,128)(2,1)S(1)}, u32[]{:S(2)}) copy-start(bf16[2,64,1152]{2,1,0:T(8,128)(2,1)S(1)} %collective-permute-done.18.refs_15_) | copy-start | bytes 884740
  47.0 11.4 %collective-permute-start.11 = (bf16[2,64,1152]{2,1,0:T(8,128)(2,1)S(1)}, bf16[2,64,1152]{2,1,0:T(8,128)(2,1)S(1)}, u32[]{:S(2)}, u32[]{:S(2)}) collective-permute-start(bf16[2,64,1152]{2,1,0:T(8,128)(2,1)S(1)} %pad_maximum_fusion.refs_0_), channel_id=1, source_target_pairs={{16,0},{32,16},{48,32},{0,48},{80,64},{96,80},{112,96},{64,112},{1... | collective-permute-start | bytes 884744 | tf_op jit(solution)/shard_map/ppermute | solution.py:442
  48.2 11.2 %copy-start.6 = (bf16[2,64,1152]{2,1,0:T(8,128)(2,1)}, bf16[2,64,1152]{2,1,0:T(8,128)(2,1)S(1)}, u32[]{:S(2)}) copy-start(bf16[2,64,1152]{2,1,0:T(8,128)(2,1)S(1)} %pad_maximum_fusion.2.refs_8_) | copy-start | bytes 884740
  48.2 34.4 %copy-start.13 = (bf16[2,64,1152]{2,1,0:T(8,128)(2,1)}, bf16[2,64,1152]{2,1,0:T(8,128)(2,1)S(1)}, u32[]{:S(2)}) copy-start(bf16[2,64,1152]{2,1,0:T(8,128)(2,1)S(1)} %collective-permute-done.12.refs_3_) | copy-start | bytes 884740
  48.2 11.2 %collective-permute-start.13 = (bf16[2,64,1152]{2,1,0:T(8,128)(2,1)S(1)}, bf16[2,64,1152]{2,1,0:T(8,128)(2,1)S(1)}, u32[]{:S(2)}, u32[]{:S(2)}) collective-permute-start(bf16[2,64,1152]{2,1,0:T(8,128)(2,1)S(1)} %pad_maximum_fusion.refs_0_), channel_id=1, source_target_pairs={{48,0},{0,16},{16,32},{32,48},{112,64},{64,80},{80,96},{96,112},{1... | collective-permute-start | bytes 884744 | tf_op jit(solution)/shard_map/ppermute | solution.py:442
  56.0 26.7 %copy-start.14 = (bf16[2,64,1152]{2,1,0:T(8,128)(2,1)}, bf16[2,64,1152]{2,1,0:T(8,128)(2,1)S(1)}, u32[]{:S(2)}) copy-start(bf16[2,64,1152]{2,1,0:T(8,128)(2,1)S(1)} %collective-permute-done.14.refs_7_) | copy-start | bytes 884740
  56.0 6.7 %collective-permute-start.15 = (bf16[2,64,1152]{2,1,0:T(8,128)(2,1)S(1)}, bf16[2,64,1152]{2,1,0:T(8,128)(2,1)S(1)}, u32[]{:S(2)}, u32[]{:S(2)}) collective-permute-start(bf16[2,64,1152]{2,1,0:T(8,128)(2,1)S(1)} %pad_maximum_fusion.2.refs_8_), channel_id=1, source_target_pairs={{64,0},{80,16},{96,32},{112,48},{128,64},{144,80},{160,96},{176,11... | collective-permute-start | bytes 884744 | tf_op jit(solution)/shard_map/ppermute | solution.py:442
  58.5 24.2 %copy-start.15 = (bf16[2,64,1152]{2,1,0:T(8,128)(2,1)}, bf16[2,64,1152]{2,1,0:T(8,128)(2,1)S(1)}, u32[]{:S(2)}) copy-start(bf16[2,64,1152]{2,1,0:T(8,128)(2,1)S(1)} %collective-permute-done.11.refs_2_) | copy-start | bytes 884740
  58.5 7.4 %collective-permute-start.17 = (bf16[2,64,1152]{2,1,0:T(8,128)(2,1)S(1)}, bf16[2,64,1152]{2,1,0:T(8,128)(2,1)S(1)}, u32[]{:S(2)}, u32[]{:S(2)}) collective-permute-start(bf16[2,64,1152]{2,1,0:T(8,128)(2,1)S(1)} %pad_maximum_fusion.2.refs_8_), channel_id=1, source_target_pairs={{192,0},{208,16},{224,32},{240,48},{0,64},{16,80},{32,96},{48,112}... | collective-permute-start | bytes 884744 | tf_op jit(solution)/shard_map/ppermute | solution.py:442
  59.4 23.8 %copy-start.16 = (bf16[2,64,1152]{2,1,0:T(8,128)(2,1)}, bf16[2,64,1152]{2,1,0:T(8,128)(2,1)S(1)}, u32[]{:S(2)}) copy-start(bf16[2,64,1152]{2,1,0:T(8,128)(2,1)S(1)} %collective-permute-done.13.refs_6_) | copy-start | bytes 884740
  62.7 20.5 %copy-start.17 = (bf16[2,64,1152]{2,1,0:T(8,128)(2,1)}, bf16[2,64,1152]{2,1,0:T(8,128)(2,1)S(1)}, u32[]{:S(2)}) copy-start(bf16[2,64,1152]{2,1,0:T(8,128)(2,1)S(1)} %collective-permute-done.15.refs_10_) | copy-start | bytes 884740
  65.9 17.4 %copy-start.18 = (bf16[2,64,1152]{2,1,0:T(8,128)(2,1)}, bf16[2,64,1152]{2,1,0:T(8,128)(2,1)S(1)}, u32[]{:S(2)}) copy-start(bf16[2,64,1152]{2,1,0:T(8,128)(2,1)S(1)} %collective-permute-done.17.refs_14_) | copy-start | bytes 884740
  65.9 16.7 %collective-permute-start.19 = (bf16[5,64,1024]{2,1,0:T(8,128)(2,1)}, bf16[5,64,1024]{2,1,0:T(8,128)(2,1)}, u32[]{:S(2)}, u32[]{:S(2)}) collective-permute-start(bf16[5,64,1024]{2,1,0:T(8,128)(2,1)} %collective-permute-done.9.refs_2_), channel_id=1, source_target_pairs={{2,0},{3,1},{4,2},{5,3},{6,4},{7,5},{8,6},{9,7},{10,8},{11,9},{12,... | collective-permute-start | bytes 1966088 | tf_op jit(solution)/shard_map/ppermute | solution.py:448
  69.2 6.7 %collective-permute-start.21 = (bf16[2,64,1152]{2,1,0:T(8,128)(2,1)S(1)}, bf16[2,64,1152]{2,1,0:T(8,128)(2,1)S(1)}, u32[]{:S(2)}, u32[]{:S(2)}) collective-permute-start(bf16[2,64,1152]{2,1,0:T(8,128)(2,1)S(1)} %collective-permute-done.11.refs_2_), channel_id=1, source_target_pairs={{16,0},{32,16},{48,32},{0,48},{80,64},{96,80},{112,96},{64,112},{1... | collective-permute-start | bytes 884744 | tf_op jit(solution)/shard_map/ppermute | solution.py:442
  69.2 7.9 %collective-permute-start.22 = (bf16[2,64,1152]{2,1,0:T(8,128)(2,1)S(1)}, bf16[2,64,1152]{2,1,0:T(8,128)(2,1)S(1)}, u32[]{:S(2)}, u32[]{:S(2)}) collective-permute-start(bf16[2,64,1152]{2,1,0:T(8,128)(2,1)S(1)} %collective-permute-done.14.refs_7_), channel_id=1, source_target_pairs={{48,0},{0,16},{16,32},{32,48},{112,64},{64,80},{80,96},{96,112},{1... | collective-permute-start | bytes 884744 | tf_op jit(solution)/shard_map/ppermute | solution.py:442
  71.2 9.0 %collective-permute-start.23 = (bf16[2,64,1152]{2,1,0:T(8,128)(2,1)S(1)}, bf16[2,64,1152]{2,1,0:T(8,128)(2,1)S(1)}, u32[]{:S(2)}, u32[]{:S(2)}) collective-permute-start(bf16[2,64,1152]{2,1,0:T(8,128)(2,1)S(1)} %collective-permute-done.15.refs_10_), channel_id=1, source_target_pairs={{64,0},{80,16},{96,32},{112,48},{128,64},{144,80},{160,96},{176,11... | collective-permute-start | bytes 884744 | tf_op jit(solution)/shard_map/ppermute | solution.py:442
  75.9 6.7 %collective-permute-start.24 = (bf16[2,64,1152]{2,1,0:T(8,128)(2,1)S(1)}, bf16[2,64,1152]{2,1,0:T(8,128)(2,1)S(1)}, u32[]{:S(2)}, u32[]{:S(2)}) collective-permute-start(bf16[2,64,1152]{2,1,0:T(8,128)(2,1)S(1)} %collective-permute-done.18.refs_15_), channel_id=1, source_target_pairs={{192,0},{208,16},{224,32},{240,48},{0,64},{16,80},{32,96},{48,112}... | collective-permute-start | bytes 884744 | tf_op jit(solution)/shard_map/ppermute | solution.py:442
  75.9 7.3 %copy-start.19 = (bf16[2,64,1152]{2,1,0:T(8,128)(2,1)}, bf16[2,64,1152]{2,1,0:T(8,128)(2,1)S(1)}, u32[]{:S(2)}) copy-start(bf16[2,64,1152]{2,1,0:T(8,128)(2,1)S(1)} %collective-permute-done.21.refs_4_) | copy-start | bytes 884740
  75.9 18.8 %collective-permute-start.26 = (bf16[5,64,1024]{2,1,0:T(8,128)(2,1)}, bf16[5,64,1024]{2,1,0:T(8,128)(2,1)}, u32[]{:S(2)}, u32[]{:S(2)}) collective-permute-start(bf16[5,64,1024]{2,1,0:T(8,128)(2,1)} %collective-permute-done.9.refs_2_), channel_id=1, source_target_pairs={{0,1},{1,0},{2,3},{3,2},{4,5},{5,4},{6,7},{7,6},{8,9},{9,8},{10,11... | collective-permute-start | bytes 1966088 | tf_op jit(solution)/shard_map/ppermute | solution.py:451
  77.1 6.2 %copy-start.20 = (bf16[2,64,1152]{2,1,0:T(8,128)(2,1)}, bf16[2,64,1152]{2,1,0:T(8,128)(2,1)S(1)}, u32[]{:S(2)}) copy-start(bf16[2,64,1152]{2,1,0:T(8,128)(2,1)S(1)} %collective-permute-done.22.refs_5_) | copy-start | bytes 884740
  77.1 17.6 %collective-permute-start.20 = (bf16[5,64,1024]{2,1,0:T(8,128)(2,1)}, bf16[5,64,1024]{2,1,0:T(8,128)(2,1)}, u32[]{:S(2)}, u32[]{:S(2)}) collective-permute-start(bf16[5,64,1024]{2,1,0:T(8,128)(2,1)} %collective-permute-done.10.refs_6_), channel_id=1, source_target_pairs={{14,0},{15,1},{0,2},{1,3},{2,4},{3,5},{4,6},{5,7},{6,8},{7,9},{8,1... | collective-permute-start | bytes 1966088 | tf_op jit(solution)/shard_map/ppermute | solution.py:448
  80.2 3.1 %copy-start.21 = (bf16[2,64,1152]{2,1,0:T(8,128)(2,1)}, bf16[2,64,1152]{2,1,0:T(8,128)(2,1)S(1)}, u32[]{:S(2)}) copy-start(bf16[2,64,1152]{2,1,0:T(8,128)(2,1)S(1)} %collective-permute-done.23.refs_12_) | copy-start | bytes 884740
  80.2 14.5 %collective-permute-start.25 = (bf16[5,64,1024]{2,1,0:T(8,128)(2,1)}, bf16[5,64,1024]{2,1,0:T(8,128)(2,1)}, u32[]{:S(2)}, u32[]{:S(2)}) collective-permute-start(bf16[5,64,1024]{2,1,0:T(8,128)(2,1)} %collective-permute-done.refs_1_), channel_id=1, source_target_pairs={{0,1},{1,0},{2,3},{3,2},{4,5},{5,4},{6,7},{7,6},{8,9},{9,8},{10,11... | collective-permute-start | bytes 1966088 | tf_op jit(solution)/shard_map/ppermute | solution.py:451
  82.7 0.7 copy-start.22
  82.7 12.1 %collective-permute-start.27 = (bf16[5,64,1024]{2,1,0:T(8,128)(2,1)}, bf16[5,64,1024]{2,1,0:T(8,128)(2,1)}, u32[]{:S(2)}, u32[]{:S(2)}) collective-permute-start(bf16[5,64,1024]{2,1,0:T(8,128)(2,1)} %collective-permute-done.1.refs_7_), channel_id=1, source_target_pairs={{0,1},{1,0},{2,3},{3,2},{4,5},{5,4},{6,7},{7,6},{8,9},{9,8},{10,11... | collective-permute-start | bytes 1966088 | tf_op jit(solution)/shard_map/ppermute | solution.py:451
  82.7 12.0 %collective-permute-start.28 = (bf16[5,64,1024]{2,1,0:T(8,128)(2,1)}, bf16[5,64,1024]{2,1,0:T(8,128)(2,1)}, u32[]{:S(2)}, u32[]{:S(2)}) collective-permute-start(bf16[5,64,1024]{2,1,0:T(8,128)(2,1)} %collective-permute-done.10.refs_6_), channel_id=1, source_target_pairs={{0,1},{1,0},{2,3},{3,2},{4,5},{5,4},{6,7},{7,6},{8,9},{9,8},{10,11... | collective-permute-start | bytes 1966088 | tf_op jit(solution)/shard_map/ppermute | solution.py:451
  95.8 9.6 %collective-permute-start.29 = (bf16[3,64,1024]{2,1,0:T(8,128)(2,1)S(1)}, bf16[3,64,1024]{2,1,0:T(8,128)(2,1)S(1)}, u32[]{:S(2)}, u32[]{:S(2)}) collective-permute-start(bf16[3,64,1024]{2,1,0:T(8,128)(2,1)S(1)} %slice.14), channel_id=1, source_target_pairs={{2,0},{3,1},{4,2},{5,3},{6,4},{7,5},{8,6},{9,7},{10,8},{11,9},{12,... | collective-permute-start | bytes 1179656 | tf_op jit(solution)/shard_map/ppermute | solution.py:448
  97.3 8.1 %collective-permute-start.30 = (bf16[2,64,1024]{2,1,0:T(8,128)(2,1)S(1)}, bf16[2,64,1024]{2,1,0:T(8,128)(2,1)S(1)}, u32[]{:S(2)}, u32[]{:S(2)}) collective-permute-start(bf16[2,64,1024]{2,1,0:T(8,128)(2,1)S(1)} %slice.15), channel_id=1, source_target_pairs={{14,0},{15,1},{0,2},{1,3},{2,4},{3,5},{4,6},{5,7},{6,8},{7,9},{8,1... | collective-permute-start | bytes 786440 | tf_op jit(solution)/shard_map/ppermute | solution.py:448
  100.3 14.7 %collective-permute-start.31 = (bf16[5,64,1024]{2,1,0:T(8,128)(2,1)}, bf16[5,64,1024]{2,1,0:T(8,128)(2,1)S(1)}, u32[]{:S(2)}, u32[]{:S(2)}) collective-permute-start(bf16[5,64,1024]{2,1,0:T(8,128)(2,1)} %collective-permute-done.19.refs_3_), channel_id=1, source_target_pairs={{0,1},{1,0},{2,3},{3,2},{4,5},{5,4},{6,7},{7,6},{8,9},{9,8},{10,11... | collective-permute-start | bytes 1966088 | tf_op jit(solution)/shard_map/ppermute | solution.py:451
  100.3 14.7 %collective-permute-start.33 = (bf16[5,64,1024]{2,1,0:T(8,128)(2,1)}, bf16[5,64,1024]{2,1,0:T(8,128)(2,1)S(1)}, u32[]{:S(2)}, u32[]{:S(2)}) collective-permute-start(bf16[5,64,1024]{2,1,0:T(8,128)(2,1)} %collective-permute-done.20.refs_5_), channel_id=1, source_target_pairs={{0,1},{1,0},{2,3},{3,2},{4,5},{5,4},{6,7},{7,6},{8,9},{9,8},{10,11... | collective-permute-start | bytes 1966088 | tf_op jit(solution)/shard_map/ppermute | solution.py:451
  105.4 3.7 %copy-start.2 = (bf16[5,64,1024]{2,1,0:T(8,128)(2,1)}, bf16[5,64,1024]{2,1,0:T(8,128)(2,1)S(1)}, u32[]{:S(2)}) copy-start(bf16[5,64,1024]{2,1,0:T(8,128)(2,1)S(1)} %constant_dynamic-update-slice_fusion.refs_4_) | copy-start | bytes 1966084
  105.4 9.6 %collective-permute-start.32 = (bf16[5,64,1024]{2,1,0:T(8,128)(2,1)S(1)}, bf16[5,64,1024]{2,1,0:T(8,128)(2,1)S(1)}, u32[]{:S(2)}, u32[]{:S(2)}) collective-permute-start(bf16[5,64,1024]{2,1,0:T(8,128)(2,1)S(1)} %constant_dynamic-update-slice_fusion.refs_4_), channel_id=1, source_target_pairs={{0,1},{1,0},{2,3},{3,2},{4,5},{5,4},{6,7},{7,6},{8,9},{9,8},{10,11... | collective-permute-start | bytes 1966088 | tf_op jit(solution)/shard_map/ppermute | solution.py:451
  115.0 0.9 copy-start.7
  115.0 1.1 copy-start.8
  115.0 1.2 copy-start.9
  136.0 3.1 %collective-permute-start.34 = (bf16[16,8,16,256]{3,2,1,0:T(8,128)(2,1)}, bf16[16,8,16,256]{3,2,1,0:T(8,128)(2,1)S(1)}, u32[]{:S(2)}, u32[]{:S(2)}) collective-permute-start(bf16[16,8,16,256]{3,2,1,0:T(8,128)(2,1)} %get-tuple-element.126), channel_id=1, source_target_pairs={{0,1},{1,0},{2,3},{3,2},{4,5},{5,4},{6,7},{7,6},{8,9},{9,8},{10,11... | collective-permute-start | bytes 3145736 | tf_op jit(solution)/shard_map/ppermute | solution.py:591
  140.6 40.9 %copy-start.25 = (f32[4,1,128]{2,1,0:T(1,128)S(1)}, f32[4,1,128]{2,1,0:T(1,128)}, u32[]{:S(2)}) copy-start(f32[4,1,128]{2,1,0:T(1,128)} %get-tuple-element.123) | copy-start | bytes 6148
  175.8 12.1 %all-to-all-start.2 = ((bf16[16,16,256]{2,1,0:T(8,128)(2,1)}), bf16[16,16,256]{2,1,0:T(8,128)(2,1)S(1)}, u32[]{:S(2)}, u32[]{:S(2)}) async-start(bf16[16,16,256]{2,1,0:T(8,128)(2,1)} %broadcast_in_dim.30), calls=%async_computation.2 | async-start | bytes 262144 | tf_op jit(solution)/shard_map/all_to_all | solution.py:598
  188.0 0.7 copy-start.10

commit v7 on v5

--- a/solution.py
+++ b/solution.py
@@ -381,7 +381,7 @@
             jax.ShapeDtypeStruct(shape, BF),
             jax.ShapeDtypeStruct(shape, BF),
         ],
-        compiler_params=pltpu.CompilerParams(vmem_limit_bytes=VMEM_BYTES),
+        compiler_params=pltpu.CompilerParams(vmem_limit_bytes=42 * 1024 * 1024),
         name="attention",
     )(
         counts,
@@ -514,9 +514,6 @@
     )
 
     arrived = lax.ppermute(other, "loader", [(i, i ^ 1) for i in range(loaders)])
-    back = lax.dot_general(slopes, query_weight, (((1,), (1,)), ((), ())), preferred_element_type=F32)
-    row_grads = (error.reshape(-1)[:, None] * self_weight + back).astype(BF)
-    mine, row_grads = lax.optimization_barrier((mine, row_grads))
     pieces = (mine.astype(F32) + arrived.astype(F32)).astype(BF)
     pieces = lax.all_to_all(pieces, "user", 0, 0, tiled=True)
     pieces = jnp.sum(pieces.astype(F32), 0).astype(BF)
@@ -528,6 +525,8 @@
     )
     query_grad = assemble(pieces, side)
 
+    back = lax.dot_general(slopes, query_weight, (((1,), (1,)), ((), ())), preferred_element_type=F32)
+    row_grads = (error.reshape(-1)[:, None] * self_weight + back).astype(BF)
     return (scores[:, 0], row_grads.reshape(nblocks, rows, width), query_grad)
 
 

time: 157 us -> 161 us (1.025)
  blocking collectives: 46.8 us -> 34.8 us
  local copies, waits for them, and re-layouts: 3.32 us -> 9.82 us
  starting transfers between devices: 27.5 us -> 33.1 us
  waiting for transfers between devices: 25.1 us -> 30.7 us
    all_to_all x1 -> x0, blocking collectives: 12 us -> none  [body(): lax.all_to_all(jnp.broadcast_to(piece[None], (users,) + piece.shape), 'us...]
    all_to_all x0 -> x1, starting transfers between devices: none -> 5.7 us  [body(): lax.all_to_all(jnp.broadcast_to(piece[None], (users,) + piece.shape), 'us...]
    unnamed x16 -> x32, local copies, waits for them, and re-layouts: 0.79 us -> 6.42 us
    all_to_all x0 -> x1, waiting for transfers between devices: none -> 2.94 us  [body(): lax.all_to_all(jnp.broadcast_to(piece[None], (users,) + piece.shape), 'us...]
    ppermute x1, waiting for transfers between devices: 0.01 us -> 2.41 us  [body(): lax.ppermute(other, 'loader', [(i, i ^ 1) for i in range(loaders)])]
  transfers between devices with their start and end apart: 20 -> 21, of which waited for: 6 -> 8; matrix products, arithmetic and copies ran while one was open for 8% -> 8% of each run, Pallas kernels for 4% -> 4%
where the time goes in v7:
time: 161 us
  blocking collectives  34.8 us (22%)
  starting transfers between devices  33.1 us (21%)
  waiting for transfers between devices  30.7 us (19%)
  Pallas kernels  26.8 us (17%)
  between operations  15 us (9%)
  local copies, waits for them, and re-layouts  9.82 us (6%)
  matrix products  5.73 us (4%)
  other arithmetic  4.84 us (3%)
    ppermute x18, starting transfers between devices, shift(): return lax.ppermute(array, 'user', moves)  27.1 us
    all_to_all x1, blocking collectives, body(): pieces = lax.all_to_all(pieces, 'user', 0, 0, tiled=True)  22.3 us
    pallas_call x1, Pallas kernels, attention(): pl.pallas_call(attention_kernel, grid_spec=pltpu.PrefetchScalarGridSpec(n...  17.1 us
    all_gather x1, waiting for transfers between devices, body(): lax.all_gather(join(mix_weight, out_weight), 'loader', axis=0, tiled=True)  16.5 us
    all_to_all x1, blocking collectives, body(): lax.all_to_all(pieces, 'loader', 0, 0, axis_index_groups=groups, tiled=True)  12.5 us
    ppermute x18, waiting for transfers between devices, shift(): return lax.ppermute(array, 'user', moves)  8.77 us
    unnamed x32, local copies, waits for them, and re-layouts  6.42 us
    pallas_call x1, Pallas kernels, prepare(): pl.pallas_call(functools.partial(prepare_kernel, nblocks), grid_spec=pltp...  5.94 us
  transfers between devices with their start and end apart: 21, of which 8 were waited for; matrix products, arithmetic and copies ran while one was open for 8% of the time, Pallas kernels for 4%

profile of v7, /device:TPU:2, one launch (start us, length us, event | category | flops | bytes accessed | tf_op | source)
XLA Modules:
  0.0 160.7 jit_solution(15703675039209571762)
XLA Ops:
  7.2 0.0 copy-start
  7.2 0.0 all-gather.2.cloned.1.call-start
  7.2 2.1 %join.1 = bf16[64,5120]{1,0:T(8,128)(2,1)} custom-call(bf16[64,4096]{1,0:T(8,128)(2,1)} %left.1, bf16[64,1024]{1,0:T(8,128)(2,1)} %right.1), custom_call_target="tpu_custom_call" | custom-call | tf_op jit(solution)/shard_map/join/pallas_call | solution.py:427
  9.3 0.0 all-gather.2.cloned.1.call-update
  9.3 0.0 copy-start.9
  10.1 0.7 convert_bitcast_fusion
  10.7 0.1 broadcast_in_dim.29
  10.8 1.1 concatenate.3
  11.9 2.2 %collective-permute-start.1 = (bf16[64,1152]{1,0:T(8,128)(2,1)S(1)}, bf16[64,1152]{1,0:T(8,128)(2,1)S(1)}, u32[]{:S(2)}, u32[]{:S(2)}) collective-permute-start(bf16[64,1152]{1,0:T(8,128)(2,1)S(1)} %get-tuple-element.25), channel_id=1, source_target_pairs={{128,0},{144,16},{160,32},{176,48},{192,64},{208,80},{224,96},{240... | collective-permute-start | bytes 442376 | tf_op jit(solution)/shard_map/ppermute | solution.py:406
  14.2 1.6 %collective-permute-start.2 = (bf16[64,1152]{1,0:T(8,128)(2,1)S(1)}, bf16[64,1152]{1,0:T(8,128)(2,1)S(1)}, u32[]{:S(2)}, u32[]{:S(2)}) collective-permute-start(bf16[64,1152]{1,0:T(8,128)(2,1)S(1)} %get-tuple-element.25), channel_id=1, source_target_pairs={{192,0},{208,16},{224,32},{240,48},{0,64},{16,80},{32,96},{48,112}... | collective-permute-start | bytes 442376 | tf_op jit(solution)/shard_map/ppermute | solution.py:406
  15.8 1.6 collective-permute-start.10
  17.4 1.1 collective-permute-start.9
  18.4 1.0 collective-permute-start.11
  19.4 2.2 %collective-permute-start = (bf16[64,1152]{1,0:T(8,128)(2,1)S(1)}, bf16[64,1152]{1,0:T(8,128)(2,1)S(1)}, u32[]{:S(2)}, u32[]{:S(2)}) collective-permute-start(bf16[64,1152]{1,0:T(8,128)(2,1)S(1)} %get-tuple-element.25), channel_id=1, source_target_pairs={{64,0},{80,16},{96,32},{112,48},{128,64},{144,80},{160,96},{176,11... | collective-permute-start | bytes 442376 | tf_op jit(solution)/shard_map/ppermute | solution.py:406
  21.6 0.8 collective-permute-done.2
  22.4 1.7 %collective-permute-start.6 = (bf16[2,64,1152]{2,1,0:T(8,128)(2,1)S(1)}, bf16[2,64,1152]{2,1,0:T(8,128)(2,1)S(1)}, u32[]{:S(2)}, u32[]{:S(2)}) collective-permute-start(bf16[2,64,1152]{2,1,0:T(8,128)(2,1)S(1)} %pad_maximum_fusion.1.refs_1_), channel_id=1, source_target_pairs={{48,0},{0,16},{16,32},{32,48},{112,64},{64,80},{80,96},{96,112},{1... | collective-permute-start | bytes 884744 | tf_op jit(solution)/shard_map/ppermute | solution.py:406
  24.1 0.8 collective-permute-done
  24.9 3.0 %collective-permute-start.4 = (bf16[2,64,1152]{2,1,0:T(8,128)(2,1)S(1)}, bf16[2,64,1152]{2,1,0:T(8,128)(2,1)S(1)}, u32[]{:S(2)}, u32[]{:S(2)}) collective-permute-start(bf16[2,64,1152]{2,1,0:T(8,128)(2,1)S(1)} %pad_maximum_fusion.1.refs_1_), channel_id=1, source_target_pairs={{16,0},{32,16},{48,32},{0,48},{80,64},{96,80},{112,96},{64,112},{1... | collective-permute-start | bytes 884744 | tf_op jit(solution)/shard_map/ppermute | solution.py:406
  27.9 0.8 pad_maximum_fusion.refs_0_
  28.7 0.0 collective-permute-done.10
  28.7 0.0 collective-permute-start.8
  28.7 0.0 collective-permute-done.11
  28.7 3.2 %collective-permute-start.3 = (bf16[2,64,1152]{2,1,0:T(8,128)(2,1)}, bf16[2,64,1152]{2,1,0:T(8,128)(2,1)}, u32[]{:S(2)}, u32[]{:S(2)}) collective-permute-start(bf16[2,64,1152]{2,1,0:T(8,128)(2,1)} %pad_maximum_fusion.refs_0_), channel_id=1, source_target_pairs={{16,0},{32,16},{48,32},{0,48},{80,64},{96,80},{112,96},{64,112},{1... | collective-permute-start | bytes 884744 | tf_op jit(solution)/shard_map/ppermute | solution.py:406
  31.9 0.7 pad_maximum_fusion.3.refs_9_
  32.7 2.0 %collective-permute-start.15 = (bf16[2,64,1152]{2,1,0:T(8,128)(2,1)}, bf16[2,64,1152]{2,1,0:T(8,128)(2,1)}, u32[]{:S(2)}, u32[]{:S(2)}) collective-permute-start(bf16[2,64,1152]{2,1,0:T(8,128)(2,1)} %pad_maximum_fusion.3.refs_9_), channel_id=1, source_target_pairs={{192,0},{208,16},{224,32},{240,48},{0,64},{16,80},{32,96},{48,112}... | collective-permute-start | bytes 884744 | tf_op jit(solution)/shard_map/ppermute | solution.py:406
  34.7 0.8 pad_maximum_fusion.2.refs_8_
  35.4 0.0 collective-permute-done.6.refs_7_
  35.4 0.0 collective-permute-start.13
  35.5 0.0 collective-permute-done.4.refs_3_
  35.5 0.7 copy-done.13
  36.2 2.7 %collective-permute-start.12 = (bf16[2,64,1152]{2,1,0:T(8,128)(2,1)}, bf16[2,64,1152]{2,1,0:T(8,128)(2,1)}, u32[]{:S(2)}, u32[]{:S(2)}) collective-permute-start(bf16[2,64,1152]{2,1,0:T(8,128)(2,1)} %pad_maximum_fusion.2.refs_8_), channel_id=1, source_target_pairs={{64,0},{80,16},{96,32},{112,48},{128,64},{144,80},{160,96},{176,11... | collective-permute-start | bytes 884744 | tf_op jit(solution)/shard_map/ppermute | solution.py:406
  38.9 2.3 %convolution_convert_fusion = bf16[512,1024]{1,0:T(8,128)(2,1)} fusion(bf16[512,1024]{1,0:T(8,128)(2,1)S(1)} %bitcast.56, bf16[1024,1024]{1,0:T(8,128)(2,1)S(1)} %copy-done), kind=kOutput, calls=%fused_computation.3 | convolution fusion | flops 1074266112 | bytes 4194304 | tf_op jit(solution)/shard_map/dot_general | solution.py:488
  41.2 0.5 multiply_add_fusion
  41.7 0.0 collective-permute-done.8.refs_6_
  41.7 0.4 collective-permute-start.7
  42.1 3.1 %collective-permute-start.5 = (bf16[2,64,1152]{2,1,0:T(8,128)(2,1)}, bf16[2,64,1152]{2,1,0:T(8,128)(2,1)}, u32[]{:S(2)}, u32[]{:S(2)}) collective-permute-start(bf16[2,64,1152]{2,1,0:T(8,128)(2,1)} %collective-permute-done.3.refs_2_), channel_id=1, source_target_pairs={{16,0},{32,16},{48,32},{0,48},{80,64},{96,80},{112,96},{64,112},{1... | collective-permute-start | bytes 884744 | tf_op jit(solution)/shard_map/ppermute | solution.py:406
  45.2 0.0 collective-permute-done.13.refs_11_
  45.2 1.3 collective-permute-start.16
  46.5 2.5 %collective-permute-done.12.refs_10_ = bf16[2,64,1152]{2,1,0:T(8,128)(2,1)} collective-permute-done((bf16[2,64,1152]{2,1,0:T(8,128)(2,1)}, bf16[2,64,1152]{2,1,0:T(8,128)(2,1)}, u32[]{:S(2)}, u32[]{:S(2)}) %collective-permute-start.12) | collective-permute-done | bytes 294944 | tf_op jit(solution)/shard_map/ppermute | solution.py:406
  49.1 0.0 collective-permute-start.14
  49.1 0.3 multiply_reduce_fusion
  49.3 1.6 copy.17
  50.9 0.6 multiply_add_fusion.1.place_a
  51.5 1.9 %collective-permute-done.16.refs_13_ = bf16[2,64,1152]{2,1,0:T(8,128)(2,1)} collective-permute-done((bf16[2,64,1152]{2,1,0:T(8,128)(2,1)}, bf16[2,64,1152]{2,1,0:T(8,128)(2,1)}, u32[]{:S(2)}, u32[]{:S(2)}) %collective-permute-start.16) | collective-permute-done | bytes 294944 | tf_op jit(solution)/shard_map/ppermute | solution.py:406
  53.4 2.7 %collective-permute-done.14.refs_12_ = bf16[2,64,1152]{2,1,0:T(8,128)(2,1)} collective-permute-done((bf16[2,64,1152]{2,1,0:T(8,128)(2,1)}, bf16[2,64,1152]{2,1,0:T(8,128)(2,1)}, u32[]{:S(2)}, u32[]{:S(2)}) %collective-permute-start.14) | collective-permute-done | bytes 294944 | tf_op jit(solution)/shard_map/ppermute | solution.py:406
  56.1 5.9 %prepare.1 = (f32[512,1024]{1,0:T(8,128)}, bf16[512,1024]{1,0:T(8,128)(2,1)}, f32[512,128]{1,0:T(8,128)}) custom-call(s32[4]{0:T(128)} %multiply_add_fusion.1.place_a, s32[4]{0:T(128)} %get-tuple-element.19.place_b, bf16[2,64,1152]{2,1,0:T(8,128)(2,1)} %pad_maximum_fusion.refs_0_, bf16[2,64,1152]{2,1,0:T(8,128)(2,1)} %copy-done.10, ...), custom_call_target="tpu_custom_call" | custom-call | tf_op jit(solution)/shard_map/prepare/pallas_call | solution.py:84
  62.1 16.5 %all-gather.2.cloned.1.call-done.weights = bf16[1024,5120]{1,0:T(8,128)(2,1)} async-done(((bf16[64,5120]{1,0:T(8,128)(2,1)}), bf16[1024,5120]{1,0:T(8,128)(2,1)}) %all-gather.2.cloned.1.call-update) | async-done | bytes 10485776 | tf_op jit(solution)/shard_map/all_gather | solution.py:472
  78.6 1.6 copy-done.1
  80.2 1.2 copy-done.2
  81.4 1.2 copy-done.3
  82.7 0.9 copy-done.4
  83.6 17.1 %attention.1 = (f32[4,1,128]{2,1,0:T(1,128)}, f32[4,1,128]{2,1,0:T(1,128)S(1)}, bf16[512,1024]{1,0:T(8,128)(2,1)S(1)}, bf16[16,8,16,256]{3,2,1,0:T(8,128)(2,1)S(1)}, bf16[16,8,16,256]{3,2,1,0:T(8,128)(2,1)S(1)}) custom-call(s32[4]{0:T(128)S(1)} %copy-done.7, s32[1]{0:T(128)} %bitcast.core, bf16[512,1024]{1,0:T(8,128)(2,1)S(1)} %copy-done.3, ...), custom_call_target="tpu_custom_call" | custom-call | tf_op jit(solution)/shard_map/attention/pallas_call | solution.py:336
  100.7 0.3 collective-permute-start.18
  101.1 2.4 %collective-permute-done.18 = bf16[16,8,16,256]{3,2,1,0:T(8,128)(2,1)S(1)} collective-permute-done((bf16[16,8,16,256]{3,2,1,0:T(8,128)(2,1)S(1)}, bf16[16,8,16,256]{3,2,1,0:T(8,128)(2,1)S(1)}, u32[]{:S(2)}, u32[]{:S(2)}) %collective-permute-start.18) | collective-permute-done | bytes 1048608 | tf_op jit(solution)/shard_map/ppermute | solution.py:516
  103.5 0.3 add_convert_fusion
  103.8 22.3 %all_to_all.15 = bf16[16,8,16,256]{3,2,1,0:T(8,128)(2,1)S(1)} all-to-all(bf16[16,8,16,256]{3,2,1,0:T(8,128)(2,1)S(1)} %add_convert_fusion), channel_id=1, replica_groups=mesh['user'=16,'loader'=16] {'user'}, dimensions={0} | all-to-all | bytes 2097152 | tf_op jit(solution)/shard_map/all_to_all | solution.py:518
  126.2 0.1 reduce_sum.34
  126.3 12.5 %all_to_all.16 = bf16[8,16,256]{2,1,0:T(8,128)(2,1)S(1)} all-to-all(bf16[8,16,256]{2,1,0:T(8,128)(2,1)S(1)} %reduce_sum.34), channel_id=1, replica_groups={{0,2,4,6,8,10,12,14},{1,3,5,7,9,11,13,15},{16,18,20,22,24,26,28,30},{17..., dimensions={0} | all-to-all | bytes 131072 | tf_op jit(solution)/shard_map/all_to_all | solution.py:521
  138.8 0.7 broadcast_in_dim.34
  139.5 5.7 %all-to-all-start.2 = ((bf16[16,16,256]{2,1,0:T(8,128)(2,1)}), bf16[16,16,256]{2,1,0:T(8,128)(2,1)S(1)}, u32[]{:S(2)}, u32[]{:S(2)}) async-start(bf16[16,16,256]{2,1,0:T(8,128)(2,1)} %broadcast_in_dim.34), calls=%async_computation.2 | async-start | bytes 262144 | tf_op jit(solution)/shard_map/all_to_all | solution.py:523
  145.2 3.5 %add_convert_fusion.1 = bf16[512,1024]{1,0:T(8,128)(2,1)} fusion(bf16[512,1024]{1,0:T(8,128)(2,1)} %copy-done.8, bf16[1024,1024]{1,0:T(8,128)(2,1)S(1)} %copy-done, f32[1024]{0:T(1024)S(1)} %copy-done.14, f32[512]{0:T(512)S(1)} %bitcast.54), kind=kOutput, calls=%fused_computation.1 | convolution fusion | flops 1075314688 | bytes 4200448 | tf_op jit(solution)/shard_map/dot_general | solution.py:528
  148.7 2.9 %all-to-all-done.2.pieces = bf16[16,16,256]{2,1,0:T(8,128)(2,1)S(1)} async-done(((bf16[16,16,256]{2,1,0:T(8,128)(2,1)}), bf16[16,16,256]{2,1,0:T(8,128)(2,1)S(1)}, u32[]{:S(2)}, u32[]{:S(2)}) %all-to-all-start.2) | async-done | bytes 131104 | tf_op jit(solution)/shard_map/all_to_all | solution.py:523
  151.6 0.6 copy-done.11
  152.2 1.6 %assemble.1 = f32[64,1024]{1,0:T(8,128)} custom-call(bf16[16,16,256]{2,1,0:T(8,128)(2,1)} %copy-done.11), custom_call_target="tpu_custom_call" | custom-call | tf_op jit(solution)/shard_map/assemble/pallas_call | solution.py:445
  (36 shorter events, 0.2 us)
Async XLA Ops:
  7.2 31.8 %copy-start = (bf16[1024,1024]{1,0:T(8,128)(2,1)S(1)}, bf16[1024,1024]{1,0:T(8,128)(2,1)}, u32[]{:S(2)}) copy-start(bf16[1024,1024]{1,0:T(8,128)(2,1)} %param.19) | copy-start | bytes 6291460
  7.2 71.4 %all-gather.2.cloned.1.call-start = ((), (), s32[]{:S(2)}) async-start(), calls=%async_computation.3 | async-start | bytes 11141120 | tf_op jit(solution)/shard_map/all_gather | solution.py:472
  9.3 29.6 %copy-start.9 = (bf16[4,128,1024]{2,1,0:T(8,128)(2,1)S(1)}, bf16[4,128,1024]{2,1,0:T(8,128)(2,1)}, u32[]{:S(2)}) copy-start(bf16[4,128,1024]{2,1,0:T(8,128)(2,1)} %param.22) | copy-start | bytes 3145732
  11.9 7.4 %collective-permute-start.1 = (bf16[64,1152]{1,0:T(8,128)(2,1)S(1)}, bf16[64,1152]{1,0:T(8,128)(2,1)S(1)}, u32[]{:S(2)}, u32[]{:S(2)}) collective-permute-start(bf16[64,1152]{1,0:T(8,128)(2,1)S(1)} %get-tuple-element.25), channel_id=1, source_target_pairs={{128,0},{144,16},{160,32},{176,48},{192,64},{208,80},{224,96},{240... | collective-permute-start | bytes 442376 | tf_op jit(solution)/shard_map/ppermute | solution.py:406
  14.2 8.2 %collective-permute-start.2 = (bf16[64,1152]{1,0:T(8,128)(2,1)S(1)}, bf16[64,1152]{1,0:T(8,128)(2,1)S(1)}, u32[]{:S(2)}, u32[]{:S(2)}) collective-permute-start(bf16[64,1152]{1,0:T(8,128)(2,1)S(1)} %get-tuple-element.25), channel_id=1, source_target_pairs={{192,0},{208,16},{224,32},{240,48},{0,64},{16,80},{32,96},{48,112}... | collective-permute-start | bytes 442376 | tf_op jit(solution)/shard_map/ppermute | solution.py:406
  15.8 12.9 %collective-permute-start.10 = (bf16[64,1152]{1,0:T(8,128)(2,1)S(1)}, bf16[64,1152]{1,0:T(8,128)(2,1)S(1)}, u32[]{:S(2)}, u32[]{:S(2)}) collective-permute-start(bf16[64,1152]{1,0:T(8,128)(2,1)S(1)} %get-tuple-element.24), channel_id=1, source_target_pairs={{32,0},{48,16},{0,32},{16,48},{96,64},{112,80},{64,96},{80,112},{1... | collective-permute-start | bytes 442376 | tf_op jit(solution)/shard_map/ppermute | solution.py:406
  17.4 15.3 %collective-permute-start.9 = (bf16[64,1152]{1,0:T(8,128)(2,1)S(1)}, bf16[64,1152]{1,0:T(8,128)(2,1)S(1)}, u32[]{:S(2)}, u32[]{:S(2)}) collective-permute-start(bf16[64,1152]{1,0:T(8,128)(2,1)S(1)} %get-tuple-element.24), channel_id=1, source_target_pairs={{16,0},{32,16},{48,32},{0,48},{80,64},{96,80},{112,96},{64,112},{1... | collective-permute-start | bytes 442376 | tf_op jit(solution)/shard_map/ppermute | solution.py:406
  18.4 10.3 %collective-permute-start.11 = (bf16[64,1152]{1,0:T(8,128)(2,1)S(1)}, bf16[64,1152]{1,0:T(8,128)(2,1)S(1)}, u32[]{:S(2)}, u32[]{:S(2)}) collective-permute-start(bf16[64,1152]{1,0:T(8,128)(2,1)S(1)} %get-tuple-element.24), channel_id=1, source_target_pairs={{48,0},{0,16},{16,32},{32,48},{112,64},{64,80},{80,96},{96,112},{1... | collective-permute-start | bytes 442376 | tf_op jit(solution)/shard_map/ppermute | solution.py:406
  19.4 5.5 %collective-permute-start = (bf16[64,1152]{1,0:T(8,128)(2,1)S(1)}, bf16[64,1152]{1,0:T(8,128)(2,1)S(1)}, u32[]{:S(2)}, u32[]{:S(2)}) collective-permute-start(bf16[64,1152]{1,0:T(8,128)(2,1)S(1)} %get-tuple-element.25), channel_id=1, source_target_pairs={{64,0},{80,16},{96,32},{112,48},{128,64},{144,80},{160,96},{176,11... | collective-permute-start | bytes 442376 | tf_op jit(solution)/shard_map/ppermute | solution.py:406
  22.4 18.8 %copy-start.10 = (bf16[2,64,1152]{2,1,0:T(8,128)(2,1)}, bf16[2,64,1152]{2,1,0:T(8,128)(2,1)S(1)}, u32[]{:S(2)}) copy-start(bf16[2,64,1152]{2,1,0:T(8,128)(2,1)S(1)} %pad_maximum_fusion.1.refs_1_) | copy-start | bytes 884740
  22.4 13.0 %collective-permute-start.6 = (bf16[2,64,1152]{2,1,0:T(8,128)(2,1)S(1)}, bf16[2,64,1152]{2,1,0:T(8,128)(2,1)S(1)}, u32[]{:S(2)}, u32[]{:S(2)}) collective-permute-start(bf16[2,64,1152]{2,1,0:T(8,128)(2,1)S(1)} %pad_maximum_fusion.1.refs_1_), channel_id=1, source_target_pairs={{48,0},{0,16},{16,32},{32,48},{112,64},{64,80},{80,96},{96,112},{1... | collective-permute-start | bytes 884744 | tf_op jit(solution)/shard_map/ppermute | solution.py:406
  24.9 10.6 %collective-permute-start.4 = (bf16[2,64,1152]{2,1,0:T(8,128)(2,1)S(1)}, bf16[2,64,1152]{2,1,0:T(8,128)(2,1)S(1)}, u32[]{:S(2)}, u32[]{:S(2)}) collective-permute-start(bf16[2,64,1152]{2,1,0:T(8,128)(2,1)S(1)} %pad_maximum_fusion.1.refs_1_), channel_id=1, source_target_pairs={{16,0},{32,16},{48,32},{0,48},{80,64},{96,80},{112,96},{64,112},{1... | collective-permute-start | bytes 884744 | tf_op jit(solution)/shard_map/ppermute | solution.py:406
  28.7 13.0 %collective-permute-start.8 = (bf16[2,64,1152]{2,1,0:T(8,128)(2,1)}, bf16[2,64,1152]{2,1,0:T(8,128)(2,1)}, u32[]{:S(2)}, u32[]{:S(2)}) collective-permute-start(bf16[2,64,1152]{2,1,0:T(8,128)(2,1)} %pad_maximum_fusion.refs_0_), channel_id=1, source_target_pairs={{48,0},{0,16},{16,32},{32,48},{112,64},{64,80},{80,96},{96,112},{1... | collective-permute-start | bytes 884744 | tf_op jit(solution)/shard_map/ppermute | solution.py:406
  28.7 13.0 %collective-permute-start.3 = (bf16[2,64,1152]{2,1,0:T(8,128)(2,1)}, bf16[2,64,1152]{2,1,0:T(8,128)(2,1)}, u32[]{:S(2)}, u32[]{:S(2)}) collective-permute-start(bf16[2,64,1152]{2,1,0:T(8,128)(2,1)} %pad_maximum_fusion.refs_0_), channel_id=1, source_target_pairs={{16,0},{32,16},{48,32},{0,48},{80,64},{96,80},{112,96},{64,112},{1... | collective-permute-start | bytes 884744 | tf_op jit(solution)/shard_map/ppermute | solution.py:406
  32.7 9.4 %collective-permute-start.15 = (bf16[2,64,1152]{2,1,0:T(8,128)(2,1)}, bf16[2,64,1152]{2,1,0:T(8,128)(2,1)}, u32[]{:S(2)}, u32[]{:S(2)}) collective-permute-start(bf16[2,64,1152]{2,1,0:T(8,128)(2,1)} %pad_maximum_fusion.3.refs_9_), channel_id=1, source_target_pairs={{192,0},{208,16},{224,32},{240,48},{0,64},{16,80},{32,96},{48,112}... | collective-permute-start | bytes 884744 | tf_op jit(solution)/shard_map/ppermute | solution.py:406
  35.4 20.7 %copy-start.12 = (bf16[2,64,1152]{2,1,0:T(8,128)(2,1)}, bf16[2,64,1152]{2,1,0:T(8,128)(2,1)S(1)}, u32[]{:S(2)}) copy-start(bf16[2,64,1152]{2,1,0:T(8,128)(2,1)S(1)} %collective-permute-done.6.refs_7_) | copy-start | bytes 884740
  35.4 9.8 %collective-permute-start.13 = (bf16[2,64,1152]{2,1,0:T(8,128)(2,1)}, bf16[2,64,1152]{2,1,0:T(8,128)(2,1)}, u32[]{:S(2)}, u32[]{:S(2)}) collective-permute-start(bf16[2,64,1152]{2,1,0:T(8,128)(2,1)} %pad_maximum_fusion.3.refs_9_), channel_id=1, source_target_pairs={{64,0},{80,16},{96,32},{112,48},{128,64},{144,80},{160,96},{176,11... | collective-permute-start | bytes 884744 | tf_op jit(solution)/shard_map/ppermute | solution.py:406
  35.5 0.8 copy-start.13
  36.2 12.8 %collective-permute-start.12 = (bf16[2,64,1152]{2,1,0:T(8,128)(2,1)}, bf16[2,64,1152]{2,1,0:T(8,128)(2,1)}, u32[]{:S(2)}, u32[]{:S(2)}) collective-permute-start(bf16[2,64,1152]{2,1,0:T(8,128)(2,1)} %pad_maximum_fusion.2.refs_8_), channel_id=1, source_target_pairs={{64,0},{80,16},{96,32},{112,48},{128,64},{144,80},{160,96},{176,11... | collective-permute-start | bytes 884744 | tf_op jit(solution)/shard_map/ppermute | solution.py:406
  38.9 2.3 %copy-start.15 = (s32[4,1]{0,1:T(1,128)S(1)}, s32[4,1]{0,1:T(1,128)}, u32[]{:S(2)}) copy-start(s32[4,1]{0,1:T(1,128)} %param.23) | copy-start | bytes 52
  38.9 10.1 %copy-start.14 = (f32[1024]{0:T(1024)S(1)}, f32[1024]{0:T(1024)}, u32[]{:S(2)}) copy-start(f32[1024]{0:T(1024)} %param.21) | copy-start | bytes 12292
  41.7 9.8 %collective-permute-start.17 = (bf16[2,64,1152]{2,1,0:T(8,128)(2,1)}, bf16[2,64,1152]{2,1,0:T(8,128)(2,1)}, u32[]{:S(2)}, u32[]{:S(2)}) collective-permute-start(bf16[2,64,1152]{2,1,0:T(8,128)(2,1)} %pad_maximum_fusion.2.refs_8_), channel_id=1, source_target_pairs={{192,0},{208,16},{224,32},{240,48},{0,64},{16,80},{32,96},{48,112}... | collective-permute-start | bytes 884744 | tf_op jit(solution)/shard_map/ppermute | solution.py:406
  41.7 9.8 %collective-permute-start.7 = (bf16[2,64,1152]{2,1,0:T(8,128)(2,1)S(1)}, bf16[2,64,1152]{2,1,0:T(8,128)(2,1)}, u32[]{:S(2)}, u32[]{:S(2)}) collective-permute-start(bf16[2,64,1152]{2,1,0:T(8,128)(2,1)S(1)} %collective-permute-done.6.refs_7_), channel_id=1, source_target_pairs={{48,0},{0,16},{16,32},{32,48},{112,64},{64,80},{80,96},{96,112},{1... | collective-permute-start | bytes 884744 | tf_op jit(solution)/shard_map/ppermute | solution.py:406
  42.1 9.4 %collective-permute-start.5 = (bf16[2,64,1152]{2,1,0:T(8,128)(2,1)}, bf16[2,64,1152]{2,1,0:T(8,128)(2,1)}, u32[]{:S(2)}, u32[]{:S(2)}) collective-permute-start(bf16[2,64,1152]{2,1,0:T(8,128)(2,1)} %collective-permute-done.3.refs_2_), channel_id=1, source_target_pairs={{16,0},{32,16},{48,32},{0,48},{80,64},{96,80},{112,96},{64,112},{1... | collective-permute-start | bytes 884744 | tf_op jit(solution)/shard_map/ppermute | solution.py:406
  45.2 8.2 %collective-permute-start.16 = (bf16[2,64,1152]{2,1,0:T(8,128)(2,1)}, bf16[2,64,1152]{2,1,0:T(8,128)(2,1)}, u32[]{:S(2)}, u32[]{:S(2)}) collective-permute-start(bf16[2,64,1152]{2,1,0:T(8,128)(2,1)} %collective-permute-done.15.refs_15_), channel_id=1, source_target_pairs={{192,0},{208,16},{224,32},{240,48},{0,64},{16,80},{32,96},{48,112}... | collective-permute-start | bytes 884744 | tf_op jit(solution)/shard_map/ppermute | solution.py:406
  49.1 7.0 %collective-permute-start.14 = (bf16[2,64,1152]{2,1,0:T(8,128)(2,1)}, bf16[2,64,1152]{2,1,0:T(8,128)(2,1)}, u32[]{:S(2)}, u32[]{:S(2)}) collective-permute-start(bf16[2,64,1152]{2,1,0:T(8,128)(2,1)} %collective-permute-done.12.refs_10_), channel_id=1, source_target_pairs={{64,0},{80,16},{96,32},{112,48},{128,64},{144,80},{160,96},{176,11... | collective-permute-start | bytes 884744 | tf_op jit(solution)/shard_map/ppermute | solution.py:406
  56.1 22.5 %copy-start.5 = (f32[1024]{0:T(1024)S(1)}, f32[1024]{0:T(1024)}, u32[]{:S(2)}) copy-start(f32[1024]{0:T(1024)} %param.20) | copy-start | bytes 12292
  56.1 22.5 %copy-start.6 = (f32[4,128]{1,0:T(4,128)S(1)}, f32[4,128]{1,0:T(4,128)}, u32[]{:S(2)}) copy-start(f32[4,128]{1,0:T(4,128)} %param.25) | copy-start | bytes 6148
  56.1 22.5 %copy-start.7 = (s32[4]{0:T(128)S(1)}, s32[4]{0:T(128)}, u32[]{:S(2)}) copy-start(s32[4]{0:T(128)} %counts.1) | copy-start | bytes 52
  78.6 1.6 copy-start.1
  80.2 1.2 copy-start.2
  81.4 1.2 copy-start.3
  82.7 0.9 copy-start.4
  100.7 3.1 %copy-start.8 = (bf16[512,1024]{1,0:T(8,128)(2,1)}, bf16[512,1024]{1,0:T(8,128)(2,1)S(1)}, u32[]{:S(2)}) copy-start(bf16[512,1024]{1,0:T(8,128)(2,1)S(1)} %get-tuple-element.16) | copy-start | bytes 3145732
  100.7 2.7 %collective-permute-start.18 = (bf16[16,8,16,256]{3,2,1,0:T(8,128)(2,1)S(1)}, bf16[16,8,16,256]{3,2,1,0:T(8,128)(2,1)S(1)}, u32[]{:S(2)}, u32[]{:S(2)}) collective-permute-start(bf16[16,8,16,256]{3,2,1,0:T(8,128)(2,1)S(1)} %get-tuple-element.18), channel_id=1, source_target_pairs={{0,1},{1,0},{2,3},{3,2},{4,5},{5,4},{6,7},{7,6},{8,9},{9,8},{10,11... | collective-permute-start | bytes 3145736 | tf_op jit(solution)/shard_map/ppermute | solution.py:516
  139.5 12.1 %all-to-all-start.2 = ((bf16[16,16,256]{2,1,0:T(8,128)(2,1)}), bf16[16,16,256]{2,1,0:T(8,128)(2,1)S(1)}, u32[]{:S(2)}, u32[]{:S(2)}) async-start(bf16[16,16,256]{2,1,0:T(8,128)(2,1)} %broadcast_in_dim.34), calls=%async_computation.2 | async-start | bytes 262144 | tf_op jit(solution)/shard_map/all_to_all | solution.py:523
  151.6 0.6 copy-start.11
Sparse Core Ops, SparseCore 0:
  9.8 68.7 all-gather.1

commit v8 on v7

--- a/solution.py
+++ b/solution.py
@@ -37,9 +37,9 @@
 
 
 def prepare_kernel(nblocks, place_a, place_b, *refs):
-    count = (len(refs) - 6) // 2
+    count = (len(refs) - 5) // 2
     halves = ((place_a, refs[:count]), (place_b, refs[count : 2 * count]))
-    table, base, normed, mask, rows_s, sems = refs[2 * count :]
+    table, base, normed, rows_s, sems = refs[2 * count :]
     block = pl.program_id(0)
     width = base.shape[1]
     actions = table.shape[0]
@@ -69,11 +69,11 @@
     value = rows[:, :width].astype(F32)
     high, middle, low = split3(table[...])
     value = value + ((dot(onehot, low) + dot(onehot, middle)) + dot(onehot, high))
+    position = lax.broadcasted_iota(jnp.int32, (HIST, 1), 0).astype(F32)
+    value = jnp.where(position < tail[:, LANES - 1 :], value, 0.0)
     scale = lax.rsqrt(jnp.mean(value * value, -1, keepdims=True) + 1e-06)
     base[...] = value
     normed[...] = (value * scale).astype(BF)
-    position = lax.broadcasted_iota(jnp.int32, (HIST, LANES), 0).astype(F32)
-    mask[...] = jnp.where(position < tail[:, LANES - 1 :], 1.0, 0.0)
 
 
 def prepare(place_a, place_b, halves_a, halves_b, table):
@@ -91,7 +91,6 @@
             out_specs=[
                 pl.BlockSpec((HIST, width), lambda b, p, q: (b, 0)),
                 pl.BlockSpec((HIST, width), lambda b, p, q: (b, 0)),
-                pl.BlockSpec((HIST, LANES), lambda b, p, q: (b, 0)),
             ],
             scratch_shapes=[
                 pltpu.VMEM((nblocks, HIST, arrays[0].shape[-1]), BF),
@@ -101,7 +100,6 @@
         out_shape=[
             jax.ShapeDtypeStruct((total, width), F32),
             jax.ShapeDtypeStruct((total, width), BF),
-            jax.ShapeDtypeStruct((total, LANES), F32),
         ],
         compiler_params=pltpu.CompilerParams(vmem_limit_bytes=VMEM_BYTES),
         name="prepare",
@@ -120,7 +118,6 @@
     weights,
     queries,
     cand_t,
-    mask,
     score_weight,
     own,
     labels,
@@ -224,13 +221,11 @@
         scale = lax.rsqrt(jnp.sum(square, -1, keepdims=True) * (1.0 / width) + 1e-06)
         for h in range(HEADS):
             gated_s[:, h * LANES : (h + 1) * LANES] = (mixed_s[h] * scale * gate_s[h]).astype(BF)
-        active = mask[:, :1] > 0.0
         base_copy.wait()
         out_copy.wait()
         for n in range(width // pair):
             cols = slice(n * pair, (n + 1) * pair)
-            value = base_s[:, cols] + dot(gated_s[...], out_s[:, cols])
-            value = jnp.where(active, value, 0.0).astype(BF)
+            value = (base_s[:, cols] + dot(gated_s[...], out_s[:, cols])).astype(BF)
             encoded_s[:, :, cols] = value.reshape(total // (GROUP * HIST), GROUP * HIST, pair)
         query_copy.wait()
         cand_copy.wait()
@@ -313,7 +308,6 @@
     core,
     normed,
     base,
-    mask,
     weights,
     queries,
     cand_t,
@@ -340,7 +334,6 @@
             grid=(ENCODE_STEPS + groups,),
             in_specs=[anywhere] * 5
             + [
-                pl.BlockSpec((total, LANES), whole),
                 pl.BlockSpec((1, width), whole),
                 row,
                 row,
@@ -381,7 +374,7 @@
             jax.ShapeDtypeStruct(shape, BF),
             jax.ShapeDtypeStruct(shape, BF),
         ],
-        compiler_params=pltpu.CompilerParams(vmem_limit_bytes=42 * 1024 * 1024),
+        compiler_params=pltpu.CompilerParams(vmem_limit_bytes=50 * 1024 * 1024),
         name="attention",
     )(
         counts,
@@ -391,8 +384,7 @@
         weights,
         queries.reshape(groups, GROUP * rows, width),
         cand_t.reshape(pairs, 2, width // (2 * pairs), total),
-        mask,
-        score_weight,
+            score_weight,
         own,
         labels,
     )
@@ -418,33 +410,61 @@
 
 
 def join_kernel(left, right, out):
-    wide = left.shape[1]
-    out[:, :wide] = left[...]
-    out[:, wide:] = right[...]
+    last = pl.program_id(0) == pl.num_programs(0) - 1
+
+    @pl.when(last)
+    def _():
+        out[...] = right[...]
+
+    @pl.when(jnp.logical_not(last))
+    def _():
+        out[...] = left[...]
 
 
 def join(left, right):
+    rows, wide = right.shape
+    groups = left.shape[1] // wide
     return pl.pallas_call(
         join_kernel,
-        out_shape=jax.ShapeDtypeStruct((left.shape[0], left.shape[1] + right.shape[1]), left.dtype),
+        grid=(groups + 1,),
+        in_specs=[
+            pl.BlockSpec((rows, wide), lambda g: (0, jnp.minimum(g, groups - 1))),
+            pl.BlockSpec((rows, wide), lambda g: (0, 0)),
+        ],
+        out_specs=pl.BlockSpec((rows, wide), lambda g: (0, g)),
+        out_shape=jax.ShapeDtypeStruct((rows, (groups + 1) * wide), left.dtype),
         name="join",
     )(left, right)
 
 
-def assemble_kernel(pieces, out):
+def assemble_kernel(pieces, out, out_s, sems):
     count, tall, wide = pieces.shape
     down = out.shape[0] // tall
+    copies = []
     for k in range(count):
         a, b = k % down, k // down
-        rows, cols = slice(a * tall, (a + 1) * tall), slice(b * wide, (b + 1) * wide)
-        out[rows, cols] = pieces[k].astype(F32)
+        copies.append(
+            pltpu.make_async_copy(
+                pieces.at[k],
+                out_s.at[pl.ds(a * tall, tall), pl.ds(b * wide, wide)],
+                sems.at[k],
+            )
+        )
+    for copy in copies:
+        copy.start()
+    for copy in copies:
+        copy.wait()
+    out[...] = out_s[...].astype(F32)
 
 
 def assemble(pieces, right):
     count, tall, wide = pieces.shape
+    shape = (count // right * tall, right * wide)
     return pl.pallas_call(
         assemble_kernel,
-        out_shape=jax.ShapeDtypeStruct((count // right * tall, right * wide), F32),
+        in_specs=[pl.BlockSpec(memory_space=pl.ANY)],
+        out_shape=jax.ShapeDtypeStruct(shape, F32),
+        scratch_shapes=[pltpu.VMEM(shape, BF), pltpu.SemaphoreType.DMA((count,))],
         name="assemble",
     )(pieces)
 
@@ -493,7 +513,7 @@
     here = lax.axis_index("user").astype(jnp.int32)
     far_x = lax.rem(owner // side - here // side + side, side)
     far_y = lax.rem(lax.rem(owner, side) - lax.rem(here, side) + side, side)
-    base, normed, mask = prepare(
+    base, normed = prepare(
         far_y * side + far_x, far_x * side + far_y, halves_a, halves_b, action_table
     )
     core = lax.rem(lax.axis_index("loader").astype(jnp.int32), 2)[None]
@@ -502,8 +522,7 @@
         core,
         normed,
         base,
-        mask,
-        weights,
+            weights,
         queries,
         cand_t,
         score_weight[None],

time: 161 us -> 159 us (0.988)
  local copies, waits for them, and re-layouts: 9.82 us -> 4.64 us
    unnamed x32 -> x22, local copies, waits for them, and re-layouts: 6.42 us -> 1.44 us
  transfers between devices with their start and end apart: 21 -> 21, of which waited for: 8 -> 8; matrix products, arithmetic and copies ran while one was open for 8% -> 7% of each run, Pallas kernels for 4% -> 4%
where the time goes in v8:
time: 159 us; the launch traced here: 158 us
  blocking collectives  34.9 us (22%)
  starting transfers between devices  33.2 us (21%)
  waiting for transfers between devices  31.8 us (20%)
  Pallas kernels  28.2 us (18%)
  between operations  14.9 us (9%)
  other arithmetic  6 us (4%)
  local copies, waits for them, and re-layouts  4.64 us (3%)
  matrix products  4.52 us (3%)
    ppermute x18, starting transfers between devices, shift(): return lax.ppermute(array, 'user', moves)  27.1 us
    all_to_all x1, blocking collectives, body(): pieces = lax.all_to_all(pieces, 'user', 0, 0, tiled=True)  22.4 us
    pallas_call x1, Pallas kernels, attention(): pl.pallas_call(attention_kernel, grid_spec=pltpu.PrefetchScalarGridSpec(n...  17.1 us
    all_gather x1, waiting for transfers between devices, body(): lax.all_gather(join(mix_weight, out_weight), 'loader', axis=0, tiled=True)  16.2 us
    all_to_all x1, blocking collectives, body(): lax.all_to_all(pieces, 'loader', 0, 0, axis_index_groups=groups, tiled=True)  12.4 us
    ppermute x18, waiting for transfers between devices, shift(): return lax.ppermute(array, 'user', moves)  9.01 us
    pallas_call x1, Pallas kernels, prepare(): pl.pallas_call(functools.partial(prepare_kernel, nblocks), grid_spec=pltp...  5.88 us
    all_to_all x1, starting transfers between devices, body(): lax.all_to_all(jnp.broadcast_to(piece[None], (users,) + piece.shape), 'us...  5.72 us
  transfers between devices with their start and end apart: 21, of which 8 were waited for; matrix products, arithmetic and copies ran while one was open for 7% of the time, Pallas kernels for 4%

profile of v8, /device:TPU:2, one launch (start us, length us, event | category | flops | bytes accessed | tf_op | source)
XLA Modules:
  0.0 158.2 jit_solution(9054796392217827853)
XLA Ops:
  7.2 0.0 copy-start
  7.2 0.0 all-gather.2.cloned.1.call-start
  7.2 3.5 %join.1 = bf16[64,5120]{1,0:T(8,128)(2,1)} custom-call(bf16[64,4096]{1,0:T(8,128)(2,1)} %left.1, bf16[64,1024]{1,0:T(8,128)(2,1)} %right.1), custom_call_target="tpu_custom_call" | custom-call | tf_op jit(solution)/shard_map/join/pallas_call | solution.py:427
  10.7 0.0 all-gather.2.cloned.1.call-update
  10.7 0.0 copy-start.4
  11.5 0.7 convert_bitcast_fusion
  12.2 0.1 broadcast_in_dim.29
  12.3 1.1 concatenate.3
  13.4 2.2 %collective-permute-start.1 = (bf16[64,1152]{1,0:T(8,128)(2,1)S(1)}, bf16[64,1152]{1,0:T(8,128)(2,1)S(1)}, u32[]{:S(2)}, u32[]{:S(2)}) collective-permute-start(bf16[64,1152]{1,0:T(8,128)(2,1)S(1)} %get-tuple-element.23), channel_id=1, source_target_pairs={{128,0},{144,16},{160,32},{176,48},{192,64},{208,80},{224,96},{240... | collective-permute-start | bytes 442376 | tf_op jit(solution)/shard_map/ppermute | solution.py:398
  15.6 1.6 %collective-permute-start.2 = (bf16[64,1152]{1,0:T(8,128)(2,1)S(1)}, bf16[64,1152]{1,0:T(8,128)(2,1)S(1)}, u32[]{:S(2)}, u32[]{:S(2)}) collective-permute-start(bf16[64,1152]{1,0:T(8,128)(2,1)S(1)} %get-tuple-element.23), channel_id=1, source_target_pairs={{192,0},{208,16},{224,32},{240,48},{0,64},{16,80},{32,96},{48,112}... | collective-permute-start | bytes 442376 | tf_op jit(solution)/shard_map/ppermute | solution.py:398
  17.2 1.6 %collective-permute-start.10 = (bf16[64,1152]{1,0:T(8,128)(2,1)S(1)}, bf16[64,1152]{1,0:T(8,128)(2,1)S(1)}, u32[]{:S(2)}, u32[]{:S(2)}) collective-permute-start(bf16[64,1152]{1,0:T(8,128)(2,1)S(1)} %get-tuple-element.22), channel_id=1, source_target_pairs={{32,0},{48,16},{0,32},{16,48},{96,64},{112,80},{64,96},{80,112},{1... | collective-permute-start | bytes 442376 | tf_op jit(solution)/shard_map/ppermute | solution.py:398
  18.8 1.1 collective-permute-start.9
  19.8 1.0 collective-permute-start.11
  20.8 0.0 collective-permute-done.1
  20.8 2.2 %collective-permute-start = (bf16[64,1152]{1,0:T(8,128)(2,1)S(1)}, bf16[64,1152]{1,0:T(8,128)(2,1)S(1)}, u32[]{:S(2)}, u32[]{:S(2)}) collective-permute-start(bf16[64,1152]{1,0:T(8,128)(2,1)S(1)} %get-tuple-element.23), channel_id=1, source_target_pairs={{64,0},{80,16},{96,32},{112,48},{128,64},{144,80},{160,96},{176,11... | collective-permute-start | bytes 442376 | tf_op jit(solution)/shard_map/ppermute | solution.py:398
  23.0 0.8 collective-permute-done.2
  23.8 1.7 %collective-permute-start.6 = (bf16[2,64,1152]{2,1,0:T(8,128)(2,1)S(1)}, bf16[2,64,1152]{2,1,0:T(8,128)(2,1)S(1)}, u32[]{:S(2)}, u32[]{:S(2)}) collective-permute-start(bf16[2,64,1152]{2,1,0:T(8,128)(2,1)S(1)} %pad_maximum_fusion.1.refs_1_), channel_id=1, source_target_pairs={{48,0},{0,16},{16,32},{32,48},{112,64},{64,80},{80,96},{96,112},{1... | collective-permute-start | bytes 884744 | tf_op jit(solution)/shard_map/ppermute | solution.py:398
  25.5 0.8 collective-permute-done
  26.3 3.0 %collective-permute-start.4 = (bf16[2,64,1152]{2,1,0:T(8,128)(2,1)S(1)}, bf16[2,64,1152]{2,1,0:T(8,128)(2,1)S(1)}, u32[]{:S(2)}, u32[]{:S(2)}) collective-permute-start(bf16[2,64,1152]{2,1,0:T(8,128)(2,1)S(1)} %pad_maximum_fusion.1.refs_1_), channel_id=1, source_target_pairs={{16,0},{32,16},{48,32},{0,48},{80,64},{96,80},{112,96},{64,112},{1... | collective-permute-start | bytes 884744 | tf_op jit(solution)/shard_map/ppermute | solution.py:398
  29.3 0.8 pad_maximum_fusion.refs_0_
  30.1 0.0 collective-permute-done.10
  30.1 0.0 collective-permute-start.8
  30.1 0.0 collective-permute-done.11
  30.1 3.2 %collective-permute-start.3 = (bf16[2,64,1152]{2,1,0:T(8,128)(2,1)}, bf16[2,64,1152]{2,1,0:T(8,128)(2,1)}, u32[]{:S(2)}, u32[]{:S(2)}) collective-permute-start(bf16[2,64,1152]{2,1,0:T(8,128)(2,1)} %pad_maximum_fusion.refs_0_), channel_id=1, source_target_pairs={{16,0},{32,16},{48,32},{0,48},{80,64},{96,80},{112,96},{64,112},{1... | collective-permute-start | bytes 884744 | tf_op jit(solution)/shard_map/ppermute | solution.py:398
  33.3 0.8 pad_maximum_fusion.3.refs_9_
  34.1 0.0 collective-permute-done.9
  34.1 2.0 %collective-permute-start.15 = (bf16[2,64,1152]{2,1,0:T(8,128)(2,1)}, bf16[2,64,1152]{2,1,0:T(8,128)(2,1)}, u32[]{:S(2)}, u32[]{:S(2)}) collective-permute-start(bf16[2,64,1152]{2,1,0:T(8,128)(2,1)} %pad_maximum_fusion.3.refs_9_), channel_id=1, source_target_pairs={{192,0},{208,16},{224,32},{240,48},{0,64},{16,80},{32,96},{48,112}... | collective-permute-start | bytes 884744 | tf_op jit(solution)/shard_map/ppermute | solution.py:398
  36.1 0.7 pad_maximum_fusion.2.refs_8_
  36.8 0.0 collective-permute-done.6.refs_7_
  36.9 0.0 collective-permute-start.13
  36.9 0.7 copy-done.8
  37.6 2.7 %collective-permute-start.12 = (bf16[2,64,1152]{2,1,0:T(8,128)(2,1)}, bf16[2,64,1152]{2,1,0:T(8,128)(2,1)}, u32[]{:S(2)}, u32[]{:S(2)}) collective-permute-start(bf16[2,64,1152]{2,1,0:T(8,128)(2,1)} %pad_maximum_fusion.2.refs_8_), channel_id=1, source_target_pairs={{64,0},{80,16},{96,32},{112,48},{128,64},{144,80},{160,96},{176,11... | collective-permute-start | bytes 884744 | tf_op jit(solution)/shard_map/ppermute | solution.py:398
  40.3 2.3 %convolution_convert_fusion = bf16[512,1024]{1,0:T(8,128)(2,1)} fusion(bf16[512,1024]{1,0:T(8,128)(2,1)S(1)} %bitcast.54, bf16[1024,1024]{1,0:T(8,128)(2,1)S(1)} %copy-done), kind=kOutput, calls=%fused_computation.3 | convolution fusion | flops 1074266112 | bytes 4194304 | tf_op jit(solution)/shard_map/dot_general | solution.py:508
  42.6 0.5 multiply_add_fusion
  43.1 0.0 collective-permute-done.8.refs_6_
  43.1 0.0 collective-permute-start.17
  43.1 0.0 collective-permute-done.3.refs_2_
  43.1 0.4 collective-permute-start.7
  43.5 0.0 collective-permute-done.15.refs_15_
  43.5 3.1 %collective-permute-start.5 = (bf16[2,64,1152]{2,1,0:T(8,128)(2,1)}, bf16[2,64,1152]{2,1,0:T(8,128)(2,1)}, u32[]{:S(2)}, u32[]{:S(2)}) collective-permute-start(bf16[2,64,1152]{2,1,0:T(8,128)(2,1)} %collective-permute-done.3.refs_2_), channel_id=1, source_target_pairs={{16,0},{32,16},{48,32},{0,48},{80,64},{96,80},{112,96},{64,112},{1... | collective-permute-start | bytes 884744 | tf_op jit(solution)/shard_map/ppermute | solution.py:398
  46.6 1.3 collective-permute-start.16
  48.0 2.5 %collective-permute-done.12.refs_10_ = bf16[2,64,1152]{2,1,0:T(8,128)(2,1)} collective-permute-done((bf16[2,64,1152]{2,1,0:T(8,128)(2,1)}, bf16[2,64,1152]{2,1,0:T(8,128)(2,1)}, u32[]{:S(2)}, u32[]{:S(2)}) %collective-permute-start.12) | collective-permute-done | bytes 294944 | tf_op jit(solution)/shard_map/ppermute | solution.py:398
  50.5 0.3 multiply_reduce_fusion
  50.8 1.3 copy.17
  52.1 0.5 multiply_add_fusion.1.place_a
  52.6 0.0 collective-permute-done.7.refs_5_
  52.6 0.0 collective-permute-done.5.refs_4_
  52.6 2.2 %collective-permute-done.16.refs_13_ = bf16[2,64,1152]{2,1,0:T(8,128)(2,1)} collective-permute-done((bf16[2,64,1152]{2,1,0:T(8,128)(2,1)}, bf16[2,64,1152]{2,1,0:T(8,128)(2,1)}, u32[]{:S(2)}, u32[]{:S(2)}) %collective-permute-start.16) | collective-permute-done | bytes 294944 | tf_op jit(solution)/shard_map/ppermute | solution.py:398
  54.9 2.6 %collective-permute-done.14.refs_12_ = bf16[2,64,1152]{2,1,0:T(8,128)(2,1)} collective-permute-done((bf16[2,64,1152]{2,1,0:T(8,128)(2,1)}, bf16[2,64,1152]{2,1,0:T(8,128)(2,1)}, u32[]{:S(2)}, u32[]{:S(2)}) %collective-permute-start.14) | collective-permute-done | bytes 294944 | tf_op jit(solution)/shard_map/ppermute | solution.py:398
  57.5 5.9 %prepare.1 = (f32[512,1024]{1,0:T(8,128)}, bf16[512,1024]{1,0:T(8,128)(2,1)}) custom-call(s32[4]{0:T(128)} %multiply_add_fusion.1.place_a, s32[4]{0:T(128)} %get-tuple-element.17.place_b, bf16[2,64,1152]{2,1,0:T(8,128)(2,1)} %pad_maximum_fusion.refs_0_, bf16[2,64,1152]{2,1,0:T(8,128)(2,1)} %copy-done.5, bf16[2,64,1152]{2,1,0:T(8,128)(2,1)} %collective-permute-done.3.refs_2_, ...), custom_call_target="tpu_custom_call" | custom-call | tf_op jit(solution)/shard_map/prepare/pallas_call | solution.py:84
  63.4 16.2 %all-gather.2.cloned.1.call-done.weights = bf16[1024,5120]{1,0:T(8,128)(2,1)} async-done(((bf16[64,5120]{1,0:T(8,128)(2,1)}), bf16[1024,5120]{1,0:T(8,128)(2,1)}) %all-gather.2.cloned.1.call-update) | async-done | bytes 10485776 | tf_op jit(solution)/shard_map/all_gather | solution.py:492
  79.6 17.1 %attention.1 = (f32[4,1,128]{2,1,0:T(1,128)}, f32[4,1,128]{2,1,0:T(1,128)S(1)}, bf16[512,1024]{1,0:T(8,128)(2,1)S(1)}, bf16[16,8,16,256]{3,2,1,0:T(8,128)(2,1)S(1)}, bf16[16,8,16,256]{3,2,1,0:T(8,128)(2,1)S(1)}) custom-call(s32[4]{0:T(128)S(1)} %copy-done.3, s32[1]{0:T(128)} %bitcast.core, bf16[512,1024]{1,0:T(8,128)(2,1)} %get-tuple-element.10.normed, ...), custom_call_target="tpu_custom_call" | custom-call | tf_op jit(solution)/shard_map/attention/pallas_call | solution.py:330
  96.8 0.3 collective-permute-start.18
  97.1 2.4 %collective-permute-done.18 = bf16[16,8,16,256]{3,2,1,0:T(8,128)(2,1)S(1)} collective-permute-done((bf16[16,8,16,256]{3,2,1,0:T(8,128)(2,1)S(1)}, bf16[16,8,16,256]{3,2,1,0:T(8,128)(2,1)S(1)}, u32[]{:S(2)}, u32[]{:S(2)}) %collective-permute-start.18) | collective-permute-done | bytes 1048608 | tf_op jit(solution)/shard_map/ppermute | solution.py:535
  99.5 0.3 add_convert_fusion
  99.9 22.4 %all_to_all.15 = bf16[16,8,16,256]{3,2,1,0:T(8,128)(2,1)} all-to-all(bf16[16,8,16,256]{3,2,1,0:T(8,128)(2,1)S(1)} %add_convert_fusion), channel_id=1, replica_groups=mesh['user'=16,'loader'=16] {'user'}, dimensions={0} | all-to-all | bytes 2097152 | tf_op jit(solution)/shard_map/all_to_all | solution.py:537
  122.3 1.4 reduce_sum.34
  123.7 12.4 %all_to_all.16 = bf16[8,16,256]{2,1,0:T(8,128)(2,1)S(1)} all-to-all(bf16[8,16,256]{2,1,0:T(8,128)(2,1)S(1)} %reduce_sum.34), channel_id=1, replica_groups={{0,2,4,6,8,10,12,14},{1,3,5,7,9,11,13,15},{16,18,20,22,24,26,28,30},{17..., dimensions={0} | all-to-all | bytes 131072 | tf_op jit(solution)/shard_map/all_to_all | solution.py:540
  136.1 0.7 broadcast_in_dim.34
  136.8 5.7 %all-to-all-start.2 = ((bf16[16,16,256]{2,1,0:T(8,128)(2,1)}), bf16[16,16,256]{2,1,0:T(8,128)(2,1)S(1)}, u32[]{:S(2)}, u32[]{:S(2)}) async-start(bf16[16,16,256]{2,1,0:T(8,128)(2,1)} %broadcast_in_dim.34), calls=%async_computation.2 | async-start | bytes 262144 | tf_op jit(solution)/shard_map/all_to_all | solution.py:542
  142.5 2.3 %add_convert_fusion.1 = bf16[512,1024]{1,0:T(8,128)(2,1)} fusion(bf16[512,1024]{1,0:T(8,128)(2,1)S(1)} %get-tuple-element.14, bf16[1024,1024]{1,0:T(8,128)(2,1)S(1)} %copy-done, f32[1024]{0:T(1024)S(1)} %copy-done.9, f32[512]{0:T(512)S(1)} %bitcast.52), kind=kOutput, calls=%fused_computation.1 | convolution fusion | flops 1075314688 | bytes 4200448 | tf_op jit(solution)/shard_map/dot_general | solution.py:547
  144.8 4.2 %all-to-all-done.2.pieces = bf16[16,16,256]{2,1,0:T(8,128)(2,1)S(1)} async-done(((bf16[16,16,256]{2,1,0:T(8,128)(2,1)}), bf16[16,16,256]{2,1,0:T(8,128)(2,1)S(1)}, u32[]{:S(2)}, u32[]{:S(2)}) %all-to-all-start.2) | async-done | bytes 131104 | tf_op jit(solution)/shard_map/all_to_all | solution.py:542
  148.9 0.6 copy-done.6
  149.6 1.7 %assemble.1 = f32[64,1024]{1,0:T(8,128)} custom-call(bf16[16,16,256]{2,1,0:T(8,128)(2,1)} %copy-done.6), custom_call_target="tpu_custom_call" | custom-call | tf_op jit(solution)/shard_map/assemble/pallas_call | solution.py:463
  (26 shorter events, 0.1 us)
Async XLA Ops:
  7.2 33.2 %copy-start = (bf16[1024,1024]{1,0:T(8,128)(2,1)S(1)}, bf16[1024,1024]{1,0:T(8,128)(2,1)}, u32[]{:S(2)}) copy-start(bf16[1024,1024]{1,0:T(8,128)(2,1)} %param.19) | copy-start | bytes 6291460
  7.2 72.4 %all-gather.2.cloned.1.call-start = ((), (), s32[]{:S(2)}) async-start(), calls=%async_computation.3 | async-start | bytes 11141120 | tf_op jit(solution)/shard_map/all_gather | solution.py:492
  10.7 29.6 %copy-start.4 = (bf16[4,128,1024]{2,1,0:T(8,128)(2,1)S(1)}, bf16[4,128,1024]{2,1,0:T(8,128)(2,1)}, u32[]{:S(2)}) copy-start(bf16[4,128,1024]{2,1,0:T(8,128)(2,1)} %param.22) | copy-start | bytes 3145732
  13.4 7.4 %collective-permute-start.1 = (bf16[64,1152]{1,0:T(8,128)(2,1)S(1)}, bf16[64,1152]{1,0:T(8,128)(2,1)S(1)}, u32[]{:S(2)}, u32[]{:S(2)}) collective-permute-start(bf16[64,1152]{1,0:T(8,128)(2,1)S(1)} %get-tuple-element.23), channel_id=1, source_target_pairs={{128,0},{144,16},{160,32},{176,48},{192,64},{208,80},{224,96},{240... | collective-permute-start | bytes 442376 | tf_op jit(solution)/shard_map/ppermute | solution.py:398
  15.6 8.2 %collective-permute-start.2 = (bf16[64,1152]{1,0:T(8,128)(2,1)S(1)}, bf16[64,1152]{1,0:T(8,128)(2,1)S(1)}, u32[]{:S(2)}, u32[]{:S(2)}) collective-permute-start(bf16[64,1152]{1,0:T(8,128)(2,1)S(1)} %get-tuple-element.23), channel_id=1, source_target_pairs={{192,0},{208,16},{224,32},{240,48},{0,64},{16,80},{32,96},{48,112}... | collective-permute-start | bytes 442376 | tf_op jit(solution)/shard_map/ppermute | solution.py:398
  17.2 12.9 %collective-permute-start.10 = (bf16[64,1152]{1,0:T(8,128)(2,1)S(1)}, bf16[64,1152]{1,0:T(8,128)(2,1)S(1)}, u32[]{:S(2)}, u32[]{:S(2)}) collective-permute-start(bf16[64,1152]{1,0:T(8,128)(2,1)S(1)} %get-tuple-element.22), channel_id=1, source_target_pairs={{32,0},{48,16},{0,32},{16,48},{96,64},{112,80},{64,96},{80,112},{1... | collective-permute-start | bytes 442376 | tf_op jit(solution)/shard_map/ppermute | solution.py:398
  18.8 15.3 %collective-permute-start.9 = (bf16[64,1152]{1,0:T(8,128)(2,1)S(1)}, bf16[64,1152]{1,0:T(8,128)(2,1)S(1)}, u32[]{:S(2)}, u32[]{:S(2)}) collective-permute-start(bf16[64,1152]{1,0:T(8,128)(2,1)S(1)} %get-tuple-element.22), channel_id=1, source_target_pairs={{16,0},{32,16},{48,32},{0,48},{80,64},{96,80},{112,96},{64,112},{1... | collective-permute-start | bytes 442376 | tf_op jit(solution)/shard_map/ppermute | solution.py:398
  19.8 10.3 %collective-permute-start.11 = (bf16[64,1152]{1,0:T(8,128)(2,1)S(1)}, bf16[64,1152]{1,0:T(8,128)(2,1)S(1)}, u32[]{:S(2)}, u32[]{:S(2)}) collective-permute-start(bf16[64,1152]{1,0:T(8,128)(2,1)S(1)} %get-tuple-element.22), channel_id=1, source_target_pairs={{48,0},{0,16},{16,32},{32,48},{112,64},{64,80},{80,96},{96,112},{1... | collective-permute-start | bytes 442376 | tf_op jit(solution)/shard_map/ppermute | solution.py:398
  20.8 5.5 %collective-permute-start = (bf16[64,1152]{1,0:T(8,128)(2,1)S(1)}, bf16[64,1152]{1,0:T(8,128)(2,1)S(1)}, u32[]{:S(2)}, u32[]{:S(2)}) collective-permute-start(bf16[64,1152]{1,0:T(8,128)(2,1)S(1)} %get-tuple-element.23), channel_id=1, source_target_pairs={{64,0},{80,16},{96,32},{112,48},{128,64},{144,80},{160,96},{176,11... | collective-permute-start | bytes 442376 | tf_op jit(solution)/shard_map/ppermute | solution.py:398
  23.8 18.8 %copy-start.5 = (bf16[2,64,1152]{2,1,0:T(8,128)(2,1)}, bf16[2,64,1152]{2,1,0:T(8,128)(2,1)S(1)}, u32[]{:S(2)}) copy-start(bf16[2,64,1152]{2,1,0:T(8,128)(2,1)S(1)} %pad_maximum_fusion.1.refs_1_) | copy-start | bytes 884740
  23.8 13.0 %collective-permute-start.6 = (bf16[2,64,1152]{2,1,0:T(8,128)(2,1)S(1)}, bf16[2,64,1152]{2,1,0:T(8,128)(2,1)S(1)}, u32[]{:S(2)}, u32[]{:S(2)}) collective-permute-start(bf16[2,64,1152]{2,1,0:T(8,128)(2,1)S(1)} %pad_maximum_fusion.1.refs_1_), channel_id=1, source_target_pairs={{48,0},{0,16},{16,32},{32,48},{112,64},{64,80},{80,96},{96,112},{1... | collective-permute-start | bytes 884744 | tf_op jit(solution)/shard_map/ppermute | solution.py:398
  26.3 10.6 %collective-permute-start.4 = (bf16[2,64,1152]{2,1,0:T(8,128)(2,1)S(1)}, bf16[2,64,1152]{2,1,0:T(8,128)(2,1)S(1)}, u32[]{:S(2)}, u32[]{:S(2)}) collective-permute-start(bf16[2,64,1152]{2,1,0:T(8,128)(2,1)S(1)} %pad_maximum_fusion.1.refs_1_), channel_id=1, source_target_pairs={{16,0},{32,16},{48,32},{0,48},{80,64},{96,80},{112,96},{64,112},{1... | collective-permute-start | bytes 884744 | tf_op jit(solution)/shard_map/ppermute | solution.py:398
  30.1 13.0 %collective-permute-start.8 = (bf16[2,64,1152]{2,1,0:T(8,128)(2,1)}, bf16[2,64,1152]{2,1,0:T(8,128)(2,1)}, u32[]{:S(2)}, u32[]{:S(2)}) collective-permute-start(bf16[2,64,1152]{2,1,0:T(8,128)(2,1)} %pad_maximum_fusion.refs_0_), channel_id=1, source_target_pairs={{48,0},{0,16},{16,32},{32,48},{112,64},{64,80},{80,96},{96,112},{1... | collective-permute-start | bytes 884744 | tf_op jit(solution)/shard_map/ppermute | solution.py:398
  30.1 13.0 %collective-permute-start.3 = (bf16[2,64,1152]{2,1,0:T(8,128)(2,1)}, bf16[2,64,1152]{2,1,0:T(8,128)(2,1)}, u32[]{:S(2)}, u32[]{:S(2)}) collective-permute-start(bf16[2,64,1152]{2,1,0:T(8,128)(2,1)} %pad_maximum_fusion.refs_0_), channel_id=1, source_target_pairs={{16,0},{32,16},{48,32},{0,48},{80,64},{96,80},{112,96},{64,112},{1... | collective-permute-start | bytes 884744 | tf_op jit(solution)/shard_map/ppermute | solution.py:398
  34.1 9.4 %collective-permute-start.15 = (bf16[2,64,1152]{2,1,0:T(8,128)(2,1)}, bf16[2,64,1152]{2,1,0:T(8,128)(2,1)}, u32[]{:S(2)}, u32[]{:S(2)}) collective-permute-start(bf16[2,64,1152]{2,1,0:T(8,128)(2,1)} %pad_maximum_fusion.3.refs_9_), channel_id=1, source_target_pairs={{192,0},{208,16},{224,32},{240,48},{0,64},{16,80},{32,96},{48,112}... | collective-permute-start | bytes 884744 | tf_op jit(solution)/shard_map/ppermute | solution.py:398
  36.8 20.7 %copy-start.7 = (bf16[2,64,1152]{2,1,0:T(8,128)(2,1)}, bf16[2,64,1152]{2,1,0:T(8,128)(2,1)S(1)}, u32[]{:S(2)}) copy-start(bf16[2,64,1152]{2,1,0:T(8,128)(2,1)S(1)} %collective-permute-done.6.refs_7_) | copy-start | bytes 884740
  36.9 9.8 %collective-permute-start.13 = (bf16[2,64,1152]{2,1,0:T(8,128)(2,1)}, bf16[2,64,1152]{2,1,0:T(8,128)(2,1)}, u32[]{:S(2)}, u32[]{:S(2)}) collective-permute-start(bf16[2,64,1152]{2,1,0:T(8,128)(2,1)} %pad_maximum_fusion.3.refs_9_), channel_id=1, source_target_pairs={{64,0},{80,16},{96,32},{112,48},{128,64},{144,80},{160,96},{176,11... | collective-permute-start | bytes 884744 | tf_op jit(solution)/shard_map/ppermute | solution.py:398
  36.9 0.8 copy-start.8
  37.6 12.8 %collective-permute-start.12 = (bf16[2,64,1152]{2,1,0:T(8,128)(2,1)}, bf16[2,64,1152]{2,1,0:T(8,128)(2,1)}, u32[]{:S(2)}, u32[]{:S(2)}) collective-permute-start(bf16[2,64,1152]{2,1,0:T(8,128)(2,1)} %pad_maximum_fusion.2.refs_8_), channel_id=1, source_target_pairs={{64,0},{80,16},{96,32},{112,48},{128,64},{144,80},{160,96},{176,11... | collective-permute-start | bytes 884744 | tf_op jit(solution)/shard_map/ppermute | solution.py:398
  40.3 2.3 %copy-start.10 = (s32[4,1]{0,1:T(1,128)S(1)}, s32[4,1]{0,1:T(1,128)}, u32[]{:S(2)}) copy-start(s32[4,1]{0,1:T(1,128)} %param.23) | copy-start | bytes 52
  40.3 10.1 %copy-start.9 = (f32[1024]{0:T(1024)S(1)}, f32[1024]{0:T(1024)}, u32[]{:S(2)}) copy-start(f32[1024]{0:T(1024)} %param.21) | copy-start | bytes 12292
  43.1 9.5 %collective-permute-start.17 = (bf16[2,64,1152]{2,1,0:T(8,128)(2,1)}, bf16[2,64,1152]{2,1,0:T(8,128)(2,1)}, u32[]{:S(2)}, u32[]{:S(2)}) collective-permute-start(bf16[2,64,1152]{2,1,0:T(8,128)(2,1)} %pad_maximum_fusion.2.refs_8_), channel_id=1, source_target_pairs={{192,0},{208,16},{224,32},{240,48},{0,64},{16,80},{32,96},{48,112}... | collective-permute-start | bytes 884744 | tf_op jit(solution)/shard_map/ppermute | solution.py:398
  43.1 9.5 %collective-permute-start.7 = (bf16[2,64,1152]{2,1,0:T(8,128)(2,1)S(1)}, bf16[2,64,1152]{2,1,0:T(8,128)(2,1)}, u32[]{:S(2)}, u32[]{:S(2)}) collective-permute-start(bf16[2,64,1152]{2,1,0:T(8,128)(2,1)S(1)} %collective-permute-done.6.refs_7_), channel_id=1, source_target_pairs={{48,0},{0,16},{16,32},{32,48},{112,64},{64,80},{80,96},{96,112},{1... | collective-permute-start | bytes 884744 | tf_op jit(solution)/shard_map/ppermute | solution.py:398
  43.5 9.1 %collective-permute-start.5 = (bf16[2,64,1152]{2,1,0:T(8,128)(2,1)}, bf16[2,64,1152]{2,1,0:T(8,128)(2,1)}, u32[]{:S(2)}, u32[]{:S(2)}) collective-permute-start(bf16[2,64,1152]{2,1,0:T(8,128)(2,1)} %collective-permute-done.3.refs_2_), channel_id=1, source_target_pairs={{16,0},{32,16},{48,32},{0,48},{80,64},{96,80},{112,96},{64,112},{1... | collective-permute-start | bytes 884744 | tf_op jit(solution)/shard_map/ppermute | solution.py:398
  46.6 8.2 %collective-permute-start.16 = (bf16[2,64,1152]{2,1,0:T(8,128)(2,1)}, bf16[2,64,1152]{2,1,0:T(8,128)(2,1)}, u32[]{:S(2)}, u32[]{:S(2)}) collective-permute-start(bf16[2,64,1152]{2,1,0:T(8,128)(2,1)} %collective-permute-done.15.refs_15_), channel_id=1, source_target_pairs={{192,0},{208,16},{224,32},{240,48},{0,64},{16,80},{32,96},{48,112}... | collective-permute-start | bytes 884744 | tf_op jit(solution)/shard_map/ppermute | solution.py:398
  50.5 7.0 %collective-permute-start.14 = (bf16[2,64,1152]{2,1,0:T(8,128)(2,1)}, bf16[2,64,1152]{2,1,0:T(8,128)(2,1)}, u32[]{:S(2)}, u32[]{:S(2)}) collective-permute-start(bf16[2,64,1152]{2,1,0:T(8,128)(2,1)} %collective-permute-done.12.refs_10_), channel_id=1, source_target_pairs={{64,0},{80,16},{96,32},{112,48},{128,64},{144,80},{160,96},{176,11... | collective-permute-start | bytes 884744 | tf_op jit(solution)/shard_map/ppermute | solution.py:398
  57.5 22.1 %copy-start.1 = (f32[1024]{0:T(1024)S(1)}, f32[1024]{0:T(1024)}, u32[]{:S(2)}) copy-start(f32[1024]{0:T(1024)} %param.20) | copy-start | bytes 12292
  57.5 22.1 %copy-start.2 = (f32[4,128]{1,0:T(4,128)S(1)}, f32[4,128]{1,0:T(4,128)}, u32[]{:S(2)}) copy-start(f32[4,128]{1,0:T(4,128)} %param.25) | copy-start | bytes 6148
  57.5 22.1 %copy-start.3 = (s32[4]{0:T(128)S(1)}, s32[4]{0:T(128)}, u32[]{:S(2)}) copy-start(s32[4]{0:T(128)} %counts.1) | copy-start | bytes 52
  96.8 2.7 %collective-permute-start.18 = (bf16[16,8,16,256]{3,2,1,0:T(8,128)(2,1)S(1)}, bf16[16,8,16,256]{3,2,1,0:T(8,128)(2,1)S(1)}, u32[]{:S(2)}, u32[]{:S(2)}) collective-permute-start(bf16[16,8,16,256]{3,2,1,0:T(8,128)(2,1)S(1)} %get-tuple-element.16), channel_id=1, source_target_pairs={{0,1},{1,0},{2,3},{3,2},{4,5},{5,4},{6,7},{7,6},{8,9},{9,8},{10,11... | collective-permute-start | bytes 3145736 | tf_op jit(solution)/shard_map/ppermute | solution.py:535
  136.8 12.1 %all-to-all-start.2 = ((bf16[16,16,256]{2,1,0:T(8,128)(2,1)}), bf16[16,16,256]{2,1,0:T(8,128)(2,1)S(1)}, u32[]{:S(2)}, u32[]{:S(2)}) async-start(bf16[16,16,256]{2,1,0:T(8,128)(2,1)} %broadcast_in_dim.34), calls=%async_computation.2 | async-start | bytes 262144 | tf_op jit(solution)/shard_map/all_to_all | solution.py:542
  148.9 0.7 copy-start.6
Sparse Core Ops, SparseCore 0:
  10.9 68.7 all-gather.1

commit v9 on v7

--- a/solution.py
+++ b/solution.py
@@ -37,9 +37,9 @@
 
 
 def prepare_kernel(nblocks, place_a, place_b, *refs):
-    count = (len(refs) - 6) // 2
+    count = (len(refs) - 5) // 2
     halves = ((place_a, refs[:count]), (place_b, refs[count : 2 * count]))
-    table, base, normed, mask, rows_s, sems = refs[2 * count :]
+    table, base, normed, rows_s, sems = refs[2 * count :]
     block = pl.program_id(0)
     width = base.shape[1]
     actions = table.shape[0]
@@ -69,11 +69,11 @@
     value = rows[:, :width].astype(F32)
     high, middle, low = split3(table[...])
     value = value + ((dot(onehot, low) + dot(onehot, middle)) + dot(onehot, high))
+    position = lax.broadcasted_iota(jnp.int32, (HIST, 1), 0).astype(F32)
+    value = jnp.where(position < tail[:, LANES - 1 :], value, 0.0)
     scale = lax.rsqrt(jnp.mean(value * value, -1, keepdims=True) + 1e-06)
     base[...] = value
     normed[...] = (value * scale).astype(BF)
-    position = lax.broadcasted_iota(jnp.int32, (HIST, LANES), 0).astype(F32)
-    mask[...] = jnp.where(position < tail[:, LANES - 1 :], 1.0, 0.0)
 
 
 def prepare(place_a, place_b, halves_a, halves_b, table):
@@ -91,7 +91,6 @@
             out_specs=[
                 pl.BlockSpec((HIST, width), lambda b, p, q: (b, 0)),
                 pl.BlockSpec((HIST, width), lambda b, p, q: (b, 0)),
-                pl.BlockSpec((HIST, LANES), lambda b, p, q: (b, 0)),
             ],
             scratch_shapes=[
                 pltpu.VMEM((nblocks, HIST, arrays[0].shape[-1]), BF),
@@ -101,7 +100,6 @@
         out_shape=[
             jax.ShapeDtypeStruct((total, width), F32),
             jax.ShapeDtypeStruct((total, width), BF),
-            jax.ShapeDtypeStruct((total, LANES), F32),
         ],
         compiler_params=pltpu.CompilerParams(vmem_limit_bytes=VMEM_BYTES),
         name="prepare",
@@ -120,14 +118,12 @@
     weights,
     queries,
     cand_t,
-    mask,
     score_weight,
     own,
     labels,
     scores,
     error,
     slopes,
-    mine,
     other,
     normed_s,
     base_s,
@@ -143,7 +139,6 @@
     logit_s,
     weight_s,
     slope_s,
-    mine_s,
     other_s,
     sems,
     mix_sems,
@@ -224,13 +219,11 @@
         scale = lax.rsqrt(jnp.sum(square, -1, keepdims=True) * (1.0 / width) + 1e-06)
         for h in range(HEADS):
             gated_s[:, h * LANES : (h + 1) * LANES] = (mixed_s[h] * scale * gate_s[h]).astype(BF)
-        active = mask[:, :1] > 0.0
         base_copy.wait()
         out_copy.wait()
         for n in range(width // pair):
             cols = slice(n * pair, (n + 1) * pair)
-            value = base_s[:, cols] + dot(gated_s[...], out_s[:, cols])
-            value = jnp.where(active, value, 0.0).astype(BF)
+            value = (base_s[:, cols] + dot(gated_s[...], out_s[:, cols])).astype(BF)
             encoded_s[:, :, cols] = value.reshape(total // (GROUP * HIST), GROUP * HIST, pair)
         query_copy.wait()
         cand_copy.wait()
@@ -268,11 +261,12 @@
         for g, part in enumerate(parts):
             partial = jnp.sum(totals[g], -1, keepdims=True).astype(BF).astype(F32)
             partial_row = jnp.broadcast_to(partial, (HIST, HIST)).T[:1]
-            active = lax.broadcasted_iota(jnp.int32, (1, HIST), 1) < counts[now * GROUP + g]
-            score = jnp.where(active, partial_row + own[g], 0.0)
-            err = jnp.where(active, sigmoid(score) - labels[g], 0.0)
-            scores[g] = score
-            error[g] = err
+            block = now * GROUP + g
+            active = lax.broadcasted_iota(jnp.int32, (1, HIST), 1) < counts[block]
+            score = jnp.where(active, partial_row + own[block], 0.0)
+            err = jnp.where(active, sigmoid(score) - labels[block], 0.0)
+            scores[block] = score
+            error[block] = err
             err_rows = jnp.broadcast_to(err, (HIST, HIST)).T
             for h in range(HEADS):
                 direction = logit_s[g * HEADS + h].astype(BF).astype(F32)
@@ -282,30 +276,72 @@
 
     @pl.when(step == pl.num_programs(0) - 1)
     def _():
-        _, pairs, tall, wide = mine.shape
+        pairs, _, piece, _ = cand_s.shape
+        _, _, tall, wide = other.shape
         right = width // wide
-        down = mine.shape[0] // right
-        piece = tall * down
+        down = piece // tall
         copies = []
         for n in range(right):
             cols = slice(n * wide, (n + 1) * wide)
             slope = slope_s[:, :, cols].reshape(-1, wide)
-            for which, store in ((core[0], mine_s), (1 - core[0], other_s)):
-                rows = cand_s[:, which].reshape(pairs * piece, -1)
-                grad = dot(rows, slope).astype(BF)
-                for p in range(pairs):
-                    for a in range(down):
-                        start = p * piece + a * tall
-                        store[n * down + a, p] = grad[start : start + tall]
+            rows = cand_s[:, 1 - core[0]].reshape(pairs * piece, -1)
+            place_pieces(dot(rows, slope).astype(BF), other_s, n * down, piece)
             chunk = pl.ds(n * down, down)
-            for k, (source, target) in enumerate(((mine_s, mine), (other_s, other))):
-                copy = pltpu.make_async_copy(
-                    source.at[chunk], target.at[chunk], grad_sems.at[k, n]
-                )
-                copy.start()
-                copies.append(copy)
+            copy = pltpu.make_async_copy(other_s.at[chunk], other.at[chunk], grad_sems.at[n])
+            copy.start()
+            copies.append(copy)
         for copy in copies:
             copy.wait()
+
+
+def place_pieces(grad, store, first, piece):
+    tall = store.shape[2]
+    for p in range(store.shape[1]):
+        for a in range(piece // tall):
+            start = p * piece + a * tall
+            store[first + a, p] = grad[start : start + tall]
+
+
+def gradient_kernel(core, cand_t, slopes, out, cand_s, slope_s, sems):
+    first = pltpu.make_async_copy(slopes, slope_s, sems.at[0])
+    second = pltpu.make_async_copy(cand_t.at[:, core[0]], cand_s, sems.at[1])
+    first.start()
+    second.start()
+    first.wait()
+    second.wait()
+    pairs, piece, total = cand_s.shape
+    _, _, tall, wide = out.shape
+    for n in range(slope_s.shape[1] // wide):
+        cols = slice(n * wide, (n + 1) * wide)
+        grad = dot(cand_s[...].reshape(pairs * piece, total), slope_s[:, cols])
+        place_pieces(grad.astype(BF), out, n * (piece // tall), piece)
+
+
+def gradient(core, cand_t, slopes, users):
+    pairs, _, piece, total = cand_t.shape
+    width = slopes.shape[1]
+    side = math.isqrt(users)
+    shape = (users, pairs, piece // side, width // side)
+    return pl.pallas_call(
+        gradient_kernel,
+        grid_spec=pltpu.PrefetchScalarGridSpec(
+            num_scalar_prefetch=1,
+            grid=(1,),
+            in_specs=[pl.BlockSpec(memory_space=pl.ANY)] * 2,
+            out_specs=pl.BlockSpec(shape, lambda n, c: (0, 0, 0, 0)),
+            scratch_shapes=[
+                pltpu.VMEM((pairs, piece, total), BF),
+                pltpu.VMEM((total, width), BF),
+                pltpu.SemaphoreType.DMA((2,)),
+            ],
+        ),
+        out_shape=jax.ShapeDtypeStruct(shape, BF),
+        cost_estimate=pl.CostEstimate(
+            flops=total * width * width, bytes_accessed=3 * total * width * 2, transcendentals=0
+        ),
+        compiler_params=pltpu.CompilerParams(vmem_limit_bytes=16 * 1024 * 1024),
+        name="gradient",
+    )(core, cand_t, slopes)
 
 
 def attention(
@@ -313,7 +349,6 @@
     core,
     normed,
     base,
-    mask,
     weights,
     queries,
     cand_t,
@@ -330,7 +365,7 @@
     side = math.isqrt(users)
     shape = (users, pairs, width // (2 * pairs * side), width // side)
     current = lambda i: jnp.maximum(i - ENCODE_STEPS, 0)
-    row = pl.BlockSpec((GROUP, 1, rows), lambda i, n, c: (current(i), 0, 0))
+    row = pl.BlockSpec((nblocks, 1, rows), lambda i, n, c: (0, 0, 0))
     whole = lambda i, n, c: (0, 0)
     anywhere = pl.BlockSpec(memory_space=pl.ANY)
     return pl.pallas_call(
@@ -340,7 +375,6 @@
             grid=(ENCODE_STEPS + groups,),
             in_specs=[anywhere] * 5
             + [
-                pl.BlockSpec((total, LANES), whole),
                 pl.BlockSpec((1, width), whole),
                 row,
                 row,
@@ -349,7 +383,6 @@
                 row,
                 row,
                 pl.BlockSpec((GROUP * rows, width), lambda i, n, c: (current(i), 0)),
-                anywhere,
                 anywhere,
             ],
             scratch_shapes=[
@@ -368,10 +401,9 @@
                 pltpu.VMEM((GROUP * HEADS, HIST, HIST), BF),
                 pltpu.VMEM((groups, GROUP * rows, width), BF),
                 pltpu.VMEM(shape, BF),
-                pltpu.VMEM(shape, BF),
                 pltpu.SemaphoreType.DMA((5,)),
                 pltpu.SemaphoreType.DMA((ENCODE_STEPS, 4)),
-                pltpu.SemaphoreType.DMA((2, side)),
+                pltpu.SemaphoreType.DMA((side,)),
             ],
         ),
         out_shape=[
@@ -379,9 +411,8 @@
             jax.ShapeDtypeStruct((nblocks, 1, rows), F32),
             jax.ShapeDtypeStruct((total, width), BF),
             jax.ShapeDtypeStruct(shape, BF),
-            jax.ShapeDtypeStruct(shape, BF),
         ],
-        compiler_params=pltpu.CompilerParams(vmem_limit_bytes=42 * 1024 * 1024),
+        compiler_params=pltpu.CompilerParams(vmem_limit_bytes=51 * 1024 * 1024),
         name="attention",
     )(
         counts,
@@ -390,8 +421,7 @@
         base,
         weights,
         queries.reshape(groups, GROUP * rows, width),
-        cand_t.reshape(pairs, 2, width // (2 * pairs), total),
-        mask,
+        cand_t,
         score_weight,
         own,
         labels,
@@ -486,23 +516,22 @@
 
     flat = candidates.reshape(-1, width)
     queries = jnp.dot(flat, query_weight, preferred_element_type=F32).astype(BF)
-    cand_t = flat.T
+    cand_t = flat.T.reshape(pairs, 2, width // loaders, -1)
     own = jnp.sum(candidates.astype(F32) * self_weight, -1)
 
     owner = block_owner[:, 0]
     here = lax.axis_index("user").astype(jnp.int32)
     far_x = lax.rem(owner // side - here // side + side, side)
     far_y = lax.rem(lax.rem(owner, side) - lax.rem(here, side) + side, side)
-    base, normed, mask = prepare(
+    base, normed = prepare(
         far_y * side + far_x, far_x * side + far_y, halves_a, halves_b, action_table
     )
     core = lax.rem(lax.axis_index("loader").astype(jnp.int32), 2)[None]
-    scores, error, slopes, mine, other = attention(
+    scores, error, slopes, other = attention(
         row_counts,
         core,
         normed,
         base,
-        mask,
         weights,
         queries,
         cand_t,
@@ -514,6 +543,7 @@
     )
 
     arrived = lax.ppermute(other, "loader", [(i, i ^ 1) for i in range(loaders)])
+    mine = gradient(core, cand_t, slopes, users)
     pieces = (mine.astype(F32) + arrived.astype(F32)).astype(BF)
     pieces = lax.all_to_all(pieces, "user", 0, 0, tiled=True)
     pieces = jnp.sum(pieces.astype(F32), 0).astype(BF)

time: 161 us -> 157 us (0.975)
  local copies, waits for them, and re-layouts: 9.82 us -> 4.63 us
    unnamed x32 -> x24, local copies, waits for them, and re-layouts: 6.42 us -> 1.43 us
  transfers between devices with their start and end apart: 21 -> 21, of which waited for: 8 -> 8; matrix products, arithmetic and copies ran while one was open for 8% -> 7% of each run, Pallas kernels for 4% -> 4%
where the time goes in v9:
time: 157 us
  blocking collectives  34.9 us (22%)
  starting transfers between devices  33.2 us (21%)
  waiting for transfers between devices  31.4 us (20%)
  Pallas kernels  27.3 us (17%)
  between operations  14.9 us (9%)
  other arithmetic  6 us (4%)
  local copies, waits for them, and re-layouts  4.63 us (3%)
  matrix products  4.51 us (3%)
    ppermute x18, starting transfers between devices, shift(): return lax.ppermute(array, 'user', moves)  27.1 us
    all_to_all x1, blocking collectives, body(): pieces = lax.all_to_all(pieces, 'user', 0, 0, tiled=True)  22.4 us
    pallas_call x1, Pallas kernels, attention(): pl.pallas_call(attention_kernel, grid_spec=pltpu.PrefetchScalarGridSpec(n...  16.9 us
    all_gather x1, waiting for transfers between devices, body(): lax.all_gather(join(mix_weight, out_weight), 'loader', axis=0, tiled=True)  16.6 us
    all_to_all x1, blocking collectives, body(): lax.all_to_all(pieces, 'loader', 0, 0, axis_index_groups=groups, tiled=True)  12.4 us
    ppermute x18, waiting for transfers between devices, shift(): return lax.ppermute(array, 'user', moves)  9.02 us
    pallas_call x1, Pallas kernels, prepare(): pl.pallas_call(functools.partial(prepare_kernel, nblocks), grid_spec=pltp...  5.86 us
    all_to_all x1, starting transfers between devices, body(): lax.all_to_all(jnp.broadcast_to(piece[None], (users,) + piece.shape), 'us...  5.71 us
  transfers between devices with their start and end apart: 21, of which 8 were waited for; matrix products, arithmetic and copies ran while one was open for 7% of the time, Pallas kernels for 4%

profile of v9, /device:TPU:2, one launch (start us, length us, event | category | flops | bytes accessed | tf_op | source)
XLA Modules:
  0.0 156.8 jit_solution(8335763796245794497)
XLA Ops:
  7.2 0.0 copy-start
  7.2 0.0 all-gather.2.cloned.1.call-start
  7.2 2.1 %join.1 = bf16[64,5120]{1,0:T(8,128)(2,1)} custom-call(bf16[64,4096]{1,0:T(8,128)(2,1)} %left.1, bf16[64,1024]{1,0:T(8,128)(2,1)} %right.1), custom_call_target="tpu_custom_call" | custom-call | tf_op jit(solution)/shard_map/join/pallas_call | solution.py:457
  9.3 0.0 all-gather.2.cloned.1.call-update
  9.4 0.0 copy-start.5
  10.1 0.7 convert_bitcast_fusion
  10.8 0.1 broadcast_in_dim.29
  10.9 1.1 concatenate.3
  12.0 2.2 %collective-permute-start.1 = (bf16[64,1152]{1,0:T(8,128)(2,1)S(1)}, bf16[64,1152]{1,0:T(8,128)(2,1)S(1)}, u32[]{:S(2)}, u32[]{:S(2)}) collective-permute-start(bf16[64,1152]{1,0:T(8,128)(2,1)S(1)} %get-tuple-element.21), channel_id=1, source_target_pairs={{128,0},{144,16},{160,32},{176,48},{192,64},{208,80},{224,96},{240... | collective-permute-start | bytes 442376 | tf_op jit(solution)/shard_map/ppermute | solution.py:436
  14.2 1.6 %collective-permute-start.2 = (bf16[64,1152]{1,0:T(8,128)(2,1)S(1)}, bf16[64,1152]{1,0:T(8,128)(2,1)S(1)}, u32[]{:S(2)}, u32[]{:S(2)}) collective-permute-start(bf16[64,1152]{1,0:T(8,128)(2,1)S(1)} %get-tuple-element.21), channel_id=1, source_target_pairs={{192,0},{208,16},{224,32},{240,48},{0,64},{16,80},{32,96},{48,112}... | collective-permute-start | bytes 442376 | tf_op jit(solution)/shard_map/ppermute | solution.py:436
  15.8 1.6 %collective-permute-start.10 = (bf16[64,1152]{1,0:T(8,128)(2,1)S(1)}, bf16[64,1152]{1,0:T(8,128)(2,1)S(1)}, u32[]{:S(2)}, u32[]{:S(2)}) collective-permute-start(bf16[64,1152]{1,0:T(8,128)(2,1)S(1)} %get-tuple-element.20), channel_id=1, source_target_pairs={{32,0},{48,16},{0,32},{16,48},{96,64},{112,80},{64,96},{80,112},{1... | collective-permute-start | bytes 442376 | tf_op jit(solution)/shard_map/ppermute | solution.py:436
  17.4 1.1 collective-permute-start.9
  18.5 1.0 collective-permute-start.11
  19.4 0.0 collective-permute-done.1
  19.4 2.2 %collective-permute-start = (bf16[64,1152]{1,0:T(8,128)(2,1)S(1)}, bf16[64,1152]{1,0:T(8,128)(2,1)S(1)}, u32[]{:S(2)}, u32[]{:S(2)}) collective-permute-start(bf16[64,1152]{1,0:T(8,128)(2,1)S(1)} %get-tuple-element.21), channel_id=1, source_target_pairs={{64,0},{80,16},{96,32},{112,48},{128,64},{144,80},{160,96},{176,11... | collective-permute-start | bytes 442376 | tf_op jit(solution)/shard_map/ppermute | solution.py:436
  21.6 0.8 collective-permute-done.2
  22.4 1.7 %collective-permute-start.6 = (bf16[2,64,1152]{2,1,0:T(8,128)(2,1)S(1)}, bf16[2,64,1152]{2,1,0:T(8,128)(2,1)S(1)}, u32[]{:S(2)}, u32[]{:S(2)}) collective-permute-start(bf16[2,64,1152]{2,1,0:T(8,128)(2,1)S(1)} %pad_maximum_fusion.1.refs_1_), channel_id=1, source_target_pairs={{48,0},{0,16},{16,32},{32,48},{112,64},{64,80},{80,96},{96,112},{1... | collective-permute-start | bytes 884744 | tf_op jit(solution)/shard_map/ppermute | solution.py:436
  24.1 0.8 collective-permute-done
  24.9 3.0 %collective-permute-start.4 = (bf16[2,64,1152]{2,1,0:T(8,128)(2,1)S(1)}, bf16[2,64,1152]{2,1,0:T(8,128)(2,1)S(1)}, u32[]{:S(2)}, u32[]{:S(2)}) collective-permute-start(bf16[2,64,1152]{2,1,0:T(8,128)(2,1)S(1)} %pad_maximum_fusion.1.refs_1_), channel_id=1, source_target_pairs={{16,0},{32,16},{48,32},{0,48},{80,64},{96,80},{112,96},{64,112},{1... | collective-permute-start | bytes 884744 | tf_op jit(solution)/shard_map/ppermute | solution.py:436
  27.9 0.8 pad_maximum_fusion.refs_0_
  28.7 0.0 collective-permute-done.10
  28.7 0.0 collective-permute-start.8
  28.7 0.0 collective-permute-done.11
  28.7 3.2 %collective-permute-start.3 = (bf16[2,64,1152]{2,1,0:T(8,128)(2,1)}, bf16[2,64,1152]{2,1,0:T(8,128)(2,1)}, u32[]{:S(2)}, u32[]{:S(2)}) collective-permute-start(bf16[2,64,1152]{2,1,0:T(8,128)(2,1)} %pad_maximum_fusion.refs_0_), channel_id=1, source_target_pairs={{16,0},{32,16},{48,32},{0,48},{80,64},{96,80},{112,96},{64,112},{1... | collective-permute-start | bytes 884744 | tf_op jit(solution)/shard_map/ppermute | solution.py:436
  31.9 0.7 pad_maximum_fusion.3.refs_9_
  32.7 2.0 %collective-permute-start.15 = (bf16[2,64,1152]{2,1,0:T(8,128)(2,1)}, bf16[2,64,1152]{2,1,0:T(8,128)(2,1)}, u32[]{:S(2)}, u32[]{:S(2)}) collective-permute-start(bf16[2,64,1152]{2,1,0:T(8,128)(2,1)} %pad_maximum_fusion.3.refs_9_), channel_id=1, source_target_pairs={{192,0},{208,16},{224,32},{240,48},{0,64},{16,80},{32,96},{48,112}... | collective-permute-start | bytes 884744 | tf_op jit(solution)/shard_map/ppermute | solution.py:436
  34.7 0.7 pad_maximum_fusion.2.refs_8_
  35.5 0.0 collective-permute-done.6.refs_7_
  35.5 0.0 collective-permute-start.13
  35.5 0.7 copy-done.9
  36.2 2.7 %collective-permute-start.12 = (bf16[2,64,1152]{2,1,0:T(8,128)(2,1)}, bf16[2,64,1152]{2,1,0:T(8,128)(2,1)}, u32[]{:S(2)}, u32[]{:S(2)}) collective-permute-start(bf16[2,64,1152]{2,1,0:T(8,128)(2,1)} %pad_maximum_fusion.2.refs_8_), channel_id=1, source_target_pairs={{64,0},{80,16},{96,32},{112,48},{128,64},{144,80},{160,96},{176,11... | collective-permute-start | bytes 884744 | tf_op jit(solution)/shard_map/ppermute | solution.py:436
  38.9 2.2 %convolution_convert_fusion = bf16[512,1024]{1,0:T(8,128)(2,1)} fusion(bf16[512,1024]{1,0:T(8,128)(2,1)S(1)} %bitcast.55, bf16[1024,1024]{1,0:T(8,128)(2,1)S(1)} %copy-done), kind=kOutput, calls=%fused_computation.3 | convolution fusion | flops 1074266112 | bytes 4194304 | tf_op jit(solution)/shard_map/dot_general | solution.py:518
  41.2 0.5 multiply_add_fusion
  41.7 0.0 collective-permute-done.8.refs_6_
  41.7 0.0 collective-permute-start.17
  41.7 0.0 collective-permute-done.3.refs_2_
  41.7 0.4 collective-permute-start.7
  42.1 0.0 collective-permute-done.15.refs_15_
  42.1 3.1 %collective-permute-start.5 = (bf16[2,64,1152]{2,1,0:T(8,128)(2,1)}, bf16[2,64,1152]{2,1,0:T(8,128)(2,1)}, u32[]{:S(2)}, u32[]{:S(2)}) collective-permute-start(bf16[2,64,1152]{2,1,0:T(8,128)(2,1)} %collective-permute-done.3.refs_2_), channel_id=1, source_target_pairs={{16,0},{32,16},{48,32},{0,48},{80,64},{96,80},{112,96},{64,112},{1... | collective-permute-start | bytes 884744 | tf_op jit(solution)/shard_map/ppermute | solution.py:436
  45.2 1.3 collective-permute-start.16
  46.6 2.5 %collective-permute-done.12.refs_10_ = bf16[2,64,1152]{2,1,0:T(8,128)(2,1)} collective-permute-done((bf16[2,64,1152]{2,1,0:T(8,128)(2,1)}, bf16[2,64,1152]{2,1,0:T(8,128)(2,1)}, u32[]{:S(2)}, u32[]{:S(2)}) %collective-permute-start.12) | collective-permute-done | bytes 294944 | tf_op jit(solution)/shard_map/ppermute | solution.py:436
  49.1 0.3 multiply_reduce_fusion
  49.4 1.3 copy.17
  50.7 0.5 multiply_add_fusion.1.place_a
  51.2 0.0 collective-permute-done.17.refs_14_
  51.2 0.0 collective-permute-done.7.refs_5_
  51.2 2.2 %collective-permute-done.16.refs_13_ = bf16[2,64,1152]{2,1,0:T(8,128)(2,1)} collective-permute-done((bf16[2,64,1152]{2,1,0:T(8,128)(2,1)}, bf16[2,64,1152]{2,1,0:T(8,128)(2,1)}, u32[]{:S(2)}, u32[]{:S(2)}) %collective-permute-start.16) | collective-permute-done | bytes 294944 | tf_op jit(solution)/shard_map/ppermute | solution.py:436
  53.5 2.7 %collective-permute-done.14.refs_12_ = bf16[2,64,1152]{2,1,0:T(8,128)(2,1)} collective-permute-done((bf16[2,64,1152]{2,1,0:T(8,128)(2,1)}, bf16[2,64,1152]{2,1,0:T(8,128)(2,1)}, u32[]{:S(2)}, u32[]{:S(2)}) %collective-permute-start.14) | collective-permute-done | bytes 294944 | tf_op jit(solution)/shard_map/ppermute | solution.py:436
  56.1 5.9 %prepare.1 = (f32[512,1024]{1,0:T(8,128)}, bf16[512,1024]{1,0:T(8,128)(2,1)}) custom-call(s32[4]{0:T(128)} %multiply_add_fusion.1.place_a, s32[4]{0:T(128)} %get-tuple-element.15.place_b, bf16[2,64,1152]{2,1,0:T(8,128)(2,1)} %pad_maximum_fusion.refs_0_, bf16[2,64,1152]{2,1,0:T(8,128)(2,1)} %copy-done.6, bf16[2,64,1152]{2,1,0:T(8,128)(2,1)} %collective-permute-done.3.refs_2_, ...), custom_call_target="tpu_custom_call" | custom-call | tf_op jit(solution)/shard_map/prepare/pallas_call | solution.py:84
  62.0 16.6 %all-gather.2.cloned.1.call-done.weights = bf16[1024,5120]{1,0:T(8,128)(2,1)} async-done(((bf16[64,5120]{1,0:T(8,128)(2,1)}), bf16[1024,5120]{1,0:T(8,128)(2,1)}) %all-gather.2.cloned.1.call-update) | async-done | bytes 10485776 | tf_op jit(solution)/shard_map/all_gather | solution.py:502
  78.6 16.9 %attention.1 = (f32[4,1,128]{2,1,0:T(1,128)}, f32[4,1,128]{2,1,0:T(1,128)S(1)}, bf16[512,1024]{1,0:T(8,128)(2,1)S(1)}, bf16[16,8,16,256]{3,2,1,0:T(8,128)(2,1)S(1)}) custom-call(s32[4]{0:T(128)S(1)} %copy-done.4, s32[1]{0:T(128)} %bitcast.core, bf16[512,1024]{1,0:T(8,128)(2,1)} %get-tuple-element.9.normed, f32[512,1024]{1,0:T(8,128)} %get-tuple-element.10.base, ...), custom_call_target="tpu_custom_call" | custom-call | tf_op jit(solution)/shard_map/attention/pallas_call | solution.py:371
  95.5 0.3 collective-permute-start.18
  95.8 0.8 gradient.1
  96.7 1.6 collective-permute-done.18
  98.2 0.3 add_convert_fusion
  98.6 22.4 %all_to_all.15 = bf16[16,8,16,256]{3,2,1,0:T(8,128)(2,1)} all-to-all(bf16[16,8,16,256]{3,2,1,0:T(8,128)(2,1)S(1)} %add_convert_fusion), channel_id=1, replica_groups=mesh['user'=16,'loader'=16] {'user'}, dimensions={0} | all-to-all | bytes 2097152 | tf_op jit(solution)/shard_map/all_to_all | solution.py:548
  121.0 1.4 reduce_sum.34
  122.4 12.4 %all_to_all.16 = bf16[8,16,256]{2,1,0:T(8,128)(2,1)S(1)} all-to-all(bf16[8,16,256]{2,1,0:T(8,128)(2,1)S(1)} %reduce_sum.34), channel_id=1, replica_groups={{0,2,4,6,8,10,12,14},{1,3,5,7,9,11,13,15},{16,18,20,22,24,26,28,30},{17..., dimensions={0} | all-to-all | bytes 131072 | tf_op jit(solution)/shard_map/all_to_all | solution.py:551
  134.9 0.7 broadcast_in_dim.34
  135.5 5.7 %all-to-all-start.2 = ((bf16[16,16,256]{2,1,0:T(8,128)(2,1)}), bf16[16,16,256]{2,1,0:T(8,128)(2,1)S(1)}, u32[]{:S(2)}, u32[]{:S(2)}) async-start(bf16[16,16,256]{2,1,0:T(8,128)(2,1)} %broadcast_in_dim.34), calls=%async_computation.2 | async-start | bytes 262144 | tf_op jit(solution)/shard_map/all_to_all | solution.py:553
  141.2 2.3 %add_convert_fusion.1 = bf16[512,1024]{1,0:T(8,128)(2,1)} fusion(bf16[512,1024]{1,0:T(8,128)(2,1)S(1)} %get-tuple-element.13.slopes, bf16[1024,1024]{1,0:T(8,128)(2,1)S(1)} %copy-done, f32[1024]{0:T(1024)S(1)} %copy-done.10, f32[512]{0:T(512)S(1)} %bitcast.54), kind=kOutput, calls=%fused_computation.1 | convolution fusion | flops 1075314688 | bytes 4200448 | tf_op jit(solution)/shard_map/dot_general | solution.py:558
  143.5 4.2 %all-to-all-done.2.pieces = bf16[16,16,256]{2,1,0:T(8,128)(2,1)S(1)} async-done(((bf16[16,16,256]{2,1,0:T(8,128)(2,1)}), bf16[16,16,256]{2,1,0:T(8,128)(2,1)S(1)}, u32[]{:S(2)}, u32[]{:S(2)}) %all-to-all-start.2) | async-done | bytes 131104 | tf_op jit(solution)/shard_map/all_to_all | solution.py:553
  147.7 0.6 copy-done.7
  148.3 1.6 %assemble.1 = f32[64,1024]{1,0:T(8,128)} custom-call(bf16[16,16,256]{2,1,0:T(8,128)(2,1)} %copy-done.7), custom_call_target="tpu_custom_call" | custom-call | tf_op jit(solution)/shard_map/assemble/pallas_call | solution.py:475
  (29 shorter events, 0.2 us)
Async XLA Ops:
  7.2 31.8 %copy-start = (bf16[1024,1024]{1,0:T(8,128)(2,1)S(1)}, bf16[1024,1024]{1,0:T(8,128)(2,1)}, u32[]{:S(2)}) copy-start(bf16[1024,1024]{1,0:T(8,128)(2,1)} %param.19) | copy-start | bytes 6291460
  7.2 71.4 %all-gather.2.cloned.1.call-start = ((), (), s32[]{:S(2)}) async-start(), calls=%async_computation.3 | async-start | bytes 11141120 | tf_op jit(solution)/shard_map/all_gather | solution.py:502
  9.4 29.6 %copy-start.5 = (bf16[4,128,1024]{2,1,0:T(8,128)(2,1)S(1)}, bf16[4,128,1024]{2,1,0:T(8,128)(2,1)}, u32[]{:S(2)}) copy-start(bf16[4,128,1024]{2,1,0:T(8,128)(2,1)} %param.22) | copy-start | bytes 3145732
  12.0 7.4 %collective-permute-start.1 = (bf16[64,1152]{1,0:T(8,128)(2,1)S(1)}, bf16[64,1152]{1,0:T(8,128)(2,1)S(1)}, u32[]{:S(2)}, u32[]{:S(2)}) collective-permute-start(bf16[64,1152]{1,0:T(8,128)(2,1)S(1)} %get-tuple-element.21), channel_id=1, source_target_pairs={{128,0},{144,16},{160,32},{176,48},{192,64},{208,80},{224,96},{240... | collective-permute-start | bytes 442376 | tf_op jit(solution)/shard_map/ppermute | solution.py:436
  14.2 8.2 %collective-permute-start.2 = (bf16[64,1152]{1,0:T(8,128)(2,1)S(1)}, bf16[64,1152]{1,0:T(8,128)(2,1)S(1)}, u32[]{:S(2)}, u32[]{:S(2)}) collective-permute-start(bf16[64,1152]{1,0:T(8,128)(2,1)S(1)} %get-tuple-element.21), channel_id=1, source_target_pairs={{192,0},{208,16},{224,32},{240,48},{0,64},{16,80},{32,96},{48,112}... | collective-permute-start | bytes 442376 | tf_op jit(solution)/shard_map/ppermute | solution.py:436
  15.8 12.9 %collective-permute-start.10 = (bf16[64,1152]{1,0:T(8,128)(2,1)S(1)}, bf16[64,1152]{1,0:T(8,128)(2,1)S(1)}, u32[]{:S(2)}, u32[]{:S(2)}) collective-permute-start(bf16[64,1152]{1,0:T(8,128)(2,1)S(1)} %get-tuple-element.20), channel_id=1, source_target_pairs={{32,0},{48,16},{0,32},{16,48},{96,64},{112,80},{64,96},{80,112},{1... | collective-permute-start | bytes 442376 | tf_op jit(solution)/shard_map/ppermute | solution.py:436
  17.4 15.3 %collective-permute-start.9 = (bf16[64,1152]{1,0:T(8,128)(2,1)S(1)}, bf16[64,1152]{1,0:T(8,128)(2,1)S(1)}, u32[]{:S(2)}, u32[]{:S(2)}) collective-permute-start(bf16[64,1152]{1,0:T(8,128)(2,1)S(1)} %get-tuple-element.20), channel_id=1, source_target_pairs={{16,0},{32,16},{48,32},{0,48},{80,64},{96,80},{112,96},{64,112},{1... | collective-permute-start | bytes 442376 | tf_op jit(solution)/shard_map/ppermute | solution.py:436
  18.5 10.3 %collective-permute-start.11 = (bf16[64,1152]{1,0:T(8,128)(2,1)S(1)}, bf16[64,1152]{1,0:T(8,128)(2,1)S(1)}, u32[]{:S(2)}, u32[]{:S(2)}) collective-permute-start(bf16[64,1152]{1,0:T(8,128)(2,1)S(1)} %get-tuple-element.20), channel_id=1, source_target_pairs={{48,0},{0,16},{16,32},{32,48},{112,64},{64,80},{80,96},{96,112},{1... | collective-permute-start | bytes 442376 | tf_op jit(solution)/shard_map/ppermute | solution.py:436
  19.4 5.5 %collective-permute-start = (bf16[64,1152]{1,0:T(8,128)(2,1)S(1)}, bf16[64,1152]{1,0:T(8,128)(2,1)S(1)}, u32[]{:S(2)}, u32[]{:S(2)}) collective-permute-start(bf16[64,1152]{1,0:T(8,128)(2,1)S(1)} %get-tuple-element.21), channel_id=1, source_target_pairs={{64,0},{80,16},{96,32},{112,48},{128,64},{144,80},{160,96},{176,11... | collective-permute-start | bytes 442376 | tf_op jit(solution)/shard_map/ppermute | solution.py:436
  22.4 18.8 %copy-start.6 = (bf16[2,64,1152]{2,1,0:T(8,128)(2,1)}, bf16[2,64,1152]{2,1,0:T(8,128)(2,1)S(1)}, u32[]{:S(2)}) copy-start(bf16[2,64,1152]{2,1,0:T(8,128)(2,1)S(1)} %pad_maximum_fusion.1.refs_1_) | copy-start | bytes 884740
  22.4 13.0 %collective-permute-start.6 = (bf16[2,64,1152]{2,1,0:T(8,128)(2,1)S(1)}, bf16[2,64,1152]{2,1,0:T(8,128)(2,1)S(1)}, u32[]{:S(2)}, u32[]{:S(2)}) collective-permute-start(bf16[2,64,1152]{2,1,0:T(8,128)(2,1)S(1)} %pad_maximum_fusion.1.refs_1_), channel_id=1, source_target_pairs={{48,0},{0,16},{16,32},{32,48},{112,64},{64,80},{80,96},{96,112},{1... | collective-permute-start | bytes 884744 | tf_op jit(solution)/shard_map/ppermute | solution.py:436
  24.9 10.5 %collective-permute-start.4 = (bf16[2,64,1152]{2,1,0:T(8,128)(2,1)S(1)}, bf16[2,64,1152]{2,1,0:T(8,128)(2,1)S(1)}, u32[]{:S(2)}, u32[]{:S(2)}) collective-permute-start(bf16[2,64,1152]{2,1,0:T(8,128)(2,1)S(1)} %pad_maximum_fusion.1.refs_1_), channel_id=1, source_target_pairs={{16,0},{32,16},{48,32},{0,48},{80,64},{96,80},{112,96},{64,112},{1... | collective-permute-start | bytes 884744 | tf_op jit(solution)/shard_map/ppermute | solution.py:436
  28.7 13.0 %collective-permute-start.8 = (bf16[2,64,1152]{2,1,0:T(8,128)(2,1)}, bf16[2,64,1152]{2,1,0:T(8,128)(2,1)}, u32[]{:S(2)}, u32[]{:S(2)}) collective-permute-start(bf16[2,64,1152]{2,1,0:T(8,128)(2,1)} %pad_maximum_fusion.refs_0_), channel_id=1, source_target_pairs={{48,0},{0,16},{16,32},{32,48},{112,64},{64,80},{80,96},{96,112},{1... | collective-permute-start | bytes 884744 | tf_op jit(solution)/shard_map/ppermute | solution.py:436
  28.7 13.0 %collective-permute-start.3 = (bf16[2,64,1152]{2,1,0:T(8,128)(2,1)}, bf16[2,64,1152]{2,1,0:T(8,128)(2,1)}, u32[]{:S(2)}, u32[]{:S(2)}) collective-permute-start(bf16[2,64,1152]{2,1,0:T(8,128)(2,1)} %pad_maximum_fusion.refs_0_), channel_id=1, source_target_pairs={{16,0},{32,16},{48,32},{0,48},{80,64},{96,80},{112,96},{64,112},{1... | collective-permute-start | bytes 884744 | tf_op jit(solution)/shard_map/ppermute | solution.py:436
  32.7 9.4 %collective-permute-start.15 = (bf16[2,64,1152]{2,1,0:T(8,128)(2,1)}, bf16[2,64,1152]{2,1,0:T(8,128)(2,1)}, u32[]{:S(2)}, u32[]{:S(2)}) collective-permute-start(bf16[2,64,1152]{2,1,0:T(8,128)(2,1)} %pad_maximum_fusion.3.refs_9_), channel_id=1, source_target_pairs={{192,0},{208,16},{224,32},{240,48},{0,64},{16,80},{32,96},{48,112}... | collective-permute-start | bytes 884744 | tf_op jit(solution)/shard_map/ppermute | solution.py:436
  35.5 20.7 %copy-start.8 = (bf16[2,64,1152]{2,1,0:T(8,128)(2,1)}, bf16[2,64,1152]{2,1,0:T(8,128)(2,1)S(1)}, u32[]{:S(2)}) copy-start(bf16[2,64,1152]{2,1,0:T(8,128)(2,1)S(1)} %collective-permute-done.6.refs_7_) | copy-start | bytes 884740
  35.5 9.8 %collective-permute-start.13 = (bf16[2,64,1152]{2,1,0:T(8,128)(2,1)}, bf16[2,64,1152]{2,1,0:T(8,128)(2,1)}, u32[]{:S(2)}, u32[]{:S(2)}) collective-permute-start(bf16[2,64,1152]{2,1,0:T(8,128)(2,1)} %pad_maximum_fusion.3.refs_9_), channel_id=1, source_target_pairs={{64,0},{80,16},{96,32},{112,48},{128,64},{144,80},{160,96},{176,11... | collective-permute-start | bytes 884744 | tf_op jit(solution)/shard_map/ppermute | solution.py:436
  35.5 0.7 copy-start.9
  36.2 12.9 %collective-permute-start.12 = (bf16[2,64,1152]{2,1,0:T(8,128)(2,1)}, bf16[2,64,1152]{2,1,0:T(8,128)(2,1)}, u32[]{:S(2)}, u32[]{:S(2)}) collective-permute-start(bf16[2,64,1152]{2,1,0:T(8,128)(2,1)} %pad_maximum_fusion.2.refs_8_), channel_id=1, source_target_pairs={{64,0},{80,16},{96,32},{112,48},{128,64},{144,80},{160,96},{176,11... | collective-permute-start | bytes 884744 | tf_op jit(solution)/shard_map/ppermute | solution.py:436
  38.9 2.3 %copy-start.11 = (s32[4,1]{0,1:T(1,128)S(1)}, s32[4,1]{0,1:T(1,128)}, u32[]{:S(2)}) copy-start(s32[4,1]{0,1:T(1,128)} %param.23) | copy-start | bytes 52
  38.9 10.2 %copy-start.10 = (f32[1024]{0:T(1024)S(1)}, f32[1024]{0:T(1024)}, u32[]{:S(2)}) copy-start(f32[1024]{0:T(1024)} %param.21) | copy-start | bytes 12292
  41.7 9.5 %collective-permute-start.17 = (bf16[2,64,1152]{2,1,0:T(8,128)(2,1)}, bf16[2,64,1152]{2,1,0:T(8,128)(2,1)}, u32[]{:S(2)}, u32[]{:S(2)}) collective-permute-start(bf16[2,64,1152]{2,1,0:T(8,128)(2,1)} %pad_maximum_fusion.2.refs_8_), channel_id=1, source_target_pairs={{192,0},{208,16},{224,32},{240,48},{0,64},{16,80},{32,96},{48,112}... | collective-permute-start | bytes 884744 | tf_op jit(solution)/shard_map/ppermute | solution.py:436
  41.7 9.5 %collective-permute-start.7 = (bf16[2,64,1152]{2,1,0:T(8,128)(2,1)S(1)}, bf16[2,64,1152]{2,1,0:T(8,128)(2,1)}, u32[]{:S(2)}, u32[]{:S(2)}) collective-permute-start(bf16[2,64,1152]{2,1,0:T(8,128)(2,1)S(1)} %collective-permute-done.6.refs_7_), channel_id=1, source_target_pairs={{48,0},{0,16},{16,32},{32,48},{112,64},{64,80},{80,96},{96,112},{1... | collective-permute-start | bytes 884744 | tf_op jit(solution)/shard_map/ppermute | solution.py:436
  42.1 9.1 %collective-permute-start.5 = (bf16[2,64,1152]{2,1,0:T(8,128)(2,1)}, bf16[2,64,1152]{2,1,0:T(8,128)(2,1)}, u32[]{:S(2)}, u32[]{:S(2)}) collective-permute-start(bf16[2,64,1152]{2,1,0:T(8,128)(2,1)} %collective-permute-done.3.refs_2_), channel_id=1, source_target_pairs={{16,0},{32,16},{48,32},{0,48},{80,64},{96,80},{112,96},{64,112},{1... | collective-permute-start | bytes 884744 | tf_op jit(solution)/shard_map/ppermute | solution.py:436
  45.2 8.2 %collective-permute-start.16 = (bf16[2,64,1152]{2,1,0:T(8,128)(2,1)}, bf16[2,64,1152]{2,1,0:T(8,128)(2,1)}, u32[]{:S(2)}, u32[]{:S(2)}) collective-permute-start(bf16[2,64,1152]{2,1,0:T(8,128)(2,1)} %collective-permute-done.15.refs_15_), channel_id=1, source_target_pairs={{192,0},{208,16},{224,32},{240,48},{0,64},{16,80},{32,96},{48,112}... | collective-permute-start | bytes 884744 | tf_op jit(solution)/shard_map/ppermute | solution.py:436
  49.1 7.0 %collective-permute-start.14 = (bf16[2,64,1152]{2,1,0:T(8,128)(2,1)}, bf16[2,64,1152]{2,1,0:T(8,128)(2,1)}, u32[]{:S(2)}, u32[]{:S(2)}) collective-permute-start(bf16[2,64,1152]{2,1,0:T(8,128)(2,1)} %collective-permute-done.12.refs_10_), channel_id=1, source_target_pairs={{64,0},{80,16},{96,32},{112,48},{128,64},{144,80},{160,96},{176,11... | collective-permute-start | bytes 884744 | tf_op jit(solution)/shard_map/ppermute | solution.py:436
  56.1 22.5 %copy-start.2 = (f32[1024]{0:T(1024)S(1)}, f32[1024]{0:T(1024)}, u32[]{:S(2)}) copy-start(f32[1024]{0:T(1024)} %param.20) | copy-start | bytes 12292
  56.1 22.5 %copy-start.3 = (f32[4,128]{1,0:T(4,128)S(1)}, f32[4,128]{1,0:T(4,128)}, u32[]{:S(2)}) copy-start(f32[4,128]{1,0:T(4,128)} %param.25) | copy-start | bytes 6148
  56.1 22.5 %copy-start.4 = (s32[4]{0:T(128)S(1)}, s32[4]{0:T(128)}, u32[]{:S(2)}) copy-start(s32[4]{0:T(128)} %counts.1) | copy-start | bytes 52
  78.6 17.2 %copy-start.1 = (bf16[512,1024]{0,1:T(8,128)(2,1)S(1)}, bf16[512,1024]{0,1:T(8,128)(2,1)}, u32[]{:S(2)}) copy-start(bf16[512,1024]{0,1:T(8,128)(2,1)} %copy.17) | copy-start | bytes 3145732
  95.5 2.7 %collective-permute-start.18 = (bf16[16,8,16,256]{3,2,1,0:T(8,128)(2,1)S(1)}, bf16[16,8,16,256]{3,2,1,0:T(8,128)(2,1)S(1)}, u32[]{:S(2)}, u32[]{:S(2)}) collective-permute-start(bf16[16,8,16,256]{3,2,1,0:T(8,128)(2,1)S(1)} %get-tuple-element.14), channel_id=1, source_target_pairs={{0,1},{1,0},{2,3},{3,2},{4,5},{5,4},{6,7},{7,6},{8,9},{9,8},{10,11... | collective-permute-start | bytes 3145736 | tf_op jit(solution)/shard_map/ppermute | solution.py:545
  135.5 12.1 %all-to-all-start.2 = ((bf16[16,16,256]{2,1,0:T(8,128)(2,1)}), bf16[16,16,256]{2,1,0:T(8,128)(2,1)S(1)}, u32[]{:S(2)}, u32[]{:S(2)}) async-start(bf16[16,16,256]{2,1,0:T(8,128)(2,1)} %broadcast_in_dim.34), calls=%async_computation.2 | async-start | bytes 262144 | tf_op jit(solution)/shard_map/all_to_all | solution.py:553
  147.7 0.7 copy-start.7
Sparse Core Ops, SparseCore 0:
  9.8 68.7 all-gather.1

commit v10 on v9

--- a/solution.py
+++ b/solution.py
@@ -138,13 +138,11 @@
     encoded_s,
     logit_s,
     weight_s,
-    slope_s,
     other_s,
     sems,
     mix_sems,
     grad_sems,
 ):
-    step = pl.program_id(0)
     total, width = normed_s.shape
     pair = 2 * LANES
 
@@ -160,15 +158,13 @@
     query_copy = pltpu.make_async_copy(queries, queries_s, sems.at[3])
     cand_copy = pltpu.make_async_copy(cand_t, cand_s, sems.at[4])
 
-    @pl.when(step == 0)
-    def _():
-        normed_copy.start()
-        for group in range(4):
-            mix_copy(0, group).start()
-        normed_copy.wait()
-
-    @pl.when(step < ENCODE_STEPS)
-    def _():
+    normed_copy.start()
+    for group in range(4):
+        mix_copy(0, group).start()
+    normed_copy.wait()
+
+    @pl.loop(0, ENCODE_STEPS, unroll=True)
+    def _(step):
         for group in range(4):
             mix_copy(step, group).wait()
 
@@ -211,26 +207,23 @@
         for n, (k, part) in enumerate(units):
             mixed_s[2 * step + k, part] = dot(weight_s[n], qkv_s[k, part, :LANES])
 
-    @pl.when(step == ENCODE_STEPS - 1)
-    def _():
-        square = mixed_s[0] * mixed_s[0]
-        for h in range(1, HEADS):
-            square = square + mixed_s[h] * mixed_s[h]
-        scale = lax.rsqrt(jnp.sum(square, -1, keepdims=True) * (1.0 / width) + 1e-06)
-        for h in range(HEADS):
-            gated_s[:, h * LANES : (h + 1) * LANES] = (mixed_s[h] * scale * gate_s[h]).astype(BF)
-        base_copy.wait()
-        out_copy.wait()
-        for n in range(width // pair):
-            cols = slice(n * pair, (n + 1) * pair)
-            value = (base_s[:, cols] + dot(gated_s[...], out_s[:, cols])).astype(BF)
-            encoded_s[:, :, cols] = value.reshape(total // (GROUP * HIST), GROUP * HIST, pair)
-        query_copy.wait()
-        cand_copy.wait()
-
-    @pl.when(step >= ENCODE_STEPS)
-    def _():
-        now = step - ENCODE_STEPS
+    square = mixed_s[0] * mixed_s[0]
+    for h in range(1, HEADS):
+        square = square + mixed_s[h] * mixed_s[h]
+    scale = lax.rsqrt(jnp.sum(square, -1, keepdims=True) * (1.0 / width) + 1e-06)
+    for h in range(HEADS):
+        gated_s[:, h * LANES : (h + 1) * LANES] = (mixed_s[h] * scale * gate_s[h]).astype(BF)
+    base_copy.wait()
+    out_copy.wait()
+    for n in range(width // pair):
+        cols = slice(n * pair, (n + 1) * pair)
+        value = (base_s[:, cols] + dot(gated_s[...], out_s[:, cols])).astype(BF)
+        encoded_s[:, :, cols] = value.reshape(total // (GROUP * HIST), GROUP * HIST, pair)
+    query_copy.wait()
+    cand_copy.wait()
+
+    @pl.loop(0, total // (GROUP * HIST), unroll=True)
+    def _(now):
         lane = lax.broadcasted_iota(jnp.int32, (HEADS, width), 1) // LANES
         head_row = lax.broadcasted_iota(jnp.int32, (HEADS, width), 0)
         spread_weight = jnp.where(lane == head_row, score_weight[...], 0.0)
@@ -271,27 +264,24 @@
             for h in range(HEADS):
                 direction = logit_s[g * HEADS + h].astype(BF).astype(F32)
                 slope = (err_rows * direction).astype(BF)
-                slopes[part, heads[h]] = slope
-                slope_s[now, part, heads[h]] = slope
-
-    @pl.when(step == pl.num_programs(0) - 1)
-    def _():
-        pairs, _, piece, _ = cand_s.shape
-        _, _, tall, wide = other.shape
-        right = width // wide
-        down = piece // tall
-        copies = []
-        for n in range(right):
-            cols = slice(n * wide, (n + 1) * wide)
-            slope = slope_s[:, :, cols].reshape(-1, wide)
-            rows = cand_s[:, 1 - core[0]].reshape(pairs * piece, -1)
-            place_pieces(dot(rows, slope).astype(BF), other_s, n * down, piece)
-            chunk = pl.ds(n * down, down)
-            copy = pltpu.make_async_copy(other_s.at[chunk], other.at[chunk], grad_sems.at[n])
-            copy.start()
-            copies.append(copy)
-        for copy in copies:
-            copy.wait()
+                slopes[now, part, heads[h]] = slope
+
+    pairs, _, piece, _ = cand_s.shape
+    _, _, tall, wide = other.shape
+    right = width // wide
+    down = piece // tall
+    copies = []
+    for n in range(right):
+        cols = slice(n * wide, (n + 1) * wide)
+        slope = slopes[:, :, cols].reshape(-1, wide)
+        rows = cand_s[:, 1 - core[0]].reshape(pairs * piece, -1)
+        place_pieces(dot(rows, slope).astype(BF), other_s, n * down, piece)
+        chunk = pl.ds(n * down, down)
+        copy = pltpu.make_async_copy(other_s.at[chunk], other.at[chunk], grad_sems.at[n])
+        copy.start()
+        copies.append(copy)
+    for copy in copies:
+        copy.wait()
 
 
 def place_pieces(grad, store, first, piece):
@@ -364,7 +354,6 @@
     groups = nblocks // GROUP
     side = math.isqrt(users)
     shape = (users, pairs, width // (2 * pairs * side), width // side)
-    current = lambda i: jnp.maximum(i - ENCODE_STEPS, 0)
     row = pl.BlockSpec((nblocks, 1, rows), lambda i, n, c: (0, 0, 0))
     whole = lambda i, n, c: (0, 0)
     anywhere = pl.BlockSpec(memory_space=pl.ANY)
@@ -372,7 +361,7 @@
         attention_kernel,
         grid_spec=pltpu.PrefetchScalarGridSpec(
             num_scalar_prefetch=2,
-            grid=(ENCODE_STEPS + groups,),
+            grid=(1,),
             in_specs=[anywhere] * 5
             + [
                 pl.BlockSpec((1, width), whole),
@@ -382,7 +371,7 @@
             out_specs=[
                 row,
                 row,
-                pl.BlockSpec((GROUP * rows, width), lambda i, n, c: (current(i), 0)),
+                pl.BlockSpec((groups, GROUP * rows, width), lambda i, n, c: (0, 0, 0)),
                 anywhere,
             ],
             scratch_shapes=[
@@ -399,7 +388,6 @@
                 pltpu.VMEM((groups, GROUP * rows, width), BF),
                 pltpu.VMEM((GROUP * HEADS, HIST, HIST), F32),
                 pltpu.VMEM((GROUP * HEADS, HIST, HIST), BF),
-                pltpu.VMEM((groups, GROUP * rows, width), BF),
                 pltpu.VMEM(shape, BF),
                 pltpu.SemaphoreType.DMA((5,)),
                 pltpu.SemaphoreType.DMA((ENCODE_STEPS, 4)),
@@ -409,7 +397,7 @@
         out_shape=[
             jax.ShapeDtypeStruct((nblocks, 1, rows), F32),
             jax.ShapeDtypeStruct((nblocks, 1, rows), F32),
-            jax.ShapeDtypeStruct((total, width), BF),
+            jax.ShapeDtypeStruct((groups, GROUP * rows, width), BF),
             jax.ShapeDtypeStruct(shape, BF),
         ],
         compiler_params=pltpu.CompilerParams(vmem_limit_bytes=51 * 1024 * 1024),
@@ -543,6 +531,7 @@
     )
 
     arrived = lax.ppermute(other, "loader", [(i, i ^ 1) for i in range(loaders)])
+    slopes = slopes.reshape(-1, width)
     mine = gradient(core, cand_t, slopes, users)
     pieces = (mine.astype(F32) + arrived.astype(F32)).astype(BF)
     pieces = lax.all_to_all(pieces, "user", 0, 0, tiled=True)

time: 157 us -> 157 us (level)
  no operation moved by 1% of the time
where the time goes in v10:
time: 157 us; the launch traced here: 156 us
  blocking collectives  34.9 us (22%)
  starting transfers between devices  33.2 us (21%)
  waiting for transfers between devices  31.4 us (20%)
  Pallas kernels  26.7 us (17%)
  between operations  14.9 us (9%)
  other arithmetic  6 us (4%)
  local copies, waits for them, and re-layouts  4.63 us (3%)
  matrix products  4.51 us (3%)
    ppermute x18, starting transfers between devices, shift(): return lax.ppermute(array, 'user', moves)  27.1 us
    all_to_all x1, blocking collectives, body(): pieces = lax.all_to_all(pieces, 'user', 0, 0, tiled=True)  22.4 us
    all_gather x1, waiting for transfers between devices, body(): lax.all_gather(join(mix_weight, out_weight), 'loader', axis=0, tiled=True)  16.6 us
    pallas_call x1, Pallas kernels, attention(): pl.pallas_call(attention_kernel, grid_spec=pltpu.PrefetchScalarGridSpec(n...  16.2 us
    all_to_all x1, blocking collectives, body(): lax.all_to_all(pieces, 'loader', 0, 0, axis_index_groups=groups, tiled=True)  12.4 us
    ppermute x18, waiting for transfers between devices, shift(): return lax.ppermute(array, 'user', moves)  9.02 us
    pallas_call x1, Pallas kernels, prepare(): pl.pallas_call(functools.partial(prepare_kernel, nblocks), grid_spec=pltp...  5.86 us
    all_to_all x1, starting transfers between devices, body(): lax.all_to_all(jnp.broadcast_to(piece[None], (users,) + piece.shape), 'us...  5.71 us
  transfers between devices with their start and end apart: 21, of which 8 were waited for; matrix products, arithmetic and copies ran while one was open for 7% of the time, Pallas kernels for 4%

profile of v10, /device:TPU:2, one launch (start us, length us, event | category | flops | bytes accessed | tf_op | source)
XLA Modules:
  0.0 156.1 jit_solution(9533802946702030784)
XLA Ops:
  7.2 0.0 copy-start
  7.2 0.0 all-gather.2.cloned.1.call-start
  7.2 2.1 %join.1 = bf16[64,5120]{1,0:T(8,128)(2,1)} custom-call(bf16[64,4096]{1,0:T(8,128)(2,1)} %left.1, bf16[64,1024]{1,0:T(8,128)(2,1)} %right.1), custom_call_target="tpu_custom_call" | custom-call | tf_op jit(solution)/shard_map/join/pallas_call | solution.py:445
  9.3 0.0 all-gather.2.cloned.1.call-update
  9.4 0.0 copy-start.5
  10.1 0.7 convert_bitcast_fusion
  10.8 0.1 broadcast_in_dim.29
  10.9 1.1 concatenate.3
  12.0 2.2 %collective-permute-start.1 = (bf16[64,1152]{1,0:T(8,128)(2,1)S(1)}, bf16[64,1152]{1,0:T(8,128)(2,1)S(1)}, u32[]{:S(2)}, u32[]{:S(2)}) collective-permute-start(bf16[64,1152]{1,0:T(8,128)(2,1)S(1)} %get-tuple-element.21), channel_id=1, source_target_pairs={{128,0},{144,16},{160,32},{176,48},{192,64},{208,80},{224,96},{240... | collective-permute-start | bytes 442376 | tf_op jit(solution)/shard_map/ppermute | solution.py:424
  14.2 1.6 %collective-permute-start.2 = (bf16[64,1152]{1,0:T(8,128)(2,1)S(1)}, bf16[64,1152]{1,0:T(8,128)(2,1)S(1)}, u32[]{:S(2)}, u32[]{:S(2)}) collective-permute-start(bf16[64,1152]{1,0:T(8,128)(2,1)S(1)} %get-tuple-element.21), channel_id=1, source_target_pairs={{192,0},{208,16},{224,32},{240,48},{0,64},{16,80},{32,96},{48,112}... | collective-permute-start | bytes 442376 | tf_op jit(solution)/shard_map/ppermute | solution.py:424
  15.8 1.6 %collective-permute-start.10 = (bf16[64,1152]{1,0:T(8,128)(2,1)S(1)}, bf16[64,1152]{1,0:T(8,128)(2,1)S(1)}, u32[]{:S(2)}, u32[]{:S(2)}) collective-permute-start(bf16[64,1152]{1,0:T(8,128)(2,1)S(1)} %get-tuple-element.20), channel_id=1, source_target_pairs={{32,0},{48,16},{0,32},{16,48},{96,64},{112,80},{64,96},{80,112},{1... | collective-permute-start | bytes 442376 | tf_op jit(solution)/shard_map/ppermute | solution.py:424
  17.4 1.1 collective-permute-start.9
  18.5 1.0 collective-permute-start.11
  19.4 0.0 collective-permute-done.1
  19.4 2.2 %collective-permute-start = (bf16[64,1152]{1,0:T(8,128)(2,1)S(1)}, bf16[64,1152]{1,0:T(8,128)(2,1)S(1)}, u32[]{:S(2)}, u32[]{:S(2)}) collective-permute-start(bf16[64,1152]{1,0:T(8,128)(2,1)S(1)} %get-tuple-element.21), channel_id=1, source_target_pairs={{64,0},{80,16},{96,32},{112,48},{128,64},{144,80},{160,96},{176,11... | collective-permute-start | bytes 442376 | tf_op jit(solution)/shard_map/ppermute | solution.py:424
  21.6 0.8 collective-permute-done.2
  22.4 1.7 %collective-permute-start.6 = (bf16[2,64,1152]{2,1,0:T(8,128)(2,1)S(1)}, bf16[2,64,1152]{2,1,0:T(8,128)(2,1)S(1)}, u32[]{:S(2)}, u32[]{:S(2)}) collective-permute-start(bf16[2,64,1152]{2,1,0:T(8,128)(2,1)S(1)} %pad_maximum_fusion.1.refs_1_), channel_id=1, source_target_pairs={{48,0},{0,16},{16,32},{32,48},{112,64},{64,80},{80,96},{96,112},{1... | collective-permute-start | bytes 884744 | tf_op jit(solution)/shard_map/ppermute | solution.py:424
  24.1 0.8 collective-permute-done
  24.9 3.0 %collective-permute-start.4 = (bf16[2,64,1152]{2,1,0:T(8,128)(2,1)S(1)}, bf16[2,64,1152]{2,1,0:T(8,128)(2,1)S(1)}, u32[]{:S(2)}, u32[]{:S(2)}) collective-permute-start(bf16[2,64,1152]{2,1,0:T(8,128)(2,1)S(1)} %pad_maximum_fusion.1.refs_1_), channel_id=1, source_target_pairs={{16,0},{32,16},{48,32},{0,48},{80,64},{96,80},{112,96},{64,112},{1... | collective-permute-start | bytes 884744 | tf_op jit(solution)/shard_map/ppermute | solution.py:424
  27.9 0.8 pad_maximum_fusion.refs_0_
  28.7 0.0 collective-permute-done.10
  28.7 0.0 collective-permute-start.8
  28.7 0.0 collective-permute-done.11
  28.7 3.2 %collective-permute-start.3 = (bf16[2,64,1152]{2,1,0:T(8,128)(2,1)}, bf16[2,64,1152]{2,1,0:T(8,128)(2,1)}, u32[]{:S(2)}, u32[]{:S(2)}) collective-permute-start(bf16[2,64,1152]{2,1,0:T(8,128)(2,1)} %pad_maximum_fusion.refs_0_), channel_id=1, source_target_pairs={{16,0},{32,16},{48,32},{0,48},{80,64},{96,80},{112,96},{64,112},{1... | collective-permute-start | bytes 884744 | tf_op jit(solution)/shard_map/ppermute | solution.py:424
  31.9 0.7 pad_maximum_fusion.3.refs_9_
  32.7 2.0 %collective-permute-start.15 = (bf16[2,64,1152]{2,1,0:T(8,128)(2,1)}, bf16[2,64,1152]{2,1,0:T(8,128)(2,1)}, u32[]{:S(2)}, u32[]{:S(2)}) collective-permute-start(bf16[2,64,1152]{2,1,0:T(8,128)(2,1)} %pad_maximum_fusion.3.refs_9_), channel_id=1, source_target_pairs={{192,0},{208,16},{224,32},{240,48},{0,64},{16,80},{32,96},{48,112}... | collective-permute-start | bytes 884744 | tf_op jit(solution)/shard_map/ppermute | solution.py:424
  34.7 0.7 pad_maximum_fusion.2.refs_8_
  35.5 0.0 collective-permute-done.6.refs_7_
  35.5 0.0 collective-permute-start.13
  35.5 0.7 copy-done.9
  36.2 2.7 %collective-permute-start.12 = (bf16[2,64,1152]{2,1,0:T(8,128)(2,1)}, bf16[2,64,1152]{2,1,0:T(8,128)(2,1)}, u32[]{:S(2)}, u32[]{:S(2)}) collective-permute-start(bf16[2,64,1152]{2,1,0:T(8,128)(2,1)} %pad_maximum_fusion.2.refs_8_), channel_id=1, source_target_pairs={{64,0},{80,16},{96,32},{112,48},{128,64},{144,80},{160,96},{176,11... | collective-permute-start | bytes 884744 | tf_op jit(solution)/shard_map/ppermute | solution.py:424
  38.9 2.2 %convolution_convert_fusion = bf16[512,1024]{1,0:T(8,128)(2,1)} fusion(bf16[512,1024]{1,0:T(8,128)(2,1)S(1)} %bitcast.58, bf16[1024,1024]{1,0:T(8,128)(2,1)S(1)} %copy-done), kind=kOutput, calls=%fused_computation.3 | convolution fusion | flops 1074266112 | bytes 4194304 | tf_op jit(solution)/shard_map/dot_general | solution.py:506
  41.2 0.5 multiply_add_fusion
  41.7 0.0 collective-permute-done.8.refs_6_
  41.7 0.0 collective-permute-start.17
  41.7 0.0 collective-permute-done.3.refs_2_
  41.7 0.4 collective-permute-start.7
  42.1 0.0 collective-permute-done.15.refs_15_
  42.1 3.1 %collective-permute-start.5 = (bf16[2,64,1152]{2,1,0:T(8,128)(2,1)}, bf16[2,64,1152]{2,1,0:T(8,128)(2,1)}, u32[]{:S(2)}, u32[]{:S(2)}) collective-permute-start(bf16[2,64,1152]{2,1,0:T(8,128)(2,1)} %collective-permute-done.3.refs_2_), channel_id=1, source_target_pairs={{16,0},{32,16},{48,32},{0,48},{80,64},{96,80},{112,96},{64,112},{1... | collective-permute-start | bytes 884744 | tf_op jit(solution)/shard_map/ppermute | solution.py:424
  45.2 1.3 collective-permute-start.16
  46.6 2.5 %collective-permute-done.12.refs_10_ = bf16[2,64,1152]{2,1,0:T(8,128)(2,1)} collective-permute-done((bf16[2,64,1152]{2,1,0:T(8,128)(2,1)}, bf16[2,64,1152]{2,1,0:T(8,128)(2,1)}, u32[]{:S(2)}, u32[]{:S(2)}) %collective-permute-start.12) | collective-permute-done | bytes 294944 | tf_op jit(solution)/shard_map/ppermute | solution.py:424
  49.1 0.3 multiply_reduce_fusion
  49.4 1.3 copy.17
  50.7 0.5 multiply_add_fusion.1.place_a
  51.2 0.0 collective-permute-done.17.refs_14_
  51.2 0.0 collective-permute-done.7.refs_5_
  51.2 2.2 %collective-permute-done.16.refs_13_ = bf16[2,64,1152]{2,1,0:T(8,128)(2,1)} collective-permute-done((bf16[2,64,1152]{2,1,0:T(8,128)(2,1)}, bf16[2,64,1152]{2,1,0:T(8,128)(2,1)}, u32[]{:S(2)}, u32[]{:S(2)}) %collective-permute-start.16) | collective-permute-done | bytes 294944 | tf_op jit(solution)/shard_map/ppermute | solution.py:424
  53.5 2.7 %collective-permute-done.14.refs_12_ = bf16[2,64,1152]{2,1,0:T(8,128)(2,1)} collective-permute-done((bf16[2,64,1152]{2,1,0:T(8,128)(2,1)}, bf16[2,64,1152]{2,1,0:T(8,128)(2,1)}, u32[]{:S(2)}, u32[]{:S(2)}) %collective-permute-start.14) | collective-permute-done | bytes 294944 | tf_op jit(solution)/shard_map/ppermute | solution.py:424
  56.1 5.9 %prepare.1 = (f32[512,1024]{1,0:T(8,128)}, bf16[512,1024]{1,0:T(8,128)(2,1)}) custom-call(s32[4]{0:T(128)} %multiply_add_fusion.1.place_a, s32[4]{0:T(128)} %get-tuple-element.15.place_b, bf16[2,64,1152]{2,1,0:T(8,128)(2,1)} %pad_maximum_fusion.refs_0_, bf16[2,64,1152]{2,1,0:T(8,128)(2,1)} %copy-done.6, bf16[2,64,1152]{2,1,0:T(8,128)(2,1)} %collective-permute-done.3.refs_2_, ...), custom_call_target="tpu_custom_call" | custom-call | tf_op jit(solution)/shard_map/prepare/pallas_call | solution.py:84
  62.0 16.6 %all-gather.2.cloned.1.call-done.weights = bf16[1024,5120]{1,0:T(8,128)(2,1)} async-done(((bf16[64,5120]{1,0:T(8,128)(2,1)}), bf16[1024,5120]{1,0:T(8,128)(2,1)}) %all-gather.2.cloned.1.call-update) | async-done | bytes 10485776 | tf_op jit(solution)/shard_map/all_gather | solution.py:490
  78.6 16.2 %attention.1 = (f32[4,1,128]{2,1,0:T(1,128)}, f32[4,1,128]{2,1,0:T(1,128)S(1)}, bf16[2,256,1024]{2,1,0:T(8,128)(2,1)S(1)}, bf16[16,8,16,256]{3,2,1,0:T(8,128)(2,1)S(1)}) custom-call(s32[4]{0:T(128)S(1)} %copy-done.4, s32[1]{0:T(128)} %bitcast.core, bf16[512,1024]{1,0:T(8,128)(2,1)} %get-tuple-element.9.normed, f32[512,1024]{1,0:T(8,128)} %get-tuple-element.10.base, ...), custom_call_target="tpu_custom_call" | custom-call | tf_op jit(solution)/shard_map/attention/pallas_call | solution.py:360
  94.9 0.3 collective-permute-start.18
  95.2 0.8 gradient.1
  96.0 1.6 collective-permute-done.18
  97.6 0.3 add_convert_fusion
  98.0 22.4 %all_to_all.15 = bf16[16,8,16,256]{3,2,1,0:T(8,128)(2,1)} all-to-all(bf16[16,8,16,256]{3,2,1,0:T(8,128)(2,1)S(1)} %add_convert_fusion), channel_id=1, replica_groups=mesh['user'=16,'loader'=16] {'user'}, dimensions={0} | all-to-all | bytes 2097152 | tf_op jit(solution)/shard_map/all_to_all | solution.py:537
  120.4 1.4 reduce_sum.34
  121.8 12.4 %all_to_all.16 = bf16[8,16,256]{2,1,0:T(8,128)(2,1)S(1)} all-to-all(bf16[8,16,256]{2,1,0:T(8,128)(2,1)S(1)} %reduce_sum.34), channel_id=1, replica_groups={{0,2,4,6,8,10,12,14},{1,3,5,7,9,11,13,15},{16,18,20,22,24,26,28,30},{17..., dimensions={0} | all-to-all | bytes 131072 | tf_op jit(solution)/shard_map/all_to_all | solution.py:540
  134.2 0.7 broadcast_in_dim.34
  134.9 5.7 %all-to-all-start.2 = ((bf16[16,16,256]{2,1,0:T(8,128)(2,1)}), bf16[16,16,256]{2,1,0:T(8,128)(2,1)S(1)}, u32[]{:S(2)}, u32[]{:S(2)}) async-start(bf16[16,16,256]{2,1,0:T(8,128)(2,1)} %broadcast_in_dim.34), calls=%async_computation.2 | async-start | bytes 262144 | tf_op jit(solution)/shard_map/all_to_all | solution.py:542
  140.6 2.3 %add_convert_fusion.1 = bf16[512,1024]{1,0:T(8,128)(2,1)} fusion(bf16[512,1024]{1,0:T(8,128)(2,1)S(1)} %bitcast.53, bf16[1024,1024]{1,0:T(8,128)(2,1)S(1)} %copy-done, f32[1024]{0:T(1024)S(1)} %copy-done.10, f32[512]{0:T(512)S(1)} %bitcast.57), kind=kOutput, calls=%fused_computation.1 | convolution fusion | flops 1075314688 | bytes 4200448 | tf_op jit(solution)/shard_map/dot_general | solution.py:547
  142.9 4.2 %all-to-all-done.2.pieces = bf16[16,16,256]{2,1,0:T(8,128)(2,1)S(1)} async-done(((bf16[16,16,256]{2,1,0:T(8,128)(2,1)}), bf16[16,16,256]{2,1,0:T(8,128)(2,1)S(1)}, u32[]{:S(2)}, u32[]{:S(2)}) %all-to-all-start.2) | async-done | bytes 131104 | tf_op jit(solution)/shard_map/all_to_all | solution.py:542
  147.0 0.6 copy-done.7
  147.7 1.6 %assemble.1 = f32[64,1024]{1,0:T(8,128)} custom-call(bf16[16,16,256]{2,1,0:T(8,128)(2,1)} %copy-done.7), custom_call_target="tpu_custom_call" | custom-call | tf_op jit(solution)/shard_map/assemble/pallas_call | solution.py:463
  (29 shorter events, 0.2 us)
Async XLA Ops:
  7.2 31.8 %copy-start = (bf16[1024,1024]{1,0:T(8,128)(2,1)S(1)}, bf16[1024,1024]{1,0:T(8,128)(2,1)}, u32[]{:S(2)}) copy-start(bf16[1024,1024]{1,0:T(8,128)(2,1)} %param.19) | copy-start | bytes 6291460
  7.2 71.4 %all-gather.2.cloned.1.call-start = ((), (), s32[]{:S(2)}) async-start(), calls=%async_computation.3 | async-start | bytes 11141120 | tf_op jit(solution)/shard_map/all_gather | solution.py:490
  9.4 29.6 %copy-start.5 = (bf16[4,128,1024]{2,1,0:T(8,128)(2,1)S(1)}, bf16[4,128,1024]{2,1,0:T(8,128)(2,1)}, u32[]{:S(2)}) copy-start(bf16[4,128,1024]{2,1,0:T(8,128)(2,1)} %param.22) | copy-start | bytes 3145732
  12.0 7.4 %collective-permute-start.1 = (bf16[64,1152]{1,0:T(8,128)(2,1)S(1)}, bf16[64,1152]{1,0:T(8,128)(2,1)S(1)}, u32[]{:S(2)}, u32[]{:S(2)}) collective-permute-start(bf16[64,1152]{1,0:T(8,128)(2,1)S(1)} %get-tuple-element.21), channel_id=1, source_target_pairs={{128,0},{144,16},{160,32},{176,48},{192,64},{208,80},{224,96},{240... | collective-permute-start | bytes 442376 | tf_op jit(solution)/shard_map/ppermute | solution.py:424
  14.2 8.2 %collective-permute-start.2 = (bf16[64,1152]{1,0:T(8,128)(2,1)S(1)}, bf16[64,1152]{1,0:T(8,128)(2,1)S(1)}, u32[]{:S(2)}, u32[]{:S(2)}) collective-permute-start(bf16[64,1152]{1,0:T(8,128)(2,1)S(1)} %get-tuple-element.21), channel_id=1, source_target_pairs={{192,0},{208,16},{224,32},{240,48},{0,64},{16,80},{32,96},{48,112}... | collective-permute-start | bytes 442376 | tf_op jit(solution)/shard_map/ppermute | solution.py:424
  15.8 12.9 %collective-permute-start.10 = (bf16[64,1152]{1,0:T(8,128)(2,1)S(1)}, bf16[64,1152]{1,0:T(8,128)(2,1)S(1)}, u32[]{:S(2)}, u32[]{:S(2)}) collective-permute-start(bf16[64,1152]{1,0:T(8,128)(2,1)S(1)} %get-tuple-element.20), channel_id=1, source_target_pairs={{32,0},{48,16},{0,32},{16,48},{96,64},{112,80},{64,96},{80,112},{1... | collective-permute-start | bytes 442376 | tf_op jit(solution)/shard_map/ppermute | solution.py:424
  17.4 15.3 %collective-permute-start.9 = (bf16[64,1152]{1,0:T(8,128)(2,1)S(1)}, bf16[64,1152]{1,0:T(8,128)(2,1)S(1)}, u32[]{:S(2)}, u32[]{:S(2)}) collective-permute-start(bf16[64,1152]{1,0:T(8,128)(2,1)S(1)} %get-tuple-element.20), channel_id=1, source_target_pairs={{16,0},{32,16},{48,32},{0,48},{80,64},{96,80},{112,96},{64,112},{1... | collective-permute-start | bytes 442376 | tf_op jit(solution)/shard_map/ppermute | solution.py:424
  18.5 10.3 %collective-permute-start.11 = (bf16[64,1152]{1,0:T(8,128)(2,1)S(1)}, bf16[64,1152]{1,0:T(8,128)(2,1)S(1)}, u32[]{:S(2)}, u32[]{:S(2)}) collective-permute-start(bf16[64,1152]{1,0:T(8,128)(2,1)S(1)} %get-tuple-element.20), channel_id=1, source_target_pairs={{48,0},{0,16},{16,32},{32,48},{112,64},{64,80},{80,96},{96,112},{1... | collective-permute-start | bytes 442376 | tf_op jit(solution)/shard_map/ppermute | solution.py:424
  19.4 5.5 %collective-permute-start = (bf16[64,1152]{1,0:T(8,128)(2,1)S(1)}, bf16[64,1152]{1,0:T(8,128)(2,1)S(1)}, u32[]{:S(2)}, u32[]{:S(2)}) collective-permute-start(bf16[64,1152]{1,0:T(8,128)(2,1)S(1)} %get-tuple-element.21), channel_id=1, source_target_pairs={{64,0},{80,16},{96,32},{112,48},{128,64},{144,80},{160,96},{176,11... | collective-permute-start | bytes 442376 | tf_op jit(solution)/shard_map/ppermute | solution.py:424
  22.4 18.8 %copy-start.6 = (bf16[2,64,1152]{2,1,0:T(8,128)(2,1)}, bf16[2,64,1152]{2,1,0:T(8,128)(2,1)S(1)}, u32[]{:S(2)}) copy-start(bf16[2,64,1152]{2,1,0:T(8,128)(2,1)S(1)} %pad_maximum_fusion.1.refs_1_) | copy-start | bytes 884740
  22.4 13.0 %collective-permute-start.6 = (bf16[2,64,1152]{2,1,0:T(8,128)(2,1)S(1)}, bf16[2,64,1152]{2,1,0:T(8,128)(2,1)S(1)}, u32[]{:S(2)}, u32[]{:S(2)}) collective-permute-start(bf16[2,64,1152]{2,1,0:T(8,128)(2,1)S(1)} %pad_maximum_fusion.1.refs_1_), channel_id=1, source_target_pairs={{48,0},{0,16},{16,32},{32,48},{112,64},{64,80},{80,96},{96,112},{1... | collective-permute-start | bytes 884744 | tf_op jit(solution)/shard_map/ppermute | solution.py:424
  24.9 10.5 %collective-permute-start.4 = (bf16[2,64,1152]{2,1,0:T(8,128)(2,1)S(1)}, bf16[2,64,1152]{2,1,0:T(8,128)(2,1)S(1)}, u32[]{:S(2)}, u32[]{:S(2)}) collective-permute-start(bf16[2,64,1152]{2,1,0:T(8,128)(2,1)S(1)} %pad_maximum_fusion.1.refs_1_), channel_id=1, source_target_pairs={{16,0},{32,16},{48,32},{0,48},{80,64},{96,80},{112,96},{64,112},{1... | collective-permute-start | bytes 884744 | tf_op jit(solution)/shard_map/ppermute | solution.py:424
  28.7 13.0 %collective-permute-start.8 = (bf16[2,64,1152]{2,1,0:T(8,128)(2,1)}, bf16[2,64,1152]{2,1,0:T(8,128)(2,1)}, u32[]{:S(2)}, u32[]{:S(2)}) collective-permute-start(bf16[2,64,1152]{2,1,0:T(8,128)(2,1)} %pad_maximum_fusion.refs_0_), channel_id=1, source_target_pairs={{48,0},{0,16},{16,32},{32,48},{112,64},{64,80},{80,96},{96,112},{1... | collective-permute-start | bytes 884744 | tf_op jit(solution)/shard_map/ppermute | solution.py:424
  28.7 13.0 %collective-permute-start.3 = (bf16[2,64,1152]{2,1,0:T(8,128)(2,1)}, bf16[2,64,1152]{2,1,0:T(8,128)(2,1)}, u32[]{:S(2)}, u32[]{:S(2)}) collective-permute-start(bf16[2,64,1152]{2,1,0:T(8,128)(2,1)} %pad_maximum_fusion.refs_0_), channel_id=1, source_target_pairs={{16,0},{32,16},{48,32},{0,48},{80,64},{96,80},{112,96},{64,112},{1... | collective-permute-start | bytes 884744 | tf_op jit(solution)/shard_map/ppermute | solution.py:424
  32.7 9.4 %collective-permute-start.15 = (bf16[2,64,1152]{2,1,0:T(8,128)(2,1)}, bf16[2,64,1152]{2,1,0:T(8,128)(2,1)}, u32[]{:S(2)}, u32[]{:S(2)}) collective-permute-start(bf16[2,64,1152]{2,1,0:T(8,128)(2,1)} %pad_maximum_fusion.3.refs_9_), channel_id=1, source_target_pairs={{192,0},{208,16},{224,32},{240,48},{0,64},{16,80},{32,96},{48,112}... | collective-permute-start | bytes 884744 | tf_op jit(solution)/shard_map/ppermute | solution.py:424
  35.5 20.7 %copy-start.8 = (bf16[2,64,1152]{2,1,0:T(8,128)(2,1)}, bf16[2,64,1152]{2,1,0:T(8,128)(2,1)S(1)}, u32[]{:S(2)}) copy-start(bf16[2,64,1152]{2,1,0:T(8,128)(2,1)S(1)} %collective-permute-done.6.refs_7_) | copy-start | bytes 884740
  35.5 9.8 %collective-permute-start.13 = (bf16[2,64,1152]{2,1,0:T(8,128)(2,1)}, bf16[2,64,1152]{2,1,0:T(8,128)(2,1)}, u32[]{:S(2)}, u32[]{:S(2)}) collective-permute-start(bf16[2,64,1152]{2,1,0:T(8,128)(2,1)} %pad_maximum_fusion.3.refs_9_), channel_id=1, source_target_pairs={{64,0},{80,16},{96,32},{112,48},{128,64},{144,80},{160,96},{176,11... | collective-permute-start | bytes 884744 | tf_op jit(solution)/shard_map/ppermute | solution.py:424
  35.5 0.7 copy-start.9
  36.2 12.9 %collective-permute-start.12 = (bf16[2,64,1152]{2,1,0:T(8,128)(2,1)}, bf16[2,64,1152]{2,1,0:T(8,128)(2,1)}, u32[]{:S(2)}, u32[]{:S(2)}) collective-permute-start(bf16[2,64,1152]{2,1,0:T(8,128)(2,1)} %pad_maximum_fusion.2.refs_8_), channel_id=1, source_target_pairs={{64,0},{80,16},{96,32},{112,48},{128,64},{144,80},{160,96},{176,11... | collective-permute-start | bytes 884744 | tf_op jit(solution)/shard_map/ppermute | solution.py:424
  38.9 2.3 %copy-start.11 = (s32[4,1]{0,1:T(1,128)S(1)}, s32[4,1]{0,1:T(1,128)}, u32[]{:S(2)}) copy-start(s32[4,1]{0,1:T(1,128)} %param.23) | copy-start | bytes 52
  38.9 10.2 %copy-start.10 = (f32[1024]{0:T(1024)S(1)}, f32[1024]{0:T(1024)}, u32[]{:S(2)}) copy-start(f32[1024]{0:T(1024)} %param.21) | copy-start | bytes 12292
  41.7 9.5 %collective-permute-start.17 = (bf16[2,64,1152]{2,1,0:T(8,128)(2,1)}, bf16[2,64,1152]{2,1,0:T(8,128)(2,1)}, u32[]{:S(2)}, u32[]{:S(2)}) collective-permute-start(bf16[2,64,1152]{2,1,0:T(8,128)(2,1)} %pad_maximum_fusion.2.refs_8_), channel_id=1, source_target_pairs={{192,0},{208,16},{224,32},{240,48},{0,64},{16,80},{32,96},{48,112}... | collective-permute-start | bytes 884744 | tf_op jit(solution)/shard_map/ppermute | solution.py:424
  41.7 9.5 %collective-permute-start.7 = (bf16[2,64,1152]{2,1,0:T(8,128)(2,1)S(1)}, bf16[2,64,1152]{2,1,0:T(8,128)(2,1)}, u32[]{:S(2)}, u32[]{:S(2)}) collective-permute-start(bf16[2,64,1152]{2,1,0:T(8,128)(2,1)S(1)} %collective-permute-done.6.refs_7_), channel_id=1, source_target_pairs={{48,0},{0,16},{16,32},{32,48},{112,64},{64,80},{80,96},{96,112},{1... | collective-permute-start | bytes 884744 | tf_op jit(solution)/shard_map/ppermute | solution.py:424
  42.1 9.1 %collective-permute-start.5 = (bf16[2,64,1152]{2,1,0:T(8,128)(2,1)}, bf16[2,64,1152]{2,1,0:T(8,128)(2,1)}, u32[]{:S(2)}, u32[]{:S(2)}) collective-permute-start(bf16[2,64,1152]{2,1,0:T(8,128)(2,1)} %collective-permute-done.3.refs_2_), channel_id=1, source_target_pairs={{16,0},{32,16},{48,32},{0,48},{80,64},{96,80},{112,96},{64,112},{1... | collective-permute-start | bytes 884744 | tf_op jit(solution)/shard_map/ppermute | solution.py:424
  45.2 8.2 %collective-permute-start.16 = (bf16[2,64,1152]{2,1,0:T(8,128)(2,1)}, bf16[2,64,1152]{2,1,0:T(8,128)(2,1)}, u32[]{:S(2)}, u32[]{:S(2)}) collective-permute-start(bf16[2,64,1152]{2,1,0:T(8,128)(2,1)} %collective-permute-done.15.refs_15_), channel_id=1, source_target_pairs={{192,0},{208,16},{224,32},{240,48},{0,64},{16,80},{32,96},{48,112}... | collective-permute-start | bytes 884744 | tf_op jit(solution)/shard_map/ppermute | solution.py:424
  49.1 7.0 %collective-permute-start.14 = (bf16[2,64,1152]{2,1,0:T(8,128)(2,1)}, bf16[2,64,1152]{2,1,0:T(8,128)(2,1)}, u32[]{:S(2)}, u32[]{:S(2)}) collective-permute-start(bf16[2,64,1152]{2,1,0:T(8,128)(2,1)} %collective-permute-done.12.refs_10_), channel_id=1, source_target_pairs={{64,0},{80,16},{96,32},{112,48},{128,64},{144,80},{160,96},{176,11... | collective-permute-start | bytes 884744 | tf_op jit(solution)/shard_map/ppermute | solution.py:424
  56.1 22.5 %copy-start.2 = (f32[1024]{0:T(1024)S(1)}, f32[1024]{0:T(1024)}, u32[]{:S(2)}) copy-start(f32[1024]{0:T(1024)} %param.20) | copy-start | bytes 12292
  56.1 22.5 %copy-start.3 = (f32[4,128]{1,0:T(4,128)S(1)}, f32[4,128]{1,0:T(4,128)}, u32[]{:S(2)}) copy-start(f32[4,128]{1,0:T(4,128)} %param.25) | copy-start | bytes 6148
  56.1 22.5 %copy-start.4 = (s32[4]{0:T(128)S(1)}, s32[4]{0:T(128)}, u32[]{:S(2)}) copy-start(s32[4]{0:T(128)} %counts.1) | copy-start | bytes 52
  78.6 16.6 %copy-start.1 = (bf16[512,1024]{0,1:T(8,128)(2,1)S(1)}, bf16[512,1024]{0,1:T(8,128)(2,1)}, u32[]{:S(2)}) copy-start(bf16[512,1024]{0,1:T(8,128)(2,1)} %copy.17) | copy-start | bytes 3145732
  94.9 2.7 %collective-permute-start.18 = (bf16[16,8,16,256]{3,2,1,0:T(8,128)(2,1)S(1)}, bf16[16,8,16,256]{3,2,1,0:T(8,128)(2,1)S(1)}, u32[]{:S(2)}, u32[]{:S(2)}) collective-permute-start(bf16[16,8,16,256]{3,2,1,0:T(8,128)(2,1)S(1)} %get-tuple-element.14), channel_id=1, source_target_pairs={{0,1},{1,0},{2,3},{3,2},{4,5},{5,4},{6,7},{7,6},{8,9},{9,8},{10,11... | collective-permute-start | bytes 3145736 | tf_op jit(solution)/shard_map/ppermute | solution.py:533
  134.9 12.1 %all-to-all-start.2 = ((bf16[16,16,256]{2,1,0:T(8,128)(2,1)}), bf16[16,16,256]{2,1,0:T(8,128)(2,1)S(1)}, u32[]{:S(2)}, u32[]{:S(2)}) async-start(bf16[16,16,256]{2,1,0:T(8,128)(2,1)} %broadcast_in_dim.34), calls=%async_computation.2 | async-start | bytes 262144 | tf_op jit(solution)/shard_map/all_to_all | solution.py:542
  147.0 0.7 copy-start.7
Sparse Core Ops, SparseCore 0:
  9.8 68.7 all-gather.1

commit v11 on v10

--- a/solution.py
+++ b/solution.py
@@ -107,7 +107,7 @@
 
 
 ENCODE_STEPS = HEADS // 2
-GROUP = 2
+GROUP = 4
 
 
 def attention_kernel(

time: 157 us -> 156 us (level)
  no operation moved by 1% of the time
where the time goes in v11:
time: 156 us
  blocking collectives  34.9 us (22%)
  starting transfers between devices  33.2 us (21%)
  waiting for transfers between devices  31.4 us (20%)
  Pallas kernels  26.5 us (17%)
  between operations  14.9 us (10%)
  other arithmetic  6 us (4%)
  local copies, waits for them, and re-layouts  4.63 us (3%)
  matrix products  4.5 us (3%)
    ppermute x18, starting transfers between devices, shift(): return lax.ppermute(array, 'user', moves)  27.1 us
    all_to_all x1, blocking collectives, body(): pieces = lax.all_to_all(pieces, 'user', 0, 0, tiled=True)  22.4 us
    all_gather x1, waiting for transfers between devices, body(): lax.all_gather(join(mix_weight, out_weight), 'loader', axis=0, tiled=True)  16.6 us
    pallas_call x1, Pallas kernels, attention(): pl.pallas_call(attention_kernel, grid_spec=pltpu.PrefetchScalarGridSpec(n...  16 us
    all_to_all x1, blocking collectives, body(): lax.all_to_all(pieces, 'loader', 0, 0, axis_index_groups=groups, tiled=True)  12.4 us
    ppermute x18, waiting for transfers between devices, shift(): return lax.ppermute(array, 'user', moves)  9.02 us
    pallas_call x1, Pallas kernels, prepare(): pl.pallas_call(functools.partial(prepare_kernel, nblocks), grid_spec=pltp...  5.86 us
    all_to_all x1, starting transfers between devices, body(): lax.all_to_all(jnp.broadcast_to(piece[None], (users,) + piece.shape), 'us...  5.71 us
  transfers between devices with their start and end apart: 21, of which 8 were waited for; matrix products, arithmetic and copies ran while one was open for 7% of the time, Pallas kernels for 4%

profile of v11, /device:TPU:2, one launch (start us, length us, event | category | flops | bytes accessed | tf_op | source)
XLA Modules:
  0.0 155.9 jit_solution(2300362994082619234)
XLA Ops:
  7.2 0.0 copy-start
  7.2 0.0 all-gather.2.cloned.1.call-start
  7.2 2.1 %join.1 = bf16[64,5120]{1,0:T(8,128)(2,1)} custom-call(bf16[64,4096]{1,0:T(8,128)(2,1)} %left.1, bf16[64,1024]{1,0:T(8,128)(2,1)} %right.1), custom_call_target="tpu_custom_call" | custom-call | tf_op jit(solution)/shard_map/join/pallas_call | solution.py:445
  9.3 0.0 all-gather.2.cloned.1.call-update
  9.4 0.0 copy-start.5
  10.1 0.7 convert_bitcast_fusion
  10.8 0.1 broadcast_in_dim.29
  10.9 1.1 concatenate.3
  12.0 2.2 %collective-permute-start.1 = (bf16[64,1152]{1,0:T(8,128)(2,1)S(1)}, bf16[64,1152]{1,0:T(8,128)(2,1)S(1)}, u32[]{:S(2)}, u32[]{:S(2)}) collective-permute-start(bf16[64,1152]{1,0:T(8,128)(2,1)S(1)} %get-tuple-element.21), channel_id=1, source_target_pairs={{128,0},{144,16},{160,32},{176,48},{192,64},{208,80},{224,96},{240... | collective-permute-start | bytes 442376 | tf_op jit(solution)/shard_map/ppermute | solution.py:424
  14.2 1.6 %collective-permute-start.2 = (bf16[64,1152]{1,0:T(8,128)(2,1)S(1)}, bf16[64,1152]{1,0:T(8,128)(2,1)S(1)}, u32[]{:S(2)}, u32[]{:S(2)}) collective-permute-start(bf16[64,1152]{1,0:T(8,128)(2,1)S(1)} %get-tuple-element.21), channel_id=1, source_target_pairs={{192,0},{208,16},{224,32},{240,48},{0,64},{16,80},{32,96},{48,112}... | collective-permute-start | bytes 442376 | tf_op jit(solution)/shard_map/ppermute | solution.py:424
  15.8 1.6 %collective-permute-start.10 = (bf16[64,1152]{1,0:T(8,128)(2,1)S(1)}, bf16[64,1152]{1,0:T(8,128)(2,1)S(1)}, u32[]{:S(2)}, u32[]{:S(2)}) collective-permute-start(bf16[64,1152]{1,0:T(8,128)(2,1)S(1)} %get-tuple-element.20), channel_id=1, source_target_pairs={{32,0},{48,16},{0,32},{16,48},{96,64},{112,80},{64,96},{80,112},{1... | collective-permute-start | bytes 442376 | tf_op jit(solution)/shard_map/ppermute | solution.py:424
  17.4 1.1 collective-permute-start.9
  18.5 1.0 collective-permute-start.11
  19.4 0.0 collective-permute-done.1
  19.4 2.2 %collective-permute-start = (bf16[64,1152]{1,0:T(8,128)(2,1)S(1)}, bf16[64,1152]{1,0:T(8,128)(2,1)S(1)}, u32[]{:S(2)}, u32[]{:S(2)}) collective-permute-start(bf16[64,1152]{1,0:T(8,128)(2,1)S(1)} %get-tuple-element.21), channel_id=1, source_target_pairs={{64,0},{80,16},{96,32},{112,48},{128,64},{144,80},{160,96},{176,11... | collective-permute-start | bytes 442376 | tf_op jit(solution)/shard_map/ppermute | solution.py:424
  21.6 0.8 collective-permute-done.2
  22.4 1.7 %collective-permute-start.6 = (bf16[2,64,1152]{2,1,0:T(8,128)(2,1)S(1)}, bf16[2,64,1152]{2,1,0:T(8,128)(2,1)S(1)}, u32[]{:S(2)}, u32[]{:S(2)}) collective-permute-start(bf16[2,64,1152]{2,1,0:T(8,128)(2,1)S(1)} %pad_maximum_fusion.1.refs_1_), channel_id=1, source_target_pairs={{48,0},{0,16},{16,32},{32,48},{112,64},{64,80},{80,96},{96,112},{1... | collective-permute-start | bytes 884744 | tf_op jit(solution)/shard_map/ppermute | solution.py:424
  24.1 0.8 collective-permute-done
  24.9 3.0 %collective-permute-start.4 = (bf16[2,64,1152]{2,1,0:T(8,128)(2,1)S(1)}, bf16[2,64,1152]{2,1,0:T(8,128)(2,1)S(1)}, u32[]{:S(2)}, u32[]{:S(2)}) collective-permute-start(bf16[2,64,1152]{2,1,0:T(8,128)(2,1)S(1)} %pad_maximum_fusion.1.refs_1_), channel_id=1, source_target_pairs={{16,0},{32,16},{48,32},{0,48},{80,64},{96,80},{112,96},{64,112},{1... | collective-permute-start | bytes 884744 | tf_op jit(solution)/shard_map/ppermute | solution.py:424
  27.9 0.8 pad_maximum_fusion.refs_0_
  28.7 0.0 collective-permute-done.10
  28.7 0.0 collective-permute-start.8
  28.7 0.0 collective-permute-done.11
  28.7 3.2 %collective-permute-start.3 = (bf16[2,64,1152]{2,1,0:T(8,128)(2,1)}, bf16[2,64,1152]{2,1,0:T(8,128)(2,1)}, u32[]{:S(2)}, u32[]{:S(2)}) collective-permute-start(bf16[2,64,1152]{2,1,0:T(8,128)(2,1)} %pad_maximum_fusion.refs_0_), channel_id=1, source_target_pairs={{16,0},{32,16},{48,32},{0,48},{80,64},{96,80},{112,96},{64,112},{1... | collective-permute-start | bytes 884744 | tf_op jit(solution)/shard_map/ppermute | solution.py:424
  31.9 0.7 pad_maximum_fusion.3.refs_9_
  32.7 2.0 %collective-permute-start.15 = (bf16[2,64,1152]{2,1,0:T(8,128)(2,1)}, bf16[2,64,1152]{2,1,0:T(8,128)(2,1)}, u32[]{:S(2)}, u32[]{:S(2)}) collective-permute-start(bf16[2,64,1152]{2,1,0:T(8,128)(2,1)} %pad_maximum_fusion.3.refs_9_), channel_id=1, source_target_pairs={{192,0},{208,16},{224,32},{240,48},{0,64},{16,80},{32,96},{48,112}... | collective-permute-start | bytes 884744 | tf_op jit(solution)/shard_map/ppermute | solution.py:424
  34.7 0.7 pad_maximum_fusion.2.refs_8_
  35.5 0.0 collective-permute-done.6.refs_7_
  35.5 0.0 collective-permute-start.13
  35.5 0.7 copy-done.9
  36.2 2.7 %collective-permute-start.12 = (bf16[2,64,1152]{2,1,0:T(8,128)(2,1)}, bf16[2,64,1152]{2,1,0:T(8,128)(2,1)}, u32[]{:S(2)}, u32[]{:S(2)}) collective-permute-start(bf16[2,64,1152]{2,1,0:T(8,128)(2,1)} %pad_maximum_fusion.2.refs_8_), channel_id=1, source_target_pairs={{64,0},{80,16},{96,32},{112,48},{128,64},{144,80},{160,96},{176,11... | collective-permute-start | bytes 884744 | tf_op jit(solution)/shard_map/ppermute | solution.py:424
  38.9 2.2 %fusion.queries = bf16[1,512,1024]{2,1,0:T(8,128)(2,1)} fusion(bf16[512,1024]{1,0:T(8,128)(2,1)S(1)} %bitcast.59, bf16[1024,1024]{1,0:T(8,128)(2,1)S(1)} %copy-done), kind=kOutput, calls=%fused_computation.4 | convolution fusion | flops 1074266112 | bytes 4194304 | tf_op jit(solution)/shard_map/dot_general | solution.py:506
  41.2 0.5 multiply_add_fusion
  41.7 0.0 collective-permute-done.8.refs_6_
  41.7 0.0 collective-permute-start.17
  41.7 0.0 collective-permute-done.3.refs_2_
  41.7 0.4 collective-permute-start.7
  42.1 0.0 collective-permute-done.15.refs_15_
  42.1 3.1 %collective-permute-start.5 = (bf16[2,64,1152]{2,1,0:T(8,128)(2,1)}, bf16[2,64,1152]{2,1,0:T(8,128)(2,1)}, u32[]{:S(2)}, u32[]{:S(2)}) collective-permute-start(bf16[2,64,1152]{2,1,0:T(8,128)(2,1)} %collective-permute-done.3.refs_2_), channel_id=1, source_target_pairs={{16,0},{32,16},{48,32},{0,48},{80,64},{96,80},{112,96},{64,112},{1... | collective-permute-start | bytes 884744 | tf_op jit(solution)/shard_map/ppermute | solution.py:424
  45.2 1.3 collective-permute-start.16
  46.6 2.5 %collective-permute-done.12.refs_10_ = bf16[2,64,1152]{2,1,0:T(8,128)(2,1)} collective-permute-done((bf16[2,64,1152]{2,1,0:T(8,128)(2,1)}, bf16[2,64,1152]{2,1,0:T(8,128)(2,1)}, u32[]{:S(2)}, u32[]{:S(2)}) %collective-permute-start.12) | collective-permute-done | bytes 294944 | tf_op jit(solution)/shard_map/ppermute | solution.py:424
  49.1 0.3 multiply_reduce_fusion
  49.4 1.3 copy.17
  50.7 0.5 multiply_add_fusion.1.place_a
  51.2 0.0 collective-permute-done.17.refs_14_
  51.2 0.0 collective-permute-done.7.refs_5_
  51.2 2.2 %collective-permute-done.16.refs_13_ = bf16[2,64,1152]{2,1,0:T(8,128)(2,1)} collective-permute-done((bf16[2,64,1152]{2,1,0:T(8,128)(2,1)}, bf16[2,64,1152]{2,1,0:T(8,128)(2,1)}, u32[]{:S(2)}, u32[]{:S(2)}) %collective-permute-start.16) | collective-permute-done | bytes 294944 | tf_op jit(solution)/shard_map/ppermute | solution.py:424
  53.5 2.7 %collective-permute-done.14.refs_12_ = bf16[2,64,1152]{2,1,0:T(8,128)(2,1)} collective-permute-done((bf16[2,64,1152]{2,1,0:T(8,128)(2,1)}, bf16[2,64,1152]{2,1,0:T(8,128)(2,1)}, u32[]{:S(2)}, u32[]{:S(2)}) %collective-permute-start.14) | collective-permute-done | bytes 294944 | tf_op jit(solution)/shard_map/ppermute | solution.py:424
  56.1 5.9 %prepare.1 = (f32[512,1024]{1,0:T(8,128)}, bf16[512,1024]{1,0:T(8,128)(2,1)}) custom-call(s32[4]{0:T(128)} %multiply_add_fusion.1.place_a, s32[4]{0:T(128)} %get-tuple-element.15.place_b, bf16[2,64,1152]{2,1,0:T(8,128)(2,1)} %pad_maximum_fusion.refs_0_, bf16[2,64,1152]{2,1,0:T(8,128)(2,1)} %copy-done.6, bf16[2,64,1152]{2,1,0:T(8,128)(2,1)} %collective-permute-done.3.refs_2_, ...), custom_call_target="tpu_custom_call" | custom-call | tf_op jit(solution)/shard_map/prepare/pallas_call | solution.py:84
  62.0 16.6 %all-gather.2.cloned.1.call-done.weights = bf16[1024,5120]{1,0:T(8,128)(2,1)} async-done(((bf16[64,5120]{1,0:T(8,128)(2,1)}), bf16[1024,5120]{1,0:T(8,128)(2,1)}) %all-gather.2.cloned.1.call-update) | async-done | bytes 10485776 | tf_op jit(solution)/shard_map/all_gather | solution.py:490
  78.6 16.0 %attention.1 = (f32[4,1,128]{2,1,0:T(1,128)}, f32[4,1,128]{2,1,0:T(1,128)S(1)}, bf16[1,512,1024]{2,1,0:T(8,128)(2,1)S(1)}, bf16[16,8,16,256]{3,2,1,0:T(8,128)(2,1)S(1)}) custom-call(s32[4]{0:T(128)S(1)} %copy-done.4, s32[1]{0:T(128)} %bitcast.core, bf16[512,1024]{1,0:T(8,128)(2,1)} %get-tuple-element.9.normed, f32[512,1024]{1,0:T(8,128)} %get-tuple-element.10.base, ...), custom_call_target="tpu_custom_call" | custom-call | tf_op jit(solution)/shard_map/attention/pallas_call | solution.py:360
  94.7 0.3 collective-permute-start.18
  95.0 0.8 gradient.1
  95.8 1.6 %collective-permute-done.18 = bf16[16,8,16,256]{3,2,1,0:T(8,128)(2,1)S(1)} collective-permute-done((bf16[16,8,16,256]{3,2,1,0:T(8,128)(2,1)S(1)}, bf16[16,8,16,256]{3,2,1,0:T(8,128)(2,1)S(1)}, u32[]{:S(2)}, u32[]{:S(2)}) %collective-permute-start.18) | collective-permute-done | bytes 1048608 | tf_op jit(solution)/shard_map/ppermute | solution.py:533
  97.4 0.3 add_convert_fusion
  97.7 22.4 %all_to_all.15 = bf16[16,8,16,256]{3,2,1,0:T(8,128)(2,1)} all-to-all(bf16[16,8,16,256]{3,2,1,0:T(8,128)(2,1)S(1)} %add_convert_fusion), channel_id=1, replica_groups=mesh['user'=16,'loader'=16] {'user'}, dimensions={0} | all-to-all | bytes 2097152 | tf_op jit(solution)/shard_map/all_to_all | solution.py:537
  120.2 1.4 reduce_sum.34
  121.6 12.4 %all_to_all.16 = bf16[8,16,256]{2,1,0:T(8,128)(2,1)S(1)} all-to-all(bf16[8,16,256]{2,1,0:T(8,128)(2,1)S(1)} %reduce_sum.34), channel_id=1, replica_groups={{0,2,4,6,8,10,12,14},{1,3,5,7,9,11,13,15},{16,18,20,22,24,26,28,30},{17..., dimensions={0} | all-to-all | bytes 131072 | tf_op jit(solution)/shard_map/all_to_all | solution.py:540
  134.0 0.7 broadcast_in_dim.34
  134.7 5.7 %all-to-all-start.2 = ((bf16[16,16,256]{2,1,0:T(8,128)(2,1)}), bf16[16,16,256]{2,1,0:T(8,128)(2,1)S(1)}, u32[]{:S(2)}, u32[]{:S(2)}) async-start(bf16[16,16,256]{2,1,0:T(8,128)(2,1)} %broadcast_in_dim.34), calls=%async_computation.2 | async-start | bytes 262144 | tf_op jit(solution)/shard_map/all_to_all | solution.py:542
  140.4 2.3 %add_convert_fusion.1 = bf16[512,1024]{1,0:T(8,128)(2,1)} fusion(bf16[1024,1024]{1,0:T(8,128)(2,1)S(1)} %copy-done, f32[1024]{0:T(1024)S(1)} %copy-done.10, f32[512]{0:T(512)S(1)} %bitcast.58, bf16[1,512,1024]{2,1,0:T(8,128)(2,1)S(1)} %get-tuple-element.13), kind=kOutput, calls=%fused_computation.1 | convolution fusion | flops 1075314688 | bytes 4200448 | tf_op jit(solution)/shard_map/dot_general | solution.py:547
  142.6 4.2 %all-to-all-done.2.pieces = bf16[16,16,256]{2,1,0:T(8,128)(2,1)S(1)} async-done(((bf16[16,16,256]{2,1,0:T(8,128)(2,1)}), bf16[16,16,256]{2,1,0:T(8,128)(2,1)S(1)}, u32[]{:S(2)}, u32[]{:S(2)}) %all-to-all-start.2) | async-done | bytes 131104 | tf_op jit(solution)/shard_map/all_to_all | solution.py:542
  146.8 0.6 copy-done.7
  147.5 1.6 %assemble.1 = f32[64,1024]{1,0:T(8,128)} custom-call(bf16[16,16,256]{2,1,0:T(8,128)(2,1)} %copy-done.7), custom_call_target="tpu_custom_call" | custom-call | tf_op jit(solution)/shard_map/assemble/pallas_call | solution.py:463
  (29 shorter events, 0.2 us)
Async XLA Ops:
  7.2 31.8 %copy-start = (bf16[1024,1024]{1,0:T(8,128)(2,1)S(1)}, bf16[1024,1024]{1,0:T(8,128)(2,1)}, u32[]{:S(2)}) copy-start(bf16[1024,1024]{1,0:T(8,128)(2,1)} %param.19) | copy-start | bytes 6291460
  7.2 71.4 %all-gather.2.cloned.1.call-start = ((), (), s32[]{:S(2)}) async-start(), calls=%async_computation.3 | async-start | bytes 11141120 | tf_op jit(solution)/shard_map/all_gather | solution.py:490
  9.4 29.6 %copy-start.5 = (bf16[4,128,1024]{2,1,0:T(8,128)(2,1)S(1)}, bf16[4,128,1024]{2,1,0:T(8,128)(2,1)}, u32[]{:S(2)}) copy-start(bf16[4,128,1024]{2,1,0:T(8,128)(2,1)} %param.22) | copy-start | bytes 3145732
  12.0 7.4 %collective-permute-start.1 = (bf16[64,1152]{1,0:T(8,128)(2,1)S(1)}, bf16[64,1152]{1,0:T(8,128)(2,1)S(1)}, u32[]{:S(2)}, u32[]{:S(2)}) collective-permute-start(bf16[64,1152]{1,0:T(8,128)(2,1)S(1)} %get-tuple-element.21), channel_id=1, source_target_pairs={{128,0},{144,16},{160,32},{176,48},{192,64},{208,80},{224,96},{240... | collective-permute-start | bytes 442376 | tf_op jit(solution)/shard_map/ppermute | solution.py:424
  14.2 8.2 %collective-permute-start.2 = (bf16[64,1152]{1,0:T(8,128)(2,1)S(1)}, bf16[64,1152]{1,0:T(8,128)(2,1)S(1)}, u32[]{:S(2)}, u32[]{:S(2)}) collective-permute-start(bf16[64,1152]{1,0:T(8,128)(2,1)S(1)} %get-tuple-element.21), channel_id=1, source_target_pairs={{192,0},{208,16},{224,32},{240,48},{0,64},{16,80},{32,96},{48,112}... | collective-permute-start | bytes 442376 | tf_op jit(solution)/shard_map/ppermute | solution.py:424
  15.8 12.9 %collective-permute-start.10 = (bf16[64,1152]{1,0:T(8,128)(2,1)S(1)}, bf16[64,1152]{1,0:T(8,128)(2,1)S(1)}, u32[]{:S(2)}, u32[]{:S(2)}) collective-permute-start(bf16[64,1152]{1,0:T(8,128)(2,1)S(1)} %get-tuple-element.20), channel_id=1, source_target_pairs={{32,0},{48,16},{0,32},{16,48},{96,64},{112,80},{64,96},{80,112},{1... | collective-permute-start | bytes 442376 | tf_op jit(solution)/shard_map/ppermute | solution.py:424
  17.4 15.3 %collective-permute-start.9 = (bf16[64,1152]{1,0:T(8,128)(2,1)S(1)}, bf16[64,1152]{1,0:T(8,128)(2,1)S(1)}, u32[]{:S(2)}, u32[]{:S(2)}) collective-permute-start(bf16[64,1152]{1,0:T(8,128)(2,1)S(1)} %get-tuple-element.20), channel_id=1, source_target_pairs={{16,0},{32,16},{48,32},{0,48},{80,64},{96,80},{112,96},{64,112},{1... | collective-permute-start | bytes 442376 | tf_op jit(solution)/shard_map/ppermute | solution.py:424
  18.5 10.3 %collective-permute-start.11 = (bf16[64,1152]{1,0:T(8,128)(2,1)S(1)}, bf16[64,1152]{1,0:T(8,128)(2,1)S(1)}, u32[]{:S(2)}, u32[]{:S(2)}) collective-permute-start(bf16[64,1152]{1,0:T(8,128)(2,1)S(1)} %get-tuple-element.20), channel_id=1, source_target_pairs={{48,0},{0,16},{16,32},{32,48},{112,64},{64,80},{80,96},{96,112},{1... | collective-permute-start | bytes 442376 | tf_op jit(solution)/shard_map/ppermute | solution.py:424
  19.4 5.5 %collective-permute-start = (bf16[64,1152]{1,0:T(8,128)(2,1)S(1)}, bf16[64,1152]{1,0:T(8,128)(2,1)S(1)}, u32[]{:S(2)}, u32[]{:S(2)}) collective-permute-start(bf16[64,1152]{1,0:T(8,128)(2,1)S(1)} %get-tuple-element.21), channel_id=1, source_target_pairs={{64,0},{80,16},{96,32},{112,48},{128,64},{144,80},{160,96},{176,11... | collective-permute-start | bytes 442376 | tf_op jit(solution)/shard_map/ppermute | solution.py:424
  22.4 18.8 %copy-start.6 = (bf16[2,64,1152]{2,1,0:T(8,128)(2,1)}, bf16[2,64,1152]{2,1,0:T(8,128)(2,1)S(1)}, u32[]{:S(2)}) copy-start(bf16[2,64,1152]{2,1,0:T(8,128)(2,1)S(1)} %pad_maximum_fusion.1.refs_1_) | copy-start | bytes 884740
  22.4 13.0 %collective-permute-start.6 = (bf16[2,64,1152]{2,1,0:T(8,128)(2,1)S(1)}, bf16[2,64,1152]{2,1,0:T(8,128)(2,1)S(1)}, u32[]{:S(2)}, u32[]{:S(2)}) collective-permute-start(bf16[2,64,1152]{2,1,0:T(8,128)(2,1)S(1)} %pad_maximum_fusion.1.refs_1_), channel_id=1, source_target_pairs={{48,0},{0,16},{16,32},{32,48},{112,64},{64,80},{80,96},{96,112},{1... | collective-permute-start | bytes 884744 | tf_op jit(solution)/shard_map/ppermute | solution.py:424
  24.9 10.5 %collective-permute-start.4 = (bf16[2,64,1152]{2,1,0:T(8,128)(2,1)S(1)}, bf16[2,64,1152]{2,1,0:T(8,128)(2,1)S(1)}, u32[]{:S(2)}, u32[]{:S(2)}) collective-permute-start(bf16[2,64,1152]{2,1,0:T(8,128)(2,1)S(1)} %pad_maximum_fusion.1.refs_1_), channel_id=1, source_target_pairs={{16,0},{32,16},{48,32},{0,48},{80,64},{96,80},{112,96},{64,112},{1... | collective-permute-start | bytes 884744 | tf_op jit(solution)/shard_map/ppermute | solution.py:424
  28.7 13.0 %collective-permute-start.8 = (bf16[2,64,1152]{2,1,0:T(8,128)(2,1)}, bf16[2,64,1152]{2,1,0:T(8,128)(2,1)}, u32[]{:S(2)}, u32[]{:S(2)}) collective-permute-start(bf16[2,64,1152]{2,1,0:T(8,128)(2,1)} %pad_maximum_fusion.refs_0_), channel_id=1, source_target_pairs={{48,0},{0,16},{16,32},{32,48},{112,64},{64,80},{80,96},{96,112},{1... | collective-permute-start | bytes 884744 | tf_op jit(solution)/shard_map/ppermute | solution.py:424
  28.7 13.0 %collective-permute-start.3 = (bf16[2,64,1152]{2,1,0:T(8,128)(2,1)}, bf16[2,64,1152]{2,1,0:T(8,128)(2,1)}, u32[]{:S(2)}, u32[]{:S(2)}) collective-permute-start(bf16[2,64,1152]{2,1,0:T(8,128)(2,1)} %pad_maximum_fusion.refs_0_), channel_id=1, source_target_pairs={{16,0},{32,16},{48,32},{0,48},{80,64},{96,80},{112,96},{64,112},{1... | collective-permute-start | bytes 884744 | tf_op jit(solution)/shard_map/ppermute | solution.py:424
  32.7 9.4 %collective-permute-start.15 = (bf16[2,64,1152]{2,1,0:T(8,128)(2,1)}, bf16[2,64,1152]{2,1,0:T(8,128)(2,1)}, u32[]{:S(2)}, u32[]{:S(2)}) collective-permute-start(bf16[2,64,1152]{2,1,0:T(8,128)(2,1)} %pad_maximum_fusion.3.refs_9_), channel_id=1, source_target_pairs={{192,0},{208,16},{224,32},{240,48},{0,64},{16,80},{32,96},{48,112}... | collective-permute-start | bytes 884744 | tf_op jit(solution)/shard_map/ppermute | solution.py:424
  35.5 20.7 %copy-start.8 = (bf16[2,64,1152]{2,1,0:T(8,128)(2,1)}, bf16[2,64,1152]{2,1,0:T(8,128)(2,1)S(1)}, u32[]{:S(2)}) copy-start(bf16[2,64,1152]{2,1,0:T(8,128)(2,1)S(1)} %collective-permute-done.6.refs_7_) | copy-start | bytes 884740
  35.5 9.8 %collective-permute-start.13 = (bf16[2,64,1152]{2,1,0:T(8,128)(2,1)}, bf16[2,64,1152]{2,1,0:T(8,128)(2,1)}, u32[]{:S(2)}, u32[]{:S(2)}) collective-permute-start(bf16[2,64,1152]{2,1,0:T(8,128)(2,1)} %pad_maximum_fusion.3.refs_9_), channel_id=1, source_target_pairs={{64,0},{80,16},{96,32},{112,48},{128,64},{144,80},{160,96},{176,11... | collective-permute-start | bytes 884744 | tf_op jit(solution)/shard_map/ppermute | solution.py:424
  35.5 0.7 copy-start.9
  36.2 12.9 %collective-permute-start.12 = (bf16[2,64,1152]{2,1,0:T(8,128)(2,1)}, bf16[2,64,1152]{2,1,0:T(8,128)(2,1)}, u32[]{:S(2)}, u32[]{:S(2)}) collective-permute-start(bf16[2,64,1152]{2,1,0:T(8,128)(2,1)} %pad_maximum_fusion.2.refs_8_), channel_id=1, source_target_pairs={{64,0},{80,16},{96,32},{112,48},{128,64},{144,80},{160,96},{176,11... | collective-permute-start | bytes 884744 | tf_op jit(solution)/shard_map/ppermute | solution.py:424
  38.9 2.3 %copy-start.11 = (s32[4,1]{0,1:T(1,128)S(1)}, s32[4,1]{0,1:T(1,128)}, u32[]{:S(2)}) copy-start(s32[4,1]{0,1:T(1,128)} %param.23) | copy-start | bytes 52
  38.9 10.2 %copy-start.10 = (f32[1024]{0:T(1024)S(1)}, f32[1024]{0:T(1024)}, u32[]{:S(2)}) copy-start(f32[1024]{0:T(1024)} %param.21) | copy-start | bytes 12292
  41.7 9.5 %collective-permute-start.17 = (bf16[2,64,1152]{2,1,0:T(8,128)(2,1)}, bf16[2,64,1152]{2,1,0:T(8,128)(2,1)}, u32[]{:S(2)}, u32[]{:S(2)}) collective-permute-start(bf16[2,64,1152]{2,1,0:T(8,128)(2,1)} %pad_maximum_fusion.2.refs_8_), channel_id=1, source_target_pairs={{192,0},{208,16},{224,32},{240,48},{0,64},{16,80},{32,96},{48,112}... | collective-permute-start | bytes 884744 | tf_op jit(solution)/shard_map/ppermute | solution.py:424
  41.7 9.5 %collective-permute-start.7 = (bf16[2,64,1152]{2,1,0:T(8,128)(2,1)S(1)}, bf16[2,64,1152]{2,1,0:T(8,128)(2,1)}, u32[]{:S(2)}, u32[]{:S(2)}) collective-permute-start(bf16[2,64,1152]{2,1,0:T(8,128)(2,1)S(1)} %collective-permute-done.6.refs_7_), channel_id=1, source_target_pairs={{48,0},{0,16},{16,32},{32,48},{112,64},{64,80},{80,96},{96,112},{1... | collective-permute-start | bytes 884744 | tf_op jit(solution)/shard_map/ppermute | solution.py:424
  42.1 9.1 %collective-permute-start.5 = (bf16[2,64,1152]{2,1,0:T(8,128)(2,1)}, bf16[2,64,1152]{2,1,0:T(8,128)(2,1)}, u32[]{:S(2)}, u32[]{:S(2)}) collective-permute-start(bf16[2,64,1152]{2,1,0:T(8,128)(2,1)} %collective-permute-done.3.refs_2_), channel_id=1, source_target_pairs={{16,0},{32,16},{48,32},{0,48},{80,64},{96,80},{112,96},{64,112},{1... | collective-permute-start | bytes 884744 | tf_op jit(solution)/shard_map/ppermute | solution.py:424
  45.2 8.2 %collective-permute-start.16 = (bf16[2,64,1152]{2,1,0:T(8,128)(2,1)}, bf16[2,64,1152]{2,1,0:T(8,128)(2,1)}, u32[]{:S(2)}, u32[]{:S(2)}) collective-permute-start(bf16[2,64,1152]{2,1,0:T(8,128)(2,1)} %collective-permute-done.15.refs_15_), channel_id=1, source_target_pairs={{192,0},{208,16},{224,32},{240,48},{0,64},{16,80},{32,96},{48,112}... | collective-permute-start | bytes 884744 | tf_op jit(solution)/shard_map/ppermute | solution.py:424
  49.1 7.0 %collective-permute-start.14 = (bf16[2,64,1152]{2,1,0:T(8,128)(2,1)}, bf16[2,64,1152]{2,1,0:T(8,128)(2,1)}, u32[]{:S(2)}, u32[]{:S(2)}) collective-permute-start(bf16[2,64,1152]{2,1,0:T(8,128)(2,1)} %collective-permute-done.12.refs_10_), channel_id=1, source_target_pairs={{64,0},{80,16},{96,32},{112,48},{128,64},{144,80},{160,96},{176,11... | collective-permute-start | bytes 884744 | tf_op jit(solution)/shard_map/ppermute | solution.py:424
  56.1 22.5 %copy-start.2 = (f32[1024]{0:T(1024)S(1)}, f32[1024]{0:T(1024)}, u32[]{:S(2)}) copy-start(f32[1024]{0:T(1024)} %param.20) | copy-start | bytes 12292
  56.1 22.5 %copy-start.3 = (f32[4,128]{1,0:T(4,128)S(1)}, f32[4,128]{1,0:T(4,128)}, u32[]{:S(2)}) copy-start(f32[4,128]{1,0:T(4,128)} %param.25) | copy-start | bytes 6148
  56.1 22.5 %copy-start.4 = (s32[4]{0:T(128)S(1)}, s32[4]{0:T(128)}, u32[]{:S(2)}) copy-start(s32[4]{0:T(128)} %counts.1) | copy-start | bytes 52
  78.6 16.4 %copy-start.1 = (bf16[512,1024]{0,1:T(8,128)(2,1)S(1)}, bf16[512,1024]{0,1:T(8,128)(2,1)}, u32[]{:S(2)}) copy-start(bf16[512,1024]{0,1:T(8,128)(2,1)} %copy.17) | copy-start | bytes 3145732
  94.7 2.7 %collective-permute-start.18 = (bf16[16,8,16,256]{3,2,1,0:T(8,128)(2,1)S(1)}, bf16[16,8,16,256]{3,2,1,0:T(8,128)(2,1)S(1)}, u32[]{:S(2)}, u32[]{:S(2)}) collective-permute-start(bf16[16,8,16,256]{3,2,1,0:T(8,128)(2,1)S(1)} %get-tuple-element.14), channel_id=1, source_target_pairs={{0,1},{1,0},{2,3},{3,2},{4,5},{5,4},{6,7},{7,6},{8,9},{9,8},{10,11... | collective-permute-start | bytes 3145736 | tf_op jit(solution)/shard_map/ppermute | solution.py:533
  134.7 12.1 %all-to-all-start.2 = ((bf16[16,16,256]{2,1,0:T(8,128)(2,1)}), bf16[16,16,256]{2,1,0:T(8,128)(2,1)S(1)}, u32[]{:S(2)}, u32[]{:S(2)}) async-start(bf16[16,16,256]{2,1,0:T(8,128)(2,1)} %broadcast_in_dim.34), calls=%async_computation.2 | async-start | bytes 262144 | tf_op jit(solution)/shard_map/all_to_all | solution.py:542
  146.8 0.7 copy-start.7
Sparse Core Ops, SparseCore 0:
  9.8 68.7 all-gather.1
